TPU v7x, 256 devices: a whole 4x4x8 slice. The times are simulated.
256 devices in a mesh: tm: 4 (over y_lo, core), space: 64 (over z, x, y_hi).
Axes of the slice: x: 4, y: 4 (y_hi: 2, y_lo: 2; y = y_hi * 2 + y_lo), z: 8, core: 2. Of those that a mesh axis runs over, the one named last changes fastest.
Arguments:
- slab_states: float32 [4, 2, 512, 32, 512], P('tm', None, 'space'), may hold values from -6 to 6
- velocity: float32 [2, 3, 512, 32, 512], P(None, None, 'space'), may hold values from -0.9 to 0.9
- snap_of_step: int32 [4, 2], P('tm'), may hold values from 0 to 1
Outputs:
- slab_starts: float32 [4, 2, 512, 32, 512], P('tm', None, 'space')
- heater_grad: float32 [512, 32, 512], P('space', 'tm')
All inputs are finite; a program needn't handle non-finite values.
Results may differ from a plain program's by a relative error of at most 0.00002.
Values sent between devices are 32-bit elements; how exact they have to be, the bound alone decides.
No kernel may reach another device: no remote copies, remote signals or barrier semaphores. Data moves between devices by JAX's collectives and lax.ppermute only.
A program may use at most 64 MiB of HBM per device.

v0:
```python
import jax
import jax.numpy as jnp
from jax import lax
from jax.sharding import PartitionSpec as P

coupling = 0.3


def with_halo(array, sides, width):
    for axis, dim in sides:
        devices, length = (lax.axis_size(axis), array.shape[dim])
        up = [(i, (i + 1) % devices) for i in range(devices - 1)]
        down = [(j, i) for i, j in up]
        last = lax.slice_in_dim(array, length - width, length, axis=dim)
        first = lax.slice_in_dim(array, 0, width, axis=dim)
        before = lax.ppermute(last, axis, up)
        after = lax.ppermute(first, axis, down)
        array = jnp.concatenate([before, array, after], axis=dim)
    return array


def passed_along(array, axis, by):
    devices = lax.axis_size(axis)
    pairs = [(i, i + by) for i in range(devices) if 0 <= i + by < devices]
    return lax.ppermute(array, axis, pairs)


def advance(widened, flow):
    centre = widened[:, 1:-1]
    east_side = widened[:, 2:]
    west_side = widened[:, :-2]
    north_side = jnp.pad(centre, ((0, 0), (0, 0), (0, 1), (0, 0)))[:, :, 1:]
    south_side = jnp.pad(centre, ((0, 0), (0, 0), (1, 0), (0, 0)))[:, :, :-1]
    upper_side = jnp.pad(centre, ((0, 0), (0, 0), (0, 0), (0, 1)))[:, :, :, 1:]
    lower_side = jnp.pad(centre, ((0, 0), (0, 0), (0, 0), (1, 0)))[:, :, :, :-1]
    laplace = (
        east_side + west_side + north_side + south_side + upper_side + lower_side - 6.0 * centre
    )
    transport = (
        flow[0] * (east_side - west_side)
        + flow[1] * (north_side - south_side)
        + flow[2] * (upper_side - lower_side)
    )
    temper = centre[0] + 0.14 * laplace[0] + 0.25 * transport[0] + coupling * centre[1]
    dopant = centre[1] + 0.06 * laplace[1] + 0.25 * transport[1]
    return jnp.stack([temper, dopant])


def sweep_local(adjoint, flow_bank, snaps, keep_total):
    steps_count = snaps.shape[0]
    total = jnp.zeros(adjoint.shape[1:], jnp.float32)
    for step_index in reversed(range(steps_count)):
        flow = lax.dynamic_index_in_dim(flow_bank, snaps[step_index], 0, keepdims=False)
        widened = with_halo(adjoint, (("space", 1),), 1)
        adjoint = advance(widened, flow)
        if keep_total:
            total = total + adjoint[0]
    return (adjoint, total)


def body(slab_states, velocity, snap_of_step):
    start = slab_states[0]
    snaps = snap_of_step[0]
    first, unused = sweep_local(start, velocity, snaps, False)
    received = passed_along(first, "tm", -1)
    is_last = lax.axis_index("tm") == lax.axis_size("tm") - 1
    carried = jnp.where(is_last, start, received)
    final, total = sweep_local(carried, velocity, snaps, True)
    gradient = lax.psum_scatter(total, "tm", scatter_dimension=1, tiled=True) / snaps.shape[0]
    return (final[None], gradient)


def solution(mesh):
    placed = (P("tm", None, "space", None, None), P(None, None, "space", None, None), P("tm", None))
    return jax.shard_map(
        body,
        mesh=mesh,
        in_specs=placed,
        out_specs=(P("tm", None, "space", None, None), P("space", "tm", None)),
        check_vma=False,
    )
```

profile of v0, /device:TPU:1, one launch (start us, length us, event | category | flops | bytes accessed | tf_op | source)
XLA Modules:
  0.0 135.3 jit_solution(15455665915636987420)
XLA Ops:
  7.2 1.0 fusion.23
  8.2 1.3 collective-permute-start
  9.5 6.3 %collective-permute-start.1 = (f32[2,1,32,512]{3,2,1,0:T(8,128)S(1)}, f32[2,1,32,512]{3,2,1,0:T(8,128)S(1)}, u32[]{:S(2)}, u32[]{:S(2)}) collective-permute-start(f32[2,1,32,512]{3,2,1,0:T(8,128)S(1)} %get-tuple-element.22), channel_id=1, source_target_pairs={{0,1},{1,2},{2,3},{3,4},{4,5},{5,6},{6,7},{7,8},{8,9},{9,10},{10,1... | collective-permute-start | bytes 393224 | tf_op jit(solution)/shard_map/ppermute | solution.py:16
  15.8 1.3 fusion.24
  21.0 2.3 %dynamic-slice_bitcast_fusion.2 = (f32[8,32,512]{2,1,0:T(8,128)S(1)}, f32[8,32,512]{2,1,0:T(8,128)S(1)}, f32[8,32,512]{2,1,0:T(8,128)S(1)}, f32[8,32,512]{2,1,0:...) fusion(f32[2,3,8,32,512]{4,3,2,1,0:T(8,128)} %param.4, s32[]{:T(128)S(6)} %select_n.19, s32[]{:T(128)S(6)} %add.292, ...), kind=kLoop, calls=%fused_computation.72 | loop fusion | bytes 6291472 | tf_op jit(solution)/shard_map/mul | solution.py:40
  25.4 1.3 collective-permute-start.2
  26.7 6.4 %collective-permute-start.3 = (f32[2,1,32,512]{3,2,1,0:T(8,128)S(1)}, f32[2,1,32,512]{3,2,1,0:T(8,128)S(1)}, u32[]{:S(2)}, u32[]{:S(2)}) collective-permute-start(f32[2,1,32,512]{3,2,1,0:T(8,128)S(1)} %get-tuple-element.20), channel_id=1, source_target_pairs={{0,1},{1,2},{2,3},{3,4},{4,5},{5,6},{6,7},{7,8},{8,9},{9,10},{10,1... | collective-permute-start | bytes 393224 | tf_op jit(solution)/shard_map/ppermute | solution.py:16
  33.5 3.5 %collective-permute-done.3 = f32[2,1,32,512]{3,2,1,0:T(8,128)S(1)} collective-permute-done((f32[2,1,32,512]{3,2,1,0:T(8,128)S(1)}, f32[2,1,32,512]{3,2,1,0:T(8,128)S(1)}, u32[]{:S(2)}, u32[]{:S(2)}) %collective-permute-start.3) | collective-permute-done | bytes 131104 | tf_op jit(solution)/shard_map/ppermute | solution.py:16
  39.1 1.1 pad_maximum_fusion.14
  40.1 3.4 %collective-permute-start.4 = (f32[2,8,32,512]{3,2,1,0:T(8,128)}, f32[2,8,32,512]{3,2,1,0:T(8,128)}, u32[]{:S(2)}, u32[]{:S(2)}) collective-permute-start(f32[2,8,32,512]{3,2,1,0:T(8,128)} %pad_maximum_fusion.14), channel_id=1, source_target_pairs={{64,0},{128,64},{192,128},{65,1},{129,65},{193,129},{66,2},{130,66... | collective-permute-start | bytes 3145736 | tf_op jit(solution)/shard_map/ppermute | solution.py:25
  43.6 15.9 %collective-permute-done.4 = f32[2,8,32,512]{3,2,1,0:T(8,128)} collective-permute-done((f32[2,8,32,512]{3,2,1,0:T(8,128)}, f32[2,8,32,512]{3,2,1,0:T(8,128)}, u32[]{:S(2)}, u32[]{:S(2)}) %collective-permute-start.4) | collective-permute-done | bytes 1048608 | tf_op jit(solution)/shard_map/ppermute | solution.py:25
  59.4 1.4 %broadcast_select_fusion = f32[2,8,32,512]{3,2,1,0:T(8,128)S(1)} fusion(f32[2,8,32,512]{3,2,1,0:T(8,128)} %collective-permute-done.4, pred[]{:T(512)S(6)} %eq.3, f32[1,2,8,32,512]{4,3,2,1,0:T(8,128)S(1)} %copy-done), kind=kLoop, calls=%fused_computation.93 | loop fusion | flops 262144 | bytes 3145729 | tf_op jit(solution)/shard_map/jit(_where)/select_n | solution.py:67
  60.9 1.4 %collective-permute-start.5 = (f32[2,1,32,512]{3,2,1,0:T(8,128)S(1)}, f32[2,1,32,512]{3,2,1,0:T(8,128)S(1)}, u32[]{:S(2)}, u32[]{:S(2)}) collective-permute-start(f32[2,1,32,512]{3,2,1,0:T(8,128)S(1)} %get-tuple-element.19), channel_id=1, source_target_pairs={{1,0},{2,1},{3,2},{4,3},{5,4},{6,5},{7,6},{8,7},{9,8},{10,9},{11,1... | collective-permute-start | bytes 393224 | tf_op jit(solution)/shard_map/ppermute | solution.py:17
  62.4 5.5 %collective-permute-start.6 = (f32[2,1,32,512]{3,2,1,0:T(8,128)S(1)}, f32[2,1,32,512]{3,2,1,0:T(8,128)S(1)}, u32[]{:S(2)}, u32[]{:S(2)}) collective-permute-start(f32[2,1,32,512]{3,2,1,0:T(8,128)S(1)} %get-tuple-element.18), channel_id=1, source_target_pairs={{0,1},{1,2},{2,3},{3,4},{4,5},{5,6},{6,7},{7,8},{8,9},{9,10},{10,1... | collective-permute-start | bytes 393224 | tf_op jit(solution)/shard_map/ppermute | solution.py:16
  67.9 1.5 %collective-permute-done.5 = f32[2,1,32,512]{3,2,1,0:T(8,128)S(1)} collective-permute-done((f32[2,1,32,512]{3,2,1,0:T(8,128)S(1)}, f32[2,1,32,512]{3,2,1,0:T(8,128)S(1)}, u32[]{:S(2)}, u32[]{:S(2)}) %collective-permute-start.5) | collective-permute-done | bytes 131104 | tf_op jit(solution)/shard_map/ppermute | solution.py:17
  69.3 4.1 %collective-permute-done.6 = f32[2,1,32,512]{3,2,1,0:T(8,128)S(1)} collective-permute-done((f32[2,1,32,512]{3,2,1,0:T(8,128)S(1)}, f32[2,1,32,512]{3,2,1,0:T(8,128)S(1)}, u32[]{:S(2)}, u32[]{:S(2)}) %collective-permute-start.6) | collective-permute-done | bytes 131104 | tf_op jit(solution)/shard_map/ppermute | solution.py:16
  75.2 1.4 %collective-permute-start.7 = (f32[2,1,32,512]{3,2,1,0:T(8,128)S(1)}, f32[2,1,32,512]{3,2,1,0:T(8,128)S(1)}, u32[]{:S(2)}, u32[]{:S(2)}) collective-permute-start(f32[2,1,32,512]{3,2,1,0:T(8,128)S(1)} %get-tuple-element.17), channel_id=1, source_target_pairs={{1,0},{2,1},{3,2},{4,3},{5,4},{6,5},{7,6},{8,7},{9,8},{10,9},{11,1... | collective-permute-start | bytes 393224 | tf_op jit(solution)/shard_map/ppermute | solution.py:17
  76.6 6.2 %collective-permute-start.8 = (f32[2,1,32,512]{3,2,1,0:T(8,128)S(1)}, f32[2,1,32,512]{3,2,1,0:T(8,128)S(1)}, u32[]{:S(2)}, u32[]{:S(2)}) collective-permute-start(f32[2,1,32,512]{3,2,1,0:T(8,128)S(1)} %get-tuple-element.16), channel_id=1, source_target_pairs={{0,1},{1,2},{2,3},{3,4},{4,5},{5,6},{6,7},{7,8},{8,9},{9,10},{10,1... | collective-permute-start | bytes 393224 | tf_op jit(solution)/shard_map/ppermute | solution.py:16
  83.3 1.9 %collective-permute-done.8 = f32[2,1,32,512]{3,2,1,0:T(8,128)S(1)} collective-permute-done((f32[2,1,32,512]{3,2,1,0:T(8,128)S(1)}, f32[2,1,32,512]{3,2,1,0:T(8,128)S(1)}, u32[]{:S(2)}, u32[]{:S(2)}) %collective-permute-start.8) | collective-permute-done | bytes 131104 | tf_op jit(solution)/shard_map/ppermute | solution.py:16
  85.1 0.8 multiply_add_fusion
  86.8 1.1 fusion.17
  88.2 1.1 maximum_bitcast_fusion
  89.3 37.6 %reduce-scatter.2.cloned.1.call-done = f32[8,8,512]{2,1,0:T(8,128)} async-done(((f32[8,32,512]{2,1,0:T(8,128)}), f32[8,8,512]{2,1,0:T(8,128)}) %reduce-scatter.2.cloned.1.call-update) | async-done | bytes 131088 | tf_op jit(solution)/shard_map/reduce_scatter | solution.py:69
  126.9 1.6 %broadcast_multiply_fusion = f32[8,8,512]{2,1,0:T(8,128)} fusion(f32[8,8,512]{2,1,0:T(8,128)} %reduce-scatter.2.cloned.1.call-done), kind=kLoop, calls=%fused_computation.98 | loop fusion | flops 32768 | bytes 262144 | tf_op jit(solution)/shard_map/div | solution.py:69
  (36 shorter events, 7.8 us)
Async XLA Ops:
  7.2 119.8 %reduce-scatter.2.cloned.1.call-start = ((), (), s32[]{:S(2)}) async-start(), calls=%async_computation.1 | async-start | bytes 655360 | tf_op jit(solution)/shard_map/reduce_scatter | solution.py:69
  8.2 15.1 %collective-permute-start = (f32[2,1,32,512]{3,2,1,0:T(8,128)S(1)}, f32[2,1,32,512]{3,2,1,0:T(8,128)S(1)}, u32[]{:S(2)}, u32[]{:S(2)}) collective-permute-start(f32[2,1,32,512]{3,2,1,0:T(8,128)S(1)} %get-tuple-element.23), channel_id=1, source_target_pairs={{1,0},{2,1},{3,2},{4,3},{5,4},{6,5},{7,6},{8,7},{9,8},{10,9},{11,1... | collective-permute-start | bytes 393224 | tf_op jit(solution)/shard_map/ppermute | solution.py:17
  9.5 13.8 %collective-permute-start.1 = (f32[2,1,32,512]{3,2,1,0:T(8,128)S(1)}, f32[2,1,32,512]{3,2,1,0:T(8,128)S(1)}, u32[]{:S(2)}, u32[]{:S(2)}) collective-permute-start(f32[2,1,32,512]{3,2,1,0:T(8,128)S(1)} %get-tuple-element.22), channel_id=1, source_target_pairs={{0,1},{1,2},{2,3},{3,4},{4,5},{5,6},{6,7},{7,8},{8,9},{9,10},{10,1... | collective-permute-start | bytes 393224 | tf_op jit(solution)/shard_map/ppermute | solution.py:16
  21.0 2.3 %copy-start = (f32[1,2,8,32,512]{4,3,2,1,0:T(8,128)S(1)}, f32[1,2,8,32,512]{4,3,2,1,0:T(8,128)}, u32[]{:S(2)}) copy-start(f32[1,2,8,32,512]{4,3,2,1,0:T(8,128)} %param.3) | copy-start | bytes 3145732
  23.3 0.8 copy-start.3
  23.3 1.0 copy-start.5
  23.3 14.5 %copy-start.1 = (f32[8,32,512]{2,1,0:T(8,128)}, f32[8,32,512]{2,1,0:T(8,128)S(1)}, u32[]{:S(2)}) copy-start(f32[8,32,512]{2,1,0:T(8,128)S(1)} %get-tuple-element.8) | copy-start | bytes 1572868
  25.4 8.1 %collective-permute-start.2 = (f32[2,1,32,512]{3,2,1,0:T(8,128)S(1)}, f32[2,1,32,512]{3,2,1,0:T(8,128)S(1)}, u32[]{:S(2)}, u32[]{:S(2)}) collective-permute-start(f32[2,1,32,512]{3,2,1,0:T(8,128)S(1)} %get-tuple-element.21), channel_id=1, source_target_pairs={{1,0},{2,1},{3,2},{4,3},{5,4},{6,5},{7,6},{8,7},{9,8},{10,9},{11,1... | collective-permute-start | bytes 393224 | tf_op jit(solution)/shard_map/ppermute | solution.py:17
  26.7 10.3 %collective-permute-start.3 = (f32[2,1,32,512]{3,2,1,0:T(8,128)S(1)}, f32[2,1,32,512]{3,2,1,0:T(8,128)S(1)}, u32[]{:S(2)}, u32[]{:S(2)}) collective-permute-start(f32[2,1,32,512]{3,2,1,0:T(8,128)S(1)} %get-tuple-element.20), channel_id=1, source_target_pairs={{0,1},{1,2},{2,3},{3,4},{4,5},{5,6},{6,7},{7,8},{8,9},{9,10},{10,1... | collective-permute-start | bytes 393224 | tf_op jit(solution)/shard_map/ppermute | solution.py:16
  40.1 19.3 %collective-permute-start.4 = (f32[2,8,32,512]{3,2,1,0:T(8,128)}, f32[2,8,32,512]{3,2,1,0:T(8,128)}, u32[]{:S(2)}, u32[]{:S(2)}) collective-permute-start(f32[2,8,32,512]{3,2,1,0:T(8,128)} %pad_maximum_fusion.14), channel_id=1, source_target_pairs={{64,0},{128,64},{192,128},{65,1},{129,65},{193,129},{66,2},{130,66... | collective-permute-start | bytes 3145736 | tf_op jit(solution)/shard_map/ppermute | solution.py:25
  60.9 13.1 %copy-start.4 = (f32[8,32,512]{2,1,0:T(8,128)S(1)}, f32[8,32,512]{2,1,0:T(8,128)}, u32[]{:S(2)}) copy-start(f32[8,32,512]{2,1,0:T(8,128)} %copy-done.3) | copy-start | bytes 1572868
  60.9 13.1 %copy-start.6 = (f32[8,32,512]{2,1,0:T(8,128)S(1)}, f32[8,32,512]{2,1,0:T(8,128)}, u32[]{:S(2)}) copy-start(f32[8,32,512]{2,1,0:T(8,128)} %copy-done.5) | copy-start | bytes 1572868
  60.9 8.4 %collective-permute-start.5 = (f32[2,1,32,512]{3,2,1,0:T(8,128)S(1)}, f32[2,1,32,512]{3,2,1,0:T(8,128)S(1)}, u32[]{:S(2)}, u32[]{:S(2)}) collective-permute-start(f32[2,1,32,512]{3,2,1,0:T(8,128)S(1)} %get-tuple-element.19), channel_id=1, source_target_pairs={{1,0},{2,1},{3,2},{4,3},{5,4},{6,5},{7,6},{8,7},{9,8},{10,9},{11,1... | collective-permute-start | bytes 393224 | tf_op jit(solution)/shard_map/ppermute | solution.py:17
  62.4 11.0 %collective-permute-start.6 = (f32[2,1,32,512]{3,2,1,0:T(8,128)S(1)}, f32[2,1,32,512]{3,2,1,0:T(8,128)S(1)}, u32[]{:S(2)}, u32[]{:S(2)}) collective-permute-start(f32[2,1,32,512]{3,2,1,0:T(8,128)S(1)} %get-tuple-element.18), channel_id=1, source_target_pairs={{0,1},{1,2},{2,3},{3,4},{4,5},{5,6},{6,7},{7,8},{8,9},{9,10},{10,1... | collective-permute-start | bytes 393224 | tf_op jit(solution)/shard_map/ppermute | solution.py:16
  75.2 10.0 %copy-start.2 = (f32[8,32,512]{2,1,0:T(8,128)S(1)}, f32[8,32,512]{2,1,0:T(8,128)}, u32[]{:S(2)}) copy-start(f32[8,32,512]{2,1,0:T(8,128)} %copy-done.1) | copy-start | bytes 1572868
  75.2 8.1 %collective-permute-start.7 = (f32[2,1,32,512]{3,2,1,0:T(8,128)S(1)}, f32[2,1,32,512]{3,2,1,0:T(8,128)S(1)}, u32[]{:S(2)}, u32[]{:S(2)}) collective-permute-start(f32[2,1,32,512]{3,2,1,0:T(8,128)S(1)} %get-tuple-element.17), channel_id=1, source_target_pairs={{1,0},{2,1},{3,2},{4,3},{5,4},{6,5},{7,6},{8,7},{9,8},{10,9},{11,1... | collective-permute-start | bytes 393224 | tf_op jit(solution)/shard_map/ppermute | solution.py:17
  76.6 8.5 %collective-permute-start.8 = (f32[2,1,32,512]{3,2,1,0:T(8,128)S(1)}, f32[2,1,32,512]{3,2,1,0:T(8,128)S(1)}, u32[]{:S(2)}, u32[]{:S(2)}) collective-permute-start(f32[2,1,32,512]{3,2,1,0:T(8,128)S(1)} %get-tuple-element.16), channel_id=1, source_target_pairs={{0,1},{1,2},{2,3},{3,4},{4,5},{5,6},{6,7},{7,8},{8,9},{9,10},{10,1... | collective-permute-start | bytes 393224 | tf_op jit(solution)/shard_map/ppermute | solution.py:16
Sparse Core Ops, SparseCore 0:
  88.0 38.9 reduce-scatter.1
where the time goes:
time: 136 us; the launch traced here: 135 us
  waiting for transfers between devices  65 us (48%)
  starting transfers between devices  33.3 us (24%)
  between operations  18.2 us (13%)
  other arithmetic  13.9 us (10%)
  local copies, waits for them, and re-layouts  4.93 us (4%)
    reduce_scatter x1, waiting for transfers between devices, body(): lax.psum_scatter(total, 'tm', scatter_dimension=1, tiled=True)  37.6 us
    ppermute x4, starting transfers between devices, with_halo(): before = lax.ppermute(last, axis, up)  24.4 us
    ppermute x1, waiting for transfers between devices, passed_along(): return lax.ppermute(array, axis, pairs)  15.9 us
    ppermute x4, waiting for transfers between devices, with_halo(): before = lax.ppermute(last, axis, up)  9.44 us
    ppermute x4, starting transfers between devices, with_halo(): after = lax.ppermute(first, axis, down)  5.43 us
    ppermute x1, starting transfers between devices, passed_along(): return lax.ppermute(array, axis, pairs)  3.44 us
    add x4, other arithmetic, advance(): flow[0] * (east_side - west_side) + flow[1] * (north_side - south_side)  3.06 us
    sub x4, other arithmetic, advance(): east_side + west_side + north_side + south_side + upper_side + lower_side  2.82 us
  transfers between devices with their start and end apart: 10, of which 8 were waited for; matrix products, arithmetic and copies ran while one was open for 4% of the time, Pallas kernels for 0%

commit v1 on v0

v1 whole, which is shorter than its diff:
```python
import functools

import jax
import jax.numpy as jnp
from jax import lax
from jax.experimental import pallas as pl
from jax.experimental.pallas import tpu as pltpu
from jax.sharding import PartitionSpec as P

coupling = 0.3
diffusion = (0.14, 0.06)
sub, lanes = 8, 128


def tiles(shape):
    rows, cols = shape
    return [(i, j) for i in range(rows // sub) for j in range(cols // lanes)]


def spot(i, j):
    return (pl.ds(i * sub, sub), pl.ds(j * lanes, lanes))


def neighbours(at, i, j, shape):
    rows, cols = shape
    centre = at(i, j)
    row = lax.broadcasted_iota(jnp.int32, (sub, lanes), 0)
    col = lax.broadcasted_iota(jnp.int32, (sub, lanes), 1)
    zero = jnp.zeros_like(centre)
    after = at(i + 1, j) if (i + 1) * sub < rows else zero
    before = at(i - 1, j) if i > 0 else zero
    north = pltpu.roll(jnp.where(row == 0, after, centre), sub - 1, 0)
    south = pltpu.roll(jnp.where(row == sub - 1, before, centre), 1, 0)
    after = at(i, j + 1) if (j + 1) * lanes < cols else zero
    before = at(i, j - 1) if j > 0 else zero
    upper = pltpu.roll(jnp.where(col == 0, after, centre), lanes - 1, 1)
    lower = pltpu.roll(jnp.where(col == lanes - 1, before, centre), 1, 1)
    return centre, (north + south) + (upper + lower), north - south, upper - lower


def advanced(fields, pairs, flow, i, j, shape):
    u, v, w = flow
    out, centres = [], []
    for f in (0, 1):
        centre, total, dy, dz = neighbours(functools.partial(fields, f), i, j, shape)
        side_sum, side_diff = pairs(f, i, j)
        c = diffusion[f]
        moved = u * side_diff + v * dy + w * dz
        out.append(((1.0 - 6.0 * c) * centre + c * (side_sum + total)) + 0.25 * moved)
        centres.append(centre)
    out[0] = out[0] + coupling * centres[1]
    return out


def layer_of(ref, l):
    return lambda f, i, j: ref[(f, l) + spot(i, j)]


def flow_of(velocity, snap, l):
    return lambda i, j: [velocity[(snap, d, l) + spot(i, j)] for d in range(3)]


def full_layer(below, here, above, flow, shape, store):
    def pairs(f, i, j):
        hi, lo = above(f, i, j), below(f, i, j)
        return hi + lo, hi - lo

    for i, j in tiles(shape):
        store(i, j, advanced(here, pairs, flow(i, j), i, j, shape))


def pack(state, velocity, snap, message, layer, inner, sign, shape):
    near, here, flow = layer_of(state, inner), layer_of(state, layer), flow_of(velocity, snap, layer)

    def pairs(f, i, j):
        value = near(f, i, j)
        return value, sign * value

    for i, j in tiles(shape):
        current = flow(i, j)
        out = advanced(here, pairs, current, i, j, shape)
        for f in (0, 1):
            message[(f,) + spot(i, j)] = here(f, i, j)
            message[(2 + f,) + spot(i, j)] = out[f]
        message[(4,) + spot(i, j)] = current[0]


def sides(depth):
    parity = lax.rem(lax.axis_index("space"), 2)
    even = parity == 0
    high = (jnp.where(even, depth - 1, 0), jnp.where(even, depth - 2, 1), jnp.where(even, -1.0, 1.0))
    low = (jnp.where(even, 0, depth - 1), jnp.where(even, 1, depth - 2), jnp.where(even, 1.0, -1.0))
    return parity, high, low


def pack_both(state, velocity, snap, message_one, message_two, depth, shape):
    unused, one, two = sides(depth)
    pack(state, velocity, snap, message_one, *one, shape)
    pack(state, velocity, snap, message_two, *two, shape)


def take_halos(blocks, state, halo_one, halo_two, halos, widened, depth, shape):
    parity, one, two = sides(depth)
    place = lax.axis_index("space")
    inside = jnp.logical_and(place > 0, place < blocks - 1)
    for halo, (edge, unused, sign), shown, high in (
        (halo_one, one, None, 1 - parity),
        (halo_two, two, inside, parity),
    ):
        for i, j in tiles(shape):
            u = halo[(4,) + spot(i, j)]
            for f in (0, 1):
                now = halo[(f,) + spot(i, j)]
                own = state[(f, edge) + spot(i, j)]
                later = halo[(2 + f,) + spot(i, j)] + (diffusion[f] + (0.25 * sign) * u) * own
                if shown is not None:
                    now = jnp.where(shown, now, 0.0)
                    later = jnp.where(shown, later, 0.0)
                halos[(high, f) + spot(i, j)] = now
                widened[(f, high * (depth + 1)) + spot(i, j)] = later


def two_steps(blocks, state, halo_one, halo_two, velocity, snaps, out, total, extra, halos, widened):
    depth, shape = state.shape[1], state.shape[2:]
    take_halos(blocks, state, halo_one, halo_two, halos, widened, depth, shape)
    halo_at = lambda h: lambda f, i, j: halos[(h, f) + spot(i, j)]

    def first_step(l, below, above):
        def store(i, j, values):
            for f in (0, 1):
                widened[(f, l + 1) + spot(i, j)] = values[f]

        full_layer(below, layer_of(state, l), above, flow_of(velocity, snaps[0, 1], l), shape, store)

    first_step(0, halo_at(0), layer_of(state, 1))
    first_step(depth - 1, layer_of(state, depth - 2), halo_at(1))

    def inner(l, carry):
        first_step(l, layer_of(state, l - 1), layer_of(state, l + 1))
        return carry

    lax.fori_loop(1, depth - 1, inner, 0)

    def outer(l, carry):
        def store(i, j, values):
            for f in (0, 1):
                out[(f, l) + spot(i, j)] = values[f]
            summed = widened[(0, l + 1) + spot(i, j)] + values[0]
            if extra is not None:
                summed = summed + extra(l, i, j)
            total[(l,) + spot(i, j)] = summed

        full_layer(
            layer_of(widened, l), layer_of(widened, l + 1), layer_of(widened, l + 2),
            flow_of(velocity, snaps[0, 0], l), shape, store,
        )
        return carry

    lax.fori_loop(0, depth, outer, 0)


def pack_kernel(snaps, state, velocity, message_one, message_two):
    pack_both(state, velocity, snaps[0, 1], message_one, message_two, state.shape[1], state.shape[2:])


def first_kernel(blocks, snaps, snaps_next, state, halo_one, halo_two, velocity,
                 out, total, message_one, message_two, halos, widened):
    two_steps(blocks, state, halo_one, halo_two, velocity, snaps_next, out, total, None, halos, widened)
    pack_both(out, velocity, snaps[0, 1], message_one, message_two, state.shape[1], state.shape[2:])


def second_kernel(blocks, slabs, snaps, state, halo_one, halo_two, velocity, total_before, from_core,
                  out, *rest):
    pieces, (total, halos, widened) = rest[:slabs], rest[slabs:]
    slab = lax.axis_index("tm")
    depth, shape = state.shape[1], state.shape[2:]
    rows = shape[0] // slabs

    @pl.when(slab == slabs - 1)
    def _():
        out[...] = from_core[...]
        for piece in pieces:
            piece[...] = jnp.zeros_like(piece)

    @pl.when(slab < slabs - 1)
    def _():
        with_last = slab == slabs - 2

        def extra(l, i, j):
            return jnp.where(with_last, total_before[(l,) + spot(i, j)], 0.0)

        two_steps(blocks, state, halo_one, halo_two, velocity, snaps, out, total, extra, halos, widened)
        for by in range(slabs):
            start = pl.multiple_of(lax.rem(slab + by, slabs) * rows, rows)
            pieces[by][...] = total[:, pl.ds(start, rows), :] * 0.5


def solution(mesh):
    slabs, blocks = mesh.shape["tm"], mesh.shape["space"]
    vmem, smem = pl.BlockSpec(memory_space=pltpu.VMEM), pl.BlockSpec(memory_space=pltpu.SMEM)
    params = pltpu.CompilerParams(vmem_limit_bytes=40 * 1024 * 1024)

    def index(t, s):
        return (t % slabs) * blocks + s % blocks

    def moved(array, to):
        pairs = [(index(t, s), index(*to(t, s))) for t in range(slabs) for s in range(blocks)]
        return lax.ppermute(array, ("tm", "space"), pairs)

    def one(s):
        return s ^ 1

    def two(s):
        return (((s + 1) ^ 1) - 1) % blocks

    def body(slab_states, velocity, snap_of_step):
        start = slab_states[0]
        fields, depth, ny, nz = start.shape
        block = jax.ShapeDtypeStruct(start.shape, jnp.float32)
        layer = jax.ShapeDtypeStruct((5, ny, nz), jnp.float32)
        scalar = jax.ShapeDtypeStruct((depth, ny, nz), jnp.float32)
        piece = jax.ShapeDtypeStruct((depth, ny // slabs, nz), jnp.float32)
        scratch = [
            pltpu.VMEM((2, fields, ny, nz), jnp.float32),
            pltpu.VMEM((fields, depth + 2, ny, nz), jnp.float32),
        ]

        state = moved(start, lambda t, s: (t - 1, s))
        snaps_next = moved(snap_of_step, lambda t, s: (t - 1, s))
        message_one, message_two = pl.pallas_call(
            pack_kernel,
            out_shape=(layer, layer),
            in_specs=[smem, vmem, vmem],
            out_specs=(vmem, vmem),
            compiler_params=params,
        )(snap_of_step, start, velocity)
        halo_one = moved(message_one, lambda t, s: (t - 1, one(s)))
        halo_two = moved(message_two, lambda t, s: (t - 1, two(s)))
        first, total_first, message_one, message_two = pl.pallas_call(
            functools.partial(first_kernel, blocks),
            out_shape=(block, scalar, layer, layer),
            in_specs=[smem, smem] + [vmem] * 4,
            out_specs=(vmem,) * 4,
            scratch_shapes=scratch,
            compiler_params=params,
        )(snap_of_step, snaps_next, state, halo_one, halo_two, velocity)
        halo_one = moved(message_one, lambda t, s: (t, one(s)))
        halo_two = moved(message_two, lambda t, s: (t, two(s)))
        from_core = moved(first, lambda t, s: (t ^ 1, s))
        results = pl.pallas_call(
            functools.partial(second_kernel, blocks, slabs),
            out_shape=(block,) + (piece,) * slabs,
            in_specs=[smem] + [vmem] * 6,
            out_specs=(vmem,) * (1 + slabs),
            scratch_shapes=[pltpu.VMEM(scalar.shape, jnp.float32)] + scratch,
            compiler_params=params,
        )(snap_of_step, first, halo_one, halo_two, velocity, total_first, from_core)
        gradient = results[1]
        for by in range(1, slabs):
            gradient = gradient + moved(results[1 + by], lambda t, s, by=by: (t + by, s))
        return (results[0][None], gradient)

    return jax.shard_map(
        body,
        mesh=mesh,
        in_specs=(P("tm", None, "space", None, None), P(None, None, "space", None, None), P("tm", None)),
        out_specs=(P("tm", None, "space", None, None), P("space", "tm", None)),
        check_vma=False,
    )
```

time: 136 us -> 61.9 us (0.46)
  waiting for transfers between devices: 65 us -> 23.8 us
  between operations: 18.2 us -> 0.66 us
  other arithmetic: 13.9 us -> 0.69 us
  starting transfers between devices: 33.3 us -> 24.6 us
  Pallas kernels: 0 us -> 8.18 us
    reduce_scatter x1 -> x0, waiting for transfers between devices: 37.6 us -> none  [body(): lax.psum_scatter(total, 'tm', scatter_dimension=1, tiled=True)]
    ppermute x9 -> x10, starting transfers between devices: 33.3 us -> 24.6 us  [moved(): return lax.ppermute(array, ('tm', 'space'), pairs)]
    pallas_call x0 -> x3, Pallas kernels: none -> 8.18 us  [the longest x1 4.08 us: body(): pl.pallas_call(functools.partial(second_kernel, blocks, slabs), out_shape...]
    add x9 -> x1, other arithmetic: 5.67 us -> 0.69 us  [body(): gradient + moved(results[1 + by], lambda t, s, by=by: (t + by, s))]
    ppermute x9 -> x10, waiting for transfers between devices: 27.4 us -> 23.8 us  [moved(): return lax.ppermute(array, ('tm', 'space'), pairs)]
    unnamed x14 -> x8, local copies, waits for them, and re-layouts: 0.34 us -> 3.77 us
    sub x4 -> x0, other arithmetic: 2.82 us -> none  [advance(): east_side + west_side + north_side + south_side + upper_side + lower_side]
    slice x3 -> x0, local copies, waits for them, and re-layouts: 2.33 us -> none  [the longest x1 1.31 us: sweep_local(): snaps[step_index]]
  transfers between devices with their start and end apart: 10 -> 10, of which waited for: 8 -> 6; matrix products, arithmetic and copies ran while one was open for 4% -> 0% of each run, Pallas kernels for 0% -> 1%
where the time goes in v1:
time: 61.9 us; the launch traced here: 61.7 us
  starting transfers between devices  24.6 us (40%)
  waiting for transfers between devices  23.8 us (38%)
  Pallas kernels  8.18 us (13%)
  local copies, waits for them, and re-layouts  3.77 us (6%)
  other arithmetic  0.69 us (1%)
  between operations  0.66 us (1%)
    ppermute x10, starting transfers between devices, moved(): return lax.ppermute(array, ('tm', 'space'), pairs)  24.6 us
    ppermute x10, waiting for transfers between devices, moved(): return lax.ppermute(array, ('tm', 'space'), pairs)  23.8 us
    pallas_call x1, Pallas kernels, body(): pl.pallas_call(functools.partial(second_kernel, blocks, slabs), out_shape...  4.08 us
    unnamed x8, local copies, waits for them, and re-layouts  3.77 us
    pallas_call x1, Pallas kernels, body(): pl.pallas_call(functools.partial(first_kernel, blocks), out_shape=(block,...  3.3 us
  transfers between devices with their start and end apart: 10, of which 6 were waited for; matrix products, arithmetic and copies ran while one was open for 0% of the time, Pallas kernels for 1%

profile of v1, /device:TPU:1, one launch (start us, length us, event | category | flops | bytes accessed | tf_op | source)
XLA Modules:
  0.0 61.7 jit_solution(12109866328660442331)
XLA Ops:
  0.6 3.3 %collective-permute-start.1 = (f32[2,8,32,512]{3,2,1,0:T(8,128)}, f32[2,8,32,512]{3,2,1,0:T(8,128)S(1)}, u32[]{:S(2)}, u32[]{:S(2)}) collective-permute-start(f32[2,8,32,512]{3,2,1,0:T(8,128)} %bitcast.2), channel_id=1, source_target_pairs={{0,192},{1,193},{2,194},{3,195},{4,196},{5,197},{6,198},{7,199},{8... | collective-permute-start | bytes 3145736 | tf_op jit(solution)/shard_map/ppermute | solution.py:208
  3.9 1.9 %copy-done = f32[2,3,8,32,512]{4,3,2,1,0:T(8,128)S(1)} copy-done((f32[2,3,8,32,512]{4,3,2,1,0:T(8,128)S(1)}, f32[2,3,8,32,512]{4,3,2,1,0:T(8,128)}, u32[]{:S(2)}) %copy-start) | copy-done | bytes 3145752
  5.8 1.2 %copy-done.2 = f32[1,2,8,32,512]{4,3,2,1,0:T(8,128)S(1)} copy-done((f32[1,2,8,32,512]{4,3,2,1,0:T(8,128)S(1)}, f32[1,2,8,32,512]{4,3,2,1,0:T(8,128)}, u32[]{:S(2)}) %copy-start.2) | copy-done | bytes 1048600
  7.1 0.7 %copy-done.3 = s32[1,2]{1,0:T(1,128)S(1)} copy-done((s32[1,2]{1,0:T(1,128)S(1)}, s32[1,2]{1,0:T(1,128)}, u32[]{:S(2)}) %copy-start.3) | copy-done | bytes 32
  7.7 0.8 %shard_map.50 = (f32[5,32,512]{2,1,0:T(8,128)S(1)}, f32[5,32,512]{2,1,0:T(8,128)S(1)}) custom-call(s32[1,2]{1,0:T(1,128)S(1)} %copy-done.3, f32[2,8,32,512]{3,2,1,0:T(8,128)S(1)} %bitcast.3, f32[2,3,8,32,512]{4,3,2,1,0:T(8,128)S(1)} %copy-done), custom_call_target="tpu_custom_call" | custom-call | tf_op jit(solution)/shard_map/pallas_call | solution.py:230
  8.5 1.9 %collective-permute-start.2 = (f32[5,32,512]{2,1,0:T(8,128)S(1)}, f32[5,32,512]{2,1,0:T(8,128)S(1)}, u32[]{:S(2)}, u32[]{:S(2)}) collective-permute-start(f32[5,32,512]{2,1,0:T(8,128)S(1)} %get-tuple-element.13), channel_id=1, source_target_pairs={{0,193},{1,192},{2,195},{3,194},{4,197},{5,196},{6,199},{7,198},{8... | collective-permute-start | bytes 983048 | tf_op jit(solution)/shard_map/ppermute | solution.py:208
  10.4 7.6 %collective-permute-start.3 = (f32[5,32,512]{2,1,0:T(8,128)S(1)}, f32[5,32,512]{2,1,0:T(8,128)S(1)}, u32[]{:S(2)}, u32[]{:S(2)}) collective-permute-start(f32[5,32,512]{2,1,0:T(8,128)S(1)} %get-tuple-element.14), channel_id=1, source_target_pairs={{0,255},{1,194},{2,193},{3,196},{4,195},{5,198},{6,197},{7,200},{8... | collective-permute-start | bytes 983048 | tf_op jit(solution)/shard_map/ppermute | solution.py:208
  18.0 0.4 collective-permute-start
  18.3 7.0 %collective-permute-done.snaps_next = s32[1,2]{1,0:T(1,128)S(1)} collective-permute-done((s32[1,2]{1,0:T(1,128)S(1)}, s32[1,2]{1,0:T(1,128)S(1)}, u32[]{:S(2)}, u32[]{:S(2)}) %collective-permute-start) | collective-permute-done | bytes 40 | tf_op jit(solution)/shard_map/ppermute | solution.py:208
  25.3 1.4 %collective-permute-done.2.halo_one = f32[5,32,512]{2,1,0:T(8,128)S(1)} collective-permute-done((f32[5,32,512]{2,1,0:T(8,128)S(1)}, f32[5,32,512]{2,1,0:T(8,128)S(1)}, u32[]{:S(2)}, u32[]{:S(2)}) %collective-permute-start.2) | collective-permute-done | bytes 327712 | tf_op jit(solution)/shard_map/ppermute | solution.py:208
  26.7 0.0 collective-permute-done.3.halo_two
  26.7 3.3 %shard_map.51 = (f32[2,8,32,512]{3,2,1,0:T(8,128)S(1)}, f32[8,32,512]{2,1,0:T(8,128)S(1)}, f32[5,32,512]{2,1,0:T(8,128)S(1)}, f32[5,32,512]{2,1,0:T(8,128)S(1)}) custom-call(s32[1,2]{1,0:T(1,128)S(1)} %copy-done.3, s32[1,2]{1,0:T(1,128)S(1)} %collective-permute-done.snaps_next, f32[2,8,32,512]{3,2,1,0:T(8,128)S(1)} %collective-permute-done.1.state, ...), custom_call_target="tpu_custom_call" | custom-call | tf_op jit(solution)/shard_map/pallas_call | solution.py:239
  30.0 0.4 collective-permute-start.6
  30.4 0.7 %collective-permute-start.4 = (f32[5,32,512]{2,1,0:T(8,128)S(1)}, f32[5,32,512]{2,1,0:T(8,128)S(1)}, u32[]{:S(2)}, u32[]{:S(2)}) collective-permute-start(f32[5,32,512]{2,1,0:T(8,128)S(1)} %get-tuple-element.16), channel_id=1, source_target_pairs={{0,1},{1,0},{2,3},{3,2},{4,5},{5,4},{6,7},{7,6},{8,9},{9,8},{10,11... | collective-permute-start | bytes 983048 | tf_op jit(solution)/shard_map/ppermute | solution.py:208
  31.1 8.0 %collective-permute-start.5 = (f32[5,32,512]{2,1,0:T(8,128)S(1)}, f32[5,32,512]{2,1,0:T(8,128)S(1)}, u32[]{:S(2)}, u32[]{:S(2)}) collective-permute-start(f32[5,32,512]{2,1,0:T(8,128)S(1)} %get-tuple-element.17), channel_id=1, source_target_pairs={{0,63},{1,2},{2,1},{3,4},{4,3},{5,6},{6,5},{7,8},{8,7},{9,10},{10,... | collective-permute-start | bytes 983048 | tf_op jit(solution)/shard_map/ppermute | solution.py:208
  39.1 8.9 %collective-permute-done.4.halo_one = f32[5,32,512]{2,1,0:T(8,128)S(1)} collective-permute-done((f32[5,32,512]{2,1,0:T(8,128)S(1)}, f32[5,32,512]{2,1,0:T(8,128)S(1)}, u32[]{:S(2)}, u32[]{:S(2)}) %collective-permute-start.4) | collective-permute-done | bytes 327712 | tf_op jit(solution)/shard_map/ppermute | solution.py:208
  48.0 4.1 %shard_map.52 = (f32[2,8,32,512]{3,2,1,0:T(8,128)}, f32[8,8,512]{2,1,0:T(8,128)S(1)}, f32[8,8,512]{2,1,0:T(8,128)S(1)}, f32[8,8,512]{2,1,0:T(8,128)S(1)}, f32[8,8,512]{2,1,0:T(8,128)S(1)}) custom-call(s32[1,2]{1,0:T(1,128)S(1)} %copy-done.3, f32[2,8,32,512]{3,2,1,0:T(8,128)S(1)} %get-tuple-element.15.state, ...), custom_call_target="tpu_custom_call" | custom-call | tf_op jit(solution)/shard_map/pallas_call | solution.py:250
  52.1 1.2 %collective-permute-start.7 = (f32[8,8,512]{2,1,0:T(8,128)S(1)}, f32[8,8,512]{2,1,0:T(8,128)S(1)}, u32[]{:S(2)}, u32[]{:S(2)}) collective-permute-start(f32[8,8,512]{2,1,0:T(8,128)S(1)} %get-tuple-element.21), channel_id=1, source_target_pairs={{0,64},{1,65},{2,66},{3,67},{4,68},{5,69},{6,70},{7,71},{8,72},{9,... | collective-permute-start | bytes 393224 | tf_op jit(solution)/shard_map/ppermute | solution.py:208
  53.3 1.2 %collective-permute-start.8 = (f32[8,8,512]{2,1,0:T(8,128)S(1)}, f32[8,8,512]{2,1,0:T(8,128)S(1)}, u32[]{:S(2)}, u32[]{:S(2)}) collective-permute-start(f32[8,8,512]{2,1,0:T(8,128)S(1)} %get-tuple-element.22), channel_id=1, source_target_pairs={{0,128},{1,129},{2,130},{3,131},{4,132},{5,133},{6,134},{7,135},{8... | collective-permute-start | bytes 393224 | tf_op jit(solution)/shard_map/ppermute | solution.py:208
  54.5 0.0 collective-permute-start.9
  54.5 1.6 %collective-permute-done.7 = f32[8,8,512]{2,1,0:T(8,128)S(1)} collective-permute-done((f32[8,8,512]{2,1,0:T(8,128)S(1)}, f32[8,8,512]{2,1,0:T(8,128)S(1)}, u32[]{:S(2)}, u32[]{:S(2)}) %collective-permute-start.7) | collective-permute-done | bytes 131104 | tf_op jit(solution)/shard_map/ppermute | solution.py:208
  56.0 4.4 %collective-permute-done.8 = f32[8,8,512]{2,1,0:T(8,128)S(1)} collective-permute-done((f32[8,8,512]{2,1,0:T(8,128)S(1)}, f32[8,8,512]{2,1,0:T(8,128)S(1)}, u32[]{:S(2)}, u32[]{:S(2)}) %collective-permute-start.8) | collective-permute-done | bytes 131104 | tf_op jit(solution)/shard_map/ppermute | solution.py:208
  60.5 0.6 collective-permute-done.9
  61.0 0.7 %add_add_fusion = f32[8,8,512]{2,1,0:T(8,128)} fusion(f32[8,8,512]{2,1,0:T(8,128)S(1)} %collective-permute-done.9, f32[8,8,512]{2,1,0:T(8,128)S(1)} %collective-permute-done.8, f32[8,8,512]{2,1,0:T(8,128)S(1)} %get-tuple-element.20, f32[8,8,512]{2,1,0:T(8,128)S(1)} %collective-permute-done.7), kind=kLoop, calls=%fused_computation | loop fusion | flops 98304 | bytes 655360 | tf_op jit(solution)/shard_map/add | solution.py:260
  (8 shorter events, 0.0 us)
Async XLA Ops:
  0.6 26.1 %collective-permute-start.1 = (f32[2,8,32,512]{3,2,1,0:T(8,128)}, f32[2,8,32,512]{3,2,1,0:T(8,128)S(1)}, u32[]{:S(2)}, u32[]{:S(2)}) collective-permute-start(f32[2,8,32,512]{3,2,1,0:T(8,128)} %bitcast.2), channel_id=1, source_target_pairs={{0,192},{1,193},{2,194},{3,195},{4,196},{5,197},{6,198},{7,199},{8... | collective-permute-start | bytes 3145736 | tf_op jit(solution)/shard_map/ppermute | solution.py:208
  3.9 1.9 %copy-start = (f32[2,3,8,32,512]{4,3,2,1,0:T(8,128)S(1)}, f32[2,3,8,32,512]{4,3,2,1,0:T(8,128)}, u32[]{:S(2)}) copy-start(f32[2,3,8,32,512]{4,3,2,1,0:T(8,128)} %velocity.5) | copy-start | bytes 9437188
  5.8 1.2 %copy-start.2 = (f32[1,2,8,32,512]{4,3,2,1,0:T(8,128)S(1)}, f32[1,2,8,32,512]{4,3,2,1,0:T(8,128)}, u32[]{:S(2)}) copy-start(f32[1,2,8,32,512]{4,3,2,1,0:T(8,128)} %param.3) | copy-start | bytes 3145732
  7.1 0.7 %copy-start.3 = (s32[1,2]{1,0:T(1,128)S(1)}, s32[1,2]{1,0:T(1,128)}, u32[]{:S(2)}) copy-start(s32[1,2]{1,0:T(1,128)} %snaps.5) | copy-start | bytes 28
  7.7 19.0 %copy-start.1 = (f32[2,3,8,32,512]{4,3,2,1,0:T(8,128)S(1)}, f32[2,3,8,32,512]{4,3,2,1,0:T(8,128)}, u32[]{:S(2)}) copy-start(f32[2,3,8,32,512]{4,3,2,1,0:T(8,128)} %velocity.5) | copy-start | bytes 9437188
  8.5 18.2 %collective-permute-start.2 = (f32[5,32,512]{2,1,0:T(8,128)S(1)}, f32[5,32,512]{2,1,0:T(8,128)S(1)}, u32[]{:S(2)}, u32[]{:S(2)}) collective-permute-start(f32[5,32,512]{2,1,0:T(8,128)S(1)} %get-tuple-element.13), channel_id=1, source_target_pairs={{0,193},{1,192},{2,195},{3,194},{4,197},{5,196},{6,199},{7,198},{8... | collective-permute-start | bytes 983048 | tf_op jit(solution)/shard_map/ppermute | solution.py:208
  10.4 16.3 %collective-permute-start.3 = (f32[5,32,512]{2,1,0:T(8,128)S(1)}, f32[5,32,512]{2,1,0:T(8,128)S(1)}, u32[]{:S(2)}, u32[]{:S(2)}) collective-permute-start(f32[5,32,512]{2,1,0:T(8,128)S(1)} %get-tuple-element.14), channel_id=1, source_target_pairs={{0,255},{1,194},{2,193},{3,196},{4,195},{5,198},{6,197},{7,200},{8... | collective-permute-start | bytes 983048 | tf_op jit(solution)/shard_map/ppermute | solution.py:208
  18.0 7.4 %collective-permute-start = (s32[1,2]{1,0:T(1,128)S(1)}, s32[1,2]{1,0:T(1,128)S(1)}, u32[]{:S(2)}, u32[]{:S(2)}) collective-permute-start(s32[1,2]{1,0:T(1,128)S(1)} %copy-done.3), channel_id=1, source_target_pairs={{0,192},{1,193},{2,194},{3,195},{4,196},{5,197},{6,198},{7,199},{8... | collective-permute-start | bytes 32 | tf_op jit(solution)/shard_map/ppermute | solution.py:208
  30.0 18.0 %collective-permute-start.6 = (f32[2,8,32,512]{3,2,1,0:T(8,128)S(1)}, f32[2,8,32,512]{3,2,1,0:T(8,128)S(1)}, u32[]{:S(2)}, u32[]{:S(2)}) collective-permute-start(f32[2,8,32,512]{3,2,1,0:T(8,128)S(1)} %get-tuple-element.15.state), channel_id=1, source_target_pairs={{0,64},{1,65},{2,66},{3,67},{4,68},{5,69},{6,70},{7,71},{8,72},{9,... | collective-permute-start | bytes 3145736 | tf_op jit(solution)/shard_map/ppermute | solution.py:208
  30.4 17.6 %collective-permute-start.4 = (f32[5,32,512]{2,1,0:T(8,128)S(1)}, f32[5,32,512]{2,1,0:T(8,128)S(1)}, u32[]{:S(2)}, u32[]{:S(2)}) collective-permute-start(f32[5,32,512]{2,1,0:T(8,128)S(1)} %get-tuple-element.16), channel_id=1, source_target_pairs={{0,1},{1,0},{2,3},{3,2},{4,5},{5,4},{6,7},{7,6},{8,9},{9,8},{10,11... | collective-permute-start | bytes 983048 | tf_op jit(solution)/shard_map/ppermute | solution.py:208
  31.1 16.9 %collective-permute-start.5 = (f32[5,32,512]{2,1,0:T(8,128)S(1)}, f32[5,32,512]{2,1,0:T(8,128)S(1)}, u32[]{:S(2)}, u32[]{:S(2)}) collective-permute-start(f32[5,32,512]{2,1,0:T(8,128)S(1)} %get-tuple-element.17), channel_id=1, source_target_pairs={{0,63},{1,2},{2,1},{3,4},{4,3},{5,6},{6,5},{7,8},{8,7},{9,10},{10,... | collective-permute-start | bytes 983048 | tf_op jit(solution)/shard_map/ppermute | solution.py:208
  52.1 4.0 %collective-permute-start.7 = (f32[8,8,512]{2,1,0:T(8,128)S(1)}, f32[8,8,512]{2,1,0:T(8,128)S(1)}, u32[]{:S(2)}, u32[]{:S(2)}) collective-permute-start(f32[8,8,512]{2,1,0:T(8,128)S(1)} %get-tuple-element.21), channel_id=1, source_target_pairs={{0,64},{1,65},{2,66},{3,67},{4,68},{5,69},{6,70},{7,71},{8,72},{9,... | collective-permute-start | bytes 393224 | tf_op jit(solution)/shard_map/ppermute | solution.py:208
  53.3 7.2 %collective-permute-start.8 = (f32[8,8,512]{2,1,0:T(8,128)S(1)}, f32[8,8,512]{2,1,0:T(8,128)S(1)}, u32[]{:S(2)}, u32[]{:S(2)}) collective-permute-start(f32[8,8,512]{2,1,0:T(8,128)S(1)} %get-tuple-element.22), channel_id=1, source_target_pairs={{0,128},{1,129},{2,130},{3,131},{4,132},{5,133},{6,134},{7,135},{8... | collective-permute-start | bytes 393224 | tf_op jit(solution)/shard_map/ppermute | solution.py:208
  54.5 6.6 %collective-permute-start.9 = (f32[8,8,512]{2,1,0:T(8,128)S(1)}, f32[8,8,512]{2,1,0:T(8,128)S(1)}, u32[]{:S(2)}, u32[]{:S(2)}) collective-permute-start(f32[8,8,512]{2,1,0:T(8,128)S(1)} %get-tuple-element.23), channel_id=1, source_target_pairs={{0,192},{1,193},{2,194},{3,195},{4,196},{5,197},{6,198},{7,199},{8... | collective-permute-start | bytes 393224 | tf_op jit(solution)/shard_map/ppermute | solution.py:208

commit v2 on v1

--- a/solution.py
+++ b/solution.py
@@ -69,8 +69,8 @@
         store(i, j, advanced(here, pairs, flow(i, j), i, j, shape))
 
 
-def pack(state, velocity, snap, message, layer, inner, sign, shape):
-    near, here, flow = layer_of(state, inner), layer_of(state, layer), flow_of(velocity, snap, layer)
+def pack(state, velocity, snap, message, layer, inner, sign, at, shape):
+    near, here, flow = layer_of(state, inner), layer_of(state, layer), flow_of(velocity, snap, at)
 
     def pairs(f, i, j):
         value = near(f, i, j)
@@ -95,8 +95,12 @@
 
 def pack_both(state, velocity, snap, message_one, message_two, depth, shape):
     unused, one, two = sides(depth)
-    pack(state, velocity, snap, message_one, *one, shape)
-    pack(state, velocity, snap, message_two, *two, shape)
+    if velocity.shape[2] == depth:
+        at_one, at_two = one[0], two[0]
+    else:
+        at_one, at_two = one[0] // (depth - 1), two[0] // (depth - 1)
+    pack(state, velocity, snap, message_one, *one, at_one, shape)
+    pack(state, velocity, snap, message_two, *two, at_two, shape)
 
 
 def take_halos(blocks, state, halo_one, halo_two, halos, widened, depth, shape):
@@ -120,7 +124,7 @@
                 widened[(f, high * (depth + 1)) + spot(i, j)] = later
 
 
-def two_steps(blocks, state, halo_one, halo_two, velocity, snaps, out, total, extra, halos, widened):
+def two_steps(blocks, state, halo_one, halo_two, velocity, snaps, out, total, halos, widened):
     depth, shape = state.shape[1], state.shape[2:]
     take_halos(blocks, state, halo_one, halo_two, halos, widened, depth, shape)
     halo_at = lambda h: lambda f, i, j: halos[(h, f) + spot(i, j)]
@@ -145,10 +149,8 @@
         def store(i, j, values):
             for f in (0, 1):
                 out[(f, l) + spot(i, j)] = values[f]
-            summed = widened[(0, l + 1) + spot(i, j)] + values[0]
-            if extra is not None:
-                summed = summed + extra(l, i, j)
-            total[(l,) + spot(i, j)] = summed
+            if total is not None:
+                total[(l,) + spot(i, j)] = widened[(0, l + 1) + spot(i, j)] + values[0]
 
         full_layer(
             layer_of(widened, l), layer_of(widened, l + 1), layer_of(widened, l + 2),
@@ -159,45 +161,52 @@
     lax.fori_loop(0, depth, outer, 0)
 
 
-def pack_kernel(snaps, state, velocity, message_one, message_two):
-    pack_both(state, velocity, snaps[0, 1], message_one, message_two, state.shape[1], state.shape[2:])
-
-
-def first_kernel(blocks, snaps, snaps_next, state, halo_one, halo_two, velocity,
-                 out, total, message_one, message_two, halos, widened):
-    two_steps(blocks, state, halo_one, halo_two, velocity, snaps_next, out, total, None, halos, widened)
-    pack_both(out, velocity, snaps[0, 1], message_one, message_two, state.shape[1], state.shape[2:])
-
-
-def second_kernel(blocks, slabs, snaps, state, halo_one, halo_two, velocity, total_before, from_core,
-                  out, *rest):
+def pack_kernel(snaps, state, velocity, message_one, message_two, scalars, edges, flows, sems):
+    depth, shape = state.shape[1], state.shape[2:]
+    copies = [
+        (snaps, scalars),
+        (state.at[:, pl.ds(0, 2)], edges.at[:, pl.ds(0, 2)]),
+        (state.at[:, pl.ds(depth - 2, 2)], edges.at[:, pl.ds(2, 2)]),
+        (velocity.at[:, :, pl.ds(0, 1)], flows.at[:, :, pl.ds(0, 1)]),
+        (velocity.at[:, :, pl.ds(depth - 1, 1)], flows.at[:, :, pl.ds(1, 1)]),
+    ]
+    copies = [pltpu.make_async_copy(*pair, sems.at[n]) for n, pair in enumerate(copies)]
+    for copy in copies:
+        copy.start()
+    for copy in copies:
+        copy.wait()
+    pack_both(edges, flows, scalars[0, 1], message_one, message_two, edges.shape[1], shape)
+
+
+def first_kernel(blocks, slabs, snaps, snaps_next, state, halo_one, halo_two, velocity, start, own_one, own_two,
+                 out, message_one, message_two, halos, widened):
+    last = lax.axis_index("tm") == slabs - 1
+
+    @pl.when(last)
+    def _():
+        pltpu.sync_copy(start, out)
+        message_one[...] = own_one[...]
+        message_two[...] = own_two[...]
+
+    @pl.when(jnp.logical_not(last))
+    def _():
+        two_steps(blocks, state, halo_one, halo_two, velocity, snaps_next, out, None, halos, widened)
+        pack_both(out, velocity, snaps[0, 1], message_one, message_two, state.shape[1], state.shape[2:])
+
+
+def second_kernel(blocks, slabs, snaps, state, halo_one, halo_two, velocity, out, *rest):
     pieces, (total, halos, widened) = rest[:slabs], rest[slabs:]
-    slab = lax.axis_index("tm")
-    depth, shape = state.shape[1], state.shape[2:]
-    rows = shape[0] // slabs
-
-    @pl.when(slab == slabs - 1)
-    def _():
-        out[...] = from_core[...]
-        for piece in pieces:
-            piece[...] = jnp.zeros_like(piece)
-
-    @pl.when(slab < slabs - 1)
-    def _():
-        with_last = slab == slabs - 2
-
-        def extra(l, i, j):
-            return jnp.where(with_last, total_before[(l,) + spot(i, j)], 0.0)
-
-        two_steps(blocks, state, halo_one, halo_two, velocity, snaps, out, total, extra, halos, widened)
-        for by in range(slabs):
-            start = pl.multiple_of(lax.rem(slab + by, slabs) * rows, rows)
-            pieces[by][...] = total[:, pl.ds(start, rows), :] * 0.5
+    rows = state.shape[2] // slabs
+    two_steps(blocks, state, halo_one, halo_two, velocity, snaps, out, total, halos, widened)
+    for by in range(slabs):
+        start = pl.multiple_of(lax.rem(lax.axis_index("tm") + by, slabs) * rows, rows)
+        pieces[by][...] = total[:, pl.ds(start, rows), :] * 0.5
 
 
 def solution(mesh):
     slabs, blocks = mesh.shape["tm"], mesh.shape["space"]
     vmem, smem = pl.BlockSpec(memory_space=pltpu.VMEM), pl.BlockSpec(memory_space=pltpu.SMEM)
+    anywhere = pl.BlockSpec(memory_space=pltpu.HBM)
     params = pltpu.CompilerParams(vmem_limit_bytes=40 * 1024 * 1024)
 
     def index(t, s):
@@ -225,36 +234,45 @@
             pltpu.VMEM((fields, depth + 2, ny, nz), jnp.float32),
         ]
 
-        state = moved(start, lambda t, s: (t - 1, s))
+        def earlier(array):
+            pairs = [(index(t, s), index(t - 1, s)) for t in range(1, slabs) for s in range(blocks)]
+            return lax.ppermute(array, ("tm", "space"), pairs)
+
+        state = earlier(start)
         snaps_next = moved(snap_of_step, lambda t, s: (t - 1, s))
-        message_one, message_two = pl.pallas_call(
+        own_one, own_two = pl.pallas_call(
             pack_kernel,
             out_shape=(layer, layer),
-            in_specs=[smem, vmem, vmem],
+            in_specs=[anywhere] * 3,
             out_specs=(vmem, vmem),
+            scratch_shapes=[
+                pltpu.SMEM(snap_of_step.shape, jnp.int32),
+                pltpu.VMEM((fields, 4, ny, nz), jnp.float32),
+                pltpu.VMEM(velocity.shape[:2] + (2, ny, nz), jnp.float32),
+                pltpu.SemaphoreType.DMA((5,)),
+            ],
             compiler_params=params,
         )(snap_of_step, start, velocity)
-        halo_one = moved(message_one, lambda t, s: (t - 1, one(s)))
-        halo_two = moved(message_two, lambda t, s: (t - 1, two(s)))
-        first, total_first, message_one, message_two = pl.pallas_call(
-            functools.partial(first_kernel, blocks),
-            out_shape=(block, scalar, layer, layer),
-            in_specs=[smem, smem] + [vmem] * 4,
-            out_specs=(vmem,) * 4,
+        halo_one = moved(own_one, lambda t, s: (t - 1, one(s)))
+        halo_two = moved(own_two, lambda t, s: (t - 1, two(s)))
+        first, message_one, message_two = pl.pallas_call(
+            functools.partial(first_kernel, blocks, slabs),
+            out_shape=(block, layer, layer),
+            in_specs=[smem, smem] + [vmem] * 4 + [anywhere, vmem, vmem],
+            out_specs=(vmem,) * 3,
             scratch_shapes=scratch,
             compiler_params=params,
-        )(snap_of_step, snaps_next, state, halo_one, halo_two, velocity)
+        )(snap_of_step, snaps_next, state, halo_one, halo_two, velocity, start, own_one, own_two)
         halo_one = moved(message_one, lambda t, s: (t, one(s)))
         halo_two = moved(message_two, lambda t, s: (t, two(s)))
-        from_core = moved(first, lambda t, s: (t ^ 1, s))
         results = pl.pallas_call(
             functools.partial(second_kernel, blocks, slabs),
             out_shape=(block,) + (piece,) * slabs,
-            in_specs=[smem] + [vmem] * 6,
+            in_specs=[smem] + [vmem] * 4,
             out_specs=(vmem,) * (1 + slabs),
             scratch_shapes=[pltpu.VMEM(scalar.shape, jnp.float32)] + scratch,
             compiler_params=params,
-        )(snap_of_step, first, halo_one, halo_two, velocity, total_first, from_core)
+        )(snap_of_step, first, halo_one, halo_two, velocity)
         gradient = results[1]
         for by in range(1, slabs):
             gradient = gradient + moved(results[1 + by], lambda t, s, by=by: (t + by, s))

time: 61.9 us -> 62.6 us (1.011)
  starting transfers between devices: 24.6 us -> 27.2 us
  waiting for transfers between devices: 23.8 us -> 21.9 us
    ppermute x0 -> x1, starting transfers between devices: none -> 5.15 us  [earlier(): return lax.ppermute(array, ('tm', 'space'), pairs)]
    ppermute x10 -> x8, starting transfers between devices: 24.6 us -> 22 us  [moved(): return lax.ppermute(array, ('tm', 'space'), pairs)]
    ppermute x10 -> x8, waiting for transfers between devices: 23.8 us -> 21.9 us  [moved(): return lax.ppermute(array, ('tm', 'space'), pairs)]
  transfers between devices with their start and end apart: 10 -> 9, of which waited for: 6 -> 6; matrix products, arithmetic and copies ran while one was open for 0% -> 0% of each run, Pallas kernels for 1% -> 1%
where the time goes in v2:
time: 62.6 us; the launch traced here: 62.4 us
  starting transfers between devices  27.2 us (43%)
  waiting for transfers between devices  21.9 us (35%)
  Pallas kernels  8.13 us (13%)
  local copies, waits for them, and re-layouts  3.77 us (6%)
  other arithmetic  0.69 us (1%)
  between operations  0.67 us (1%)
    ppermute x8, starting transfers between devices, moved(): return lax.ppermute(array, ('tm', 'space'), pairs)  22 us
    ppermute x8, waiting for transfers between devices, moved(): return lax.ppermute(array, ('tm', 'space'), pairs)  21.9 us
    ppermute x1, starting transfers between devices, earlier(): return lax.ppermute(array, ('tm', 'space'), pairs)  5.15 us
    pallas_call x1, Pallas kernels, body(): pl.pallas_call(functools.partial(second_kernel, blocks, slabs), out_shape...  3.98 us
    unnamed x8, local copies, waits for them, and re-layouts  3.77 us
    pallas_call x1, Pallas kernels, body(): pl.pallas_call(functools.partial(first_kernel, blocks, slabs), out_shape=...  3.31 us
  transfers between devices with their start and end apart: 9, of which 6 were waited for; matrix products, arithmetic and copies ran while one was open for 0% of the time, Pallas kernels for 1%

profile of v2, /device:TPU:1, one launch (start us, length us, event | category | flops | bytes accessed | tf_op | source)
XLA Modules:
  0.0 62.4 jit_solution(15721497793775783299)
XLA Ops:
  0.6 5.1 %collective-permute-start.1 = (f32[2,8,32,512]{3,2,1,0:T(8,128)}, f32[2,8,32,512]{3,2,1,0:T(8,128)S(1)}, u32[]{:S(2)}, u32[]{:S(2)}) collective-permute-start(f32[2,8,32,512]{3,2,1,0:T(8,128)} %bitcast.2), channel_id=1, source_target_pairs={{64,0},{65,1},{66,2},{67,3},{68,4},{69,5},{70,6},{71,7},{72,8},{73... | collective-permute-start | bytes 3145736 | tf_op jit(solution)/shard_map/ppermute | solution.py:239
  5.8 0.0 copy-start
  5.8 1.9 %copy-done = f32[2,3,8,32,512]{4,3,2,1,0:T(8,128)S(1)} copy-done((f32[2,3,8,32,512]{4,3,2,1,0:T(8,128)S(1)}, f32[2,3,8,32,512]{4,3,2,1,0:T(8,128)}, u32[]{:S(2)}) %copy-start) | copy-done | bytes 3145752
  7.7 1.2 %copy-done.2 = f32[1,2,8,32,512]{4,3,2,1,0:T(8,128)S(1)} copy-done((f32[1,2,8,32,512]{4,3,2,1,0:T(8,128)S(1)}, f32[1,2,8,32,512]{4,3,2,1,0:T(8,128)}, u32[]{:S(2)}) %copy-start.2) | copy-done | bytes 1048600
  8.9 0.7 %copy-done.3 = s32[1,2]{1,0:T(1,128)S(1)} copy-done((s32[1,2]{1,0:T(1,128)S(1)}, s32[1,2]{1,0:T(1,128)}, u32[]{:S(2)}) %copy-start.3) | copy-done | bytes 32
  9.6 0.8 %shard_map.50 = (f32[5,32,512]{2,1,0:T(8,128)S(1)}, f32[5,32,512]{2,1,0:T(8,128)S(1)}) custom-call(s32[1,2]{1,0:T(1,128)S(1)} %copy-done.3, f32[2,8,32,512]{3,2,1,0:T(8,128)S(1)} %bitcast.3, f32[2,3,8,32,512]{4,3,2,1,0:T(8,128)S(1)} %copy-done), custom_call_target="tpu_custom_call" | custom-call | tf_op jit(solution)/shard_map/pallas_call | solution.py:243
  10.4 0.5 collective-permute-start.2
  10.9 8.7 %collective-permute-start.3 = (f32[5,32,512]{2,1,0:T(8,128)S(1)}, f32[5,32,512]{2,1,0:T(8,128)S(1)}, u32[]{:S(2)}, u32[]{:S(2)}) collective-permute-start(f32[5,32,512]{2,1,0:T(8,128)S(1)} %get-tuple-element.13.own_two), channel_id=1, source_target_pairs={{0,255},{1,194},{2,193},{3,196},{4,195},{5,198},{6,197},{7,200},{8... | collective-permute-start | bytes 983048 | tf_op jit(solution)/shard_map/ppermute | solution.py:217
  19.7 0.6 collective-permute-start
  20.2 6.7 %collective-permute-done.snaps_next = s32[1,2]{1,0:T(1,128)S(1)} collective-permute-done((s32[1,2]{1,0:T(1,128)S(1)}, s32[1,2]{1,0:T(1,128)S(1)}, u32[]{:S(2)}, u32[]{:S(2)}) %collective-permute-start) | collective-permute-done | bytes 40 | tf_op jit(solution)/shard_map/ppermute | solution.py:217
  26.9 0.8 %collective-permute-done.2.halo_one = f32[5,32,512]{2,1,0:T(8,128)S(1)} collective-permute-done((f32[5,32,512]{2,1,0:T(8,128)S(1)}, f32[5,32,512]{2,1,0:T(8,128)S(1)}, u32[]{:S(2)}, u32[]{:S(2)}) %collective-permute-start.2) | collective-permute-done | bytes 327712 | tf_op jit(solution)/shard_map/ppermute | solution.py:217
  27.7 0.0 collective-permute-done.3.halo_two
  27.7 0.0 collective-permute-done.1.state
  27.7 3.3 %shard_map.51 = (f32[2,8,32,512]{3,2,1,0:T(8,128)S(1)}, f32[5,32,512]{2,1,0:T(8,128)S(1)}, f32[5,32,512]{2,1,0:T(8,128)S(1)}) custom-call(s32[1,2]{1,0:T(1,128)S(1)} %copy-done.3, s32[1,2]{1,0:T(1,128)S(1)} %collective-permute-done.snaps_next, f32[2,8,32,512]{3,2,1,0:T(8,128)S(1)} %collective-permute-done.1.state, ...), custom_call_target="tpu_custom_call" | custom-call | tf_op jit(solution)/shard_map/pallas_call | solution.py:258
  31.0 1.1 %collective-permute-start.4 = (f32[5,32,512]{2,1,0:T(8,128)S(1)}, f32[5,32,512]{2,1,0:T(8,128)S(1)}, u32[]{:S(2)}, u32[]{:S(2)}) collective-permute-start(f32[5,32,512]{2,1,0:T(8,128)S(1)} %get-tuple-element.15), channel_id=1, source_target_pairs={{0,1},{1,0},{2,3},{3,2},{4,5},{5,4},{6,7},{7,6},{8,9},{9,8},{10,11... | collective-permute-start | bytes 983048 | tf_op jit(solution)/shard_map/ppermute | solution.py:217
  32.1 8.8 %collective-permute-start.5 = (f32[5,32,512]{2,1,0:T(8,128)S(1)}, f32[5,32,512]{2,1,0:T(8,128)S(1)}, u32[]{:S(2)}, u32[]{:S(2)}) collective-permute-start(f32[5,32,512]{2,1,0:T(8,128)S(1)} %get-tuple-element.16), channel_id=1, source_target_pairs={{0,63},{1,2},{2,1},{3,4},{4,3},{5,6},{6,5},{7,8},{8,7},{9,10},{10,... | collective-permute-start | bytes 983048 | tf_op jit(solution)/shard_map/ppermute | solution.py:217
  40.9 5.0 %collective-permute-done.4.halo_one = f32[5,32,512]{2,1,0:T(8,128)S(1)} collective-permute-done((f32[5,32,512]{2,1,0:T(8,128)S(1)}, f32[5,32,512]{2,1,0:T(8,128)S(1)}, u32[]{:S(2)}, u32[]{:S(2)}) %collective-permute-start.4) | collective-permute-done | bytes 327712 | tf_op jit(solution)/shard_map/ppermute | solution.py:217
  45.9 2.9 %collective-permute-done.5.halo_two = f32[5,32,512]{2,1,0:T(8,128)S(1)} collective-permute-done((f32[5,32,512]{2,1,0:T(8,128)S(1)}, f32[5,32,512]{2,1,0:T(8,128)S(1)}, u32[]{:S(2)}, u32[]{:S(2)}) %collective-permute-start.5) | collective-permute-done | bytes 327712 | tf_op jit(solution)/shard_map/ppermute | solution.py:217
  48.8 4.0 %shard_map.52 = (f32[2,8,32,512]{3,2,1,0:T(8,128)}, f32[8,8,512]{2,1,0:T(8,128)S(1)}, f32[8,8,512]{2,1,0:T(8,128)S(1)}, f32[8,8,512]{2,1,0:T(8,128)S(1)}, f32[8,8,512]{2,1,0:T(8,128)S(1)}) custom-call(s32[1,2]{1,0:T(1,128)S(1)} %copy-done.3, f32[2,8,32,512]{3,2,1,0:T(8,128)S(1)} %get-tuple-element.14.state, ...), custom_call_target="tpu_custom_call" | custom-call | tf_op jit(solution)/shard_map/pallas_call | solution.py:268
  52.7 0.0 collective-permute-start.6
  52.7 2.4 %collective-permute-start.7 = (f32[8,8,512]{2,1,0:T(8,128)S(1)}, f32[8,8,512]{2,1,0:T(8,128)S(1)}, u32[]{:S(2)}, u32[]{:S(2)}) collective-permute-start(f32[8,8,512]{2,1,0:T(8,128)S(1)} %get-tuple-element.20), channel_id=1, source_target_pairs={{0,128},{1,129},{2,130},{3,131},{4,132},{5,133},{6,134},{7,135},{8... | collective-permute-start | bytes 393224 | tf_op jit(solution)/shard_map/ppermute | solution.py:217
  55.1 6.0 %collective-permute-done.7 = f32[8,8,512]{2,1,0:T(8,128)S(1)} collective-permute-done((f32[8,8,512]{2,1,0:T(8,128)S(1)}, f32[8,8,512]{2,1,0:T(8,128)S(1)}, u32[]{:S(2)}, u32[]{:S(2)}) %collective-permute-start.7) | collective-permute-done | bytes 131104 | tf_op jit(solution)/shard_map/ppermute | solution.py:217
  61.1 0.6 collective-permute-done.8
  61.7 0.7 %add_add_fusion = f32[8,8,512]{2,1,0:T(8,128)} fusion(f32[8,8,512]{2,1,0:T(8,128)S(1)} %collective-permute-done.8, f32[8,8,512]{2,1,0:T(8,128)S(1)} %collective-permute-done.7, f32[8,8,512]{2,1,0:T(8,128)S(1)} %get-tuple-element.18, f32[8,8,512]{2,1,0:T(8,128)S(1)} %collective-permute-done.6), kind=kLoop, calls=%fused_computation | loop fusion | flops 98304 | bytes 655360 | tf_op jit(solution)/shard_map/add | solution.py:278
  (6 shorter events, 0.0 us)
Async XLA Ops:
  0.6 27.1 %collective-permute-start.1 = (f32[2,8,32,512]{3,2,1,0:T(8,128)}, f32[2,8,32,512]{3,2,1,0:T(8,128)S(1)}, u32[]{:S(2)}, u32[]{:S(2)}) collective-permute-start(f32[2,8,32,512]{3,2,1,0:T(8,128)} %bitcast.2), channel_id=1, source_target_pairs={{64,0},{65,1},{66,2},{67,3},{68,4},{69,5},{70,6},{71,7},{72,8},{73... | collective-permute-start | bytes 3145736 | tf_op jit(solution)/shard_map/ppermute | solution.py:239
  5.8 1.9 %copy-start = (f32[2,3,8,32,512]{4,3,2,1,0:T(8,128)S(1)}, f32[2,3,8,32,512]{4,3,2,1,0:T(8,128)}, u32[]{:S(2)}) copy-start(f32[2,3,8,32,512]{4,3,2,1,0:T(8,128)} %velocity.5) | copy-start | bytes 9437188
  7.7 1.2 %copy-start.2 = (f32[1,2,8,32,512]{4,3,2,1,0:T(8,128)S(1)}, f32[1,2,8,32,512]{4,3,2,1,0:T(8,128)}, u32[]{:S(2)}) copy-start(f32[1,2,8,32,512]{4,3,2,1,0:T(8,128)} %param.3) | copy-start | bytes 3145732
  8.9 0.7 %copy-start.3 = (s32[1,2]{1,0:T(1,128)S(1)}, s32[1,2]{1,0:T(1,128)}, u32[]{:S(2)}) copy-start(s32[1,2]{1,0:T(1,128)} %snaps.5) | copy-start | bytes 28
  10.4 17.3 %collective-permute-start.2 = (f32[5,32,512]{2,1,0:T(8,128)S(1)}, f32[5,32,512]{2,1,0:T(8,128)S(1)}, u32[]{:S(2)}, u32[]{:S(2)}) collective-permute-start(f32[5,32,512]{2,1,0:T(8,128)S(1)} %get-tuple-element.12.own_one), channel_id=1, source_target_pairs={{0,193},{1,192},{2,195},{3,194},{4,197},{5,196},{6,199},{7,198},{8... | collective-permute-start | bytes 983048 | tf_op jit(solution)/shard_map/ppermute | solution.py:217
  10.9 37.8 %copy-start.1 = (f32[2,3,8,32,512]{4,3,2,1,0:T(8,128)S(1)}, f32[2,3,8,32,512]{4,3,2,1,0:T(8,128)}, u32[]{:S(2)}) copy-start(f32[2,3,8,32,512]{4,3,2,1,0:T(8,128)} %velocity.5) | copy-start | bytes 9437188
  10.9 16.8 %collective-permute-start.3 = (f32[5,32,512]{2,1,0:T(8,128)S(1)}, f32[5,32,512]{2,1,0:T(8,128)S(1)}, u32[]{:S(2)}, u32[]{:S(2)}) collective-permute-start(f32[5,32,512]{2,1,0:T(8,128)S(1)} %get-tuple-element.13.own_two), channel_id=1, source_target_pairs={{0,255},{1,194},{2,193},{3,196},{4,195},{5,198},{6,197},{7,200},{8... | collective-permute-start | bytes 983048 | tf_op jit(solution)/shard_map/ppermute | solution.py:217
  19.7 7.2 %collective-permute-start = (s32[1,2]{1,0:T(1,128)S(1)}, s32[1,2]{1,0:T(1,128)S(1)}, u32[]{:S(2)}, u32[]{:S(2)}) collective-permute-start(s32[1,2]{1,0:T(1,128)S(1)} %copy-done.3), channel_id=1, source_target_pairs={{0,192},{1,193},{2,194},{3,195},{4,196},{5,197},{6,198},{7,199},{8... | collective-permute-start | bytes 32 | tf_op jit(solution)/shard_map/ppermute | solution.py:217
  31.0 14.8 %collective-permute-start.4 = (f32[5,32,512]{2,1,0:T(8,128)S(1)}, f32[5,32,512]{2,1,0:T(8,128)S(1)}, u32[]{:S(2)}, u32[]{:S(2)}) collective-permute-start(f32[5,32,512]{2,1,0:T(8,128)S(1)} %get-tuple-element.15), channel_id=1, source_target_pairs={{0,1},{1,0},{2,3},{3,2},{4,5},{5,4},{6,7},{7,6},{8,9},{9,8},{10,11... | collective-permute-start | bytes 983048 | tf_op jit(solution)/shard_map/ppermute | solution.py:217
  32.1 16.6 %collective-permute-start.5 = (f32[5,32,512]{2,1,0:T(8,128)S(1)}, f32[5,32,512]{2,1,0:T(8,128)S(1)}, u32[]{:S(2)}, u32[]{:S(2)}) collective-permute-start(f32[5,32,512]{2,1,0:T(8,128)S(1)} %get-tuple-element.16), channel_id=1, source_target_pairs={{0,63},{1,2},{2,1},{3,4},{4,3},{5,6},{6,5},{7,8},{8,7},{9,10},{10,... | collective-permute-start | bytes 983048 | tf_op jit(solution)/shard_map/ppermute | solution.py:217
  52.7 2.4 %collective-permute-start.6 = (f32[8,8,512]{2,1,0:T(8,128)S(1)}, f32[8,8,512]{2,1,0:T(8,128)S(1)}, u32[]{:S(2)}, u32[]{:S(2)}) collective-permute-start(f32[8,8,512]{2,1,0:T(8,128)S(1)} %get-tuple-element.19), channel_id=1, source_target_pairs={{0,64},{1,65},{2,66},{3,67},{4,68},{5,69},{6,70},{7,71},{8,72},{9,... | collective-permute-start | bytes 393224 | tf_op jit(solution)/shard_map/ppermute | solution.py:217
  52.7 8.4 %collective-permute-start.7 = (f32[8,8,512]{2,1,0:T(8,128)S(1)}, f32[8,8,512]{2,1,0:T(8,128)S(1)}, u32[]{:S(2)}, u32[]{:S(2)}) collective-permute-start(f32[8,8,512]{2,1,0:T(8,128)S(1)} %get-tuple-element.20), channel_id=1, source_target_pairs={{0,128},{1,129},{2,130},{3,131},{4,132},{5,133},{6,134},{7,135},{8... | collective-permute-start | bytes 393224 | tf_op jit(solution)/shard_map/ppermute | solution.py:217
  55.1 6.6 %collective-permute-start.8 = (f32[8,8,512]{2,1,0:T(8,128)S(1)}, f32[8,8,512]{2,1,0:T(8,128)S(1)}, u32[]{:S(2)}, u32[]{:S(2)}) collective-permute-start(f32[8,8,512]{2,1,0:T(8,128)S(1)} %get-tuple-element.21), channel_id=1, source_target_pairs={{0,192},{1,193},{2,194},{3,195},{4,196},{5,197},{6,198},{7,199},{8... | collective-permute-start | bytes 393224 | tf_op jit(solution)/shard_map/ppermute | solution.py:217

commit v3 on v2

v3 whole, which is shorter than its diff:
```python
import functools

import jax
import jax.numpy as jnp
from jax import lax
from jax.experimental import pallas as pl
from jax.experimental.pallas import tpu as pltpu
from jax.sharding import PartitionSpec as P

coupling = 0.3
diffusion = (0.14, 0.06)
sub, lanes = 8, 128
edge_count = 4


def tiles(shape):
    rows, cols = shape
    return [(i, j) for i in range(rows // sub) for j in range(cols // lanes)]


def spot(i, j):
    return (pl.ds(i * sub, sub), pl.ds(j * lanes, lanes))


def neighbours(at, i, j, shape):
    rows, cols = shape
    centre = at(i, j)
    row = lax.broadcasted_iota(jnp.int32, (sub, lanes), 0)
    col = lax.broadcasted_iota(jnp.int32, (sub, lanes), 1)
    zero = jnp.zeros_like(centre)
    after = at(i + 1, j) if (i + 1) * sub < rows else zero
    before = at(i - 1, j) if i > 0 else zero
    north = pltpu.roll(jnp.where(row == 0, after, centre), sub - 1, 0)
    south = pltpu.roll(jnp.where(row == sub - 1, before, centre), 1, 0)
    after = at(i, j + 1) if (j + 1) * lanes < cols else zero
    before = at(i, j - 1) if j > 0 else zero
    upper = pltpu.roll(jnp.where(col == 0, after, centre), lanes - 1, 1)
    lower = pltpu.roll(jnp.where(col == lanes - 1, before, centre), 1, 1)
    return centre, (north + south) + (upper + lower), north - south, upper - lower


def advanced(fields, pairs, flow, i, j, shape, wanted=(0, 1)):
    u, v, w = flow
    out = []
    for f in wanted:
        centre, total, dy, dz = neighbours(functools.partial(fields, f), i, j, shape)
        side_sum, side_diff = pairs(f, i, j)
        c = diffusion[f]
        moved = u * side_diff + v * dy + w * dz
        new = ((1.0 - 6.0 * c) * centre + c * (side_sum + total)) + 0.25 * moved
        if f == 0:
            new = new + coupling * fields(1, i, j)
        out.append(new)
    return out


def layer_of(ref, l):
    return lambda f, i, j: ref[(f, l) + spot(i, j)]


def flow_of(velocity, snap, l):
    return lambda i, j: [velocity[(snap, d, l) + spot(i, j)] for d in range(3)]


def full_layer(below, here, above, flow, shape, store, wanted=(0, 1)):
    def pairs(f, i, j):
        hi, lo = above(f, i, j), below(f, i, j)
        return hi + lo, hi - lo

    for i, j in tiles(shape):
        store(i, j, advanced(here, pairs, flow(i, j), i, j, shape, wanted))


def into(ref, l):
    def store(i, j, values):
        for f, value in enumerate(values):
            ref[(f, l) + spot(i, j)] = value

    return store


def sides(depth):
    parity = lax.rem(lax.axis_index("space"), 2)
    even = parity == 0
    high = (jnp.where(even, depth - 1, 0), jnp.where(even, depth - 2, 1), jnp.where(even, -1.0, 1.0))
    low = (jnp.where(even, 0, depth - 1), jnp.where(even, 1, depth - 2), jnp.where(even, 1.0, -1.0))
    return parity, high, low


def pack(edges, velocity, snap, message, layer, inner, sign):
    shape = edges.shape[2:]
    at = (layer // (edge_count - 1)) * (velocity.shape[2] - 1)
    near, here, flow = layer_of(edges, inner), layer_of(edges, layer), flow_of(velocity, snap, at)

    def pairs(f, i, j):
        value = near(f, i, j)
        return value, sign * value

    for i, j in tiles(shape):
        current = flow(i, j)
        out = advanced(here, pairs, current, i, j, shape)
        for f in (0, 1):
            message[(f,) + spot(i, j)] = here(f, i, j)
            message[(2 + f,) + spot(i, j)] = out[f]
        message[(4,) + spot(i, j)] = current[0]


def pack_both(edges, velocity, snap, message_one, message_two):
    unused, one, two = sides(edge_count)
    pack(edges, velocity, snap, message_one, *one)
    pack(edges, velocity, snap, message_two, *two)


def take_halos(blocks, state, halo_one, halo_two, halos, after, depth):
    shape = state.shape[2:]
    parity, one, two = sides(depth)
    place = lax.axis_index("space")
    inside = jnp.logical_and(place > 0, place < blocks - 1)
    outer = after.shape[1] - 1
    for halo, (edge, unused, sign), shown, high in (
        (halo_one, one, None, 1 - parity),
        (halo_two, two, inside, parity),
    ):
        for i, j in tiles(shape):
            u = halo[(4,) + spot(i, j)]
            for f in (0, 1):
                now = halo[(f,) + spot(i, j)]
                own = state[(f, edge) + spot(i, j)]
                later = halo[(2 + f,) + spot(i, j)] + (diffusion[f] + (0.25 * sign) * u) * own
                if shown is not None:
                    now = jnp.where(shown, now, 0.0)
                    later = jnp.where(shown, later, 0.0)
                halos[(high, f) + spot(i, j)] = now
                after[(f, high * outer) + spot(i, j)] = later


def halo_at(halos, h):
    return lambda f, i, j: halos[(h, f) + spot(i, j)]


def split_rows(total, pieces):
    rows = total.shape[1] // len(pieces)
    for by, piece in enumerate(pieces):
        start = pl.multiple_of(lax.rem(lax.axis_index("tm") + by, len(pieces)) * rows, rows)
        piece[...] = total[:, pl.ds(start, rows), :] * 0.5


def each(low, high, run):
    def step(l, carry):
        run(l)
        return carry

    lax.fori_loop(low, high, step, 0)


def start_kernel(snaps, state, velocity, message_one, message_two, scalars, edges, flows, sems):
    depth = state.shape[1]
    copies = [
        (snaps, scalars),
        (state.at[:, pl.ds(0, 2)], edges.at[:, pl.ds(0, 2)]),
        (state.at[:, pl.ds(depth - 2, 2)], edges.at[:, pl.ds(2, 2)]),
        (velocity.at[:, :, pl.ds(0, 1)], flows.at[:, :, pl.ds(0, 1)]),
        (velocity.at[:, :, pl.ds(depth - 1, 1)], flows.at[:, :, pl.ds(1, 1)]),
    ]
    copies = [pltpu.make_async_copy(*pair, sems.at[n]) for n, pair in enumerate(copies)]
    for copy in copies:
        copy.start()
    for copy in copies:
        copy.wait()
    pack_both(edges, flows, scalars[0, 1], message_one, message_two)


def first_kernel(blocks, slabs, snaps, snaps_next, state, halo_one, halo_two, velocity, start,
                 widened, edges, message_one, message_two, halos):
    depth, shape = state.shape[1], state.shape[2:]
    last = lax.axis_index("tm") == slabs - 1

    @pl.when(last)
    def _():
        pltpu.sync_copy(start.at[:, pl.ds(0, 2)], edges.at[:, pl.ds(0, 2)])
        pltpu.sync_copy(start.at[:, pl.ds(depth - 2, 2)], edges.at[:, pl.ds(2, 2)])

    @pl.when(jnp.logical_not(last))
    def _():
        take_halos(blocks, state, halo_one, halo_two, halos, widened, depth)

        def first_step(l, below, above):
            flow = flow_of(velocity, snaps_next[0, 1], l)
            full_layer(below, layer_of(state, l), above, flow, shape, into(widened, l + 1))

        first_step(0, halo_at(halos, 0), layer_of(state, 1))
        first_step(depth - 1, layer_of(state, depth - 2), halo_at(halos, 1))
        each(1, depth - 1, lambda l: first_step(l, layer_of(state, l - 1), layer_of(state, l + 1)))

        def second_step(e):
            l = e + (e // 2) * (depth - edge_count)
            flow = flow_of(velocity, snaps_next[0, 0], l)
            here = layer_of(widened, l + 1)
            full_layer(layer_of(widened, l), here, layer_of(widened, l + 2), flow, shape, into(edges, e))

        each(0, edge_count, second_step)

    pack_both(edges, velocity, snaps[0, 1], message_one, message_two)


def inner_kernel(slabs, snaps, snaps_next, widened, edges, velocity, start, carried_on, inner, *rest):
    pieces, (state, final, total, sem) = rest[:slabs], rest[slabs:]
    depth, shape = state.shape[1], state.shape[2:]
    last = lax.axis_index("tm") == slabs - 1

    @pl.when(last)
    def _():
        pltpu.sync_copy(start, state)

    @pl.when(jnp.logical_not(last))
    def _():
        def second_step(l):
            flow = flow_of(velocity, snaps_next[0, 0], l)
            here = layer_of(widened, l + 1)
            full_layer(layer_of(widened, l), here, layer_of(widened, l + 2), flow, shape, into(state, l))

        each(2, depth - 2, second_step)
        state[:, 0:2] = edges[:, 0:2]
        state[:, depth - 2 : depth] = edges[:, 2:4]

    def third_step(l):
        flow = flow_of(velocity, snaps[0, 1], l)
        here = layer_of(state, l)
        full_layer(layer_of(state, l - 1), here, layer_of(state, l + 1), flow, shape, into(carried_on, l))

    each(1, depth - 1, third_step)

    def fourth_step(l):
        def store(i, j, values):
            into(final, l - 2)(i, j, values)
            total[(l - 2,) + spot(i, j)] = carried_on[(0, l) + spot(i, j)] + values[0]

        flow = flow_of(velocity, snaps[0, 0], l)
        here = layer_of(carried_on, l)
        full_layer(layer_of(carried_on, l - 1), here, layer_of(carried_on, l + 1), flow, shape, store)

    each(2, depth - 2, fourth_step)
    copy = pltpu.make_async_copy(final, inner.at[:, pl.ds(2, depth - 4)], sem)
    copy.start()
    split_rows(total, pieces)
    copy.wait()


def last_steps(snaps, carried_on, outer, velocity, store, wanted):
    depth, shape = carried_on.shape[1], carried_on.shape[2:]
    ring = [layer_of(outer, 0), layer_of(outer, 1), layer_of(carried_on, 1), layer_of(carried_on, 2)]
    ring += [layer_of(carried_on, depth - 3), layer_of(carried_on, depth - 2), layer_of(outer, 2), layer_of(outer, 3)]
    for e, at in enumerate((1, 2, 5, 6)):
        l = e + (e // 2) * (depth - edge_count)
        flow = flow_of(velocity, snaps[0, 0], l)
        full_layer(ring[at - 1], ring[at], ring[at + 1], flow, shape, functools.partial(store, e, ring[at]), wanted)


def outer_kernel(blocks, slabs, snaps, edges, halo_one, halo_two, carried_on, velocity, outer, *rest):
    pieces, (halos, total) = rest[:slabs], rest[slabs:]
    depth, shape = carried_on.shape[1], carried_on.shape[2:]
    take_halos(blocks, edges, halo_one, halo_two, halos, outer, edge_count)
    flow = flow_of(velocity, snaps[0, 1], 0)
    full_layer(halo_at(halos, 0), layer_of(edges, 0), layer_of(edges, 1), flow, shape, into(outer, 1))
    flow = flow_of(velocity, snaps[0, 1], depth - 1)
    full_layer(layer_of(edges, 2), layer_of(edges, 3), halo_at(halos, 1), flow, shape, into(outer, 2))

    def store(e, here, i, j, values):
        total[(e,) + spot(i, j)] = here(0, i, j) + values[0]

    last_steps(snaps, carried_on, outer, velocity, store, (0,))
    split_rows(total, pieces)


def finish_kernel(snaps, carried_on, outer, velocity, inner, out, final, sems):
    depth = carried_on.shape[1]

    def store(e, here, i, j, values):
        into(final, e)(i, j, values)

    last_steps(snaps, carried_on, outer, velocity, store, (0, 1))
    copies = [
        pltpu.make_async_copy(final.at[:, pl.ds(0, 2)], out.at[:, pl.ds(0, 2)], sems.at[0]),
        pltpu.make_async_copy(final.at[:, pl.ds(2, 2)], out.at[:, pl.ds(depth - 2, 2)], sems.at[1]),
    ]
    for copy in copies:
        copy.start()
    for copy in copies:
        copy.wait()


def sum_kernel(*refs):
    ins, out = refs[:-1], refs[-1]
    half = len(ins) // 2
    depth = out.shape[0]
    inner = functools.reduce(jnp.add, [ref[...] for ref in ins[:half]])
    outer = functools.reduce(jnp.add, [ref[...] for ref in ins[half:]])
    out[2 : depth - 2] = inner
    out[0:2] = outer[0:2]
    out[depth - 2 : depth] = outer[2:4]


def solution(mesh):
    slabs, blocks = mesh.shape["tm"], mesh.shape["space"]
    vmem, smem = pl.BlockSpec(memory_space=pltpu.VMEM), pl.BlockSpec(memory_space=pltpu.SMEM)
    hbm = pl.BlockSpec(memory_space=pltpu.HBM)
    sem = pltpu.SemaphoreType.DMA

    def params(mebibytes):
        return pltpu.CompilerParams(vmem_limit_bytes=mebibytes * 1024 * 1024)

    def cost(microseconds):
        return pl.CostEstimate(flops=0, bytes_accessed=int(microseconds * 3.6e6), transcendentals=0)

    def index(t, s):
        return (t % slabs) * blocks + s % blocks

    def moved(array, to):
        pairs = [(index(t, s), index(*to(t, s))) for t in range(slabs) for s in range(blocks)]
        return lax.ppermute(array, ("tm", "space"), pairs)

    def one(s):
        return s ^ 1

    def two(s):
        return (((s + 1) ^ 1) - 1) % blocks

    def body(slab_states, velocity, snap_of_step):
        start = slab_states[0]
        fields, depth, ny, nz = start.shape

        def shaped(*lead, rows=ny):
            return jax.ShapeDtypeStruct(lead + (rows, nz), jnp.float32)

        def room(*lead):
            return pltpu.VMEM(lead + (ny, nz), jnp.float32)

        layer = shaped(5)
        pieces = (shaped(4, rows=ny // slabs),) * slabs

        state = moved(start, lambda t, s: (t - 1, s))
        snaps_next = moved(snap_of_step, lambda t, s: (t - 1, s))
        message_one, message_two = pl.pallas_call(
            start_kernel,
            out_shape=(layer, layer),
            in_specs=[hbm] * 3,
            out_specs=(vmem, vmem),
            scratch_shapes=[
                pltpu.SMEM(snap_of_step.shape, jnp.int32),
                room(fields, edge_count),
                room(*velocity.shape[:2], 2),
                sem((5,)),
            ],
            compiler_params=params(56),
            cost_estimate=cost(2),
        )(snap_of_step, start, velocity)
        halo_one = moved(message_one, lambda t, s: (t - 1, one(s)))
        halo_two = moved(message_two, lambda t, s: (t - 1, two(s)))
        widened, edges, message_one, message_two = pl.pallas_call(
            functools.partial(first_kernel, blocks, slabs),
            out_shape=(shaped(fields, depth + 2), shaped(fields, edge_count), layer, layer),
            in_specs=[smem, smem] + [vmem] * 4 + [hbm],
            out_specs=(vmem,) * 4,
            scratch_shapes=[room(2, fields)],
            compiler_params=params(32),
            cost_estimate=cost(2.5),
        )(snap_of_step, snaps_next, state, halo_one, halo_two, velocity, start)
        halo_one = moved(message_one, lambda t, s: (t, one(s)))
        halo_two = moved(message_two, lambda t, s: (t, two(s)))
        carried_on, inner, *inner_pieces = pl.pallas_call(
            functools.partial(inner_kernel, slabs),
            out_shape=(shaped(fields, depth), shaped(fields, depth)) + pieces,
            in_specs=[smem, smem, vmem, vmem, vmem, hbm],
            out_specs=(vmem, hbm) + (vmem,) * slabs,
            scratch_shapes=[room(fields, depth), room(fields, depth - 4), room(depth - 4), sem(())],
            compiler_params=params(32),
            cost_estimate=cost(3),
        )(snap_of_step, snaps_next, widened, edges, velocity, start)
        inner_parts = inner_pieces[:1] + [
            moved(inner_pieces[by], lambda t, s, by=by: (t + by, s)) for by in range(1, slabs)
        ]
        outer, *outer_pieces = pl.pallas_call(
            functools.partial(outer_kernel, blocks, slabs),
            out_shape=(shaped(fields, edge_count),) + pieces,
            in_specs=[smem] + [vmem] * 5,
            out_specs=(vmem,) * (1 + slabs),
            scratch_shapes=[room(2, fields), room(edge_count)],
            compiler_params=params(32),
            cost_estimate=cost(1),
        )(snap_of_step, edges, halo_one, halo_two, carried_on, velocity)
        outer_parts = outer_pieces[:1] + [
            moved(outer_pieces[by], lambda t, s, by=by: (t + by, s)) for by in range(1, slabs)
        ]
        final = pl.pallas_call(
            finish_kernel,
            out_shape=shaped(fields, depth),
            in_specs=[smem, vmem, vmem, vmem, hbm],
            out_specs=hbm,
            scratch_shapes=[room(fields, edge_count), sem((2,))],
            input_output_aliases={4: 0},
            compiler_params=params(32),
            cost_estimate=cost(1),
        )(snap_of_step, carried_on, outer, velocity, inner)
        gradient = pl.pallas_call(
            sum_kernel,
            out_shape=shaped(depth, rows=ny // slabs),
            in_specs=[vmem] * (2 * slabs),
            out_specs=vmem,
            compiler_params=params(16),
            cost_estimate=cost(0.5),
        )(*inner_parts, *outer_parts)
        return (final[None], gradient)

    return jax.shard_map(
        body,
        mesh=mesh,
        in_specs=(P("tm", None, "space", None, None), P(None, None, "space", None, None), P("tm", None)),
        out_specs=(P("tm", None, "space", None, None), P("space", "tm", None)),
        check_vma=False,
    )
```

time: 62.6 us -> 54.3 us (0.87)
  waiting for transfers between devices: 21.9 us -> 13.7 us
  Pallas kernels: 8.13 us -> 12.2 us
  local copies, waits for them, and re-layouts: 3.77 us -> 0.01 us
  other arithmetic: 0.69 us -> 0 us
    ppermute x8 -> x12, waiting for transfers between devices: 21.9 us -> 13.7 us  [moved(): return lax.ppermute(array, ('tm', 'space'), pairs)]
    ppermute x8 -> x12, starting transfers between devices: 22 us -> 27.6 us  [moved(): return lax.ppermute(array, ('tm', 'space'), pairs)]
    ppermute x1 -> x0, starting transfers between devices: 5.15 us -> none  [earlier(): return lax.ppermute(array, ('tm', 'space'), pairs)]
    pallas_call x2 -> x5, Pallas kernels: 4.82 us -> 9.5 us  [the longest x1 3.54 us: body(): pl.pallas_call(functools.partial(inner_kernel, slabs), out_shape=(shaped(...]
    unnamed x8 -> x6, local copies, waits for them, and re-layouts: 3.77 us -> 0.01 us
    add x1 -> x0, other arithmetic: 0.69 us -> none  [body(): gradient + moved(results[1 + by], lambda t, s, by=by: (t + by, s))]
    pallas_call x1, Pallas kernels: 3.31 us -> 2.66 us  [body(): pl.pallas_call(functools.partial(first_kernel, blocks, slabs), out_shape=...]
  transfers between devices with their start and end apart: 9 -> 12, of which waited for: 6 -> 4; matrix products, arithmetic and copies ran while one was open for 0% -> 0% of each run, Pallas kernels for 1% -> 16%
where the time goes in v3:
time: 54.3 us; the launch traced here: 54.2 us
  starting transfers between devices  27.6 us (51%)
  waiting for transfers between devices  13.7 us (25%)
  Pallas kernels  12.2 us (22%)
  between operations  0.74 us (1%)
    ppermute x12, starting transfers between devices, moved(): return lax.ppermute(array, ('tm', 'space'), pairs)  27.6 us
    ppermute x12, waiting for transfers between devices, moved(): return lax.ppermute(array, ('tm', 'space'), pairs)  13.7 us
    pallas_call x1, Pallas kernels, body(): pl.pallas_call(functools.partial(inner_kernel, slabs), out_shape=(shaped(...  3.54 us
    pallas_call x1, Pallas kernels, body(): pl.pallas_call(functools.partial(first_kernel, blocks, slabs), out_shape=...  2.66 us
    pallas_call x1, Pallas kernels, body(): pl.pallas_call(start_kernel, out_shape=(layer, layer), in_specs=[hbm] * 3...  2.31 us
    pallas_call x1, Pallas kernels, body(): pl.pallas_call(finish_kernel, out_shape=shaped(fields, depth), in_specs=[...  1.81 us
    pallas_call x1, Pallas kernels, body(): pl.pallas_call(functools.partial(outer_kernel, blocks, slabs), out_shape=...  1.15 us
  transfers between devices with their start and end apart: 12, of which 4 were waited for; matrix products, arithmetic and copies ran while one was open for 0% of the time, Pallas kernels for 16%

profile of v3, /device:TPU:1, one launch (start us, length us, event | category | flops | bytes accessed | tf_op | source)
XLA Modules:
  0.0 54.2 jit_solution(5353049444710153405)
XLA Ops:
  0.7 3.3 %collective-permute-start.1 = (f32[2,8,32,512]{3,2,1,0:T(8,128)}, f32[2,8,32,512]{3,2,1,0:T(8,128)S(1)}, u32[]{:S(2)}, u32[]{:S(2)}) collective-permute-start(f32[2,8,32,512]{3,2,1,0:T(8,128)} %bitcast.2), channel_id=1, source_target_pairs={{0,192},{1,193},{2,194},{3,195},{4,196},{5,197},{6,198},{7,199},{8... | collective-permute-start | bytes 3145736 | tf_op jit(solution)/shard_map/ppermute | solution.py:320
  4.0 2.3 %shard_map.50 = (f32[5,32,512]{2,1,0:T(8,128)}, f32[5,32,512]{2,1,0:T(8,128)}) custom-call(s32[1,2]{1,0:T(1,128)} %snaps.9, f32[2,8,32,512]{3,2,1,0:T(8,128)} %bitcast.3, f32[2,3,8,32,512]{4,3,2,1,0:T(8,128)} %velocity.9), custom_call_target="tpu_custom_call" | custom-call | bytes 7200000 | tf_op jit(solution)/shard_map/pallas_call | solution.py:343
  6.3 2.3 %collective-permute-start.2 = (f32[5,32,512]{2,1,0:T(8,128)}, f32[5,32,512]{2,1,0:T(8,128)S(1)}, u32[]{:S(2)}, u32[]{:S(2)}) collective-permute-start(f32[5,32,512]{2,1,0:T(8,128)} %get-tuple-element.19), channel_id=1, source_target_pairs={{0,193},{1,192},{2,195},{3,194},{4,197},{5,196},{6,199},{7,198},{8... | collective-permute-start | bytes 983048 | tf_op jit(solution)/shard_map/ppermute | solution.py:320
  8.6 7.6 %collective-permute-start.3 = (f32[5,32,512]{2,1,0:T(8,128)}, f32[5,32,512]{2,1,0:T(8,128)S(1)}, u32[]{:S(2)}, u32[]{:S(2)}) collective-permute-start(f32[5,32,512]{2,1,0:T(8,128)} %get-tuple-element.20), channel_id=1, source_target_pairs={{0,255},{1,194},{2,193},{3,196},{4,195},{5,198},{6,197},{7,200},{8... | collective-permute-start | bytes 983048 | tf_op jit(solution)/shard_map/ppermute | solution.py:320
  16.2 0.1 collective-permute-start
  16.3 8.8 %collective-permute-done.snaps_next = s32[1,2]{1,0:T(1,128)S(1)} collective-permute-done((s32[1,2]{1,0:T(1,128)S(1)}, s32[1,2]{1,0:T(1,128)S(1)}, u32[]{:S(2)}, u32[]{:S(2)}) %collective-permute-start) | collective-permute-done | bytes 40 | tf_op jit(solution)/shard_map/ppermute | solution.py:320
  25.0 0.0 collective-permute-done.1.state
  25.1 2.7 %shard_map.51 = (f32[2,10,32,512]{3,2,1,0:T(8,128)S(1)}, f32[2,4,32,512]{3,2,1,0:T(8,128)S(1)}, f32[5,32,512]{2,1,0:T(8,128)S(1)}, f32[5,32,512]{2,1,0:T(8,128)S(1)}) custom-call(s32[1,2]{1,0:T(1,128)S(1)} %copy-done.2, s32[1,2]{1,0:T(1,128)S(1)} %collective-permute-done.snaps_next, f32[2,8,32,512]{3,2,1,0:T(8,128)S(1)} %collective-permute-done.1.state, ...), custom_call_target="tpu_custom_call" | custom-call | bytes 9000000 | tf_op jit(solution)/shard_map/pallas_call | solution.py:359
  27.7 1.0 %collective-permute-start.4 = (f32[5,32,512]{2,1,0:T(8,128)S(1)}, f32[5,32,512]{2,1,0:T(8,128)S(1)}, u32[]{:S(2)}, u32[]{:S(2)}) collective-permute-start(f32[5,32,512]{2,1,0:T(8,128)S(1)} %get-tuple-element.24), channel_id=1, source_target_pairs={{0,1},{1,0},{2,3},{3,2},{4,5},{5,4},{6,7},{7,6},{8,9},{9,8},{10,11... | collective-permute-start | bytes 983048 | tf_op jit(solution)/shard_map/ppermute | solution.py:320
  28.8 9.7 %collective-permute-start.5 = (f32[5,32,512]{2,1,0:T(8,128)S(1)}, f32[5,32,512]{2,1,0:T(8,128)S(1)}, u32[]{:S(2)}, u32[]{:S(2)}) collective-permute-start(f32[5,32,512]{2,1,0:T(8,128)S(1)} %get-tuple-element.25), channel_id=1, source_target_pairs={{0,63},{1,2},{2,1},{3,4},{4,3},{5,6},{6,5},{7,8},{8,7},{9,10},{10,... | collective-permute-start | bytes 983048 | tf_op jit(solution)/shard_map/ppermute | solution.py:320
  38.4 3.5 %shard_map.52 = (f32[2,8,32,512]{3,2,1,0:T(8,128)S(1)}, f32[2,8,32,512]{3,2,1,0:T(8,128)}, f32[4,8,512]{2,1,0:T(8,128)S(1)}, f32[4,8,512]{2,1,0:T(8,128)S(1)}, f...) custom-call(s32[1,2]{1,0:T(1,128)S(1)} %copy-done.2, s32[1,2]{1,0:T(1,128)S(1)} %collective-permute-done.snaps_next, ...), custom_call_target="tpu_custom_call" | custom-call | bytes 10800000 | tf_op jit(solution)/shard_map/pallas_call | solution.py:370
  42.0 0.1 collective-permute-start.6
  42.1 1.5 %collective-permute-start.7 = (f32[4,8,512]{2,1,0:T(8,128)S(1)}, f32[4,8,512]{2,1,0:T(8,128)S(1)}, u32[]{:S(2)}, u32[]{:S(2)}) collective-permute-start(f32[4,8,512]{2,1,0:T(8,128)S(1)} %get-tuple-element.30), channel_id=1, source_target_pairs={{0,128},{1,129},{2,130},{3,131},{4,132},{5,133},{6,134},{7,135},{8... | collective-permute-start | bytes 196616 | tf_op jit(solution)/shard_map/ppermute | solution.py:320
  43.6 3.0 %collective-permute-done.5.halo_two = f32[5,32,512]{2,1,0:T(8,128)S(1)} collective-permute-done((f32[5,32,512]{2,1,0:T(8,128)S(1)}, f32[5,32,512]{2,1,0:T(8,128)S(1)}, u32[]{:S(2)}, u32[]{:S(2)}) %collective-permute-start.5) | collective-permute-done | bytes 327712 | tf_op jit(solution)/shard_map/ppermute | solution.py:320
  46.6 1.2 %shard_map.53 = (f32[2,4,32,512]{3,2,1,0:T(8,128)S(1)}, f32[4,8,512]{2,1,0:T(8,128)S(1)}, f32[4,8,512]{2,1,0:T(8,128)S(1)}, f32[4,8,512]{2,1,0:T(8,128)S(1)}, f32[4,8,512]{2,1,0:T(8,128)S(1)}) custom-call(s32[1,2]{1,0:T(1,128)S(1)} %copy-done.2, f32[2,4,32,512]{3,2,1,0:T(8,128)S(1)} %get-tuple-element.22.edges, ...), custom_call_target="tpu_custom_call" | custom-call | bytes 3600000 | tf_op jit(solution)/shard_map/pallas_call | solution.py:382
  47.8 0.3 collective-permute-start.9
  48.1 1.7 %collective-permute-start.10 = (f32[4,8,512]{2,1,0:T(8,128)S(1)}, f32[4,8,512]{2,1,0:T(8,128)S(1)}, u32[]{:S(2)}, u32[]{:S(2)}) collective-permute-start(f32[4,8,512]{2,1,0:T(8,128)S(1)} %get-tuple-element.34), channel_id=1, source_target_pairs={{0,128},{1,129},{2,130},{3,131},{4,132},{5,133},{6,134},{7,135},{8... | collective-permute-start | bytes 196616 | tf_op jit(solution)/shard_map/ppermute | solution.py:320
  49.8 0.0 collective-permute-done.6.refs_1_
  49.8 0.0 collective-permute-start.11
  49.8 1.8 %shard_map.54 = f32[2,8,32,512]{3,2,1,0:T(8,128)} custom-call(s32[1,2]{1,0:T(1,128)S(1)} %copy-done.2, f32[2,8,32,512]{3,2,1,0:T(8,128)S(1)} %get-tuple-element.23.carried_on, f32[2,4,32,512]{3,2,1,0:T(8,128)S(1)} %get-tuple-element.26.outer, f32[2,3,8,32,512]{4,3,2,1,0:T(8,128)S(1)} %copy-done, ...), custom_call_target="tpu_custom_call", output_to_operand_aliasing={{}: (4, {})} | custom-call | bytes 3600000 | tf_op jit(solution)/shard_map/pallas_call | solution.py:394
  51.6 0.0 collective-permute-done.8.refs_3_
  51.7 1.4 %collective-permute-done.10.refs_6_ = f32[4,8,512]{2,1,0:T(8,128)S(1)} collective-permute-done((f32[4,8,512]{2,1,0:T(8,128)S(1)}, f32[4,8,512]{2,1,0:T(8,128)S(1)}, u32[]{:S(2)}, u32[]{:S(2)}) %collective-permute-start.10) | collective-permute-done | bytes 65568 | tf_op jit(solution)/shard_map/ppermute | solution.py:320
  53.1 0.5 collective-permute-done.11.refs_7_
  53.5 0.7 %shard_map.55 = f32[8,8,512]{2,1,0:T(8,128)} custom-call(f32[4,8,512]{2,1,0:T(8,128)S(1)} %get-tuple-element.28.refs_0_, f32[4,8,512]{2,1,0:T(8,128)S(1)} %collective-permute-done.6.refs_1_, f32[4,8,512]{2,1,0:T(8,128)S(1)} %collective-permute-done.7.refs_2_, f32[4,8,512]{2,1,0:T(8,128)S(1)} %collective-permute-done.8.refs_3_, ...), custom_call_target="tpu_custom_call" | custom-call | bytes 1800000 | tf_op jit(solution)/shard_map/pallas_call | solution.py:404
  (12 shorter events, 0.0 us)
Async XLA Ops:
  0.6 24.4 %copy-start.1 = (f32[1,2,8,32,512]{4,3,2,1,0:T(8,128)S(1)}, f32[1,2,8,32,512]{4,3,2,1,0:T(8,128)}, u32[]{:S(2)}) copy-start(f32[1,2,8,32,512]{4,3,2,1,0:T(8,128)} %param.3) | copy-start | bytes 3145732
  0.6 15.5 %copy-start.2 = (s32[1,2]{1,0:T(1,128)S(1)}, s32[1,2]{1,0:T(1,128)}, u32[]{:S(2)}) copy-start(s32[1,2]{1,0:T(1,128)} %snaps.9) | copy-start | bytes 28
  0.6 24.4 %copy-start = (f32[2,3,8,32,512]{4,3,2,1,0:T(8,128)S(1)}, f32[2,3,8,32,512]{4,3,2,1,0:T(8,128)}, u32[]{:S(2)}) copy-start(f32[2,3,8,32,512]{4,3,2,1,0:T(8,128)} %velocity.9) | copy-start | bytes 9437188
  0.7 24.4 %collective-permute-start.1 = (f32[2,8,32,512]{3,2,1,0:T(8,128)}, f32[2,8,32,512]{3,2,1,0:T(8,128)S(1)}, u32[]{:S(2)}, u32[]{:S(2)}) collective-permute-start(f32[2,8,32,512]{3,2,1,0:T(8,128)} %bitcast.2), channel_id=1, source_target_pairs={{0,192},{1,193},{2,194},{3,195},{4,196},{5,197},{6,198},{7,199},{8... | collective-permute-start | bytes 3145736 | tf_op jit(solution)/shard_map/ppermute | solution.py:320
  6.3 18.7 %collective-permute-start.2 = (f32[5,32,512]{2,1,0:T(8,128)}, f32[5,32,512]{2,1,0:T(8,128)S(1)}, u32[]{:S(2)}, u32[]{:S(2)}) collective-permute-start(f32[5,32,512]{2,1,0:T(8,128)} %get-tuple-element.19), channel_id=1, source_target_pairs={{0,193},{1,192},{2,195},{3,194},{4,197},{5,196},{6,199},{7,198},{8... | collective-permute-start | bytes 983048 | tf_op jit(solution)/shard_map/ppermute | solution.py:320
  8.6 16.5 %collective-permute-start.3 = (f32[5,32,512]{2,1,0:T(8,128)}, f32[5,32,512]{2,1,0:T(8,128)S(1)}, u32[]{:S(2)}, u32[]{:S(2)}) collective-permute-start(f32[5,32,512]{2,1,0:T(8,128)} %get-tuple-element.20), channel_id=1, source_target_pairs={{0,255},{1,194},{2,193},{3,196},{4,195},{5,198},{6,197},{7,200},{8... | collective-permute-start | bytes 983048 | tf_op jit(solution)/shard_map/ppermute | solution.py:320
  16.2 8.9 %collective-permute-start = (s32[1,2]{1,0:T(1,128)S(1)}, s32[1,2]{1,0:T(1,128)S(1)}, u32[]{:S(2)}, u32[]{:S(2)}) collective-permute-start(s32[1,2]{1,0:T(1,128)S(1)} %copy-done.2), channel_id=1, source_target_pairs={{0,192},{1,193},{2,194},{3,195},{4,196},{5,197},{6,198},{7,199},{8... | collective-permute-start | bytes 32 | tf_op jit(solution)/shard_map/ppermute | solution.py:320
  27.7 15.9 %collective-permute-start.4 = (f32[5,32,512]{2,1,0:T(8,128)S(1)}, f32[5,32,512]{2,1,0:T(8,128)S(1)}, u32[]{:S(2)}, u32[]{:S(2)}) collective-permute-start(f32[5,32,512]{2,1,0:T(8,128)S(1)} %get-tuple-element.24), channel_id=1, source_target_pairs={{0,1},{1,0},{2,3},{3,2},{4,5},{5,4},{6,7},{7,6},{8,9},{9,8},{10,11... | collective-permute-start | bytes 983048 | tf_op jit(solution)/shard_map/ppermute | solution.py:320
  28.8 17.8 %collective-permute-start.5 = (f32[5,32,512]{2,1,0:T(8,128)S(1)}, f32[5,32,512]{2,1,0:T(8,128)S(1)}, u32[]{:S(2)}, u32[]{:S(2)}) collective-permute-start(f32[5,32,512]{2,1,0:T(8,128)S(1)} %get-tuple-element.25), channel_id=1, source_target_pairs={{0,63},{1,2},{2,1},{3,4},{4,3},{5,6},{6,5},{7,8},{8,7},{9,10},{10,... | collective-permute-start | bytes 983048 | tf_op jit(solution)/shard_map/ppermute | solution.py:320
  42.0 7.8 %collective-permute-start.6 = (f32[4,8,512]{2,1,0:T(8,128)S(1)}, f32[4,8,512]{2,1,0:T(8,128)S(1)}, u32[]{:S(2)}, u32[]{:S(2)}) collective-permute-start(f32[4,8,512]{2,1,0:T(8,128)S(1)} %get-tuple-element.29), channel_id=1, source_target_pairs={{0,64},{1,65},{2,66},{3,67},{4,68},{5,69},{6,70},{7,71},{8,72},{9,... | collective-permute-start | bytes 196616 | tf_op jit(solution)/shard_map/ppermute | solution.py:320
  42.1 9.5 %collective-permute-start.7 = (f32[4,8,512]{2,1,0:T(8,128)S(1)}, f32[4,8,512]{2,1,0:T(8,128)S(1)}, u32[]{:S(2)}, u32[]{:S(2)}) collective-permute-start(f32[4,8,512]{2,1,0:T(8,128)S(1)} %get-tuple-element.30), channel_id=1, source_target_pairs={{0,128},{1,129},{2,130},{3,131},{4,132},{5,133},{6,134},{7,135},{8... | collective-permute-start | bytes 196616 | tf_op jit(solution)/shard_map/ppermute | solution.py:320
  43.6 8.0 %collective-permute-start.8 = (f32[4,8,512]{2,1,0:T(8,128)S(1)}, f32[4,8,512]{2,1,0:T(8,128)S(1)}, u32[]{:S(2)}, u32[]{:S(2)}) collective-permute-start(f32[4,8,512]{2,1,0:T(8,128)S(1)} %get-tuple-element.31), channel_id=1, source_target_pairs={{0,192},{1,193},{2,194},{3,195},{4,196},{5,197},{6,198},{7,199},{8... | collective-permute-start | bytes 196616 | tf_op jit(solution)/shard_map/ppermute | solution.py:320
  47.8 3.9 %collective-permute-start.9 = (f32[4,8,512]{2,1,0:T(8,128)S(1)}, f32[4,8,512]{2,1,0:T(8,128)S(1)}, u32[]{:S(2)}, u32[]{:S(2)}) collective-permute-start(f32[4,8,512]{2,1,0:T(8,128)S(1)} %get-tuple-element.33), channel_id=1, source_target_pairs={{0,64},{1,65},{2,66},{3,67},{4,68},{5,69},{6,70},{7,71},{8,72},{9,... | collective-permute-start | bytes 196616 | tf_op jit(solution)/shard_map/ppermute | solution.py:320
  48.1 5.0 %collective-permute-start.10 = (f32[4,8,512]{2,1,0:T(8,128)S(1)}, f32[4,8,512]{2,1,0:T(8,128)S(1)}, u32[]{:S(2)}, u32[]{:S(2)}) collective-permute-start(f32[4,8,512]{2,1,0:T(8,128)S(1)} %get-tuple-element.34), channel_id=1, source_target_pairs={{0,128},{1,129},{2,130},{3,131},{4,132},{5,133},{6,134},{7,135},{8... | collective-permute-start | bytes 196616 | tf_op jit(solution)/shard_map/ppermute | solution.py:320
  49.8 3.8 %collective-permute-start.11 = (f32[4,8,512]{2,1,0:T(8,128)S(1)}, f32[4,8,512]{2,1,0:T(8,128)S(1)}, u32[]{:S(2)}, u32[]{:S(2)}) collective-permute-start(f32[4,8,512]{2,1,0:T(8,128)S(1)} %get-tuple-element.35), channel_id=1, source_target_pairs={{0,192},{1,193},{2,194},{3,195},{4,196},{5,197},{6,198},{7,199},{8... | collective-permute-start | bytes 196616 | tf_op jit(solution)/shard_map/ppermute | solution.py:320

commit v4 on v3

--- a/solution.py
+++ b/solution.py
@@ -97,12 +97,10 @@
         return value, sign * value
 
     for i, j in tiles(shape):
-        current = flow(i, j)
-        out = advanced(here, pairs, current, i, j, shape)
+        out = advanced(here, pairs, flow(i, j), i, j, shape)
         for f in (0, 1):
             message[(f,) + spot(i, j)] = here(f, i, j)
             message[(2 + f,) + spot(i, j)] = out[f]
-        message[(4,) + spot(i, j)] = current[0]
 
 
 def pack_both(edges, velocity, snap, message_one, message_two):
@@ -111,18 +109,19 @@
     pack(edges, velocity, snap, message_two, *two)
 
 
-def take_halos(blocks, state, halo_one, halo_two, halos, after, depth):
+def take_halos(blocks, state, halo_one, halo_two, own_flow, other_flow, snap, halos, after, depth):
     shape = state.shape[2:]
     parity, one, two = sides(depth)
     place = lax.axis_index("space")
     inside = jnp.logical_and(place > 0, place < blocks - 1)
     outer = after.shape[1] - 1
+    fetched = lax.rem(lax.axis_index("tm"), 2)
     for halo, (edge, unused, sign), shown, high in (
         (halo_one, one, None, 1 - parity),
         (halo_two, two, inside, parity),
     ):
         for i, j in tiles(shape):
-            u = halo[(4,) + spot(i, j)]
+            u = jnp.where(high == fetched, own_flow[(snap,) + spot(i, j)], other_flow[(snap,) + spot(i, j)])
             for f in (0, 1):
                 now = halo[(f,) + spot(i, j)]
                 own = state[(f, edge) + spot(i, j)]
@@ -153,7 +152,7 @@
     lax.fori_loop(low, high, step, 0)
 
 
-def start_kernel(snaps, state, velocity, message_one, message_two, scalars, edges, flows, sems):
+def start_kernel(snaps, state, velocity, message_one, message_two, flow_out, scalars, edges, flows, sems):
     depth = state.shape[1]
     copies = [
         (snaps, scalars),
@@ -168,9 +167,10 @@
     for copy in copies:
         copy.wait()
     pack_both(edges, flows, scalars[0, 1], message_one, message_two)
-
-
-def first_kernel(blocks, slabs, snaps, snaps_next, state, halo_one, halo_two, velocity, start,
+    flow_out[...] = flows[:, 0, 1 - lax.rem(lax.axis_index("tm"), 2)]
+
+
+def first_kernel(blocks, slabs, snaps, snaps_next, state, halo_one, halo_two, own_flow, other_flow, velocity, start,
                  widened, edges, message_one, message_two, halos):
     depth, shape = state.shape[1], state.shape[2:]
     last = lax.axis_index("tm") == slabs - 1
@@ -182,7 +182,9 @@
 
     @pl.when(jnp.logical_not(last))
     def _():
-        take_halos(blocks, state, halo_one, halo_two, halos, widened, depth)
+        take_halos(
+            blocks, state, halo_one, halo_two, own_flow, other_flow, snaps_next[0, 1], halos, widened, depth
+        )
 
         def first_step(l, below, above):
             flow = flow_of(velocity, snaps_next[0, 1], l)
@@ -256,10 +258,13 @@
         full_layer(ring[at - 1], ring[at], ring[at + 1], flow, shape, functools.partial(store, e, ring[at]), wanted)
 
 
-def outer_kernel(blocks, slabs, snaps, edges, halo_one, halo_two, carried_on, velocity, outer, *rest):
+def outer_kernel(blocks, slabs, snaps, edges, halo_one, halo_two, own_flow, other_flow, carried_on, velocity,
+                 outer, *rest):
     pieces, (halos, total) = rest[:slabs], rest[slabs:]
     depth, shape = carried_on.shape[1], carried_on.shape[2:]
-    take_halos(blocks, edges, halo_one, halo_two, halos, outer, edge_count)
+    take_halos(
+        blocks, edges, halo_one, halo_two, own_flow, other_flow, snaps[0, 1], halos, outer, edge_count
+    )
     flow = flow_of(velocity, snaps[0, 1], 0)
     full_layer(halo_at(halos, 0), layer_of(edges, 0), layer_of(edges, 1), flow, shape, into(outer, 1))
     flow = flow_of(velocity, snaps[0, 1], depth - 1)
@@ -335,16 +340,16 @@
         def room(*lead):
             return pltpu.VMEM(lead + (ny, nz), jnp.float32)
 
-        layer = shaped(5)
+        layer = shaped(4)
         pieces = (shaped(4, rows=ny // slabs),) * slabs
 
         state = moved(start, lambda t, s: (t - 1, s))
         snaps_next = moved(snap_of_step, lambda t, s: (t - 1, s))
-        message_one, message_two = pl.pallas_call(
+        message_one, message_two, flow_out = pl.pallas_call(
             start_kernel,
-            out_shape=(layer, layer),
+            out_shape=(layer, layer, shaped(velocity.shape[0])),
             in_specs=[hbm] * 3,
-            out_specs=(vmem, vmem),
+            out_specs=(vmem,) * 3,
             scratch_shapes=[
                 pltpu.SMEM(snap_of_step.shape, jnp.int32),
                 room(fields, edge_count),
@@ -356,15 +361,17 @@
         )(snap_of_step, start, velocity)
         halo_one = moved(message_one, lambda t, s: (t - 1, one(s)))
         halo_two = moved(message_two, lambda t, s: (t - 1, two(s)))
+        own_flow = moved(flow_out, lambda t, s: (t ^ 2, s + 1 - 2 * (t % 2)))
+        other_flow = moved(own_flow, lambda t, s: (t ^ 1, s))
         widened, edges, message_one, message_two = pl.pallas_call(
             functools.partial(first_kernel, blocks, slabs),
             out_shape=(shaped(fields, depth + 2), shaped(fields, edge_count), layer, layer),
-            in_specs=[smem, smem] + [vmem] * 4 + [hbm],
+            in_specs=[smem, smem] + [vmem] * 6 + [hbm],
             out_specs=(vmem,) * 4,
             scratch_shapes=[room(2, fields)],
             compiler_params=params(32),
             cost_estimate=cost(2.5),
-        )(snap_of_step, snaps_next, state, halo_one, halo_two, velocity, start)
+        )(snap_of_step, snaps_next, state, halo_one, halo_two, own_flow, other_flow, velocity, start)
         halo_one = moved(message_one, lambda t, s: (t, one(s)))
         halo_two = moved(message_two, lambda t, s: (t, two(s)))
         carried_on, inner, *inner_pieces = pl.pallas_call(
@@ -382,12 +389,12 @@
         outer, *outer_pieces = pl.pallas_call(
             functools.partial(outer_kernel, blocks, slabs),
             out_shape=(shaped(fields, edge_count),) + pieces,
-            in_specs=[smem] + [vmem] * 5,
+            in_specs=[smem] + [vmem] * 7,
             out_specs=(vmem,) * (1 + slabs),
             scratch_shapes=[room(2, fields), room(edge_count)],
             compiler_params=params(32),
             cost_estimate=cost(1),
-        )(snap_of_step, edges, halo_one, halo_two, carried_on, velocity)
+        )(snap_of_step, edges, halo_one, halo_two, own_flow, other_flow, carried_on, velocity)
         outer_parts = outer_pieces[:1] + [
             moved(outer_pieces[by], lambda t, s, by=by: (t + by, s)) for by in range(1, slabs)
         ]

time: 54.3 us -> 52.5 us (0.967)
  starting transfers between devices: 27.6 us -> 26.6 us
  waiting for transfers between devices: 13.7 us -> 13 us
    ppermute x12 -> x14, starting transfers between devices: 27.6 us -> 26.6 us  [moved(): return lax.ppermute(array, ('tm', 'space'), pairs)]
    ppermute x12 -> x14, waiting for transfers between devices: 13.7 us -> 13 us  [moved(): return lax.ppermute(array, ('tm', 'space'), pairs)]
  transfers between devices with their start and end apart: 12 -> 14, of which waited for: 4 -> 6; matrix products, arithmetic and copies ran while one was open for 0% -> 0% of each run, Pallas kernels for 16% -> 17%
where the time goes in v4:
time: 52.5 us; the launch traced here: 52.4 us
  starting transfers between devices  26.6 us (51%)
  waiting for transfers between devices  13 us (25%)
  Pallas kernels  12.1 us (23%)
  between operations  0.74 us (1%)
    ppermute x14, starting transfers between devices, moved(): return lax.ppermute(array, ('tm', 'space'), pairs)  26.6 us
    ppermute x14, waiting for transfers between devices, moved(): return lax.ppermute(array, ('tm', 'space'), pairs)  13 us
    pallas_call x1, Pallas kernels, body(): pl.pallas_call(functools.partial(inner_kernel, slabs), out_shape=(shaped(...  3.54 us
    pallas_call x1, Pallas kernels, body(): pl.pallas_call(functools.partial(first_kernel, blocks, slabs), out_shape=...  2.66 us
    pallas_call x1, Pallas kernels, body(): pl.pallas_call(start_kernel, out_shape=(layer, layer, shaped(velocity.sha...  2.3 us
    pallas_call x1, Pallas kernels, body(): pl.pallas_call(finish_kernel, out_shape=shaped(fields, depth), in_specs=[...  1.81 us
    pallas_call x1, Pallas kernels, body(): pl.pallas_call(functools.partial(outer_kernel, blocks, slabs), out_shape=...  1.14 us
  transfers between devices with their start and end apart: 14, of which 6 were waited for; matrix products, arithmetic and copies ran while one was open for 0% of the time, Pallas kernels for 17%

profile of v4, /device:TPU:1, one launch (start us, length us, event | category | flops | bytes accessed | tf_op | source)
XLA Modules:
  0.0 52.4 jit_solution(1084260549172269166)
XLA Ops:
  0.7 3.3 %collective-permute-start.1 = (f32[2,8,32,512]{3,2,1,0:T(8,128)}, f32[2,8,32,512]{3,2,1,0:T(8,128)S(1)}, u32[]{:S(2)}, u32[]{:S(2)}) collective-permute-start(f32[2,8,32,512]{3,2,1,0:T(8,128)} %bitcast.2), channel_id=1, source_target_pairs={{0,192},{1,193},{2,194},{3,195},{4,196},{5,197},{6,198},{7,199},{8... | collective-permute-start | bytes 3145736 | tf_op jit(solution)/shard_map/ppermute | solution.py:325
  4.0 2.3 %shard_map.50 = (f32[4,32,512]{2,1,0:T(8,128)}, f32[4,32,512]{2,1,0:T(8,128)}, f32[2,32,512]{2,1,0:T(8,128)}) custom-call(s32[1,2]{1,0:T(1,128)} %snaps.9, f32[2,8,32,512]{3,2,1,0:T(8,128)} %bitcast.3, f32[2,3,8,32,512]{4,3,2,1,0:T(8,128)} %velocity.9), custom_call_target="tpu_custom_call" | custom-call | bytes 7200000 | tf_op jit(solution)/shard_map/pallas_call | solution.py:348
  6.3 9.0 %collective-permute-start.4 = (f32[2,32,512]{2,1,0:T(8,128)}, f32[2,32,512]{2,1,0:T(8,128)S(1)}, u32[]{:S(2)}, u32[]{:S(2)}) collective-permute-start(f32[2,32,512]{2,1,0:T(8,128)} %get-tuple-element.22), channel_id=1, source_target_pairs={{0,129},{1,130},{2,131},{3,132},{4,133},{5,134},{6,135},{7,136},{8... | collective-permute-start | bytes 393224 | tf_op jit(solution)/shard_map/ppermute | solution.py:325
  15.3 2.2 %collective-permute-start.3 = (f32[4,32,512]{2,1,0:T(8,128)}, f32[4,32,512]{2,1,0:T(8,128)S(1)}, u32[]{:S(2)}, u32[]{:S(2)}) collective-permute-start(f32[4,32,512]{2,1,0:T(8,128)} %get-tuple-element.21), channel_id=1, source_target_pairs={{0,255},{1,194},{2,193},{3,196},{4,195},{5,198},{6,197},{7,200},{8... | collective-permute-start | bytes 786440 | tf_op jit(solution)/shard_map/ppermute | solution.py:325
  17.4 0.1 collective-permute-done.4.own_flow
  17.5 1.7 %collective-permute-start.5 = (f32[2,32,512]{2,1,0:T(8,128)S(1)}, f32[2,32,512]{2,1,0:T(8,128)S(1)}, u32[]{:S(2)}, u32[]{:S(2)}) collective-permute-start(f32[2,32,512]{2,1,0:T(8,128)S(1)} %collective-permute-done.4.own_flow), channel_id=1, source_target_pairs={{0,64},{1,65},{2,66},{3,67},{4,68},{5,69},{6,70},{7,71},{8,72},{9,... | collective-permute-start | bytes 393224 | tf_op jit(solution)/shard_map/ppermute | solution.py:325
  19.2 0.0 collective-permute-start
  19.2 3.3 %collective-permute-done.snaps_next = s32[1,2]{1,0:T(1,128)S(1)} collective-permute-done((s32[1,2]{1,0:T(1,128)S(1)}, s32[1,2]{1,0:T(1,128)S(1)}, u32[]{:S(2)}, u32[]{:S(2)}) %collective-permute-start) | collective-permute-done | bytes 40 | tf_op jit(solution)/shard_map/ppermute | solution.py:325
  22.5 5.5 %collective-permute-done.2.halo_one = f32[4,32,512]{2,1,0:T(8,128)S(1)} collective-permute-done((f32[4,32,512]{2,1,0:T(8,128)}, f32[4,32,512]{2,1,0:T(8,128)S(1)}, u32[]{:S(2)}, u32[]{:S(2)}) %collective-permute-start.2) | collective-permute-done | bytes 262176 | tf_op jit(solution)/shard_map/ppermute | solution.py:325
  28.0 2.7 %shard_map.51 = (f32[2,10,32,512]{3,2,1,0:T(8,128)S(1)}, f32[2,4,32,512]{3,2,1,0:T(8,128)S(1)}, f32[4,32,512]{2,1,0:T(8,128)S(1)}, f32[4,32,512]{2,1,0:T(8,128)S(1)}) custom-call(s32[1,2]{1,0:T(1,128)S(1)} %copy-done.2, s32[1,2]{1,0:T(1,128)S(1)} %collective-permute-done.snaps_next, f32[2,8,32,512]{3,2,1,0:T(8,128)S(1)} %collective-permute-done.1.state, ...), custom_call_target="tpu_custom_call" | custom-call | bytes 9000000 | tf_op jit(solution)/shard_map/pallas_call | solution.py:366
  30.7 0.1 collective-permute-start.6
  30.8 6.1 %collective-permute-start.7 = (f32[4,32,512]{2,1,0:T(8,128)S(1)}, f32[4,32,512]{2,1,0:T(8,128)S(1)}, u32[]{:S(2)}, u32[]{:S(2)}) collective-permute-start(f32[4,32,512]{2,1,0:T(8,128)S(1)} %get-tuple-element.27), channel_id=1, source_target_pairs={{0,63},{1,2},{2,1},{3,4},{4,3},{5,6},{6,5},{7,8},{8,7},{9,10},{10,... | collective-permute-start | bytes 786440 | tf_op jit(solution)/shard_map/ppermute | solution.py:325
  36.9 3.5 %shard_map.52 = (f32[2,8,32,512]{3,2,1,0:T(8,128)S(1)}, f32[2,8,32,512]{3,2,1,0:T(8,128)}, f32[4,8,512]{2,1,0:T(8,128)S(1)}, f32[4,8,512]{2,1,0:T(8,128)S(1)}, f...) custom-call(s32[1,2]{1,0:T(1,128)S(1)} %copy-done.2, s32[1,2]{1,0:T(1,128)S(1)} %collective-permute-done.snaps_next, ...), custom_call_target="tpu_custom_call" | custom-call | bytes 10800000 | tf_op jit(solution)/shard_map/pallas_call | solution.py:377
  40.4 1.0 %collective-permute-start.8 = (f32[4,8,512]{2,1,0:T(8,128)S(1)}, f32[4,8,512]{2,1,0:T(8,128)S(1)}, u32[]{:S(2)}, u32[]{:S(2)}) collective-permute-start(f32[4,8,512]{2,1,0:T(8,128)S(1)} %get-tuple-element.31), channel_id=1, source_target_pairs={{0,64},{1,65},{2,66},{3,67},{4,68},{5,69},{6,70},{7,71},{8,72},{9,... | collective-permute-start | bytes 196616 | tf_op jit(solution)/shard_map/ppermute | solution.py:325
  41.4 0.8 %collective-permute-start.9 = (f32[4,8,512]{2,1,0:T(8,128)S(1)}, f32[4,8,512]{2,1,0:T(8,128)S(1)}, u32[]{:S(2)}, u32[]{:S(2)}) collective-permute-start(f32[4,8,512]{2,1,0:T(8,128)S(1)} %get-tuple-element.32), channel_id=1, source_target_pairs={{0,128},{1,129},{2,130},{3,131},{4,132},{5,133},{6,134},{7,135},{8... | collective-permute-start | bytes 196616 | tf_op jit(solution)/shard_map/ppermute | solution.py:325
  42.2 0.0 collective-permute-done.6.halo_one
  42.2 2.2 %collective-permute-done.7.halo_two = f32[4,32,512]{2,1,0:T(8,128)S(1)} collective-permute-done((f32[4,32,512]{2,1,0:T(8,128)S(1)}, f32[4,32,512]{2,1,0:T(8,128)S(1)}, u32[]{:S(2)}, u32[]{:S(2)}) %collective-permute-start.7) | collective-permute-done | bytes 262176 | tf_op jit(solution)/shard_map/ppermute | solution.py:325
  44.4 1.1 %shard_map.53 = (f32[2,4,32,512]{3,2,1,0:T(8,128)S(1)}, f32[4,8,512]{2,1,0:T(8,128)S(1)}, f32[4,8,512]{2,1,0:T(8,128)S(1)}, f32[4,8,512]{2,1,0:T(8,128)S(1)}, f32[4,8,512]{2,1,0:T(8,128)S(1)}) custom-call(s32[1,2]{1,0:T(1,128)S(1)} %copy-done.2, f32[2,4,32,512]{3,2,1,0:T(8,128)S(1)} %get-tuple-element.24.edges, ...), custom_call_target="tpu_custom_call" | custom-call | bytes 3600000 | tf_op jit(solution)/shard_map/pallas_call | solution.py:389
  45.5 0.1 collective-permute-start.11
  45.6 2.4 %collective-permute-start.12 = (f32[4,8,512]{2,1,0:T(8,128)S(1)}, f32[4,8,512]{2,1,0:T(8,128)S(1)}, u32[]{:S(2)}, u32[]{:S(2)}) collective-permute-start(f32[4,8,512]{2,1,0:T(8,128)S(1)} %get-tuple-element.36), channel_id=1, source_target_pairs={{0,128},{1,129},{2,130},{3,131},{4,132},{5,133},{6,134},{7,135},{8... | collective-permute-start | bytes 196616 | tf_op jit(solution)/shard_map/ppermute | solution.py:325
  48.0 1.8 %shard_map.54 = f32[2,8,32,512]{3,2,1,0:T(8,128)} custom-call(s32[1,2]{1,0:T(1,128)S(1)} %copy-done.2, f32[2,8,32,512]{3,2,1,0:T(8,128)S(1)} %get-tuple-element.25.carried_on, f32[2,4,32,512]{3,2,1,0:T(8,128)S(1)} %get-tuple-element.28.outer, f32[2,3,8,32,512]{4,3,2,1,0:T(8,128)S(1)} %copy-done, ...), custom_call_target="tpu_custom_call", output_to_operand_aliasing={{}: (4, {})} | custom-call | bytes 3600000 | tf_op jit(solution)/shard_map/pallas_call | solution.py:401
  49.9 1.4 %collective-permute-done.12.refs_6_ = f32[4,8,512]{2,1,0:T(8,128)S(1)} collective-permute-done((f32[4,8,512]{2,1,0:T(8,128)S(1)}, f32[4,8,512]{2,1,0:T(8,128)S(1)}, u32[]{:S(2)}, u32[]{:S(2)}) %collective-permute-start.12) | collective-permute-done | bytes 65568 | tf_op jit(solution)/shard_map/ppermute | solution.py:325
  51.3 0.5 collective-permute-done.13.refs_7_
  51.8 0.7 %shard_map.55 = f32[8,8,512]{2,1,0:T(8,128)} custom-call(f32[4,8,512]{2,1,0:T(8,128)S(1)} %get-tuple-element.30.refs_0_, f32[4,8,512]{2,1,0:T(8,128)S(1)} %collective-permute-done.8.refs_1_, f32[4,8,512]{2,1,0:T(8,128)S(1)} %collective-permute-done.9.refs_2_, f32[4,8,512]{2,1,0:T(8,128)S(1)} %collective-permute-done.10.refs_3_, ...), custom_call_target="tpu_custom_call" | custom-call | bytes 1800000 | tf_op jit(solution)/shard_map/pallas_call | solution.py:411
  (16 shorter events, 0.0 us)
Async XLA Ops:
  0.6 27.4 %copy-start.1 = (f32[1,2,8,32,512]{4,3,2,1,0:T(8,128)S(1)}, f32[1,2,8,32,512]{4,3,2,1,0:T(8,128)}, u32[]{:S(2)}) copy-start(f32[1,2,8,32,512]{4,3,2,1,0:T(8,128)} %param.3) | copy-start | bytes 3145732
  0.6 18.6 %copy-start.2 = (s32[1,2]{1,0:T(1,128)S(1)}, s32[1,2]{1,0:T(1,128)}, u32[]{:S(2)}) copy-start(s32[1,2]{1,0:T(1,128)} %snaps.9) | copy-start | bytes 28
  0.6 27.4 %copy-start = (f32[2,3,8,32,512]{4,3,2,1,0:T(8,128)S(1)}, f32[2,3,8,32,512]{4,3,2,1,0:T(8,128)}, u32[]{:S(2)}) copy-start(f32[2,3,8,32,512]{4,3,2,1,0:T(8,128)} %velocity.9) | copy-start | bytes 9437188
  0.7 27.4 %collective-permute-start.1 = (f32[2,8,32,512]{3,2,1,0:T(8,128)}, f32[2,8,32,512]{3,2,1,0:T(8,128)S(1)}, u32[]{:S(2)}, u32[]{:S(2)}) collective-permute-start(f32[2,8,32,512]{3,2,1,0:T(8,128)} %bitcast.2), channel_id=1, source_target_pairs={{0,192},{1,193},{2,194},{3,195},{4,196},{5,197},{6,198},{7,199},{8... | collective-permute-start | bytes 3145736 | tf_op jit(solution)/shard_map/ppermute | solution.py:325
  6.3 11.2 %collective-permute-start.4 = (f32[2,32,512]{2,1,0:T(8,128)}, f32[2,32,512]{2,1,0:T(8,128)S(1)}, u32[]{:S(2)}, u32[]{:S(2)}) collective-permute-start(f32[2,32,512]{2,1,0:T(8,128)} %get-tuple-element.22), channel_id=1, source_target_pairs={{0,129},{1,130},{2,131},{3,132},{4,133},{5,134},{6,135},{7,136},{8... | collective-permute-start | bytes 393224 | tf_op jit(solution)/shard_map/ppermute | solution.py:325
  15.2 12.8 %collective-permute-start.2 = (f32[4,32,512]{2,1,0:T(8,128)}, f32[4,32,512]{2,1,0:T(8,128)S(1)}, u32[]{:S(2)}, u32[]{:S(2)}) collective-permute-start(f32[4,32,512]{2,1,0:T(8,128)} %get-tuple-element.20), channel_id=1, source_target_pairs={{0,193},{1,192},{2,195},{3,194},{4,197},{5,196},{6,199},{7,198},{8... | collective-permute-start | bytes 786440 | tf_op jit(solution)/shard_map/ppermute | solution.py:325
  15.3 12.8 %collective-permute-start.3 = (f32[4,32,512]{2,1,0:T(8,128)}, f32[4,32,512]{2,1,0:T(8,128)S(1)}, u32[]{:S(2)}, u32[]{:S(2)}) collective-permute-start(f32[4,32,512]{2,1,0:T(8,128)} %get-tuple-element.21), channel_id=1, source_target_pairs={{0,255},{1,194},{2,193},{3,196},{4,195},{5,198},{6,197},{7,200},{8... | collective-permute-start | bytes 786440 | tf_op jit(solution)/shard_map/ppermute | solution.py:325
  17.5 5.0 %collective-permute-start.5 = (f32[2,32,512]{2,1,0:T(8,128)S(1)}, f32[2,32,512]{2,1,0:T(8,128)S(1)}, u32[]{:S(2)}, u32[]{:S(2)}) collective-permute-start(f32[2,32,512]{2,1,0:T(8,128)S(1)} %collective-permute-done.4.own_flow), channel_id=1, source_target_pairs={{0,64},{1,65},{2,66},{3,67},{4,68},{5,69},{6,70},{7,71},{8,72},{9,... | collective-permute-start | bytes 393224 | tf_op jit(solution)/shard_map/ppermute | solution.py:325
  19.2 3.3 %collective-permute-start = (s32[1,2]{1,0:T(1,128)S(1)}, s32[1,2]{1,0:T(1,128)S(1)}, u32[]{:S(2)}, u32[]{:S(2)}) collective-permute-start(s32[1,2]{1,0:T(1,128)S(1)} %copy-done.2), channel_id=1, source_target_pairs={{0,192},{1,193},{2,194},{3,195},{4,196},{5,197},{6,198},{7,199},{8... | collective-permute-start | bytes 32 | tf_op jit(solution)/shard_map/ppermute | solution.py:325
  30.7 11.5 %collective-permute-start.6 = (f32[4,32,512]{2,1,0:T(8,128)S(1)}, f32[4,32,512]{2,1,0:T(8,128)S(1)}, u32[]{:S(2)}, u32[]{:S(2)}) collective-permute-start(f32[4,32,512]{2,1,0:T(8,128)S(1)} %get-tuple-element.26), channel_id=1, source_target_pairs={{0,1},{1,0},{2,3},{3,2},{4,5},{5,4},{6,7},{7,6},{8,9},{9,8},{10,11... | collective-permute-start | bytes 786440 | tf_op jit(solution)/shard_map/ppermute | solution.py:325
  30.8 13.6 %collective-permute-start.7 = (f32[4,32,512]{2,1,0:T(8,128)S(1)}, f32[4,32,512]{2,1,0:T(8,128)S(1)}, u32[]{:S(2)}, u32[]{:S(2)}) collective-permute-start(f32[4,32,512]{2,1,0:T(8,128)S(1)} %get-tuple-element.27), channel_id=1, source_target_pairs={{0,63},{1,2},{2,1},{3,4},{4,3},{5,6},{6,5},{7,8},{8,7},{9,10},{10,... | collective-permute-start | bytes 786440 | tf_op jit(solution)/shard_map/ppermute | solution.py:325
  40.4 7.6 %collective-permute-start.8 = (f32[4,8,512]{2,1,0:T(8,128)S(1)}, f32[4,8,512]{2,1,0:T(8,128)S(1)}, u32[]{:S(2)}, u32[]{:S(2)}) collective-permute-start(f32[4,8,512]{2,1,0:T(8,128)S(1)} %get-tuple-element.31), channel_id=1, source_target_pairs={{0,64},{1,65},{2,66},{3,67},{4,68},{5,69},{6,70},{7,71},{8,72},{9,... | collective-permute-start | bytes 196616 | tf_op jit(solution)/shard_map/ppermute | solution.py:325
  41.4 8.4 %collective-permute-start.9 = (f32[4,8,512]{2,1,0:T(8,128)S(1)}, f32[4,8,512]{2,1,0:T(8,128)S(1)}, u32[]{:S(2)}, u32[]{:S(2)}) collective-permute-start(f32[4,8,512]{2,1,0:T(8,128)S(1)} %get-tuple-element.32), channel_id=1, source_target_pairs={{0,128},{1,129},{2,130},{3,131},{4,132},{5,133},{6,134},{7,135},{8... | collective-permute-start | bytes 196616 | tf_op jit(solution)/shard_map/ppermute | solution.py:325
  42.2 7.7 %collective-permute-start.10 = (f32[4,8,512]{2,1,0:T(8,128)S(1)}, f32[4,8,512]{2,1,0:T(8,128)S(1)}, u32[]{:S(2)}, u32[]{:S(2)}) collective-permute-start(f32[4,8,512]{2,1,0:T(8,128)S(1)} %get-tuple-element.33), channel_id=1, source_target_pairs={{0,192},{1,193},{2,194},{3,195},{4,196},{5,197},{6,198},{7,199},{8... | collective-permute-start | bytes 196616 | tf_op jit(solution)/shard_map/ppermute | solution.py:325
  45.5 4.4 %collective-permute-start.11 = (f32[4,8,512]{2,1,0:T(8,128)S(1)}, f32[4,8,512]{2,1,0:T(8,128)S(1)}, u32[]{:S(2)}, u32[]{:S(2)}) collective-permute-start(f32[4,8,512]{2,1,0:T(8,128)S(1)} %get-tuple-element.35), channel_id=1, source_target_pairs={{0,64},{1,65},{2,66},{3,67},{4,68},{5,69},{6,70},{7,71},{8,72},{9,... | collective-permute-start | bytes 196616 | tf_op jit(solution)/shard_map/ppermute | solution.py:325
  45.6 5.6 %collective-permute-start.12 = (f32[4,8,512]{2,1,0:T(8,128)S(1)}, f32[4,8,512]{2,1,0:T(8,128)S(1)}, u32[]{:S(2)}, u32[]{:S(2)}) collective-permute-start(f32[4,8,512]{2,1,0:T(8,128)S(1)} %get-tuple-element.36), channel_id=1, source_target_pairs={{0,128},{1,129},{2,130},{3,131},{4,132},{5,133},{6,134},{7,135},{8... | collective-permute-start | bytes 196616 | tf_op jit(solution)/shard_map/ppermute | solution.py:325
  48.0 3.8 %collective-permute-start.13 = (f32[4,8,512]{2,1,0:T(8,128)S(1)}, f32[4,8,512]{2,1,0:T(8,128)S(1)}, u32[]{:S(2)}, u32[]{:S(2)}) collective-permute-start(f32[4,8,512]{2,1,0:T(8,128)S(1)} %get-tuple-element.37), channel_id=1, source_target_pairs={{0,192},{1,193},{2,194},{3,195},{4,196},{5,197},{6,198},{7,199},{8... | collective-permute-start | bytes 196616 | tf_op jit(solution)/shard_map/ppermute | solution.py:325

commit v5 on v4

--- a/solution.py
+++ b/solution.py
@@ -324,11 +324,16 @@
         pairs = [(index(t, s), index(*to(t, s))) for t in range(slabs) for s in range(blocks)]
         return lax.ppermute(array, ("tm", "space"), pairs)
 
-    def one(s):
-        return s ^ 1
-
-    def two(s):
-        return (((s + 1) ^ 1) - 1) % blocks
+    def exchanged(array, by, earlier):
+        def to(t, s):
+            partner = ((s + by) ^ 1) - by
+            return (t - earlier, partner) if 0 <= partner < blocks else (t ^ 1, s)
+
+        return moved(array, to)
+
+    def fetched(t, s):
+        source = s + 1 - 2 * (t % 2)
+        return (t ^ 2, source) if 0 <= source < blocks else (t ^ 1, s)
 
     def body(slab_states, velocity, snap_of_step):
         start = slab_states[0]
@@ -359,9 +364,9 @@
             compiler_params=params(56),
             cost_estimate=cost(2),
         )(snap_of_step, start, velocity)
-        halo_one = moved(message_one, lambda t, s: (t - 1, one(s)))
-        halo_two = moved(message_two, lambda t, s: (t - 1, two(s)))
-        own_flow = moved(flow_out, lambda t, s: (t ^ 2, s + 1 - 2 * (t % 2)))
+        halo_one = exchanged(message_one, 0, 1)
+        halo_two = exchanged(message_two, 1, 1)
+        own_flow = moved(flow_out, fetched)
         other_flow = moved(own_flow, lambda t, s: (t ^ 1, s))
         widened, edges, message_one, message_two = pl.pallas_call(
             functools.partial(first_kernel, blocks, slabs),
@@ -372,8 +377,8 @@
             compiler_params=params(32),
             cost_estimate=cost(2.5),
         )(snap_of_step, snaps_next, state, halo_one, halo_two, own_flow, other_flow, velocity, start)
-        halo_one = moved(message_one, lambda t, s: (t, one(s)))
-        halo_two = moved(message_two, lambda t, s: (t, two(s)))
+        halo_one = exchanged(message_one, 0, 0)
+        halo_two = exchanged(message_two, 1, 0)
         carried_on, inner, *inner_pieces = pl.pallas_call(
             functools.partial(inner_kernel, slabs),
             out_shape=(shaped(fields, depth), shaped(fields, depth)) + pieces,

time: 52.5 us -> 49.3 us (0.939)
  starting transfers between devices: 26.6 us -> 23 us
    ppermute x14, starting transfers between devices: 26.6 us -> 23 us  [moved(): return lax.ppermute(array, ('tm', 'space'), pairs)]
  transfers between devices with their start and end apart: 14 -> 14, of which waited for: 6 -> 5; matrix products, arithmetic and copies ran while one was open for 0% -> 0% of each run, Pallas kernels for 17% -> 18%
where the time goes in v5:
time: 49.3 us; the launch traced here: 49.2 us
  starting transfers between devices  23 us (47%)
  waiting for transfers between devices  13.3 us (27%)
  Pallas kernels  12.1 us (25%)
  between operations  0.76 us (2%)
    ppermute x14, starting transfers between devices, moved(): return lax.ppermute(array, ('tm', 'space'), pairs)  23 us
    ppermute x14, waiting for transfers between devices, moved(): return lax.ppermute(array, ('tm', 'space'), pairs)  13.3 us
    pallas_call x1, Pallas kernels, body(): pl.pallas_call(functools.partial(inner_kernel, slabs), out_shape=(shaped(...  3.54 us
    pallas_call x1, Pallas kernels, body(): pl.pallas_call(functools.partial(first_kernel, blocks, slabs), out_shape=...  2.66 us
    pallas_call x1, Pallas kernels, body(): pl.pallas_call(start_kernel, out_shape=(layer, layer, shaped(velocity.sha...  2.3 us
    pallas_call x1, Pallas kernels, body(): pl.pallas_call(finish_kernel, out_shape=shaped(fields, depth), in_specs=[...  1.81 us
    pallas_call x1, Pallas kernels, body(): pl.pallas_call(functools.partial(outer_kernel, blocks, slabs), out_shape=...  1.14 us
  transfers between devices with their start and end apart: 14, of which 5 were waited for; matrix products, arithmetic and copies ran while one was open for 0% of the time, Pallas kernels for 18%

profile of v5, /device:TPU:1, one launch (start us, length us, event | category | flops | bytes accessed | tf_op | source)
XLA Modules:
  0.0 49.2 jit_solution(1443090877793915689)
XLA Ops:
  0.7 3.3 %collective-permute-start.1 = (f32[2,8,32,512]{3,2,1,0:T(8,128)}, f32[2,8,32,512]{3,2,1,0:T(8,128)S(1)}, u32[]{:S(2)}, u32[]{:S(2)}) collective-permute-start(f32[2,8,32,512]{3,2,1,0:T(8,128)} %bitcast.2), channel_id=1, source_target_pairs={{0,192},{1,193},{2,194},{3,195},{4,196},{5,197},{6,198},{7,199},{8... | collective-permute-start | bytes 3145736 | tf_op jit(solution)/shard_map/ppermute | solution.py:325
  4.0 2.3 %shard_map.50 = (f32[4,32,512]{2,1,0:T(8,128)}, f32[4,32,512]{2,1,0:T(8,128)}, f32[2,32,512]{2,1,0:T(8,128)}) custom-call(s32[1,2]{1,0:T(1,128)} %snaps.9, f32[2,8,32,512]{3,2,1,0:T(8,128)} %bitcast.3, f32[2,3,8,32,512]{4,3,2,1,0:T(8,128)} %velocity.9), custom_call_target="tpu_custom_call" | custom-call | bytes 7200000 | tf_op jit(solution)/shard_map/pallas_call | solution.py:353
  6.3 0.2 collective-permute-start.4
  6.5 2.4 %collective-permute-start.2 = (f32[4,32,512]{2,1,0:T(8,128)}, f32[4,32,512]{2,1,0:T(8,128)S(1)}, u32[]{:S(2)}, u32[]{:S(2)}) collective-permute-start(f32[4,32,512]{2,1,0:T(8,128)} %get-tuple-element.20), channel_id=1, source_target_pairs={{0,193},{1,192},{2,195},{3,194},{4,197},{5,196},{6,199},{7,198},{8... | collective-permute-start | bytes 786440 | tf_op jit(solution)/shard_map/ppermute | solution.py:325
  9.0 0.5 collective-permute-start.3
  9.4 3.2 %collective-permute-done.4.own_flow = f32[2,32,512]{2,1,0:T(8,128)S(1)} collective-permute-done((f32[2,32,512]{2,1,0:T(8,128)}, f32[2,32,512]{2,1,0:T(8,128)S(1)}, u32[]{:S(2)}, u32[]{:S(2)}) %collective-permute-start.4) | collective-permute-done | bytes 131104 | tf_op jit(solution)/shard_map/ppermute | solution.py:325
  12.7 8.0 %collective-permute-start.5 = (f32[2,32,512]{2,1,0:T(8,128)S(1)}, f32[2,32,512]{2,1,0:T(8,128)S(1)}, u32[]{:S(2)}, u32[]{:S(2)}) collective-permute-start(f32[2,32,512]{2,1,0:T(8,128)S(1)} %collective-permute-done.4.own_flow), channel_id=1, source_target_pairs={{0,64},{1,65},{2,66},{3,67},{4,68},{5,69},{6,70},{7,71},{8,72},{9,... | collective-permute-start | bytes 393224 | tf_op jit(solution)/shard_map/ppermute | solution.py:325
  20.6 0.0 collective-permute-start
  20.7 3.0 %collective-permute-done.snaps_next = s32[1,2]{1,0:T(1,128)S(1)} collective-permute-done((s32[1,2]{1,0:T(1,128)S(1)}, s32[1,2]{1,0:T(1,128)S(1)}, u32[]{:S(2)}, u32[]{:S(2)}) %collective-permute-start) | collective-permute-done | bytes 40 | tf_op jit(solution)/shard_map/ppermute | solution.py:325
  23.6 0.0 collective-permute-done.5.other_flow
  23.7 2.7 %shard_map.51 = (f32[2,10,32,512]{3,2,1,0:T(8,128)S(1)}, f32[2,4,32,512]{3,2,1,0:T(8,128)S(1)}, f32[4,32,512]{2,1,0:T(8,128)S(1)}, f32[4,32,512]{2,1,0:T(8,128)S(1)}) custom-call(s32[1,2]{1,0:T(1,128)S(1)} %copy-done.2, s32[1,2]{1,0:T(1,128)S(1)} %collective-permute-done.snaps_next, f32[2,8,32,512]{3,2,1,0:T(8,128)S(1)} %collective-permute-done.1.state, ...), custom_call_target="tpu_custom_call" | custom-call | bytes 9000000 | tf_op jit(solution)/shard_map/pallas_call | solution.py:371
  26.3 2.8 %collective-permute-start.6 = (f32[4,32,512]{2,1,0:T(8,128)S(1)}, f32[4,32,512]{2,1,0:T(8,128)S(1)}, u32[]{:S(2)}, u32[]{:S(2)}) collective-permute-start(f32[4,32,512]{2,1,0:T(8,128)S(1)} %get-tuple-element.26), channel_id=1, source_target_pairs={{0,1},{1,0},{2,3},{3,2},{4,5},{5,4},{6,7},{7,6},{8,9},{9,8},{10,11... | collective-permute-start | bytes 786440 | tf_op jit(solution)/shard_map/ppermute | solution.py:325
  29.2 0.7 %collective-permute-start.7 = (f32[4,32,512]{2,1,0:T(8,128)S(1)}, f32[4,32,512]{2,1,0:T(8,128)S(1)}, u32[]{:S(2)}, u32[]{:S(2)}) collective-permute-start(f32[4,32,512]{2,1,0:T(8,128)S(1)} %get-tuple-element.27), channel_id=1, source_target_pairs={{0,64},{1,2},{2,1},{3,4},{4,3},{5,6},{6,5},{7,8},{8,7},{9,10},{10,... | collective-permute-start | bytes 786440 | tf_op jit(solution)/shard_map/ppermute | solution.py:325
  29.9 3.5 %shard_map.52 = (f32[2,8,32,512]{3,2,1,0:T(8,128)S(1)}, f32[2,8,32,512]{3,2,1,0:T(8,128)}, f32[4,8,512]{2,1,0:T(8,128)S(1)}, f32[4,8,512]{2,1,0:T(8,128)S(1)}, f...) custom-call(s32[1,2]{1,0:T(1,128)S(1)} %copy-done.2, s32[1,2]{1,0:T(1,128)S(1)} %collective-permute-done.snaps_next, ...), custom_call_target="tpu_custom_call" | custom-call | bytes 10800000 | tf_op jit(solution)/shard_map/pallas_call | solution.py:382
  33.4 0.1 collective-permute-start.8
  33.5 1.3 %collective-permute-start.9 = (f32[4,8,512]{2,1,0:T(8,128)S(1)}, f32[4,8,512]{2,1,0:T(8,128)S(1)}, u32[]{:S(2)}, u32[]{:S(2)}) collective-permute-start(f32[4,8,512]{2,1,0:T(8,128)S(1)} %get-tuple-element.32), channel_id=1, source_target_pairs={{0,128},{1,129},{2,130},{3,131},{4,132},{5,133},{6,134},{7,135},{8... | collective-permute-start | bytes 196616 | tf_op jit(solution)/shard_map/ppermute | solution.py:325
  34.9 5.2 %collective-permute-done.6.halo_one = f32[4,32,512]{2,1,0:T(8,128)S(1)} collective-permute-done((f32[4,32,512]{2,1,0:T(8,128)S(1)}, f32[4,32,512]{2,1,0:T(8,128)S(1)}, u32[]{:S(2)}, u32[]{:S(2)}) %collective-permute-start.6) | collective-permute-done | bytes 262176 | tf_op jit(solution)/shard_map/ppermute | solution.py:325
  40.0 1.1 %shard_map.53 = (f32[2,4,32,512]{3,2,1,0:T(8,128)S(1)}, f32[4,8,512]{2,1,0:T(8,128)S(1)}, f32[4,8,512]{2,1,0:T(8,128)S(1)}, f32[4,8,512]{2,1,0:T(8,128)S(1)}, f32[4,8,512]{2,1,0:T(8,128)S(1)}) custom-call(s32[1,2]{1,0:T(1,128)S(1)} %copy-done.2, f32[2,4,32,512]{3,2,1,0:T(8,128)S(1)} %get-tuple-element.24.edges, ...), custom_call_target="tpu_custom_call" | custom-call | bytes 3600000 | tf_op jit(solution)/shard_map/pallas_call | solution.py:394
  41.2 1.2 %collective-permute-start.11 = (f32[4,8,512]{2,1,0:T(8,128)S(1)}, f32[4,8,512]{2,1,0:T(8,128)S(1)}, u32[]{:S(2)}, u32[]{:S(2)}) collective-permute-start(f32[4,8,512]{2,1,0:T(8,128)S(1)} %get-tuple-element.35), channel_id=1, source_target_pairs={{0,64},{1,65},{2,66},{3,67},{4,68},{5,69},{6,70},{7,71},{8,72},{9,... | collective-permute-start | bytes 196616 | tf_op jit(solution)/shard_map/ppermute | solution.py:325
  42.4 2.3 %collective-permute-start.12 = (f32[4,8,512]{2,1,0:T(8,128)S(1)}, f32[4,8,512]{2,1,0:T(8,128)S(1)}, u32[]{:S(2)}, u32[]{:S(2)}) collective-permute-start(f32[4,8,512]{2,1,0:T(8,128)S(1)} %get-tuple-element.36), channel_id=1, source_target_pairs={{0,128},{1,129},{2,130},{3,131},{4,132},{5,133},{6,134},{7,135},{8... | collective-permute-start | bytes 196616 | tf_op jit(solution)/shard_map/ppermute | solution.py:325
  44.7 1.8 %shard_map.54 = f32[2,8,32,512]{3,2,1,0:T(8,128)} custom-call(s32[1,2]{1,0:T(1,128)S(1)} %copy-done.2, f32[2,8,32,512]{3,2,1,0:T(8,128)S(1)} %get-tuple-element.25.carried_on, f32[2,4,32,512]{3,2,1,0:T(8,128)S(1)} %get-tuple-element.28.outer, f32[2,3,8,32,512]{4,3,2,1,0:T(8,128)S(1)} %copy-done, ...), custom_call_target="tpu_custom_call", output_to_operand_aliasing={{}: (4, {})} | custom-call | bytes 3600000 | tf_op jit(solution)/shard_map/pallas_call | solution.py:406
  46.6 1.4 %collective-permute-done.12.refs_6_ = f32[4,8,512]{2,1,0:T(8,128)S(1)} collective-permute-done((f32[4,8,512]{2,1,0:T(8,128)S(1)}, f32[4,8,512]{2,1,0:T(8,128)S(1)}, u32[]{:S(2)}, u32[]{:S(2)}) %collective-permute-start.12) | collective-permute-done | bytes 65568 | tf_op jit(solution)/shard_map/ppermute | solution.py:325
  48.0 0.5 collective-permute-done.13.refs_7_
  48.5 0.7 %shard_map.55 = f32[8,8,512]{2,1,0:T(8,128)} custom-call(f32[4,8,512]{2,1,0:T(8,128)S(1)} %get-tuple-element.30.refs_0_, f32[4,8,512]{2,1,0:T(8,128)S(1)} %collective-permute-done.8.refs_1_, f32[4,8,512]{2,1,0:T(8,128)S(1)} %collective-permute-done.9.refs_2_, f32[4,8,512]{2,1,0:T(8,128)S(1)} %collective-permute-done.10.refs_3_, ...), custom_call_target="tpu_custom_call" | custom-call | bytes 1800000 | tf_op jit(solution)/shard_map/pallas_call | solution.py:416
  (16 shorter events, 0.0 us)
Async XLA Ops:
  0.6 23.0 %copy-start.1 = (f32[1,2,8,32,512]{4,3,2,1,0:T(8,128)S(1)}, f32[1,2,8,32,512]{4,3,2,1,0:T(8,128)}, u32[]{:S(2)}) copy-start(f32[1,2,8,32,512]{4,3,2,1,0:T(8,128)} %param.3) | copy-start | bytes 3145732
  0.6 20.0 %copy-start.2 = (s32[1,2]{1,0:T(1,128)S(1)}, s32[1,2]{1,0:T(1,128)}, u32[]{:S(2)}) copy-start(s32[1,2]{1,0:T(1,128)} %snaps.9) | copy-start | bytes 28
  0.6 23.0 %copy-start = (f32[2,3,8,32,512]{4,3,2,1,0:T(8,128)S(1)}, f32[2,3,8,32,512]{4,3,2,1,0:T(8,128)}, u32[]{:S(2)}) copy-start(f32[2,3,8,32,512]{4,3,2,1,0:T(8,128)} %velocity.9) | copy-start | bytes 9437188
  0.7 23.0 %collective-permute-start.1 = (f32[2,8,32,512]{3,2,1,0:T(8,128)}, f32[2,8,32,512]{3,2,1,0:T(8,128)S(1)}, u32[]{:S(2)}, u32[]{:S(2)}) collective-permute-start(f32[2,8,32,512]{3,2,1,0:T(8,128)} %bitcast.2), channel_id=1, source_target_pairs={{0,192},{1,193},{2,194},{3,195},{4,196},{5,197},{6,198},{7,199},{8... | collective-permute-start | bytes 3145736 | tf_op jit(solution)/shard_map/ppermute | solution.py:325
  6.3 6.4 %collective-permute-start.4 = (f32[2,32,512]{2,1,0:T(8,128)}, f32[2,32,512]{2,1,0:T(8,128)S(1)}, u32[]{:S(2)}, u32[]{:S(2)}) collective-permute-start(f32[2,32,512]{2,1,0:T(8,128)} %get-tuple-element.22), channel_id=1, source_target_pairs={{0,129},{1,130},{2,131},{3,132},{4,133},{5,134},{6,135},{7,136},{8... | collective-permute-start | bytes 393224 | tf_op jit(solution)/shard_map/ppermute | solution.py:325
  6.5 17.1 %collective-permute-start.2 = (f32[4,32,512]{2,1,0:T(8,128)}, f32[4,32,512]{2,1,0:T(8,128)S(1)}, u32[]{:S(2)}, u32[]{:S(2)}) collective-permute-start(f32[4,32,512]{2,1,0:T(8,128)} %get-tuple-element.20), channel_id=1, source_target_pairs={{0,193},{1,192},{2,195},{3,194},{4,197},{5,196},{6,199},{7,198},{8... | collective-permute-start | bytes 786440 | tf_op jit(solution)/shard_map/ppermute | solution.py:325
  9.0 14.6 %collective-permute-start.3 = (f32[4,32,512]{2,1,0:T(8,128)}, f32[4,32,512]{2,1,0:T(8,128)S(1)}, u32[]{:S(2)}, u32[]{:S(2)}) collective-permute-start(f32[4,32,512]{2,1,0:T(8,128)} %get-tuple-element.21), channel_id=1, source_target_pairs={{0,64},{1,194},{2,193},{3,196},{4,195},{5,198},{6,197},{7,200},{8,... | collective-permute-start | bytes 786440 | tf_op jit(solution)/shard_map/ppermute | solution.py:325
  12.7 11.0 %collective-permute-start.5 = (f32[2,32,512]{2,1,0:T(8,128)S(1)}, f32[2,32,512]{2,1,0:T(8,128)S(1)}, u32[]{:S(2)}, u32[]{:S(2)}) collective-permute-start(f32[2,32,512]{2,1,0:T(8,128)S(1)} %collective-permute-done.4.own_flow), channel_id=1, source_target_pairs={{0,64},{1,65},{2,66},{3,67},{4,68},{5,69},{6,70},{7,71},{8,72},{9,... | collective-permute-start | bytes 393224 | tf_op jit(solution)/shard_map/ppermute | solution.py:325
  20.6 3.0 %collective-permute-start = (s32[1,2]{1,0:T(1,128)S(1)}, s32[1,2]{1,0:T(1,128)S(1)}, u32[]{:S(2)}, u32[]{:S(2)}) collective-permute-start(s32[1,2]{1,0:T(1,128)S(1)} %copy-done.2), channel_id=1, source_target_pairs={{0,192},{1,193},{2,194},{3,195},{4,196},{5,197},{6,198},{7,199},{8... | collective-permute-start | bytes 32 | tf_op jit(solution)/shard_map/ppermute | solution.py:325
  26.3 13.7 %collective-permute-start.6 = (f32[4,32,512]{2,1,0:T(8,128)S(1)}, f32[4,32,512]{2,1,0:T(8,128)S(1)}, u32[]{:S(2)}, u32[]{:S(2)}) collective-permute-start(f32[4,32,512]{2,1,0:T(8,128)S(1)} %get-tuple-element.26), channel_id=1, source_target_pairs={{0,1},{1,0},{2,3},{3,2},{4,5},{5,4},{6,7},{7,6},{8,9},{9,8},{10,11... | collective-permute-start | bytes 786440 | tf_op jit(solution)/shard_map/ppermute | solution.py:325
  29.2 10.9 %collective-permute-start.7 = (f32[4,32,512]{2,1,0:T(8,128)S(1)}, f32[4,32,512]{2,1,0:T(8,128)S(1)}, u32[]{:S(2)}, u32[]{:S(2)}) collective-permute-start(f32[4,32,512]{2,1,0:T(8,128)S(1)} %get-tuple-element.27), channel_id=1, source_target_pairs={{0,64},{1,2},{2,1},{3,4},{4,3},{5,6},{6,5},{7,8},{8,7},{9,10},{10,... | collective-permute-start | bytes 786440 | tf_op jit(solution)/shard_map/ppermute | solution.py:325
  33.4 11.3 %collective-permute-start.8 = (f32[4,8,512]{2,1,0:T(8,128)S(1)}, f32[4,8,512]{2,1,0:T(8,128)S(1)}, u32[]{:S(2)}, u32[]{:S(2)}) collective-permute-start(f32[4,8,512]{2,1,0:T(8,128)S(1)} %get-tuple-element.31), channel_id=1, source_target_pairs={{0,64},{1,65},{2,66},{3,67},{4,68},{5,69},{6,70},{7,71},{8,72},{9,... | collective-permute-start | bytes 196616 | tf_op jit(solution)/shard_map/ppermute | solution.py:325
  33.5 13.1 %collective-permute-start.9 = (f32[4,8,512]{2,1,0:T(8,128)S(1)}, f32[4,8,512]{2,1,0:T(8,128)S(1)}, u32[]{:S(2)}, u32[]{:S(2)}) collective-permute-start(f32[4,8,512]{2,1,0:T(8,128)S(1)} %get-tuple-element.32), channel_id=1, source_target_pairs={{0,128},{1,129},{2,130},{3,131},{4,132},{5,133},{6,134},{7,135},{8... | collective-permute-start | bytes 196616 | tf_op jit(solution)/shard_map/ppermute | solution.py:325
  34.9 11.7 %collective-permute-start.10 = (f32[4,8,512]{2,1,0:T(8,128)S(1)}, f32[4,8,512]{2,1,0:T(8,128)S(1)}, u32[]{:S(2)}, u32[]{:S(2)}) collective-permute-start(f32[4,8,512]{2,1,0:T(8,128)S(1)} %get-tuple-element.33), channel_id=1, source_target_pairs={{0,192},{1,193},{2,194},{3,195},{4,196},{5,197},{6,198},{7,199},{8... | collective-permute-start | bytes 196616 | tf_op jit(solution)/shard_map/ppermute | solution.py:325
  41.2 5.4 %collective-permute-start.11 = (f32[4,8,512]{2,1,0:T(8,128)S(1)}, f32[4,8,512]{2,1,0:T(8,128)S(1)}, u32[]{:S(2)}, u32[]{:S(2)}) collective-permute-start(f32[4,8,512]{2,1,0:T(8,128)S(1)} %get-tuple-element.35), channel_id=1, source_target_pairs={{0,64},{1,65},{2,66},{3,67},{4,68},{5,69},{6,70},{7,71},{8,72},{9,... | collective-permute-start | bytes 196616 | tf_op jit(solution)/shard_map/ppermute | solution.py:325
  42.4 5.6 %collective-permute-start.12 = (f32[4,8,512]{2,1,0:T(8,128)S(1)}, f32[4,8,512]{2,1,0:T(8,128)S(1)}, u32[]{:S(2)}, u32[]{:S(2)}) collective-permute-start(f32[4,8,512]{2,1,0:T(8,128)S(1)} %get-tuple-element.36), channel_id=1, source_target_pairs={{0,128},{1,129},{2,130},{3,131},{4,132},{5,133},{6,134},{7,135},{8... | collective-permute-start | bytes 196616 | tf_op jit(solution)/shard_map/ppermute | solution.py:325
  44.7 3.8 %collective-permute-start.13 = (f32[4,8,512]{2,1,0:T(8,128)S(1)}, f32[4,8,512]{2,1,0:T(8,128)S(1)}, u32[]{:S(2)}, u32[]{:S(2)}) collective-permute-start(f32[4,8,512]{2,1,0:T(8,128)S(1)} %get-tuple-element.37), channel_id=1, source_target_pairs={{0,192},{1,193},{2,194},{3,195},{4,196},{5,197},{6,198},{7,199},{8... | collective-permute-start | bytes 196616 | tf_op jit(solution)/shard_map/ppermute | solution.py:325

commit v6 on v5

--- a/solution.py
+++ b/solution.py
@@ -140,7 +140,7 @@
 def split_rows(total, pieces):
     rows = total.shape[1] // len(pieces)
     for by, piece in enumerate(pieces):
-        start = pl.multiple_of(lax.rem(lax.axis_index("tm") + by, len(pieces)) * rows, rows)
+        start = pl.multiple_of(lax.bitwise_xor(lax.axis_index("tm"), by) * rows, rows)
         piece[...] = total[:, pl.ds(start, rows), :] * 0.5
 
 
@@ -170,17 +170,11 @@
     flow_out[...] = flows[:, 0, 1 - lax.rem(lax.axis_index("tm"), 2)]
 
 
-def first_kernel(blocks, slabs, snaps, snaps_next, state, halo_one, halo_two, own_flow, other_flow, velocity, start,
+def first_kernel(blocks, slabs, snaps, snaps_next, state, halo_one, halo_two, own_flow, other_flow, velocity,
                  widened, edges, message_one, message_two, halos):
     depth, shape = state.shape[1], state.shape[2:]
-    last = lax.axis_index("tm") == slabs - 1
-
-    @pl.when(last)
-    def _():
-        pltpu.sync_copy(start.at[:, pl.ds(0, 2)], edges.at[:, pl.ds(0, 2)])
-        pltpu.sync_copy(start.at[:, pl.ds(depth - 2, 2)], edges.at[:, pl.ds(2, 2)])
-
-    @pl.when(jnp.logical_not(last))
+
+    @pl.when(lax.axis_index("tm") < slabs - 1)
     def _():
         take_halos(
             blocks, state, halo_one, halo_two, own_flow, other_flow, snaps_next[0, 1], halos, widened, depth
@@ -201,8 +195,7 @@
             full_layer(layer_of(widened, l), here, layer_of(widened, l + 2), flow, shape, into(edges, e))
 
         each(0, edge_count, second_step)
-
-    pack_both(edges, velocity, snaps[0, 1], message_one, message_two)
+        pack_both(edges, velocity, snaps[0, 1], message_one, message_two)
 
 
 def inner_kernel(slabs, snaps, snaps_next, widened, edges, velocity, start, carried_on, inner, *rest):
@@ -258,32 +251,61 @@
         full_layer(ring[at - 1], ring[at], ring[at + 1], flow, shape, functools.partial(store, e, ring[at]), wanted)
 
 
-def outer_kernel(blocks, slabs, snaps, edges, halo_one, halo_two, own_flow, other_flow, carried_on, velocity,
-                 outer, *rest):
+def outer_kernel(blocks, slabs, snaps, edges, halo_one, halo_two, own_flow, other_flow, carried_on, widened, velocity,
+                 *rest):
+    parts, (inner_sum, outer, to_core), rest = rest[:slabs], rest[slabs : slabs + 3], rest[slabs + 3 :]
     pieces, (halos, total) = rest[:slabs], rest[slabs:]
     depth, shape = carried_on.shape[1], carried_on.shape[2:]
-    take_halos(
-        blocks, edges, halo_one, halo_two, own_flow, other_flow, snaps[0, 1], halos, outer, edge_count
-    )
-    flow = flow_of(velocity, snaps[0, 1], 0)
-    full_layer(halo_at(halos, 0), layer_of(edges, 0), layer_of(edges, 1), flow, shape, into(outer, 1))
-    flow = flow_of(velocity, snaps[0, 1], depth - 1)
-    full_layer(layer_of(edges, 2), layer_of(edges, 3), halo_at(halos, 1), flow, shape, into(outer, 2))
-
-    def store(e, here, i, j, values):
-        total[(e,) + spot(i, j)] = here(0, i, j) + values[0]
-
-    last_steps(snaps, carried_on, outer, velocity, store, (0,))
+    slab = lax.axis_index("tm")
+    inner_sum[...] = functools.reduce(jnp.add, [part[...] for part in parts])
+
+    @pl.when(slab == slabs - 1)
+    def _():
+        total[...] = jnp.zeros_like(total)
+
+    @pl.when(slab < slabs - 1)
+    def _():
+        take_halos(
+            blocks, edges, halo_one, halo_two, own_flow, other_flow, snaps[0, 1], halos, outer, edge_count
+        )
+        flow = flow_of(velocity, snaps[0, 1], 0)
+        full_layer(halo_at(halos, 0), layer_of(edges, 0), layer_of(edges, 1), flow, shape, into(outer, 1))
+        flow = flow_of(velocity, snaps[0, 1], depth - 1)
+        full_layer(layer_of(edges, 2), layer_of(edges, 3), halo_at(halos, 1), flow, shape, into(outer, 2))
+        with_last = slab == slabs - 2
+
+        def store(e, here, i, j, values):
+            l = e + (e // 2) * (depth - edge_count)
+            before = widened[(0, l + 1) + spot(i, j)] + edges[(0, e) + spot(i, j)]
+            total[(e,) + spot(i, j)] = here(0, i, j) + values[0] + jnp.where(with_last, before, 0.0)
+
+        last_steps(snaps, carried_on, outer, velocity, store, (0,))
+
     split_rows(total, pieces)
-
-
-def finish_kernel(snaps, carried_on, outer, velocity, inner, out, final, sems):
+    rows = shape[0] // slabs
+    for f in (0, 1):
+        to_core[f * edge_count : (f + 1) * edge_count] = edges[f]
+    for e in range(edge_count):
+        to_core[2 * edge_count, e * rows : (e + 1) * rows] = pieces[1][e]
+
+
+def finish_kernel(slabs, snaps, carried_on, outer, velocity, from_core, inner_sum, inner, inner_sum_out, out, final, sems):
     depth = carried_on.shape[1]
 
     def store(e, here, i, j, values):
         into(final, e)(i, j, values)
 
-    last_steps(snaps, carried_on, outer, velocity, store, (0, 1))
+    last = lax.axis_index("tm") == slabs - 1
+
+    @pl.when(last)
+    def _():
+        for f in (0, 1):
+            final[f] = from_core[f * edge_count : (f + 1) * edge_count]
+
+    @pl.when(jnp.logical_not(last))
+    def _():
+        last_steps(snaps, carried_on, outer, velocity, store, (0, 1))
+
     copies = [
         pltpu.make_async_copy(final.at[:, pl.ds(0, 2)], out.at[:, pl.ds(0, 2)], sems.at[0]),
         pltpu.make_async_copy(final.at[:, pl.ds(2, 2)], out.at[:, pl.ds(depth - 2, 2)], sems.at[1]),
@@ -294,15 +316,13 @@
         copy.wait()
 
 
-def sum_kernel(*refs):
-    ins, out = refs[:-1], refs[-1]
-    half = len(ins) // 2
-    depth = out.shape[0]
-    inner = functools.reduce(jnp.add, [ref[...] for ref in ins[:half]])
-    outer = functools.reduce(jnp.add, [ref[...] for ref in ins[half:]])
-    out[2 : depth - 2] = inner
-    out[0:2] = outer[0:2]
-    out[depth - 2 : depth] = outer[2:4]
+def sum_kernel(inner_sum, from_core, *refs):
+    parts, out = refs[:-1], refs[-1]
+    depth, rows = out.shape[:2]
+    out[2 : depth - 2] = inner_sum[...]
+    for e in range(edge_count):
+        l = e + (e // 2) * (depth - edge_count)
+        out[l] = functools.reduce(jnp.add, [part[e] for part in parts]) + from_core[2 * edge_count, pl.ds(e * rows, rows)]
 
 
 def solution(mesh):
@@ -325,9 +345,13 @@
         return lax.ppermute(array, ("tm", "space"), pairs)
 
     def exchanged(array, by, earlier):
+        part = slabs if earlier else slabs - 1
+
         def to(t, s):
             partner = ((s + by) ^ 1) - by
-            return (t - earlier, partner) if 0 <= partner < blocks else (t ^ 1, s)
+            if t >= part:
+                return (t, s // 8 * 8 + (s + 2 - 4 * by) % 8)
+            return (t - earlier, partner) if 0 <= partner < blocks else ((t + 1) % part, s)
 
         return moved(array, to)
 
@@ -371,12 +395,12 @@
         widened, edges, message_one, message_two = pl.pallas_call(
             functools.partial(first_kernel, blocks, slabs),
             out_shape=(shaped(fields, depth + 2), shaped(fields, edge_count), layer, layer),
-            in_specs=[smem, smem] + [vmem] * 6 + [hbm],
+            in_specs=[smem, smem] + [vmem] * 6,
             out_specs=(vmem,) * 4,
             scratch_shapes=[room(2, fields)],
             compiler_params=params(32),
             cost_estimate=cost(2.5),
-        )(snap_of_step, snaps_next, state, halo_one, halo_two, own_flow, other_flow, velocity, start)
+        )(snap_of_step, snaps_next, state, halo_one, halo_two, own_flow, other_flow, velocity)
         halo_one = exchanged(message_one, 0, 0)
         halo_two = exchanged(message_two, 1, 0)
         carried_on, inner, *inner_pieces = pl.pallas_call(
@@ -389,38 +413,37 @@
             cost_estimate=cost(3),
         )(snap_of_step, snaps_next, widened, edges, velocity, start)
         inner_parts = inner_pieces[:1] + [
-            moved(inner_pieces[by], lambda t, s, by=by: (t + by, s)) for by in range(1, slabs)
+            moved(inner_pieces[by], lambda t, s, by=by: (t ^ by, s)) for by in range(1, slabs)
         ]
-        outer, *outer_pieces = pl.pallas_call(
+        inner_sum, outer, to_core, *outer_pieces = pl.pallas_call(
             functools.partial(outer_kernel, blocks, slabs),
-            out_shape=(shaped(fields, edge_count),) + pieces,
-            in_specs=[smem] + [vmem] * 7,
-            out_specs=(vmem,) * (1 + slabs),
+            out_shape=(pieces[0], shaped(fields, edge_count), shaped(2 * edge_count + 1)) + pieces,
+            in_specs=[smem] + [vmem] * (8 + slabs),
+            out_specs=(vmem,) * (3 + slabs),
             scratch_shapes=[room(2, fields), room(edge_count)],
             compiler_params=params(32),
             cost_estimate=cost(1),
-        )(snap_of_step, edges, halo_one, halo_two, own_flow, other_flow, carried_on, velocity)
-        outer_parts = outer_pieces[:1] + [
-            moved(outer_pieces[by], lambda t, s, by=by: (t + by, s)) for by in range(1, slabs)
-        ]
-        final = pl.pallas_call(
-            finish_kernel,
-            out_shape=shaped(fields, depth),
-            in_specs=[smem, vmem, vmem, vmem, hbm],
-            out_specs=hbm,
+        )(snap_of_step, edges, halo_one, halo_two, own_flow, other_flow, carried_on, widened, velocity, *inner_parts)
+        across = [moved(outer_pieces[by], lambda t, s, by=by: (t ^ by, s)) for by in (2, 3)]
+        from_core = moved(to_core, lambda t, s: (t ^ 1, s))
+        inner_sum, final = pl.pallas_call(
+            functools.partial(finish_kernel, slabs),
+            out_shape=(pieces[0], shaped(fields, depth)),
+            in_specs=[smem] + [vmem] * 5 + [hbm],
+            out_specs=(vmem, hbm),
             scratch_shapes=[room(fields, edge_count), sem((2,))],
-            input_output_aliases={4: 0},
+            input_output_aliases={5: 0, 6: 1},
             compiler_params=params(32),
             cost_estimate=cost(1),
-        )(snap_of_step, carried_on, outer, velocity, inner)
+        )(snap_of_step, carried_on, outer, velocity, from_core, inner_sum, inner)
         gradient = pl.pallas_call(
             sum_kernel,
             out_shape=shaped(depth, rows=ny // slabs),
-            in_specs=[vmem] * (2 * slabs),
+            in_specs=[vmem] * 5,
             out_specs=vmem,
             compiler_params=params(16),
             cost_estimate=cost(0.5),
-        )(*inner_parts, *outer_parts)
+        )(inner_sum, from_core, outer_pieces[0], *across)
         return (final[None], gradient)
 
     return jax.shard_map(

time: 49.3 us -> 55.6 us (1.13)
  waiting for transfers between devices: 13.3 us -> 20.9 us
  starting transfers between devices: 23 us -> 21 us
  Pallas kernels: 12.1 us -> 12.8 us
    ppermute x14, waiting for transfers between devices: 13.3 us -> 20.9 us  [moved(): return lax.ppermute(array, ('tm', 'space'), pairs)]
    ppermute x14, starting transfers between devices: 23 us -> 21 us  [moved(): return lax.ppermute(array, ('tm', 'space'), pairs)]
    pallas_call x1, Pallas kernels: 1.14 us -> 1.87 us  [body(): pl.pallas_call(functools.partial(outer_kernel, blocks, slabs), out_shape=...]
  transfers between devices with their start and end apart: 14 -> 14, of which waited for: 5 -> 6; matrix products, arithmetic and copies ran while one was open for 0% -> 0% of each run, Pallas kernels for 18% -> 14%
where the time goes in v6:
time: 55.6 us; the launch traced here: 55.5 us
  starting transfers between devices  21 us (38%)
  waiting for transfers between devices  20.9 us (38%)
  Pallas kernels  12.8 us (23%)
  between operations  0.72 us (1%)
    ppermute x14, starting transfers between devices, moved(): return lax.ppermute(array, ('tm', 'space'), pairs)  21 us
    ppermute x14, waiting for transfers between devices, moved(): return lax.ppermute(array, ('tm', 'space'), pairs)  20.9 us
    pallas_call x1, Pallas kernels, body(): pl.pallas_call(functools.partial(inner_kernel, slabs), out_shape=(shaped(...  3.54 us
    pallas_call x1, Pallas kernels, body(): pl.pallas_call(functools.partial(first_kernel, blocks, slabs), out_shape=...  2.63 us
    pallas_call x1, Pallas kernels, body(): pl.pallas_call(start_kernel, out_shape=(layer, layer, shaped(velocity.sha...  2.3 us
    pallas_call x1, Pallas kernels, body(): pl.pallas_call(functools.partial(outer_kernel, blocks, slabs), out_shape=...  1.87 us
    pallas_call x1, Pallas kernels, body(): pl.pallas_call(functools.partial(finish_kernel, slabs), out_shape=(pieces...  1.83 us
  transfers between devices with their start and end apart: 14, of which 6 were waited for; matrix products, arithmetic and copies ran while one was open for 0% of the time, Pallas kernels for 14%

profile of v6, /device:TPU:1, one launch (start us, length us, event | category | flops | bytes accessed | tf_op | source)
XLA Modules:
  0.0 55.5 jit_solution(15486237256226189488)
XLA Ops:
  0.6 3.3 %collective-permute-start.1 = (f32[2,8,32,512]{3,2,1,0:T(8,128)}, f32[2,8,32,512]{3,2,1,0:T(8,128)S(1)}, u32[]{:S(2)}, u32[]{:S(2)}) collective-permute-start(f32[2,8,32,512]{3,2,1,0:T(8,128)} %bitcast.2), channel_id=1, source_target_pairs={{0,192},{1,193},{2,194},{3,195},{4,196},{5,197},{6,198},{7,199},{8... | collective-permute-start | bytes 3145736 | tf_op jit(solution)/shard_map/ppermute | solution.py:345
  4.0 2.3 %shard_map.50 = (f32[4,32,512]{2,1,0:T(8,128)}, f32[4,32,512]{2,1,0:T(8,128)}, f32[2,32,512]{2,1,0:T(8,128)}) custom-call(s32[1,2]{1,0:T(1,128)} %snaps.9, f32[2,8,32,512]{3,2,1,0:T(8,128)} %bitcast.3, f32[2,3,8,32,512]{4,3,2,1,0:T(8,128)} %velocity.9), custom_call_target="tpu_custom_call" | custom-call | bytes 7200000 | tf_op jit(solution)/shard_map/pallas_call | solution.py:377
  6.3 0.0 copy-start.1
  6.3 0.3 collective-permute-start.4
  6.5 2.4 %collective-permute-start.2 = (f32[4,32,512]{2,1,0:T(8,128)}, f32[4,32,512]{2,1,0:T(8,128)S(1)}, u32[]{:S(2)}, u32[]{:S(2)}) collective-permute-start(f32[4,32,512]{2,1,0:T(8,128)} %get-tuple-element.23), channel_id=1, source_target_pairs={{0,193},{1,192},{2,195},{3,194},{4,197},{5,196},{6,199},{7,198},{8... | collective-permute-start | bytes 786440 | tf_op jit(solution)/shard_map/ppermute | solution.py:345
  9.0 3.9 %collective-permute-done.4.own_flow = f32[2,32,512]{2,1,0:T(8,128)S(1)} collective-permute-done((f32[2,32,512]{2,1,0:T(8,128)}, f32[2,32,512]{2,1,0:T(8,128)S(1)}, u32[]{:S(2)}, u32[]{:S(2)}) %collective-permute-start.4) | collective-permute-done | bytes 131104 | tf_op jit(solution)/shard_map/ppermute | solution.py:345
  12.9 7.8 %collective-permute-start.5 = (f32[2,32,512]{2,1,0:T(8,128)S(1)}, f32[2,32,512]{2,1,0:T(8,128)S(1)}, u32[]{:S(2)}, u32[]{:S(2)}) collective-permute-start(f32[2,32,512]{2,1,0:T(8,128)S(1)} %collective-permute-done.4.own_flow), channel_id=1, source_target_pairs={{0,64},{1,65},{2,66},{3,67},{4,68},{5,69},{6,70},{7,71},{8,72},{9,... | collective-permute-start | bytes 393224 | tf_op jit(solution)/shard_map/ppermute | solution.py:345
  20.6 0.0 collective-permute-start
  20.6 4.0 %collective-permute-done.snaps_next = s32[1,2]{1,0:T(1,128)S(1)} collective-permute-done((s32[1,2]{1,0:T(1,128)S(1)}, s32[1,2]{1,0:T(1,128)S(1)}, u32[]{:S(2)}, u32[]{:S(2)}) %collective-permute-start) | collective-permute-done | bytes 40 | tf_op jit(solution)/shard_map/ppermute | solution.py:345
  24.6 2.6 %shard_map.51 = (f32[2,10,32,512]{3,2,1,0:T(8,128)S(1)}, f32[2,4,32,512]{3,2,1,0:T(8,128)S(1)}, f32[4,32,512]{2,1,0:T(8,128)S(1)}, f32[4,32,512]{2,1,0:T(8,128)S(1)}) custom-call(s32[1,2]{1,0:T(1,128)S(1)} %copy-done.2, s32[1,2]{1,0:T(1,128)S(1)} %collective-permute-done.snaps_next, f32[2,8,32,512]{3,2,1,0:T(8,128)S(1)} %collective-permute-done.1.state, ...), custom_call_target="tpu_custom_call" | custom-call | bytes 9000000 | tf_op jit(solution)/shard_map/pallas_call | solution.py:395
  27.3 1.7 %collective-permute-start.6 = (f32[4,32,512]{2,1,0:T(8,128)S(1)}, f32[4,32,512]{2,1,0:T(8,128)S(1)}, u32[]{:S(2)}, u32[]{:S(2)}) collective-permute-start(f32[4,32,512]{2,1,0:T(8,128)S(1)} %get-tuple-element.29), channel_id=1, source_target_pairs={{0,1},{1,0},{2,3},{3,2},{4,5},{5,4},{6,7},{7,6},{8,9},{9,8},{10,11... | collective-permute-start | bytes 786440 | tf_op jit(solution)/shard_map/ppermute | solution.py:345
  29.0 0.7 %collective-permute-start.7 = (f32[4,32,512]{2,1,0:T(8,128)S(1)}, f32[4,32,512]{2,1,0:T(8,128)S(1)}, u32[]{:S(2)}, u32[]{:S(2)}) collective-permute-start(f32[4,32,512]{2,1,0:T(8,128)S(1)} %get-tuple-element.30), channel_id=1, source_target_pairs={{0,64},{1,2},{2,1},{3,4},{4,3},{5,6},{6,5},{7,8},{8,7},{9,10},{10,... | collective-permute-start | bytes 786440 | tf_op jit(solution)/shard_map/ppermute | solution.py:345
  29.6 3.5 %shard_map.52 = (f32[2,8,32,512]{3,2,1,0:T(8,128)S(1)}, f32[2,8,32,512]{3,2,1,0:T(8,128)}, f32[4,8,512]{2,1,0:T(8,128)S(1)}, f32[4,8,512]{2,1,0:T(8,128)S(1)}, f...) custom-call(s32[1,2]{1,0:T(1,128)S(1)} %copy-done.2, s32[1,2]{1,0:T(1,128)S(1)} %collective-permute-done.snaps_next, ...), custom_call_target="tpu_custom_call" | custom-call | bytes 10800000 | tf_op jit(solution)/shard_map/pallas_call | solution.py:406
  33.2 0.3 collective-permute-start.8
  33.5 1.8 %collective-permute-start.9 = (f32[4,8,512]{2,1,0:T(8,128)S(1)}, f32[4,8,512]{2,1,0:T(8,128)S(1)}, u32[]{:S(2)}, u32[]{:S(2)}) collective-permute-start(f32[4,8,512]{2,1,0:T(8,128)S(1)} %get-tuple-element.33), channel_id=1, source_target_pairs={{0,128},{1,129},{2,130},{3,131},{4,132},{5,133},{6,134},{7,135},{8... | collective-permute-start | bytes 196616 | tf_op jit(solution)/shard_map/ppermute | solution.py:345
  35.2 0.2 collective-permute-start.10
  35.4 10.2 %collective-permute-done.9.rest_2_ = f32[4,8,512]{2,1,0:T(8,128)S(1)} collective-permute-done((f32[4,8,512]{2,1,0:T(8,128)S(1)}, f32[4,8,512]{2,1,0:T(8,128)S(1)}, u32[]{:S(2)}, u32[]{:S(2)}) %collective-permute-start.9) | collective-permute-done | bytes 65568 | tf_op jit(solution)/shard_map/ppermute | solution.py:345
  45.6 0.7 %collective-permute-done.10.rest_3_ = f32[4,8,512]{2,1,0:T(8,128)S(1)} collective-permute-done((f32[4,8,512]{2,1,0:T(8,128)S(1)}, f32[4,8,512]{2,1,0:T(8,128)S(1)}, u32[]{:S(2)}, u32[]{:S(2)}) %collective-permute-start.10) | collective-permute-done | bytes 65568 | tf_op jit(solution)/shard_map/ppermute | solution.py:345
  46.3 1.9 %shard_map.53 = (f32[4,8,512]{2,1,0:T(8,128)S(1)}, f32[2,4,32,512]{3,2,1,0:T(8,128)S(1)}, f32[9,32,512]{2,1,0:T(8,128)S(1)}, f32[4,8,512]{2,1,0:T(8,128)S(1)}, f...) custom-call(s32[1,2]{1,0:T(1,128)S(1)} %copy-done.2, ...), custom_call_target="tpu_custom_call" | custom-call | bytes 3600000 | tf_op jit(solution)/shard_map/pallas_call | solution.py:418
  48.2 2.6 %collective-permute-start.12 = (f32[4,8,512]{2,1,0:T(8,128)S(1)}, f32[4,8,512]{2,1,0:T(8,128)S(1)}, u32[]{:S(2)}, u32[]{:S(2)}) collective-permute-start(f32[4,8,512]{2,1,0:T(8,128)S(1)} %get-tuple-element.42), channel_id=1, source_target_pairs={{0,128},{1,129},{2,130},{3,131},{4,132},{5,133},{6,134},{7,135},{8... | collective-permute-start | bytes 196616 | tf_op jit(solution)/shard_map/ppermute | solution.py:345
  50.8 1.8 %shard_map.54 = (f32[4,8,512]{2,1,0:T(8,128)S(1)}, f32[2,8,32,512]{3,2,1,0:T(8,128)}) custom-call(s32[1,2]{1,0:T(1,128)S(1)} %copy-done.2, f32[2,8,32,512]{3,2,1,0:T(8,128)S(1)} %get-tuple-element.28.carried_on, f32[2,4,32,512]{3,2,1,0:T(8,128)S(1)} %get-tuple-element.35.outer, ...), custom_call_target="tpu_custom_call", output_to_operand_aliasing={{0}: (5, {}), {1}: (6, {})} | custom-call | bytes 3600000 | tf_op jit(solution)/shard_map/pallas_call | solution.py:429
  52.6 0.6 %collective-permute-done.12.refs_1_ = f32[4,8,512]{2,1,0:T(8,128)S(1)} collective-permute-done((f32[4,8,512]{2,1,0:T(8,128)S(1)}, f32[4,8,512]{2,1,0:T(8,128)S(1)}, u32[]{:S(2)}, u32[]{:S(2)}) %collective-permute-start.12) | collective-permute-done | bytes 65568 | tf_op jit(solution)/shard_map/ppermute | solution.py:345
  53.3 1.5 %collective-permute-done.13.refs_2_ = f32[4,8,512]{2,1,0:T(8,128)S(1)} collective-permute-done((f32[4,8,512]{2,1,0:T(8,128)S(1)}, f32[4,8,512]{2,1,0:T(8,128)S(1)}, u32[]{:S(2)}, u32[]{:S(2)}) %collective-permute-start.13) | collective-permute-done | bytes 65568 | tf_op jit(solution)/shard_map/ppermute | solution.py:345
  54.8 0.7 %shard_map.55 = f32[8,8,512]{2,1,0:T(8,128)} custom-call(f32[4,8,512]{2,1,0:T(8,128)S(1)} %get-tuple-element.40.inner_sum, f32[9,32,512]{2,1,0:T(8,128)S(1)} %collective-permute-done.11.from_core, f32[4,8,512]{2,1,0:T(8,128)S(1)} %get-tuple-element.41.refs_0_, f32[4,8,512]{2,1,0:T(8,128)S(1)} %collective-permute-done.12.refs_1_, ...), custom_call_target="tpu_custom_call" | custom-call | bytes 1800000 | tf_op jit(solution)/shard_map/pallas_call | solution.py:439
  (16 shorter events, 0.0 us)
Async XLA Ops:
  0.6 20.0 %copy-start.2 = (s32[1,2]{1,0:T(1,128)S(1)}, s32[1,2]{1,0:T(1,128)}, u32[]{:S(2)}) copy-start(s32[1,2]{1,0:T(1,128)} %snaps.9) | copy-start | bytes 28
  0.6 24.0 %copy-start = (f32[2,3,8,32,512]{4,3,2,1,0:T(8,128)S(1)}, f32[2,3,8,32,512]{4,3,2,1,0:T(8,128)}, u32[]{:S(2)}) copy-start(f32[2,3,8,32,512]{4,3,2,1,0:T(8,128)} %velocity.9) | copy-start | bytes 9437188
  0.6 24.0 %collective-permute-start.1 = (f32[2,8,32,512]{3,2,1,0:T(8,128)}, f32[2,8,32,512]{3,2,1,0:T(8,128)S(1)}, u32[]{:S(2)}, u32[]{:S(2)}) collective-permute-start(f32[2,8,32,512]{3,2,1,0:T(8,128)} %bitcast.2), channel_id=1, source_target_pairs={{0,192},{1,193},{2,194},{3,195},{4,196},{5,197},{6,198},{7,199},{8... | collective-permute-start | bytes 3145736 | tf_op jit(solution)/shard_map/ppermute | solution.py:345
  6.3 23.3 %copy-start.1 = (f32[1,2,8,32,512]{4,3,2,1,0:T(8,128)S(1)}, f32[1,2,8,32,512]{4,3,2,1,0:T(8,128)}, u32[]{:S(2)}) copy-start(f32[1,2,8,32,512]{4,3,2,1,0:T(8,128)} %param.3) | copy-start | bytes 3145732
  6.3 6.6 %collective-permute-start.4 = (f32[2,32,512]{2,1,0:T(8,128)}, f32[2,32,512]{2,1,0:T(8,128)S(1)}, u32[]{:S(2)}, u32[]{:S(2)}) collective-permute-start(f32[2,32,512]{2,1,0:T(8,128)} %get-tuple-element.25), channel_id=1, source_target_pairs={{0,129},{1,130},{2,131},{3,132},{4,133},{5,134},{6,135},{7,136},{8... | collective-permute-start | bytes 393224 | tf_op jit(solution)/shard_map/ppermute | solution.py:345
  6.5 18.1 %collective-permute-start.2 = (f32[4,32,512]{2,1,0:T(8,128)}, f32[4,32,512]{2,1,0:T(8,128)S(1)}, u32[]{:S(2)}, u32[]{:S(2)}) collective-permute-start(f32[4,32,512]{2,1,0:T(8,128)} %get-tuple-element.23), channel_id=1, source_target_pairs={{0,193},{1,192},{2,195},{3,194},{4,197},{5,196},{6,199},{7,198},{8... | collective-permute-start | bytes 786440 | tf_op jit(solution)/shard_map/ppermute | solution.py:345
  9.0 15.6 %collective-permute-start.3 = (f32[4,32,512]{2,1,0:T(8,128)}, f32[4,32,512]{2,1,0:T(8,128)S(1)}, u32[]{:S(2)}, u32[]{:S(2)}) collective-permute-start(f32[4,32,512]{2,1,0:T(8,128)} %get-tuple-element.24), channel_id=1, source_target_pairs={{0,64},{1,194},{2,193},{3,196},{4,195},{5,198},{6,197},{7,200},{8,... | collective-permute-start | bytes 786440 | tf_op jit(solution)/shard_map/ppermute | solution.py:345
  12.9 11.8 %collective-permute-start.5 = (f32[2,32,512]{2,1,0:T(8,128)S(1)}, f32[2,32,512]{2,1,0:T(8,128)S(1)}, u32[]{:S(2)}, u32[]{:S(2)}) collective-permute-start(f32[2,32,512]{2,1,0:T(8,128)S(1)} %collective-permute-done.4.own_flow), channel_id=1, source_target_pairs={{0,64},{1,65},{2,66},{3,67},{4,68},{5,69},{6,70},{7,71},{8,72},{9,... | collective-permute-start | bytes 393224 | tf_op jit(solution)/shard_map/ppermute | solution.py:345
  20.6 4.0 %collective-permute-start = (s32[1,2]{1,0:T(1,128)S(1)}, s32[1,2]{1,0:T(1,128)S(1)}, u32[]{:S(2)}, u32[]{:S(2)}) collective-permute-start(s32[1,2]{1,0:T(1,128)S(1)} %copy-done.2), channel_id=1, source_target_pairs={{0,192},{1,193},{2,194},{3,195},{4,196},{5,197},{6,198},{7,199},{8... | collective-permute-start | bytes 32 | tf_op jit(solution)/shard_map/ppermute | solution.py:345
  27.3 19.0 %collective-permute-start.6 = (f32[4,32,512]{2,1,0:T(8,128)S(1)}, f32[4,32,512]{2,1,0:T(8,128)S(1)}, u32[]{:S(2)}, u32[]{:S(2)}) collective-permute-start(f32[4,32,512]{2,1,0:T(8,128)S(1)} %get-tuple-element.29), channel_id=1, source_target_pairs={{0,1},{1,0},{2,3},{3,2},{4,5},{5,4},{6,7},{7,6},{8,9},{9,8},{10,11... | collective-permute-start | bytes 786440 | tf_op jit(solution)/shard_map/ppermute | solution.py:345
  29.0 17.4 %collective-permute-start.7 = (f32[4,32,512]{2,1,0:T(8,128)S(1)}, f32[4,32,512]{2,1,0:T(8,128)S(1)}, u32[]{:S(2)}, u32[]{:S(2)}) collective-permute-start(f32[4,32,512]{2,1,0:T(8,128)S(1)} %get-tuple-element.30), channel_id=1, source_target_pairs={{0,64},{1,2},{2,1},{3,4},{4,3},{5,6},{6,5},{7,8},{8,7},{9,10},{10,... | collective-permute-start | bytes 786440 | tf_op jit(solution)/shard_map/ppermute | solution.py:345
  33.2 2.2 %collective-permute-start.8 = (f32[4,8,512]{2,1,0:T(8,128)S(1)}, f32[4,8,512]{2,1,0:T(8,128)S(1)}, u32[]{:S(2)}, u32[]{:S(2)}) collective-permute-start(f32[4,8,512]{2,1,0:T(8,128)S(1)} %get-tuple-element.32), channel_id=1, source_target_pairs={{0,64},{1,65},{2,66},{3,67},{4,68},{5,69},{6,70},{7,71},{8,72},{9,... | collective-permute-start | bytes 196616 | tf_op jit(solution)/shard_map/ppermute | solution.py:345
  33.5 12.2 %collective-permute-start.9 = (f32[4,8,512]{2,1,0:T(8,128)S(1)}, f32[4,8,512]{2,1,0:T(8,128)S(1)}, u32[]{:S(2)}, u32[]{:S(2)}) collective-permute-start(f32[4,8,512]{2,1,0:T(8,128)S(1)} %get-tuple-element.33), channel_id=1, source_target_pairs={{0,128},{1,129},{2,130},{3,131},{4,132},{5,133},{6,134},{7,135},{8... | collective-permute-start | bytes 196616 | tf_op jit(solution)/shard_map/ppermute | solution.py:345
  35.2 11.1 %collective-permute-start.10 = (f32[4,8,512]{2,1,0:T(8,128)S(1)}, f32[4,8,512]{2,1,0:T(8,128)S(1)}, u32[]{:S(2)}, u32[]{:S(2)}) collective-permute-start(f32[4,8,512]{2,1,0:T(8,128)S(1)} %get-tuple-element.34), channel_id=1, source_target_pairs={{0,192},{1,193},{2,194},{3,195},{4,196},{5,197},{6,198},{7,199},{8... | collective-permute-start | bytes 196616 | tf_op jit(solution)/shard_map/ppermute | solution.py:345
  48.2 2.6 %collective-permute-start.11 = (f32[9,32,512]{2,1,0:T(8,128)S(1)}, f32[9,32,512]{2,1,0:T(8,128)S(1)}, u32[]{:S(2)}, u32[]{:S(2)}) collective-permute-start(f32[9,32,512]{2,1,0:T(8,128)S(1)} %get-tuple-element.36), channel_id=1, source_target_pairs={{0,64},{1,65},{2,66},{3,67},{4,68},{5,69},{6,70},{7,71},{8,72},{9,... | collective-permute-start | bytes 1769480 | tf_op jit(solution)/shard_map/ppermute | solution.py:345
  48.2 5.1 %collective-permute-start.12 = (f32[4,8,512]{2,1,0:T(8,128)S(1)}, f32[4,8,512]{2,1,0:T(8,128)S(1)}, u32[]{:S(2)}, u32[]{:S(2)}) collective-permute-start(f32[4,8,512]{2,1,0:T(8,128)S(1)} %get-tuple-element.42), channel_id=1, source_target_pairs={{0,128},{1,129},{2,130},{3,131},{4,132},{5,133},{6,134},{7,135},{8... | collective-permute-start | bytes 196616 | tf_op jit(solution)/shard_map/ppermute | solution.py:345
  50.8 4.0 %collective-permute-start.13 = (f32[4,8,512]{2,1,0:T(8,128)S(1)}, f32[4,8,512]{2,1,0:T(8,128)S(1)}, u32[]{:S(2)}, u32[]{:S(2)}) collective-permute-start(f32[4,8,512]{2,1,0:T(8,128)S(1)} %get-tuple-element.43), channel_id=1, source_target_pairs={{0,192},{1,193},{2,194},{3,195},{4,196},{5,197},{6,198},{7,199},{8... | collective-permute-start | bytes 196616 | tf_op jit(solution)/shard_map/ppermute | solution.py:345

commit v7 on v5

--- a/solution.py
+++ b/solution.py
@@ -170,9 +170,39 @@
     flow_out[...] = flows[:, 0, 1 - lax.rem(lax.axis_index("tm"), 2)]
 
 
-def first_kernel(blocks, slabs, snaps, snaps_next, state, halo_one, halo_two, own_flow, other_flow, velocity, start,
-                 widened, edges, message_one, message_two, halos):
+def share_kernel(slabs, core_state, start, *refs):
+    both = refs[3]
+
+    @pl.when(lax.axis_index("tm") == slabs - 1)
+    def _():
+        both[...] = core_state[1]
+
+    @pl.when(lax.axis_index("tm") < slabs - 1)
+    def _():
+        pltpu.sync_copy(start.at[0], both)
+
+
+def split_kernel(cross, *pieces):
+    for n, piece in enumerate(pieces):
+        piece[...] = cross[4 * n : 4 * n + 4]
+
+
+def first_kernel(blocks, slabs, snaps, snaps_next, core_state, cross, halo_one, halo_two, own_flow, other_flow, velocity, start,
+                 *rest):
+    hops, (widened, edges, message_one, message_two, state, halos) = rest[:-6], rest[-6:]
     depth, shape = state.shape[1], state.shape[2:]
+    crossed = lax.rem(lax.axis_index("tm"), 2) == 1
+
+    @pl.when(crossed)
+    def _():
+        state[0] = cross[...]
+        for n, hop in enumerate(hops):
+            state[1, 4 * n : 4 * n + 4] = hop[...]
+
+    @pl.when(jnp.logical_not(crossed))
+    def _():
+        state[...] = core_state[...]
+
     last = lax.axis_index("tm") == slabs - 1
 
     @pl.when(last)
@@ -348,7 +378,7 @@
         layer = shaped(4)
         pieces = (shaped(4, rows=ny // slabs),) * slabs
 
-        state = moved(start, lambda t, s: (t - 1, s))
+        core_state = moved(start, lambda t, s: (t ^ 1, s))
         snaps_next = moved(snap_of_step, lambda t, s: (t - 1, s))
         message_one, message_two, flow_out = pl.pallas_call(
             start_kernel,
@@ -361,22 +391,41 @@
                 room(*velocity.shape[:2], 2),
                 sem((5,)),
             ],
-            compiler_params=params(56),
+            compiler_params=params(53),
             cost_estimate=cost(2),
         )(snap_of_step, start, velocity)
+        both, message_one, message_two, flow_out = pl.pallas_call(
+            functools.partial(share_kernel, slabs),
+            out_shape=(shaped(depth), layer, layer, shaped(velocity.shape[0])),
+            in_specs=[vmem] + [hbm] * 4,
+            out_specs=(vmem,) + (hbm,) * 3,
+            input_output_aliases={2: 1, 3: 2, 4: 3},
+            compiler_params=params(32),
+            cost_estimate=cost(0.5),
+        )(core_state, start, message_one, message_two, flow_out)
+        cross = moved(both, lambda t, s: (t ^ 3, s))
         halo_one = exchanged(message_one, 0, 1)
         halo_two = exchanged(message_two, 1, 1)
         own_flow = moved(flow_out, fetched)
         other_flow = moved(own_flow, lambda t, s: (t ^ 1, s))
+        hops = pl.pallas_call(
+            split_kernel,
+            out_shape=(shaped(4),) * (depth // 4),
+            in_specs=[vmem],
+            out_specs=(vmem,) * (depth // 4),
+            compiler_params=params(16),
+            cost_estimate=cost(0.5),
+        )(cross)
+        hops = [moved(hop, lambda t, s: (t ^ 1, s)) for hop in hops]
         widened, edges, message_one, message_two = pl.pallas_call(
             functools.partial(first_kernel, blocks, slabs),
             out_shape=(shaped(fields, depth + 2), shaped(fields, edge_count), layer, layer),
-            in_specs=[smem, smem] + [vmem] * 6 + [hbm],
+            in_specs=[smem, smem] + [vmem] * 7 + [hbm] + [vmem] * len(hops),
             out_specs=(vmem,) * 4,
-            scratch_shapes=[room(2, fields)],
+            scratch_shapes=[room(fields, depth), room(2, fields)],
             compiler_params=params(32),
             cost_estimate=cost(2.5),
-        )(snap_of_step, snaps_next, state, halo_one, halo_two, own_flow, other_flow, velocity, start)
+        )(snap_of_step, snaps_next, core_state, cross, halo_one, halo_two, own_flow, other_flow, velocity, start, *hops)
         halo_one = exchanged(message_one, 0, 0)
         halo_two = exchanged(message_two, 1, 0)
         carried_on, inner, *inner_pieces = pl.pallas_call(

time: 49.3 us -> 53.1 us (1.077)
  the two profiles are of different devices: /device:TPU:1 before, /device:TPU:129 now
where the time goes in v7:
time: 53.1 us; the launch traced here: 53 us
  starting transfers between devices  21.7 us (41%)
  waiting for transfers between devices  17.8 us (34%)
  Pallas kernels  11.7 us (22%)
  local copies, waits for them, and re-layouts  1.05 us (2%)
  between operations  0.78 us (1%)
    ppermute x17, starting transfers between devices, moved(): return lax.ppermute(array, ('tm', 'space'), pairs)  21.7 us
    ppermute x17, waiting for transfers between devices, moved(): return lax.ppermute(array, ('tm', 'space'), pairs)  17.8 us
    pallas_call x1, Pallas kernels, body(): pl.pallas_call(functools.partial(inner_kernel, slabs), out_shape=(shaped(...  3.57 us
    pallas_call x1, Pallas kernels, body(): pl.pallas_call(functools.partial(first_kernel, blocks, slabs), out_shape=...  2.81 us
    pallas_call x1, Pallas kernels, body(): pl.pallas_call(finish_kernel, out_shape=shaped(fields, depth), in_specs=[...  1.81 us
    pallas_call x1, Pallas kernels, body(): pl.pallas_call(start_kernel, out_shape=(layer, layer, shaped(velocity.sha...  1.56 us
    pallas_call x1, Pallas kernels, body(): pl.pallas_call(functools.partial(outer_kernel, blocks, slabs), out_shape=...  1.14 us
  transfers between devices with their start and end apart: 17, of which 6 were waited for; matrix products, arithmetic and copies ran while one was open for 0% of the time, Pallas kernels for 15%

profile of v7, /device:TPU:129, one launch (start us, length us, event | category | flops | bytes accessed | tf_op | source)
XLA Modules:
  0.0 53.0 jit_solution(8931878366993326144)
XLA Ops:
  0.6 0.8 %collective-permute-start.1 = (f32[2,8,32,512]{3,2,1,0:T(8,128)}, f32[2,8,32,512]{3,2,1,0:T(8,128)S(1)}, u32[]{:S(2)}, u32[]{:S(2)}) collective-permute-start(f32[2,8,32,512]{3,2,1,0:T(8,128)} %bitcast.2), channel_id=1, source_target_pairs={{0,64},{1,65},{2,66},{3,67},{4,68},{5,69},{6,70},{7,71},{8,72},{9,... | collective-permute-start | bytes 3145736 | tf_op jit(solution)/shard_map/ppermute | solution.py:355
  1.4 1.0 %copy-done.2 = s32[1,2]{1,0:T(1,128)S(1)} copy-done((s32[1,2]{1,0:T(1,128)S(1)}, s32[1,2]{1,0:T(1,128)}, u32[]{:S(2)}) %copy-start.2) | copy-done | bytes 32
  2.5 1.6 %shard_map.50 = (f32[4,32,512]{2,1,0:T(8,128)S(1)}, f32[4,32,512]{2,1,0:T(8,128)S(1)}, f32[2,32,512]{2,1,0:T(8,128)S(1)}) custom-call(s32[1,2]{1,0:T(1,128)S(1)} %copy-done.2, f32[2,8,32,512]{3,2,1,0:T(8,128)} %bitcast.3, f32[2,3,8,32,512]{4,3,2,1,0:T(8,128)} %velocity.9), custom_call_target="tpu_custom_call" | custom-call | bytes 7200000 | tf_op jit(solution)/shard_map/pallas_call | solution.py:383
  4.1 1.5 %collective-permute-start.2 = (f32[8,32,512]{2,1,0:T(8,128)S(1)}, f32[8,32,512]{2,1,0:T(8,128)S(1)}, u32[]{:S(2)}, u32[]{:S(2)}) collective-permute-start(f32[8,32,512]{2,1,0:T(8,128)S(1)} %get-tuple-element.29), channel_id=1, source_target_pairs={{0,192},{1,193},{2,194},{3,195},{4,196},{5,197},{6,198},{7,199},{8... | collective-permute-start | bytes 1572872 | tf_op jit(solution)/shard_map/ppermute | solution.py:355
  5.9 3.6 %collective-permute-start.5 = (f32[2,32,512]{2,1,0:T(8,128)S(1)}, f32[2,32,512]{2,1,0:T(8,128)S(1)}, u32[]{:S(2)}, u32[]{:S(2)}) collective-permute-start(f32[2,32,512]{2,1,0:T(8,128)S(1)} %get-tuple-element.32), channel_id=1, source_target_pairs={{0,129},{1,130},{2,131},{3,132},{4,133},{5,134},{6,135},{7,136},{8... | collective-permute-start | bytes 393224 | tf_op jit(solution)/shard_map/ppermute | solution.py:355
  9.5 0.8 %collective-permute-start.3 = (f32[4,32,512]{2,1,0:T(8,128)S(1)}, f32[4,32,512]{2,1,0:T(8,128)S(1)}, u32[]{:S(2)}, u32[]{:S(2)}) collective-permute-start(f32[4,32,512]{2,1,0:T(8,128)S(1)} %get-tuple-element.30), channel_id=1, source_target_pairs={{0,193},{1,192},{2,195},{3,194},{4,197},{5,196},{6,199},{7,198},{8... | collective-permute-start | bytes 786440 | tf_op jit(solution)/shard_map/ppermute | solution.py:355
  10.3 3.3 %collective-permute-start.4 = (f32[4,32,512]{2,1,0:T(8,128)S(1)}, f32[4,32,512]{2,1,0:T(8,128)S(1)}, u32[]{:S(2)}, u32[]{:S(2)}) collective-permute-start(f32[4,32,512]{2,1,0:T(8,128)S(1)} %get-tuple-element.31), channel_id=1, source_target_pairs={{0,64},{1,194},{2,193},{3,196},{4,195},{5,198},{6,197},{7,200},{8,... | collective-permute-start | bytes 786440 | tf_op jit(solution)/shard_map/ppermute | solution.py:355
  13.6 7.8 %collective-permute-done.2.cross = f32[8,32,512]{2,1,0:T(8,128)S(1)} collective-permute-done((f32[8,32,512]{2,1,0:T(8,128)S(1)}, f32[8,32,512]{2,1,0:T(8,128)S(1)}, u32[]{:S(2)}, u32[]{:S(2)}) %collective-permute-start.2) | collective-permute-done | bytes 524320 | tf_op jit(solution)/shard_map/ppermute | solution.py:355
  21.6 0.5 collective-permute-start.8
  22.2 1.5 %collective-permute-done.6.other_flow = f32[2,32,512]{2,1,0:T(8,128)S(1)} collective-permute-done((f32[2,32,512]{2,1,0:T(8,128)S(1)}, f32[2,32,512]{2,1,0:T(8,128)S(1)}, u32[]{:S(2)}, u32[]{:S(2)}) %collective-permute-start.6) | collective-permute-done | bytes 131104 | tf_op jit(solution)/shard_map/ppermute | solution.py:355
  23.7 2.7 %collective-permute-done.3.halo_one = f32[4,32,512]{2,1,0:T(8,128)S(1)} collective-permute-done((f32[4,32,512]{2,1,0:T(8,128)S(1)}, f32[4,32,512]{2,1,0:T(8,128)S(1)}, u32[]{:S(2)}, u32[]{:S(2)}) %collective-permute-start.3) | collective-permute-done | bytes 262176 | tf_op jit(solution)/shard_map/ppermute | solution.py:355
  26.4 2.8 %shard_map.53 = (f32[2,10,32,512]{3,2,1,0:T(8,128)S(1)}, f32[2,4,32,512]{3,2,1,0:T(8,128)S(1)}, f32[4,32,512]{2,1,0:T(8,128)S(1)}, f32[4,32,512]{2,1,0:T(8,128)S(1)}) custom-call(s32[1,2]{1,0:T(1,128)S(1)} %copy-done.2, s32[1,2]{1,0:T(1,128)S(1)} %collective-permute-done.snaps_next, f32[2,8,32,512]{3,2,1,0:T(8,128)S(1)} %collective-permute-done.1.core_state, ...), custom_call_target="tpu_custom_call" | custom-call | bytes 9000000 | tf_op jit(solution)/shard_map/pallas_call | solution.py:420
  29.2 0.3 collective-permute-start.9
  29.5 2.7 %collective-permute-start.10 = (f32[4,32,512]{2,1,0:T(8,128)S(1)}, f32[4,32,512]{2,1,0:T(8,128)S(1)}, u32[]{:S(2)}, u32[]{:S(2)}) collective-permute-start(f32[4,32,512]{2,1,0:T(8,128)S(1)} %get-tuple-element.39), channel_id=1, source_target_pairs={{0,64},{1,2},{2,1},{3,4},{4,3},{5,6},{6,5},{7,8},{8,7},{9,10},{10,... | collective-permute-start | bytes 786440 | tf_op jit(solution)/shard_map/ppermute | solution.py:355
  32.2 3.6 %shard_map.54 = (f32[2,8,32,512]{3,2,1,0:T(8,128)S(1)}, f32[2,8,32,512]{3,2,1,0:T(8,128)}, f32[4,8,512]{2,1,0:T(8,128)S(1)}, f32[4,8,512]{2,1,0:T(8,128)S(1)}, f...) custom-call(s32[1,2]{1,0:T(1,128)S(1)} %copy-done.2, s32[1,2]{1,0:T(1,128)S(1)} %collective-permute-done.snaps_next, ...), custom_call_target="tpu_custom_call" | custom-call | bytes 10800000 | tf_op jit(solution)/shard_map/pallas_call | solution.py:431
  35.8 2.5 %collective-permute-start.11 = (f32[4,8,512]{2,1,0:T(8,128)S(1)}, f32[4,8,512]{2,1,0:T(8,128)S(1)}, u32[]{:S(2)}, u32[]{:S(2)}) collective-permute-start(f32[4,8,512]{2,1,0:T(8,128)S(1)} %get-tuple-element.43), channel_id=1, source_target_pairs={{0,64},{1,65},{2,66},{3,67},{4,68},{5,69},{6,70},{7,71},{8,72},{9,... | collective-permute-start | bytes 196616 | tf_op jit(solution)/shard_map/ppermute | solution.py:355
  38.3 1.6 %collective-permute-start.12 = (f32[4,8,512]{2,1,0:T(8,128)S(1)}, f32[4,8,512]{2,1,0:T(8,128)S(1)}, u32[]{:S(2)}, u32[]{:S(2)}) collective-permute-start(f32[4,8,512]{2,1,0:T(8,128)S(1)} %get-tuple-element.44), channel_id=1, source_target_pairs={{0,128},{1,129},{2,130},{3,131},{4,132},{5,133},{6,134},{7,135},{8... | collective-permute-start | bytes 196616 | tf_op jit(solution)/shard_map/ppermute | solution.py:355
  39.9 3.9 %collective-permute-done.9.halo_one = f32[4,32,512]{2,1,0:T(8,128)S(1)} collective-permute-done((f32[4,32,512]{2,1,0:T(8,128)S(1)}, f32[4,32,512]{2,1,0:T(8,128)S(1)}, u32[]{:S(2)}, u32[]{:S(2)}) %collective-permute-start.9) | collective-permute-done | bytes 262176 | tf_op jit(solution)/shard_map/ppermute | solution.py:355
  43.9 1.1 %shard_map.55 = (f32[2,4,32,512]{3,2,1,0:T(8,128)S(1)}, f32[4,8,512]{2,1,0:T(8,128)S(1)}, f32[4,8,512]{2,1,0:T(8,128)S(1)}, f32[4,8,512]{2,1,0:T(8,128)S(1)}, f32[4,8,512]{2,1,0:T(8,128)S(1)}) custom-call(s32[1,2]{1,0:T(1,128)S(1)} %copy-done.2, f32[2,4,32,512]{3,2,1,0:T(8,128)S(1)} %get-tuple-element.36.edges, ...), custom_call_target="tpu_custom_call" | custom-call | bytes 3600000 | tf_op jit(solution)/shard_map/pallas_call | solution.py:443
  45.1 3.5 %collective-permute-start.15 = (f32[4,8,512]{2,1,0:T(8,128)S(1)}, f32[4,8,512]{2,1,0:T(8,128)S(1)}, u32[]{:S(2)}, u32[]{:S(2)}) collective-permute-start(f32[4,8,512]{2,1,0:T(8,128)S(1)} %get-tuple-element.48), channel_id=1, source_target_pairs={{0,128},{1,129},{2,130},{3,131},{4,132},{5,133},{6,134},{7,135},{8... | collective-permute-start | bytes 196616 | tf_op jit(solution)/shard_map/ppermute | solution.py:355
  48.6 1.8 %shard_map.56 = f32[2,8,32,512]{3,2,1,0:T(8,128)} custom-call(s32[1,2]{1,0:T(1,128)S(1)} %copy-done.2, f32[2,8,32,512]{3,2,1,0:T(8,128)S(1)} %get-tuple-element.37.carried_on, f32[2,4,32,512]{3,2,1,0:T(8,128)S(1)} %get-tuple-element.40.outer, f32[2,3,8,32,512]{4,3,2,1,0:T(8,128)S(1)} %copy-done, ...), custom_call_target="tpu_custom_call", output_to_operand_aliasing={{}: (4, {})} | custom-call | bytes 3600000 | tf_op jit(solution)/shard_map/pallas_call | solution.py:455
  50.4 1.4 %collective-permute-done.15.refs_6_ = f32[4,8,512]{2,1,0:T(8,128)S(1)} collective-permute-done((f32[4,8,512]{2,1,0:T(8,128)S(1)}, f32[4,8,512]{2,1,0:T(8,128)S(1)}, u32[]{:S(2)}, u32[]{:S(2)}) %collective-permute-start.15) | collective-permute-done | bytes 65568 | tf_op jit(solution)/shard_map/ppermute | solution.py:355
  51.9 0.5 collective-permute-done.16.refs_7_
  52.3 0.7 %shard_map.57 = f32[8,8,512]{2,1,0:T(8,128)} custom-call(f32[4,8,512]{2,1,0:T(8,128)S(1)} %get-tuple-element.42.refs_0_, f32[4,8,512]{2,1,0:T(8,128)S(1)} %collective-permute-done.11.refs_1_, f32[4,8,512]{2,1,0:T(8,128)S(1)} %collective-permute-done.12.refs_2_, f32[4,8,512]{2,1,0:T(8,128)S(1)} %collective-permute-done.13.refs_3_, ...), custom_call_target="tpu_custom_call" | custom-call | bytes 1800000 | tf_op jit(solution)/shard_map/pallas_call | solution.py:465
  (24 shorter events, 0.7 us)
Async XLA Ops:
  0.6 3.4 %copy-start.1 = (f32[1,2,8,32,512]{4,3,2,1,0:T(8,128)S(1)}, f32[1,2,8,32,512]{4,3,2,1,0:T(8,128)}, u32[]{:S(2)}) copy-start(f32[1,2,8,32,512]{4,3,2,1,0:T(8,128)} %param.3) | copy-start | bytes 3145732
  0.6 25.7 %copy-start = (f32[2,3,8,32,512]{4,3,2,1,0:T(8,128)S(1)}, f32[2,3,8,32,512]{4,3,2,1,0:T(8,128)}, u32[]{:S(2)}) copy-start(f32[2,3,8,32,512]{4,3,2,1,0:T(8,128)} %velocity.9) | copy-start | bytes 9437188
  0.6 3.4 %collective-permute-start.1 = (f32[2,8,32,512]{3,2,1,0:T(8,128)}, f32[2,8,32,512]{3,2,1,0:T(8,128)S(1)}, u32[]{:S(2)}, u32[]{:S(2)}) collective-permute-start(f32[2,8,32,512]{3,2,1,0:T(8,128)} %bitcast.2), channel_id=1, source_target_pairs={{0,64},{1,65},{2,66},{3,67},{4,68},{5,69},{6,70},{7,71},{8,72},{9,... | collective-permute-start | bytes 3145736 | tf_op jit(solution)/shard_map/ppermute | solution.py:355
  1.4 1.0 %copy-start.2 = (s32[1,2]{1,0:T(1,128)S(1)}, s32[1,2]{1,0:T(1,128)}, u32[]{:S(2)}) copy-start(s32[1,2]{1,0:T(1,128)} %snaps.9) | copy-start | bytes 28
  4.1 17.3 %collective-permute-start.2 = (f32[8,32,512]{2,1,0:T(8,128)S(1)}, f32[8,32,512]{2,1,0:T(8,128)S(1)}, u32[]{:S(2)}, u32[]{:S(2)}) collective-permute-start(f32[8,32,512]{2,1,0:T(8,128)S(1)} %get-tuple-element.29), channel_id=1, source_target_pairs={{0,192},{1,193},{2,194},{3,195},{4,196},{5,197},{6,198},{7,199},{8... | collective-permute-start | bytes 1572872 | tf_op jit(solution)/shard_map/ppermute | solution.py:355
  5.6 16.0 %collective-permute-start = (s32[1,2]{1,0:T(1,128)S(1)}, s32[1,2]{1,0:T(1,128)S(1)}, u32[]{:S(2)}, u32[]{:S(2)}) collective-permute-start(s32[1,2]{1,0:T(1,128)S(1)} %copy-done.2), channel_id=1, source_target_pairs={{0,192},{1,193},{2,194},{3,195},{4,196},{5,197},{6,198},{7,199},{8... | collective-permute-start | bytes 32 | tf_op jit(solution)/shard_map/ppermute | solution.py:355
  5.9 16.2 %collective-permute-start.5 = (f32[2,32,512]{2,1,0:T(8,128)S(1)}, f32[2,32,512]{2,1,0:T(8,128)S(1)}, u32[]{:S(2)}, u32[]{:S(2)}) collective-permute-start(f32[2,32,512]{2,1,0:T(8,128)S(1)} %get-tuple-element.32), channel_id=1, source_target_pairs={{0,129},{1,130},{2,131},{3,132},{4,133},{5,134},{6,135},{7,136},{8... | collective-permute-start | bytes 393224 | tf_op jit(solution)/shard_map/ppermute | solution.py:355
  9.5 16.8 %collective-permute-start.3 = (f32[4,32,512]{2,1,0:T(8,128)S(1)}, f32[4,32,512]{2,1,0:T(8,128)S(1)}, u32[]{:S(2)}, u32[]{:S(2)}) collective-permute-start(f32[4,32,512]{2,1,0:T(8,128)S(1)} %get-tuple-element.30), channel_id=1, source_target_pairs={{0,193},{1,192},{2,195},{3,194},{4,197},{5,196},{6,199},{7,198},{8... | collective-permute-start | bytes 786440 | tf_op jit(solution)/shard_map/ppermute | solution.py:355
  10.3 16.0 %collective-permute-start.4 = (f32[4,32,512]{2,1,0:T(8,128)S(1)}, f32[4,32,512]{2,1,0:T(8,128)S(1)}, u32[]{:S(2)}, u32[]{:S(2)}) collective-permute-start(f32[4,32,512]{2,1,0:T(8,128)S(1)} %get-tuple-element.31), channel_id=1, source_target_pairs={{0,64},{1,194},{2,193},{3,196},{4,195},{5,198},{6,197},{7,200},{8,... | collective-permute-start | bytes 786440 | tf_op jit(solution)/shard_map/ppermute | solution.py:355
  21.5 4.9 %collective-permute-start.7 = (f32[4,32,512]{2,1,0:T(8,128)S(1)}, f32[4,32,512]{2,1,0:T(8,128)S(1)}, u32[]{:S(2)}, u32[]{:S(2)}) collective-permute-start(f32[4,32,512]{2,1,0:T(8,128)S(1)} %get-tuple-element.33), channel_id=1, source_target_pairs={{0,64},{1,65},{2,66},{3,67},{4,68},{5,69},{6,70},{7,71},{8,72},{9,... | collective-permute-start | bytes 786440 | tf_op jit(solution)/shard_map/ppermute | solution.py:355
  21.6 4.8 %collective-permute-start.8 = (f32[4,32,512]{2,1,0:T(8,128)S(1)}, f32[4,32,512]{2,1,0:T(8,128)S(1)}, u32[]{:S(2)}, u32[]{:S(2)}) collective-permute-start(f32[4,32,512]{2,1,0:T(8,128)S(1)} %get-tuple-element.34), channel_id=1, source_target_pairs={{0,64},{1,65},{2,66},{3,67},{4,68},{5,69},{6,70},{7,71},{8,72},{9,... | collective-permute-start | bytes 786440 | tf_op jit(solution)/shard_map/ppermute | solution.py:355
  22.1 1.6 %collective-permute-start.6 = (f32[2,32,512]{2,1,0:T(8,128)S(1)}, f32[2,32,512]{2,1,0:T(8,128)S(1)}, u32[]{:S(2)}, u32[]{:S(2)}) collective-permute-start(f32[2,32,512]{2,1,0:T(8,128)S(1)} %collective-permute-done.5.own_flow), channel_id=1, source_target_pairs={{0,64},{1,65},{2,66},{3,67},{4,68},{5,69},{6,70},{7,71},{8,72},{9,... | collective-permute-start | bytes 393224 | tf_op jit(solution)/shard_map/ppermute | solution.py:355
  29.2 14.7 %collective-permute-start.9 = (f32[4,32,512]{2,1,0:T(8,128)S(1)}, f32[4,32,512]{2,1,0:T(8,128)S(1)}, u32[]{:S(2)}, u32[]{:S(2)}) collective-permute-start(f32[4,32,512]{2,1,0:T(8,128)S(1)} %get-tuple-element.38), channel_id=1, source_target_pairs={{0,1},{1,0},{2,3},{3,2},{4,5},{5,4},{6,7},{7,6},{8,9},{9,8},{10,11... | collective-permute-start | bytes 786440 | tf_op jit(solution)/shard_map/ppermute | solution.py:355
  29.5 14.3 %collective-permute-start.10 = (f32[4,32,512]{2,1,0:T(8,128)S(1)}, f32[4,32,512]{2,1,0:T(8,128)S(1)}, u32[]{:S(2)}, u32[]{:S(2)}) collective-permute-start(f32[4,32,512]{2,1,0:T(8,128)S(1)} %get-tuple-element.39), channel_id=1, source_target_pairs={{0,64},{1,2},{2,1},{3,4},{4,3},{5,6},{6,5},{7,8},{8,7},{9,10},{10,... | collective-permute-start | bytes 786440 | tf_op jit(solution)/shard_map/ppermute | solution.py:355
  35.8 12.8 %collective-permute-start.11 = (f32[4,8,512]{2,1,0:T(8,128)S(1)}, f32[4,8,512]{2,1,0:T(8,128)S(1)}, u32[]{:S(2)}, u32[]{:S(2)}) collective-permute-start(f32[4,8,512]{2,1,0:T(8,128)S(1)} %get-tuple-element.43), channel_id=1, source_target_pairs={{0,64},{1,65},{2,66},{3,67},{4,68},{5,69},{6,70},{7,71},{8,72},{9,... | collective-permute-start | bytes 196616 | tf_op jit(solution)/shard_map/ppermute | solution.py:355
  38.3 12.1 %collective-permute-start.12 = (f32[4,8,512]{2,1,0:T(8,128)S(1)}, f32[4,8,512]{2,1,0:T(8,128)S(1)}, u32[]{:S(2)}, u32[]{:S(2)}) collective-permute-start(f32[4,8,512]{2,1,0:T(8,128)S(1)} %get-tuple-element.44), channel_id=1, source_target_pairs={{0,128},{1,129},{2,130},{3,131},{4,132},{5,133},{6,134},{7,135},{8... | collective-permute-start | bytes 196616 | tf_op jit(solution)/shard_map/ppermute | solution.py:355
  39.9 10.5 %collective-permute-start.13 = (f32[4,8,512]{2,1,0:T(8,128)S(1)}, f32[4,8,512]{2,1,0:T(8,128)S(1)}, u32[]{:S(2)}, u32[]{:S(2)}) collective-permute-start(f32[4,8,512]{2,1,0:T(8,128)S(1)} %get-tuple-element.45), channel_id=1, source_target_pairs={{0,192},{1,193},{2,194},{3,195},{4,196},{5,197},{6,198},{7,199},{8... | collective-permute-start | bytes 196616 | tf_op jit(solution)/shard_map/ppermute | solution.py:355
  45.0 5.4 %collective-permute-start.14 = (f32[4,8,512]{2,1,0:T(8,128)S(1)}, f32[4,8,512]{2,1,0:T(8,128)S(1)}, u32[]{:S(2)}, u32[]{:S(2)}) collective-permute-start(f32[4,8,512]{2,1,0:T(8,128)S(1)} %get-tuple-element.47), channel_id=1, source_target_pairs={{0,64},{1,65},{2,66},{3,67},{4,68},{5,69},{6,70},{7,71},{8,72},{9,... | collective-permute-start | bytes 196616 | tf_op jit(solution)/shard_map/ppermute | solution.py:355
  45.1 6.8 %collective-permute-start.15 = (f32[4,8,512]{2,1,0:T(8,128)S(1)}, f32[4,8,512]{2,1,0:T(8,128)S(1)}, u32[]{:S(2)}, u32[]{:S(2)}) collective-permute-start(f32[4,8,512]{2,1,0:T(8,128)S(1)} %get-tuple-element.48), channel_id=1, source_target_pairs={{0,128},{1,129},{2,130},{3,131},{4,132},{5,133},{6,134},{7,135},{8... | collective-permute-start | bytes 196616 | tf_op jit(solution)/shard_map/ppermute | solution.py:355
  48.6 3.8 %collective-permute-start.16 = (f32[4,8,512]{2,1,0:T(8,128)S(1)}, f32[4,8,512]{2,1,0:T(8,128)S(1)}, u32[]{:S(2)}, u32[]{:S(2)}) collective-permute-start(f32[4,8,512]{2,1,0:T(8,128)S(1)} %get-tuple-element.49), channel_id=1, source_target_pairs={{0,192},{1,193},{2,194},{3,195},{4,196},{5,197},{6,198},{7,199},{8... | collective-permute-start | bytes 196616 | tf_op jit(solution)/shard_map/ppermute | solution.py:355

commit v8 on v5

--- a/solution.py
+++ b/solution.py
@@ -79,62 +79,54 @@
     return store
 
 
-def sides(depth):
+def side_of(partner):
     parity = lax.rem(lax.axis_index("space"), 2)
-    even = parity == 0
-    high = (jnp.where(even, depth - 1, 0), jnp.where(even, depth - 2, 1), jnp.where(even, -1.0, 1.0))
-    low = (jnp.where(even, 0, depth - 1), jnp.where(even, 1, depth - 2), jnp.where(even, 1.0, -1.0))
-    return parity, high, low
-
-
-def pack(edges, velocity, snap, message, layer, inner, sign):
-    shape = edges.shape[2:]
-    at = (layer // (edge_count - 1)) * (velocity.shape[2] - 1)
-    near, here, flow = layer_of(edges, inner), layer_of(edges, layer), flow_of(velocity, snap, at)
-
+    high = 1 - parity if partner == 0 else parity
+    return high, (2 * high - 1).astype(jnp.float32)
+
+
+def side_layer(outer, here, inner, flow, sign, shape, store, wanted=(0, 1)):
     def pairs(f, i, j):
-        value = near(f, i, j)
-        return value, sign * value
+        far, near = outer(f, i, j), inner(f, i, j)
+        return far + near, far - near
 
     for i, j in tiles(shape):
-        out = advanced(here, pairs, flow(i, j), i, j, shape)
+        u, v, w = flow(i, j)
+        store(i, j, advanced(here, pairs, (sign * u, v, w), i, j, shape, wanted))
+
+
+def pack(here, inner, flow, sign, message, shape):
+    def pairs(f, i, j):
+        value = inner(f, i, j)
+        return value, value
+
+    for i, j in tiles(shape):
+        u, v, w = flow(i, j)
+        out = advanced(here, pairs, (-sign * u, v, w), i, j, shape)
         for f in (0, 1):
             message[(f,) + spot(i, j)] = here(f, i, j)
             message[(2 + f,) + spot(i, j)] = out[f]
 
 
-def pack_both(edges, velocity, snap, message_one, message_two):
-    unused, one, two = sides(edge_count)
-    pack(edges, velocity, snap, message_one, *one)
-    pack(edges, velocity, snap, message_two, *two)
-
-
-def take_halos(blocks, state, halo_one, halo_two, own_flow, other_flow, snap, halos, after, depth):
-    shape = state.shape[2:]
-    parity, one, two = sides(depth)
+def take_halo(blocks, partner, halo, own, own_flow, other_flow, snap, now, after, shape):
+    high, sign = side_of(partner)
     place = lax.axis_index("space")
     inside = jnp.logical_and(place > 0, place < blocks - 1)
-    outer = after.shape[1] - 1
     fetched = lax.rem(lax.axis_index("tm"), 2)
-    for halo, (edge, unused, sign), shown, high in (
-        (halo_one, one, None, 1 - parity),
-        (halo_two, two, inside, parity),
-    ):
-        for i, j in tiles(shape):
-            u = jnp.where(high == fetched, own_flow[(snap,) + spot(i, j)], other_flow[(snap,) + spot(i, j)])
-            for f in (0, 1):
-                now = halo[(f,) + spot(i, j)]
-                own = state[(f, edge) + spot(i, j)]
-                later = halo[(2 + f,) + spot(i, j)] + (diffusion[f] + (0.25 * sign) * u) * own
-                if shown is not None:
-                    now = jnp.where(shown, now, 0.0)
-                    later = jnp.where(shown, later, 0.0)
-                halos[(high, f) + spot(i, j)] = now
-                after[(f, high * outer) + spot(i, j)] = later
-
-
-def halo_at(halos, h):
-    return lambda f, i, j: halos[(h, f) + spot(i, j)]
+    for i, j in tiles(shape):
+        u = jnp.where(high == fetched, own_flow[(snap,) + spot(i, j)], other_flow[(snap,) + spot(i, j)])
+        for f in (0, 1):
+            current = halo[(f,) + spot(i, j)]
+            later = halo[(2 + f,) + spot(i, j)] + (diffusion[f] - (0.25 * sign) * u) * own(f, i, j)
+            if partner == 1:
+                current = jnp.where(inside, current, 0.0)
+                later = jnp.where(inside, later, 0.0)
+            now[(f,) + spot(i, j)] = current
+            after[(f, 0) + spot(i, j)] = later
+
+
+def plain(ref):
+    return lambda f, i, j: ref[(f,) + spot(i, j)]
 
 
 def split_rows(total, pieces):
@@ -166,47 +158,46 @@
         copy.start()
     for copy in copies:
         copy.wait()
-    pack_both(edges, flows, scalars[0, 1], message_one, message_two)
+    for partner, message in enumerate((message_one, message_two)):
+        high, sign = side_of(partner)
+        here, inner = layer_of(edges, 3 * high), layer_of(edges, 1 + high)
+        pack(here, inner, flow_of(flows, scalars[0, 1], high), sign, message, edges.shape[2:])
     flow_out[...] = flows[:, 0, 1 - lax.rem(lax.axis_index("tm"), 2)]
 
 
-def first_kernel(blocks, slabs, snaps, snaps_next, state, halo_one, halo_two, own_flow, other_flow, velocity, start,
-                 widened, edges, message_one, message_two, halos):
+def first_kernel(blocks, slabs, partner, snaps, snaps_next, state, halo, own_flow, other_flow, velocity, start,
+                 widened, edges, message, now):
     depth, shape = state.shape[1], state.shape[2:]
     last = lax.axis_index("tm") == slabs - 1
+    high, sign = side_of(partner)
+
+    def at(k):
+        return high * (depth - 1) + k * (1 - 2 * high)
 
     @pl.when(last)
     def _():
-        pltpu.sync_copy(start.at[:, pl.ds(0, 2)], edges.at[:, pl.ds(0, 2)])
-        pltpu.sync_copy(start.at[:, pl.ds(depth - 2, 2)], edges.at[:, pl.ds(2, 2)])
+        pltpu.sync_copy(start.at[:, pl.ds(at(0), 1)], edges.at[:, pl.ds(0, 1)])
+        pltpu.sync_copy(start.at[:, pl.ds(at(1), 1)], edges.at[:, pl.ds(1, 1)])
 
     @pl.when(jnp.logical_not(last))
     def _():
-        take_halos(
-            blocks, state, halo_one, halo_two, own_flow, other_flow, snaps_next[0, 1], halos, widened, depth
-        )
-
-        def first_step(l, below, above):
-            flow = flow_of(velocity, snaps_next[0, 1], l)
-            full_layer(below, layer_of(state, l), above, flow, shape, into(widened, l + 1))
-
-        first_step(0, halo_at(halos, 0), layer_of(state, 1))
-        first_step(depth - 1, layer_of(state, depth - 2), halo_at(halos, 1))
-        each(1, depth - 1, lambda l: first_step(l, layer_of(state, l - 1), layer_of(state, l + 1)))
-
-        def second_step(e):
-            l = e + (e // 2) * (depth - edge_count)
-            flow = flow_of(velocity, snaps_next[0, 0], l)
-            here = layer_of(widened, l + 1)
-            full_layer(layer_of(widened, l), here, layer_of(widened, l + 2), flow, shape, into(edges, e))
-
-        each(0, edge_count, second_step)
-
-    pack_both(edges, velocity, snaps[0, 1], message_one, message_two)
-
-
-def inner_kernel(slabs, snaps, snaps_next, widened, edges, velocity, start, carried_on, inner, *rest):
-    pieces, (state, final, total, sem) = rest[:slabs], rest[slabs:]
+        snap = snaps_next[0, 1]
+        take_halo(blocks, partner, halo, layer_of(state, at(0)), own_flow, other_flow, snap, now, widened, shape)
+        for k in range(3):
+            outer = plain(now) if k == 0 else layer_of(state, at(k - 1))
+            here, inner, flow = layer_of(state, at(k)), layer_of(state, at(k + 1)), flow_of(velocity, snap, at(k))
+            side_layer(outer, here, inner, flow, sign, shape, into(widened, k + 1))
+        for k in range(2):
+            outer, here, inner = [layer_of(widened, k + n) for n in range(3)]
+            flow = flow_of(velocity, snaps_next[0, 0], at(k))
+            side_layer(outer, here, inner, flow, sign, shape, into(edges, k))
+
+    pack(layer_of(edges, 0), layer_of(edges, 1), flow_of(velocity, snaps[0, 1], at(0)), sign, message, shape)
+
+
+def inner_kernel(slabs, snaps, snaps_next, before, widened_one, widened_two, edges_one, edges_two, velocity, start,
+                 carried_on, inner, *rest):
+    pieces, (state, widened, final, total, sem) = rest[:slabs], rest[slabs:]
     depth, shape = state.shape[1], state.shape[2:]
     last = lax.axis_index("tm") == slabs - 1
 
@@ -216,14 +207,26 @@
 
     @pl.when(jnp.logical_not(last))
     def _():
+        for partner, wide, edges in ((0, widened_one, edges_one), (1, widened_two, edges_two)):
+            high, unused = side_of(partner)
+            for k in range(4):
+                widened[:, high * (depth + 1) + k * (1 - 2 * high)] = wide[:, k]
+            for k in range(2):
+                state[:, high * (depth - 1) + k * (1 - 2 * high)] = edges[:, k]
+
+        def first_step(l):
+            flow = flow_of(velocity, snaps_next[0, 1], l)
+            here = layer_of(before, l)
+            full_layer(layer_of(before, l - 1), here, layer_of(before, l + 1), flow, shape, into(widened, l + 1))
+
+        each(3, depth - 3, first_step)
+
         def second_step(l):
             flow = flow_of(velocity, snaps_next[0, 0], l)
             here = layer_of(widened, l + 1)
             full_layer(layer_of(widened, l), here, layer_of(widened, l + 2), flow, shape, into(state, l))
 
         each(2, depth - 2, second_step)
-        state[:, 0:2] = edges[:, 0:2]
-        state[:, depth - 2 : depth] = edges[:, 2:4]
 
     def third_step(l):
         flow = flow_of(velocity, snaps[0, 1], l)
@@ -248,42 +251,53 @@
     copy.wait()
 
 
-def last_steps(snaps, carried_on, outer, velocity, store, wanted):
+def last_steps(partner, snaps, carried_on, outer, velocity, store, wanted):
     depth, shape = carried_on.shape[1], carried_on.shape[2:]
-    ring = [layer_of(outer, 0), layer_of(outer, 1), layer_of(carried_on, 1), layer_of(carried_on, 2)]
-    ring += [layer_of(carried_on, depth - 3), layer_of(carried_on, depth - 2), layer_of(outer, 2), layer_of(outer, 3)]
-    for e, at in enumerate((1, 2, 5, 6)):
-        l = e + (e // 2) * (depth - edge_count)
-        flow = flow_of(velocity, snaps[0, 0], l)
-        full_layer(ring[at - 1], ring[at], ring[at + 1], flow, shape, functools.partial(store, e, ring[at]), wanted)
-
-
-def outer_kernel(blocks, slabs, snaps, edges, halo_one, halo_two, own_flow, other_flow, carried_on, velocity,
-                 outer, *rest):
-    pieces, (halos, total) = rest[:slabs], rest[slabs:]
+    high, sign = side_of(partner)
+
+    def at(k):
+        return high * (depth - 1) + k * (1 - 2 * high)
+
+    ring = [layer_of(outer, 0), layer_of(outer, 1), layer_of(carried_on, at(1)), layer_of(carried_on, at(2))]
+    for k in range(2):
+        flow = flow_of(velocity, snaps[0, 0], at(k))
+        keep = functools.partial(store, k, ring[k + 1])
+        side_layer(ring[k], ring[k + 1], ring[k + 2], flow, sign, shape, keep, wanted)
+
+
+def outer_kernel(blocks, slabs, partner, snaps, edges, halo, own_flow, other_flow, carried_on, velocity, *rest):
+    before, rest = rest[:partner], rest[partner:]
+    if partner == 0:
+        outer, total, now = rest
+    else:
+        outer, pieces, (now, total, whole) = rest[0], rest[1 : slabs + 1], rest[slabs + 1 :]
     depth, shape = carried_on.shape[1], carried_on.shape[2:]
-    take_halos(
-        blocks, edges, halo_one, halo_two, own_flow, other_flow, snaps[0, 1], halos, outer, edge_count
-    )
-    flow = flow_of(velocity, snaps[0, 1], 0)
-    full_layer(halo_at(halos, 0), layer_of(edges, 0), layer_of(edges, 1), flow, shape, into(outer, 1))
-    flow = flow_of(velocity, snaps[0, 1], depth - 1)
-    full_layer(layer_of(edges, 2), layer_of(edges, 3), halo_at(halos, 1), flow, shape, into(outer, 2))
-
-    def store(e, here, i, j, values):
-        total[(e,) + spot(i, j)] = here(0, i, j) + values[0]
-
-    last_steps(snaps, carried_on, outer, velocity, store, (0,))
-    split_rows(total, pieces)
-
-
-def finish_kernel(snaps, carried_on, outer, velocity, inner, out, final, sems):
+    high, sign = side_of(partner)
+    snap = snaps[0, 1]
+    take_halo(blocks, partner, halo, layer_of(edges, 0), own_flow, other_flow, snap, now, outer, shape)
+    flow = flow_of(velocity, snap, high * (depth - 1))
+    side_layer(plain(now), layer_of(edges, 0), layer_of(edges, 1), flow, sign, shape, into(outer, 1))
+
+    def store(k, here, i, j, values):
+        total[(k,) + spot(i, j)] = here(0, i, j) + values[0]
+
+    last_steps(partner, snaps, carried_on, outer, velocity, store, (0,))
+    if partner == 1:
+        for k in range(2):
+            whole[high * (edge_count - 1) + k * (1 - 2 * high)] = total[k]
+            whole[(1 - high) * (edge_count - 1) - k * (1 - 2 * high)] = before[0][k]
+        split_rows(whole, pieces)
+
+
+def finish_kernel(snaps, carried_on, outer_one, outer_two, velocity, inner, out, final, sems):
     depth = carried_on.shape[1]
-
-    def store(e, here, i, j, values):
-        into(final, e)(i, j, values)
-
-    last_steps(snaps, carried_on, outer, velocity, store, (0, 1))
+    for partner, outer in enumerate((outer_one, outer_two)):
+        high, unused = side_of(partner)
+
+        def store(k, here, i, j, values, high=high):
+            into(final, high * (edge_count - 1) + k * (1 - 2 * high))(i, j, values)
+
+        last_steps(partner, snaps, carried_on, outer, velocity, store, (0, 1))
     copies = [
         pltpu.make_async_copy(final.at[:, pl.ds(0, 2)], out.at[:, pl.ds(0, 2)], sems.at[0]),
         pltpu.make_async_copy(final.at[:, pl.ds(2, 2)], out.at[:, pl.ds(depth - 2, 2)], sems.at[1]),
@@ -368,51 +382,63 @@
         halo_two = exchanged(message_two, 1, 1)
         own_flow = moved(flow_out, fetched)
         other_flow = moved(own_flow, lambda t, s: (t ^ 1, s))
-        widened, edges, message_one, message_two = pl.pallas_call(
-            functools.partial(first_kernel, blocks, slabs),
-            out_shape=(shaped(fields, depth + 2), shaped(fields, edge_count), layer, layer),
-            in_specs=[smem, smem] + [vmem] * 6 + [hbm],
-            out_specs=(vmem,) * 4,
-            scratch_shapes=[room(2, fields)],
-            compiler_params=params(32),
-            cost_estimate=cost(2.5),
-        )(snap_of_step, snaps_next, state, halo_one, halo_two, own_flow, other_flow, velocity, start)
-        halo_one = exchanged(message_one, 0, 0)
-        halo_two = exchanged(message_two, 1, 0)
+        widened, edges, halo = [None] * 2, [None] * 2, [halo_one, halo_two]
+        for partner in (0, 1):
+            widened[partner], edges[partner], message = pl.pallas_call(
+                functools.partial(first_kernel, blocks, slabs, partner),
+                out_shape=(shaped(fields, 4), shaped(fields, 2), layer),
+                in_specs=[smem, smem] + [vmem] * 5 + [hbm],
+                out_specs=(vmem,) * 3,
+                scratch_shapes=[room(fields)],
+                compiler_params=params(32),
+                cost_estimate=cost(1.5),
+            )(snap_of_step, snaps_next, state, halo[partner], own_flow, other_flow, velocity, start)
+            halo[partner] = exchanged(message, partner, 0)
         carried_on, inner, *inner_pieces = pl.pallas_call(
             functools.partial(inner_kernel, slabs),
             out_shape=(shaped(fields, depth), shaped(fields, depth)) + pieces,
-            in_specs=[smem, smem, vmem, vmem, vmem, hbm],
+            in_specs=[smem, smem] + [vmem] * 6 + [hbm],
             out_specs=(vmem, hbm) + (vmem,) * slabs,
-            scratch_shapes=[room(fields, depth), room(fields, depth - 4), room(depth - 4), sem(())],
+            scratch_shapes=[
+                room(fields, depth), room(fields, depth + 2), room(fields, depth - 4), room(depth - 4), sem(()),
+            ],
             compiler_params=params(32),
             cost_estimate=cost(3),
-        )(snap_of_step, snaps_next, widened, edges, velocity, start)
+        )(snap_of_step, snaps_next, state, *widened, *edges, velocity, start)
         inner_parts = inner_pieces[:1] + [
             moved(inner_pieces[by], lambda t, s, by=by: (t + by, s)) for by in range(1, slabs)
         ]
-        outer, *outer_pieces = pl.pallas_call(
-            functools.partial(outer_kernel, blocks, slabs),
-            out_shape=(shaped(fields, edge_count),) + pieces,
+        outer_one, total_one = pl.pallas_call(
+            functools.partial(outer_kernel, blocks, slabs, 0),
+            out_shape=(shaped(fields, 2), shaped(2)),
+            in_specs=[smem] + [vmem] * 6,
+            out_specs=(vmem,) * 2,
+            scratch_shapes=[room(fields)],
+            compiler_params=params(32),
+            cost_estimate=cost(0.5),
+        )(snap_of_step, edges[0], halo[0], own_flow, other_flow, carried_on, velocity)
+        outer_two, *outer_pieces = pl.pallas_call(
+            functools.partial(outer_kernel, blocks, slabs, 1),
+            out_shape=(shaped(fields, 2),) + pieces,
             in_specs=[smem] + [vmem] * 7,
             out_specs=(vmem,) * (1 + slabs),
-            scratch_shapes=[room(2, fields), room(edge_count)],
+            scratch_shapes=[room(fields), room(2), room(edge_count)],
             compiler_params=params(32),
-            cost_estimate=cost(1),
-        )(snap_of_step, edges, halo_one, halo_two, own_flow, other_flow, carried_on, velocity)
+            cost_estimate=cost(0.5),
+        )(snap_of_step, edges[1], halo[1], own_flow, other_flow, carried_on, velocity, total_one)
         outer_parts = outer_pieces[:1] + [
             moved(outer_pieces[by], lambda t, s, by=by: (t + by, s)) for by in range(1, slabs)
         ]
         final = pl.pallas_call(
             finish_kernel,
             out_shape=shaped(fields, depth),
-            in_specs=[smem, vmem, vmem, vmem, hbm],
+            in_specs=[smem, vmem, vmem, vmem, vmem, hbm],
             out_specs=hbm,
             scratch_shapes=[room(fields, edge_count), sem((2,))],
-            input_output_aliases={4: 0},
+            input_output_aliases={5: 0},
             compiler_params=params(32),
             cost_estimate=cost(1),
-        )(snap_of_step, carried_on, outer, velocity, inner)
+        )(snap_of_step, carried_on, outer_one, outer_two, velocity, inner)
         gradient = pl.pallas_call(
             sum_kernel,
             out_shape=shaped(depth, rows=ny // slabs),

time: 49.3 us -> 49 us (level)
  waiting for transfers between devices: 13.3 us -> 11.5 us
  Pallas kernels: 12.1 us -> 13 us
    ppermute x14, waiting for transfers between devices: 13.3 us -> 11.5 us  [moved(): return lax.ppermute(array, ('tm', 'space'), pairs)]
    pallas_call x2 -> x4, Pallas kernels: 3.8 us -> 4.31 us  [the longest x2 2.58 us: body(): pl.pallas_call(functools.partial(first_kernel, blocks, slabs, partner), o...]
  transfers between devices with their start and end apart: 14 -> 14, of which waited for: 5 -> 5; matrix products, arithmetic and copies ran while one was open for 0% -> 0% of each run, Pallas kernels for 18% -> 25%
where the time goes in v8:
time: 49 us; the launch traced here: 48.4 us
  starting transfers between devices  23.1 us (47%)
  Pallas kernels  13 us (27%)
  waiting for transfers between devices  11.5 us (23%)
  between operations  0.77 us (2%)
    ppermute x14, starting transfers between devices, moved(): return lax.ppermute(array, ('tm', 'space'), pairs)  23.1 us
    ppermute x14, waiting for transfers between devices, moved(): return lax.ppermute(array, ('tm', 'space'), pairs)  11.5 us
    pallas_call x1, Pallas kernels, body(): pl.pallas_call(functools.partial(inner_kernel, slabs), out_shape=(shaped(...  3.86 us
    pallas_call x2, Pallas kernels, body(): pl.pallas_call(functools.partial(first_kernel, blocks, slabs, partner), o...  2.58 us
    pallas_call x1, Pallas kernels, body(): pl.pallas_call(start_kernel, out_shape=(layer, layer, shaped(velocity.sha...  2.3 us
    pallas_call x1, Pallas kernels, body(): pl.pallas_call(finish_kernel, out_shape=shaped(fields, depth), in_specs=[...  1.83 us
  transfers between devices with their start and end apart: 14, of which 5 were waited for; matrix products, arithmetic and copies ran while one was open for 0% of the time, Pallas kernels for 25%

profile of v8, /device:TPU:1, one launch (start us, length us, event | category | flops | bytes accessed | tf_op | source)
XLA Modules:
  0.0 48.4 jit_solution(4499093940869677156)
XLA Ops:
  0.7 3.3 %collective-permute-start.1 = (f32[2,8,32,512]{3,2,1,0:T(8,128)}, f32[2,8,32,512]{3,2,1,0:T(8,128)S(1)}, u32[]{:S(2)}, u32[]{:S(2)}) collective-permute-start(f32[2,8,32,512]{3,2,1,0:T(8,128)} %bitcast.2), channel_id=1, source_target_pairs={{0,192},{1,193},{2,194},{3,195},{4,196},{5,197},{6,198},{7,199},{8... | collective-permute-start | bytes 3145736 | tf_op jit(solution)/shard_map/ppermute | solution.py:339
  4.0 2.3 %shard_map.50 = (f32[4,32,512]{2,1,0:T(8,128)}, f32[4,32,512]{2,1,0:T(8,128)}, f32[2,32,512]{2,1,0:T(8,128)}) custom-call(s32[1,2]{1,0:T(1,128)} %snaps.13, f32[2,8,32,512]{3,2,1,0:T(8,128)} %bitcast.3, f32[2,3,8,32,512]{4,3,2,1,0:T(8,128)} %velocity.13), custom_call_target="tpu_custom_call" | custom-call | bytes 7200000 | tf_op jit(solution)/shard_map/pallas_call | solution.py:367
  6.3 0.2 collective-permute-start.3
  6.5 2.4 %collective-permute-start.2 = (f32[4,32,512]{2,1,0:T(8,128)}, f32[4,32,512]{2,1,0:T(8,128)S(1)}, u32[]{:S(2)}, u32[]{:S(2)}) collective-permute-start(f32[4,32,512]{2,1,0:T(8,128)} %get-tuple-element.24), channel_id=1, source_target_pairs={{0,193},{1,192},{2,195},{3,194},{4,197},{5,196},{6,199},{7,198},{8... | collective-permute-start | bytes 786440 | tf_op jit(solution)/shard_map/ppermute | solution.py:339
  9.0 0.5 collective-permute-start.5
  9.4 3.2 %collective-permute-done.3.own_flow = f32[2,32,512]{2,1,0:T(8,128)S(1)} collective-permute-done((f32[2,32,512]{2,1,0:T(8,128)}, f32[2,32,512]{2,1,0:T(8,128)S(1)}, u32[]{:S(2)}, u32[]{:S(2)}) %collective-permute-start.3) | collective-permute-done | bytes 131104 | tf_op jit(solution)/shard_map/ppermute | solution.py:339
  12.7 8.0 %collective-permute-start.4 = (f32[2,32,512]{2,1,0:T(8,128)S(1)}, f32[2,32,512]{2,1,0:T(8,128)S(1)}, u32[]{:S(2)}, u32[]{:S(2)}) collective-permute-start(f32[2,32,512]{2,1,0:T(8,128)S(1)} %collective-permute-done.3.own_flow), channel_id=1, source_target_pairs={{0,64},{1,65},{2,66},{3,67},{4,68},{5,69},{6,70},{7,71},{8,72},{9,... | collective-permute-start | bytes 393224 | tf_op jit(solution)/shard_map/ppermute | solution.py:339
  20.7 3.0 %collective-permute-done.snaps_next = s32[1,2]{1,0:T(1,128)S(1)} collective-permute-done((s32[1,2]{1,0:T(1,128)S(1)}, s32[1,2]{1,0:T(1,128)S(1)}, u32[]{:S(2)}, u32[]{:S(2)}) %collective-permute-start) | collective-permute-done | bytes 40 | tf_op jit(solution)/shard_map/ppermute | solution.py:339
  23.6 1.3 %shard_map.51 = (f32[2,4,32,512]{3,2,1,0:T(8,128)S(1)}, f32[2,2,32,512]{3,2,1,0:T(8,128)S(1)}, f32[4,32,512]{2,1,0:T(8,128)S(1)}) custom-call(s32[1,2]{1,0:T(1,128)S(1)} %copy-done.2, s32[1,2]{1,0:T(1,128)S(1)} %collective-permute-done.snaps_next, f32[2,8,32,512]{3,2,1,0:T(8,128)S(1)} %collective-permute-done.1.state.before, ...), custom_call_target="tpu_custom_call" | custom-call | bytes 5400000 | tf_op jit(solution)/shard_map/pallas_call | solution.py:387
  24.9 2.8 %collective-permute-start.6 = (f32[4,32,512]{2,1,0:T(8,128)S(1)}, f32[4,32,512]{2,1,0:T(8,128)S(1)}, u32[]{:S(2)}, u32[]{:S(2)}) collective-permute-start(f32[4,32,512]{2,1,0:T(8,128)S(1)} %get-tuple-element.32), channel_id=1, source_target_pairs={{0,1},{1,0},{2,3},{3,2},{4,5},{5,4},{6,7},{7,6},{8,9},{9,8},{10,11... | collective-permute-start | bytes 786440 | tf_op jit(solution)/shard_map/ppermute | solution.py:339
  27.8 1.3 %shard_map.52 = (f32[2,4,32,512]{3,2,1,0:T(8,128)S(1)}, f32[2,2,32,512]{3,2,1,0:T(8,128)S(1)}, f32[4,32,512]{2,1,0:T(8,128)S(1)}) custom-call(s32[1,2]{1,0:T(1,128)S(1)} %copy-done.2, s32[1,2]{1,0:T(1,128)S(1)} %collective-permute-done.snaps_next, f32[2,8,32,512]{3,2,1,0:T(8,128)S(1)} %collective-permute-done.1.state.before, ...), custom_call_target="tpu_custom_call" | custom-call | bytes 5400000 | tf_op jit(solution)/shard_map/pallas_call | solution.py:387
  29.1 0.8 %collective-permute-start.7 = (f32[4,32,512]{2,1,0:T(8,128)S(1)}, f32[4,32,512]{2,1,0:T(8,128)S(1)}, u32[]{:S(2)}, u32[]{:S(2)}) collective-permute-start(f32[4,32,512]{2,1,0:T(8,128)S(1)} %get-tuple-element.34), channel_id=1, source_target_pairs={{0,64},{1,2},{2,1},{3,4},{4,3},{5,6},{6,5},{7,8},{8,7},{9,10},{10,... | collective-permute-start | bytes 786440 | tf_op jit(solution)/shard_map/ppermute | solution.py:339
  29.9 3.9 %shard_map.53 = (f32[2,8,32,512]{3,2,1,0:T(8,128)S(1)}, f32[2,8,32,512]{3,2,1,0:T(8,128)}, f32[4,8,512]{2,1,0:T(8,128)S(1)}, f32[4,8,512]{2,1,0:T(8,128)S(1)}, f...) custom-call(s32[1,2]{1,0:T(1,128)S(1)} %copy-done.2, s32[1,2]{1,0:T(1,128)S(1)} %collective-permute-done.snaps_next, ...), custom_call_target="tpu_custom_call" | custom-call | bytes 10800000 | tf_op jit(solution)/shard_map/pallas_call | solution.py:397
  33.8 0.1 collective-permute-start.8
  33.8 1.4 %collective-permute-start.9 = (f32[4,8,512]{2,1,0:T(8,128)S(1)}, f32[4,8,512]{2,1,0:T(8,128)S(1)}, u32[]{:S(2)}, u32[]{:S(2)}) collective-permute-start(f32[4,8,512]{2,1,0:T(8,128)S(1)} %get-tuple-element.40), channel_id=1, source_target_pairs={{0,128},{1,129},{2,130},{3,131},{4,132},{5,133},{6,134},{7,135},{8... | collective-permute-start | bytes 196616 | tf_op jit(solution)/shard_map/ppermute | solution.py:339
  35.2 3.4 %collective-permute-done.6.halo = f32[4,32,512]{2,1,0:T(8,128)S(1)} collective-permute-done((f32[4,32,512]{2,1,0:T(8,128)S(1)}, f32[4,32,512]{2,1,0:T(8,128)S(1)}, u32[]{:S(2)}, u32[]{:S(2)}) %collective-permute-start.6) | collective-permute-done | bytes 262176 | tf_op jit(solution)/shard_map/ppermute | solution.py:339
  38.6 0.9 %shard_map.54 = (f32[2,2,32,512]{3,2,1,0:T(8,128)S(1)}, f32[2,32,512]{2,1,0:T(8,128)S(1)}) custom-call(s32[1,2]{1,0:T(1,128)S(1)} %copy-done.2, f32[2,2,32,512]{3,2,1,0:T(8,128)S(1)} %get-tuple-element.29.edges_one.edges, f32[4,32,512]{2,1,0:T(8,128)S(1)} %collective-permute-done.6.halo, f32[2,32,512]{2,1,0:T(8,128)S(1)} %collective-permute-done.3.own_flow, ...), custom_call_target="tpu_custom_call" | custom-call | bytes 1800000 | tf_op jit(solution)/shard_map/pallas_call | solution.py:411
  39.5 0.9 %shard_map.55 = (f32[2,2,32,512]{3,2,1,0:T(8,128)S(1)}, f32[4,8,512]{2,1,0:T(8,128)S(1)}, f32[4,8,512]{2,1,0:T(8,128)S(1)}, f32[4,8,512]{2,1,0:T(8,128)S(1)}, f32[4,8,512]{2,1,0:T(8,128)S(1)}) custom-call(s32[1,2]{1,0:T(1,128)S(1)} %copy-done.2, f32[2,2,32,512]{3,2,1,0:T(8,128)S(1)} %get-tuple-element.30.edges_two.edges, ...), custom_call_target="tpu_custom_call" | custom-call | bytes 1800000 | tf_op jit(solution)/shard_map/pallas_call | solution.py:420
  40.4 0.7 %collective-permute-start.11 = (f32[4,8,512]{2,1,0:T(8,128)S(1)}, f32[4,8,512]{2,1,0:T(8,128)S(1)}, u32[]{:S(2)}, u32[]{:S(2)}) collective-permute-start(f32[4,8,512]{2,1,0:T(8,128)S(1)} %get-tuple-element.43), channel_id=1, source_target_pairs={{0,64},{1,65},{2,66},{3,67},{4,68},{5,69},{6,70},{7,71},{8,72},{9,... | collective-permute-start | bytes 196616 | tf_op jit(solution)/shard_map/ppermute | solution.py:339
  41.1 2.9 %collective-permute-start.12 = (f32[4,8,512]{2,1,0:T(8,128)S(1)}, f32[4,8,512]{2,1,0:T(8,128)S(1)}, u32[]{:S(2)}, u32[]{:S(2)}) collective-permute-start(f32[4,8,512]{2,1,0:T(8,128)S(1)} %get-tuple-element.44), channel_id=1, source_target_pairs={{0,128},{1,129},{2,130},{3,131},{4,132},{5,133},{6,134},{7,135},{8... | collective-permute-start | bytes 196616 | tf_op jit(solution)/shard_map/ppermute | solution.py:339
  44.0 1.8 %shard_map.56 = f32[2,8,32,512]{3,2,1,0:T(8,128)} custom-call(s32[1,2]{1,0:T(1,128)S(1)} %copy-done.2, f32[2,8,32,512]{3,2,1,0:T(8,128)S(1)} %get-tuple-element.31.carried_on, f32[2,2,32,512]{3,2,1,0:T(8,128)S(1)} %get-tuple-element.33.outer_one, f32[2,2,32,512]{3,2,1,0:T(8,128)S(1)} %get-tuple-element.36.outer_two, ...), custom_call_target="tpu_custom_call", output_to_operand_aliasing={{}: (5, {})} | custom-call | bytes 3600000 | tf_op jit(solution)/shard_map/pallas_call | solution.py:432
  45.8 1.4 %collective-permute-done.12.refs_6_ = f32[4,8,512]{2,1,0:T(8,128)S(1)} collective-permute-done((f32[4,8,512]{2,1,0:T(8,128)S(1)}, f32[4,8,512]{2,1,0:T(8,128)S(1)}, u32[]{:S(2)}, u32[]{:S(2)}) %collective-permute-start.12) | collective-permute-done | bytes 65568 | tf_op jit(solution)/shard_map/ppermute | solution.py:339
  47.2 0.5 collective-permute-done.13.refs_7_
  47.7 0.7 %shard_map.57 = f32[8,8,512]{2,1,0:T(8,128)} custom-call(f32[4,8,512]{2,1,0:T(8,128)S(1)} %get-tuple-element.38.refs_0_, f32[4,8,512]{2,1,0:T(8,128)S(1)} %collective-permute-done.8.refs_1_, f32[4,8,512]{2,1,0:T(8,128)S(1)} %collective-permute-done.9.refs_2_, f32[4,8,512]{2,1,0:T(8,128)S(1)} %collective-permute-done.10.refs_3_, ...), custom_call_target="tpu_custom_call" | custom-call | bytes 1800000 | tf_op jit(solution)/shard_map/pallas_call | solution.py:442
  (18 shorter events, 0.0 us)
Async XLA Ops:
  0.6 23.0 %copy-start.1 = (f32[1,2,8,32,512]{4,3,2,1,0:T(8,128)S(1)}, f32[1,2,8,32,512]{4,3,2,1,0:T(8,128)}, u32[]{:S(2)}) copy-start(f32[1,2,8,32,512]{4,3,2,1,0:T(8,128)} %param.3) | copy-start | bytes 3145732
  0.6 20.0 %copy-start.2 = (s32[1,2]{1,0:T(1,128)S(1)}, s32[1,2]{1,0:T(1,128)}, u32[]{:S(2)}) copy-start(s32[1,2]{1,0:T(1,128)} %snaps.13) | copy-start | bytes 28
  0.6 23.0 %copy-start = (f32[2,3,8,32,512]{4,3,2,1,0:T(8,128)S(1)}, f32[2,3,8,32,512]{4,3,2,1,0:T(8,128)}, u32[]{:S(2)}) copy-start(f32[2,3,8,32,512]{4,3,2,1,0:T(8,128)} %velocity.13) | copy-start | bytes 9437188
  0.7 23.0 %collective-permute-start.1 = (f32[2,8,32,512]{3,2,1,0:T(8,128)}, f32[2,8,32,512]{3,2,1,0:T(8,128)S(1)}, u32[]{:S(2)}, u32[]{:S(2)}) collective-permute-start(f32[2,8,32,512]{3,2,1,0:T(8,128)} %bitcast.2), channel_id=1, source_target_pairs={{0,192},{1,193},{2,194},{3,195},{4,196},{5,197},{6,198},{7,199},{8... | collective-permute-start | bytes 3145736 | tf_op jit(solution)/shard_map/ppermute | solution.py:339
  6.3 6.4 %collective-permute-start.3 = (f32[2,32,512]{2,1,0:T(8,128)}, f32[2,32,512]{2,1,0:T(8,128)S(1)}, u32[]{:S(2)}, u32[]{:S(2)}) collective-permute-start(f32[2,32,512]{2,1,0:T(8,128)} %get-tuple-element.25), channel_id=1, source_target_pairs={{0,129},{1,130},{2,131},{3,132},{4,133},{5,134},{6,135},{7,136},{8... | collective-permute-start | bytes 393224 | tf_op jit(solution)/shard_map/ppermute | solution.py:339
  6.5 17.1 %collective-permute-start.2 = (f32[4,32,512]{2,1,0:T(8,128)}, f32[4,32,512]{2,1,0:T(8,128)S(1)}, u32[]{:S(2)}, u32[]{:S(2)}) collective-permute-start(f32[4,32,512]{2,1,0:T(8,128)} %get-tuple-element.24), channel_id=1, source_target_pairs={{0,193},{1,192},{2,195},{3,194},{4,197},{5,196},{6,199},{7,198},{8... | collective-permute-start | bytes 786440 | tf_op jit(solution)/shard_map/ppermute | solution.py:339
  9.0 18.8 %collective-permute-start.5 = (f32[4,32,512]{2,1,0:T(8,128)}, f32[4,32,512]{2,1,0:T(8,128)S(1)}, u32[]{:S(2)}, u32[]{:S(2)}) collective-permute-start(f32[4,32,512]{2,1,0:T(8,128)} %get-tuple-element.27), channel_id=1, source_target_pairs={{0,64},{1,194},{2,193},{3,196},{4,195},{5,198},{6,197},{7,200},{8,... | collective-permute-start | bytes 786440 | tf_op jit(solution)/shard_map/ppermute | solution.py:339
  12.7 11.0 %collective-permute-start.4 = (f32[2,32,512]{2,1,0:T(8,128)S(1)}, f32[2,32,512]{2,1,0:T(8,128)S(1)}, u32[]{:S(2)}, u32[]{:S(2)}) collective-permute-start(f32[2,32,512]{2,1,0:T(8,128)S(1)} %collective-permute-done.3.own_flow), channel_id=1, source_target_pairs={{0,64},{1,65},{2,66},{3,67},{4,68},{5,69},{6,70},{7,71},{8,72},{9,... | collective-permute-start | bytes 393224 | tf_op jit(solution)/shard_map/ppermute | solution.py:339
  20.6 3.0 %collective-permute-start = (s32[1,2]{1,0:T(1,128)S(1)}, s32[1,2]{1,0:T(1,128)S(1)}, u32[]{:S(2)}, u32[]{:S(2)}) collective-permute-start(s32[1,2]{1,0:T(1,128)S(1)} %copy-done.2), channel_id=1, source_target_pairs={{0,192},{1,193},{2,194},{3,195},{4,196},{5,197},{6,198},{7,199},{8... | collective-permute-start | bytes 32 | tf_op jit(solution)/shard_map/ppermute | solution.py:339
  24.9 13.7 %collective-permute-start.6 = (f32[4,32,512]{2,1,0:T(8,128)S(1)}, f32[4,32,512]{2,1,0:T(8,128)S(1)}, u32[]{:S(2)}, u32[]{:S(2)}) collective-permute-start(f32[4,32,512]{2,1,0:T(8,128)S(1)} %get-tuple-element.32), channel_id=1, source_target_pairs={{0,1},{1,0},{2,3},{3,2},{4,5},{5,4},{6,7},{7,6},{8,9},{9,8},{10,11... | collective-permute-start | bytes 786440 | tf_op jit(solution)/shard_map/ppermute | solution.py:339
  29.1 10.4 %collective-permute-start.7 = (f32[4,32,512]{2,1,0:T(8,128)S(1)}, f32[4,32,512]{2,1,0:T(8,128)S(1)}, u32[]{:S(2)}, u32[]{:S(2)}) collective-permute-start(f32[4,32,512]{2,1,0:T(8,128)S(1)} %get-tuple-element.34), channel_id=1, source_target_pairs={{0,64},{1,2},{2,1},{3,4},{4,3},{5,6},{6,5},{7,8},{8,7},{9,10},{10,... | collective-permute-start | bytes 786440 | tf_op jit(solution)/shard_map/ppermute | solution.py:339
  33.8 10.2 %collective-permute-start.8 = (f32[4,8,512]{2,1,0:T(8,128)S(1)}, f32[4,8,512]{2,1,0:T(8,128)S(1)}, u32[]{:S(2)}, u32[]{:S(2)}) collective-permute-start(f32[4,8,512]{2,1,0:T(8,128)S(1)} %get-tuple-element.39), channel_id=1, source_target_pairs={{0,64},{1,65},{2,66},{3,67},{4,68},{5,69},{6,70},{7,71},{8,72},{9,... | collective-permute-start | bytes 196616 | tf_op jit(solution)/shard_map/ppermute | solution.py:339
  33.8 12.0 %collective-permute-start.9 = (f32[4,8,512]{2,1,0:T(8,128)S(1)}, f32[4,8,512]{2,1,0:T(8,128)S(1)}, u32[]{:S(2)}, u32[]{:S(2)}) collective-permute-start(f32[4,8,512]{2,1,0:T(8,128)S(1)} %get-tuple-element.40), channel_id=1, source_target_pairs={{0,128},{1,129},{2,130},{3,131},{4,132},{5,133},{6,134},{7,135},{8... | collective-permute-start | bytes 196616 | tf_op jit(solution)/shard_map/ppermute | solution.py:339
  35.2 10.6 %collective-permute-start.10 = (f32[4,8,512]{2,1,0:T(8,128)S(1)}, f32[4,8,512]{2,1,0:T(8,128)S(1)}, u32[]{:S(2)}, u32[]{:S(2)}) collective-permute-start(f32[4,8,512]{2,1,0:T(8,128)S(1)} %get-tuple-element.41), channel_id=1, source_target_pairs={{0,192},{1,193},{2,194},{3,195},{4,196},{5,197},{6,198},{7,199},{8... | collective-permute-start | bytes 196616 | tf_op jit(solution)/shard_map/ppermute | solution.py:339
  40.4 5.4 %collective-permute-start.11 = (f32[4,8,512]{2,1,0:T(8,128)S(1)}, f32[4,8,512]{2,1,0:T(8,128)S(1)}, u32[]{:S(2)}, u32[]{:S(2)}) collective-permute-start(f32[4,8,512]{2,1,0:T(8,128)S(1)} %get-tuple-element.43), channel_id=1, source_target_pairs={{0,64},{1,65},{2,66},{3,67},{4,68},{5,69},{6,70},{7,71},{8,72},{9,... | collective-permute-start | bytes 196616 | tf_op jit(solution)/shard_map/ppermute | solution.py:339
  41.1 6.2 %collective-permute-start.12 = (f32[4,8,512]{2,1,0:T(8,128)S(1)}, f32[4,8,512]{2,1,0:T(8,128)S(1)}, u32[]{:S(2)}, u32[]{:S(2)}) collective-permute-start(f32[4,8,512]{2,1,0:T(8,128)S(1)} %get-tuple-element.44), channel_id=1, source_target_pairs={{0,128},{1,129},{2,130},{3,131},{4,132},{5,133},{6,134},{7,135},{8... | collective-permute-start | bytes 196616 | tf_op jit(solution)/shard_map/ppermute | solution.py:339
  44.0 3.8 %collective-permute-start.13 = (f32[4,8,512]{2,1,0:T(8,128)S(1)}, f32[4,8,512]{2,1,0:T(8,128)S(1)}, u32[]{:S(2)}, u32[]{:S(2)}) collective-permute-start(f32[4,8,512]{2,1,0:T(8,128)S(1)} %get-tuple-element.45), channel_id=1, source_target_pairs={{0,192},{1,193},{2,194},{3,195},{4,196},{5,197},{6,198},{7,199},{8... | collective-permute-start | bytes 196616 | tf_op jit(solution)/shard_map/ppermute | solution.py:339

commit v9 on v8

--- a/solution.py
+++ b/solution.py
@@ -132,7 +132,7 @@
 def split_rows(total, pieces):
     rows = total.shape[1] // len(pieces)
     for by, piece in enumerate(pieces):
-        start = pl.multiple_of(lax.rem(lax.axis_index("tm") + by, len(pieces)) * rows, rows)
+        start = pl.multiple_of(lax.bitwise_xor(lax.axis_index("tm"), by) * rows, rows)
         piece[...] = total[:, pl.ds(start, rows), :] * 0.5
 
 
@@ -196,8 +196,7 @@
 
 
 def inner_kernel(slabs, snaps, snaps_next, before, widened_one, widened_two, edges_one, edges_two, velocity, start,
-                 carried_on, inner, *rest):
-    pieces, (state, widened, final, total, sem) = rest[:slabs], rest[slabs:]
+                 carried_on, inner, kept, to_core, state, widened, final, total, sem):
     depth, shape = state.shape[1], state.shape[2:]
     last = lax.axis_index("tm") == slabs - 1
 
@@ -247,8 +246,13 @@
     each(2, depth - 2, fourth_step)
     copy = pltpu.make_async_copy(final, inner.at[:, pl.ds(2, depth - 4)], sem)
     copy.start()
-    split_rows(total, pieces)
+    split_rows(total, [kept.at[0], to_core.at[0], kept.at[1], to_core.at[1]])
     copy.wait()
+
+
+def chip_kernel(kept, from_core, own, across):
+    own[...] = kept[0] + from_core[0]
+    across[...] = kept[1] + from_core[1]
 
 
 def last_steps(partner, snaps, carried_on, outer, velocity, store, wanted):
@@ -308,13 +312,11 @@
         copy.wait()
 
 
-def sum_kernel(*refs):
-    ins, out = refs[:-1], refs[-1]
-    half = len(ins) // 2
+def sum_kernel(inner, inner_across, *refs):
+    parts, out = refs[:-1], refs[-1]
     depth = out.shape[0]
-    inner = functools.reduce(jnp.add, [ref[...] for ref in ins[:half]])
-    outer = functools.reduce(jnp.add, [ref[...] for ref in ins[half:]])
-    out[2 : depth - 2] = inner
+    outer = functools.reduce(jnp.add, [part[...] for part in parts])
+    out[2 : depth - 2] = inner[...] + inner_across[...]
     out[0:2] = outer[0:2]
     out[depth - 2 : depth] = outer[2:4]
 
@@ -394,20 +396,27 @@
                 cost_estimate=cost(1.5),
             )(snap_of_step, snaps_next, state, halo[partner], own_flow, other_flow, velocity, start)
             halo[partner] = exchanged(message, partner, 0)
-        carried_on, inner, *inner_pieces = pl.pallas_call(
+        pair = jax.ShapeDtypeStruct((2,) + pieces[0].shape, jnp.float32)
+        carried_on, inner, kept, to_core = pl.pallas_call(
             functools.partial(inner_kernel, slabs),
-            out_shape=(shaped(fields, depth), shaped(fields, depth)) + pieces,
+            out_shape=(shaped(fields, depth), shaped(fields, depth), pair, pair),
             in_specs=[smem, smem] + [vmem] * 6 + [hbm],
-            out_specs=(vmem, hbm) + (vmem,) * slabs,
+            out_specs=(vmem, hbm, vmem, vmem),
             scratch_shapes=[
                 room(fields, depth), room(fields, depth + 2), room(fields, depth - 4), room(depth - 4), sem(()),
             ],
             compiler_params=params(32),
             cost_estimate=cost(3),
         )(snap_of_step, snaps_next, state, *widened, *edges, velocity, start)
-        inner_parts = inner_pieces[:1] + [
-            moved(inner_pieces[by], lambda t, s, by=by: (t + by, s)) for by in range(1, slabs)
-        ]
+        inner_own, inner_across = pl.pallas_call(
+            chip_kernel,
+            out_shape=pieces[:2],
+            in_specs=[vmem, vmem],
+            out_specs=(vmem, vmem),
+            compiler_params=params(16),
+            cost_estimate=cost(0.5),
+        )(kept, moved(to_core, lambda t, s: (t ^ 1, s)))
+        inner_across = moved(inner_across, lambda t, s: (t ^ 2, s))
         outer_one, total_one = pl.pallas_call(
             functools.partial(outer_kernel, blocks, slabs, 0),
             out_shape=(shaped(fields, 2), shaped(2)),
@@ -427,7 +436,7 @@
             cost_estimate=cost(0.5),
         )(snap_of_step, edges[1], halo[1], own_flow, other_flow, carried_on, velocity, total_one)
         outer_parts = outer_pieces[:1] + [
-            moved(outer_pieces[by], lambda t, s, by=by: (t + by, s)) for by in range(1, slabs)
+            moved(outer_pieces[by], lambda t, s, by=by: (t ^ by, s)) for by in range(1, slabs)
         ]
         final = pl.pallas_call(
             finish_kernel,
@@ -442,11 +451,11 @@
         gradient = pl.pallas_call(
             sum_kernel,
             out_shape=shaped(depth, rows=ny // slabs),
-            in_specs=[vmem] * (2 * slabs),
+            in_specs=[vmem] * (2 + slabs),
             out_specs=vmem,
             compiler_params=params(16),
             cost_estimate=cost(0.5),
-        )(*inner_parts, *outer_parts)
+        )(inner_own, inner_across, *outer_parts)
         return (final[None], gradient)
 
     return jax.shard_map(

time: 49 us -> 49.2 us (level)
  starting transfers between devices: 23.1 us -> 22.1 us
  waiting for transfers between devices: 11.5 us -> 12.5 us
    ppermute x14 -> x13, starting transfers between devices: 23.1 us -> 22.1 us  [moved(): return lax.ppermute(array, ('tm', 'space'), pairs)]
    ppermute x14 -> x13, waiting for transfers between devices: 11.5 us -> 12.5 us  [moved(): return lax.ppermute(array, ('tm', 'space'), pairs)]
  transfers between devices with their start and end apart: 14 -> 13, of which waited for: 5 -> 6; matrix products, arithmetic and copies ran while one was open for 0% -> 0% of each run, Pallas kernels for 25% -> 25%
where the time goes in v9:
time: 49.2 us; the launch traced here: 48.4 us
  starting transfers between devices  22.1 us (45%)
  Pallas kernels  13 us (26%)
  waiting for transfers between devices  12.5 us (25%)
  between operations  0.76 us (2%)
    ppermute x13, starting transfers between devices, moved(): return lax.ppermute(array, ('tm', 'space'), pairs)  22.1 us
    ppermute x13, waiting for transfers between devices, moved(): return lax.ppermute(array, ('tm', 'space'), pairs)  12.5 us
    pallas_call x1, Pallas kernels, body(): pl.pallas_call(functools.partial(inner_kernel, slabs), out_shape=(shaped(...  3.86 us
    pallas_call x2, Pallas kernels, body(): pl.pallas_call(functools.partial(first_kernel, blocks, slabs, partner), o...  2.58 us
    pallas_call x1, Pallas kernels, body(): pl.pallas_call(start_kernel, out_shape=(layer, layer, shaped(velocity.sha...  2.3 us
    pallas_call x1, Pallas kernels, body(): pl.pallas_call(finish_kernel, out_shape=shaped(fields, depth), in_specs=[...  1.82 us
  transfers between devices with their start and end apart: 13, of which 6 were waited for; matrix products, arithmetic and copies ran while one was open for 0% of the time, Pallas kernels for 25%

profile of v9, /device:TPU:1, one launch (start us, length us, event | category | flops | bytes accessed | tf_op | source)
XLA Modules:
  0.0 48.4 jit_solution(7159305055330666715)
XLA Ops:
  0.7 3.3 %collective-permute-start.1 = (f32[2,8,32,512]{3,2,1,0:T(8,128)}, f32[2,8,32,512]{3,2,1,0:T(8,128)S(1)}, u32[]{:S(2)}, u32[]{:S(2)}) collective-permute-start(f32[2,8,32,512]{3,2,1,0:T(8,128)} %bitcast.2), channel_id=1, source_target_pairs={{0,192},{1,193},{2,194},{3,195},{4,196},{5,197},{6,198},{7,199},{8... | collective-permute-start | bytes 3145736 | tf_op jit(solution)/shard_map/ppermute | solution.py:341
  4.0 2.3 %shard_map.50 = (f32[4,32,512]{2,1,0:T(8,128)}, f32[4,32,512]{2,1,0:T(8,128)}, f32[2,32,512]{2,1,0:T(8,128)}) custom-call(s32[1,2]{1,0:T(1,128)} %snaps.13, f32[2,8,32,512]{3,2,1,0:T(8,128)} %bitcast.3, f32[2,3,8,32,512]{4,3,2,1,0:T(8,128)} %velocity.13), custom_call_target="tpu_custom_call" | custom-call | bytes 7200000 | tf_op jit(solution)/shard_map/pallas_call | solution.py:369
  6.3 0.2 collective-permute-start.3
  6.5 2.4 %collective-permute-start.2 = (f32[4,32,512]{2,1,0:T(8,128)}, f32[4,32,512]{2,1,0:T(8,128)S(1)}, u32[]{:S(2)}, u32[]{:S(2)}) collective-permute-start(f32[4,32,512]{2,1,0:T(8,128)} %get-tuple-element.24), channel_id=1, source_target_pairs={{0,193},{1,192},{2,195},{3,194},{4,197},{5,196},{6,199},{7,198},{8... | collective-permute-start | bytes 786440 | tf_op jit(solution)/shard_map/ppermute | solution.py:341
  9.0 0.5 collective-permute-start.5
  9.4 3.2 %collective-permute-done.3.own_flow = f32[2,32,512]{2,1,0:T(8,128)S(1)} collective-permute-done((f32[2,32,512]{2,1,0:T(8,128)}, f32[2,32,512]{2,1,0:T(8,128)S(1)}, u32[]{:S(2)}, u32[]{:S(2)}) %collective-permute-start.3) | collective-permute-done | bytes 131104 | tf_op jit(solution)/shard_map/ppermute | solution.py:341
  12.7 8.0 %collective-permute-start.4 = (f32[2,32,512]{2,1,0:T(8,128)S(1)}, f32[2,32,512]{2,1,0:T(8,128)S(1)}, u32[]{:S(2)}, u32[]{:S(2)}) collective-permute-start(f32[2,32,512]{2,1,0:T(8,128)S(1)} %collective-permute-done.3.own_flow), channel_id=1, source_target_pairs={{0,64},{1,65},{2,66},{3,67},{4,68},{5,69},{6,70},{7,71},{8,72},{9,... | collective-permute-start | bytes 393224 | tf_op jit(solution)/shard_map/ppermute | solution.py:341
  20.7 3.0 %collective-permute-done.snaps_next = s32[1,2]{1,0:T(1,128)S(1)} collective-permute-done((s32[1,2]{1,0:T(1,128)S(1)}, s32[1,2]{1,0:T(1,128)S(1)}, u32[]{:S(2)}, u32[]{:S(2)}) %collective-permute-start) | collective-permute-done | bytes 40 | tf_op jit(solution)/shard_map/ppermute | solution.py:341
  23.6 1.3 %shard_map.51 = (f32[2,4,32,512]{3,2,1,0:T(8,128)S(1)}, f32[2,2,32,512]{3,2,1,0:T(8,128)S(1)}, f32[4,32,512]{2,1,0:T(8,128)S(1)}) custom-call(s32[1,2]{1,0:T(1,128)S(1)} %copy-done.2, s32[1,2]{1,0:T(1,128)S(1)} %collective-permute-done.snaps_next, f32[2,8,32,512]{3,2,1,0:T(8,128)S(1)} %collective-permute-done.1.state.before, ...), custom_call_target="tpu_custom_call" | custom-call | bytes 5400000 | tf_op jit(solution)/shard_map/pallas_call | solution.py:389
  24.9 2.8 %collective-permute-start.6 = (f32[4,32,512]{2,1,0:T(8,128)S(1)}, f32[4,32,512]{2,1,0:T(8,128)S(1)}, u32[]{:S(2)}, u32[]{:S(2)}) collective-permute-start(f32[4,32,512]{2,1,0:T(8,128)S(1)} %get-tuple-element.32), channel_id=1, source_target_pairs={{0,1},{1,0},{2,3},{3,2},{4,5},{5,4},{6,7},{7,6},{8,9},{9,8},{10,11... | collective-permute-start | bytes 786440 | tf_op jit(solution)/shard_map/ppermute | solution.py:341
  27.8 1.3 %shard_map.52 = (f32[2,4,32,512]{3,2,1,0:T(8,128)S(1)}, f32[2,2,32,512]{3,2,1,0:T(8,128)S(1)}, f32[4,32,512]{2,1,0:T(8,128)S(1)}) custom-call(s32[1,2]{1,0:T(1,128)S(1)} %copy-done.2, s32[1,2]{1,0:T(1,128)S(1)} %collective-permute-done.snaps_next, f32[2,8,32,512]{3,2,1,0:T(8,128)S(1)} %collective-permute-done.1.state.before, ...), custom_call_target="tpu_custom_call" | custom-call | bytes 5400000 | tf_op jit(solution)/shard_map/pallas_call | solution.py:389
  29.1 0.8 %collective-permute-start.7 = (f32[4,32,512]{2,1,0:T(8,128)S(1)}, f32[4,32,512]{2,1,0:T(8,128)S(1)}, u32[]{:S(2)}, u32[]{:S(2)}) collective-permute-start(f32[4,32,512]{2,1,0:T(8,128)S(1)} %get-tuple-element.34), channel_id=1, source_target_pairs={{0,64},{1,2},{2,1},{3,4},{4,3},{5,6},{6,5},{7,8},{8,7},{9,10},{10,... | collective-permute-start | bytes 786440 | tf_op jit(solution)/shard_map/ppermute | solution.py:341
  29.9 3.9 %shard_map.53 = (f32[2,8,32,512]{3,2,1,0:T(8,128)S(1)}, f32[2,8,32,512]{3,2,1,0:T(8,128)}, f32[2,4,8,512]{3,2,1,0:T(8,128)S(1)}, f32[2,4,8,512]{3,2,1,0:T(8,128)S(1)}) custom-call(s32[1,2]{1,0:T(1,128)S(1)} %copy-done.2, s32[1,2]{1,0:T(1,128)S(1)} %collective-permute-done.snaps_next, f32[2,8,32,512]{3,2,1,0:T(8,128)S(1)} %collective-permute-done.1.state.before, ...), custom_call_target="tpu_custom_call" | custom-call | bytes 10800000 | tf_op jit(solution)/shard_map/pallas_call | solution.py:400
  33.8 0.1 collective-permute-start.8
  33.9 1.3 %collective-permute-done.8.from_core = f32[2,4,8,512]{3,2,1,0:T(8,128)S(1)} collective-permute-done((f32[2,4,8,512]{3,2,1,0:T(8,128)S(1)}, f32[2,4,8,512]{3,2,1,0:T(8,128)S(1)}, u32[]{:S(2)}, u32[]{:S(2)}) %collective-permute-start.8) | collective-permute-done | bytes 131104 | tf_op jit(solution)/shard_map/ppermute | solution.py:341
  35.2 0.1 collective-permute-start.9
  35.3 3.3 %collective-permute-done.6.halo = f32[4,32,512]{2,1,0:T(8,128)S(1)} collective-permute-done((f32[4,32,512]{2,1,0:T(8,128)S(1)}, f32[4,32,512]{2,1,0:T(8,128)S(1)}, u32[]{:S(2)}, u32[]{:S(2)}) %collective-permute-start.6) | collective-permute-done | bytes 262176 | tf_op jit(solution)/shard_map/ppermute | solution.py:341
  38.6 0.9 %shard_map.54 = (f32[2,2,32,512]{3,2,1,0:T(8,128)S(1)}, f32[2,32,512]{2,1,0:T(8,128)S(1)}) custom-call(s32[1,2]{1,0:T(1,128)S(1)} %copy-done.2, f32[2,2,32,512]{3,2,1,0:T(8,128)S(1)} %get-tuple-element.29.edges_one.edges, f32[4,32,512]{2,1,0:T(8,128)S(1)} %collective-permute-done.6.halo, f32[2,32,512]{2,1,0:T(8,128)S(1)} %collective-permute-done.3.own_flow, ...), custom_call_target="tpu_custom_call" | custom-call | bytes 1800000 | tf_op jit(solution)/shard_map/pallas_call | solution.py:420
  39.5 0.9 %shard_map.55 = (f32[2,2,32,512]{3,2,1,0:T(8,128)S(1)}, f32[4,8,512]{2,1,0:T(8,128)S(1)}, f32[4,8,512]{2,1,0:T(8,128)S(1)}, f32[4,8,512]{2,1,0:T(8,128)S(1)}, f32[4,8,512]{2,1,0:T(8,128)S(1)}) custom-call(s32[1,2]{1,0:T(1,128)S(1)} %copy-done.2, f32[2,2,32,512]{3,2,1,0:T(8,128)S(1)} %get-tuple-element.30.edges_two.edges, ...), custom_call_target="tpu_custom_call" | custom-call | bytes 1800000 | tf_op jit(solution)/shard_map/pallas_call | solution.py:429
  40.4 2.1 %collective-permute-start.10 = (f32[4,8,512]{2,1,0:T(8,128)S(1)}, f32[4,8,512]{2,1,0:T(8,128)S(1)}, u32[]{:S(2)}, u32[]{:S(2)}) collective-permute-start(f32[4,8,512]{2,1,0:T(8,128)S(1)} %get-tuple-element.43), channel_id=1, source_target_pairs={{0,64},{1,65},{2,66},{3,67},{4,68},{5,69},{6,70},{7,71},{8,72},{9,... | collective-permute-start | bytes 196616 | tf_op jit(solution)/shard_map/ppermute | solution.py:341
  42.5 1.7 %collective-permute-start.12 = (f32[4,8,512]{2,1,0:T(8,128)S(1)}, f32[4,8,512]{2,1,0:T(8,128)S(1)}, u32[]{:S(2)}, u32[]{:S(2)}) collective-permute-start(f32[4,8,512]{2,1,0:T(8,128)S(1)} %get-tuple-element.45), channel_id=1, source_target_pairs={{0,192},{1,193},{2,194},{3,195},{4,196},{5,197},{6,198},{7,199},{8... | collective-permute-start | bytes 196616 | tf_op jit(solution)/shard_map/ppermute | solution.py:341
  44.2 1.8 %shard_map.56 = f32[2,8,32,512]{3,2,1,0:T(8,128)} custom-call(s32[1,2]{1,0:T(1,128)S(1)} %copy-done.2, f32[2,8,32,512]{3,2,1,0:T(8,128)S(1)} %get-tuple-element.31.carried_on, f32[2,2,32,512]{3,2,1,0:T(8,128)S(1)} %get-tuple-element.33.outer_one, f32[2,2,32,512]{3,2,1,0:T(8,128)S(1)} %get-tuple-element.36.outer_two, ...), custom_call_target="tpu_custom_call", output_to_operand_aliasing={{}: (5, {})} | custom-call | bytes 3600000 | tf_op jit(solution)/shard_map/pallas_call | solution.py:441
  46.1 1.6 %collective-permute-done.12.refs_3_ = f32[4,8,512]{2,1,0:T(8,128)S(1)} collective-permute-done((f32[4,8,512]{2,1,0:T(8,128)S(1)}, f32[4,8,512]{2,1,0:T(8,128)S(1)}, u32[]{:S(2)}, u32[]{:S(2)}) %collective-permute-start.12) | collective-permute-done | bytes 65568 | tf_op jit(solution)/shard_map/ppermute | solution.py:341
  47.7 0.7 %shard_map.58 = f32[8,8,512]{2,1,0:T(8,128)} custom-call(f32[4,8,512]{2,1,0:T(8,128)S(1)} %get-tuple-element.40.inner, f32[4,8,512]{2,1,0:T(8,128)S(1)} %collective-permute-done.9.inner_across, f32[4,8,512]{2,1,0:T(8,128)S(1)} %get-tuple-element.42.refs_0_, f32[4,8,512]{2,1,0:T(8,128)S(1)} %collective-permute-done.10.refs_1_, ...), custom_call_target="tpu_custom_call" | custom-call | bytes 1800000 | tf_op jit(solution)/shard_map/pallas_call | solution.py:451
  (17 shorter events, 0.1 us)
Async XLA Ops:
  0.6 23.0 %copy-start.1 = (f32[1,2,8,32,512]{4,3,2,1,0:T(8,128)S(1)}, f32[1,2,8,32,512]{4,3,2,1,0:T(8,128)}, u32[]{:S(2)}) copy-start(f32[1,2,8,32,512]{4,3,2,1,0:T(8,128)} %param.3) | copy-start | bytes 3145732
  0.6 20.0 %copy-start.2 = (s32[1,2]{1,0:T(1,128)S(1)}, s32[1,2]{1,0:T(1,128)}, u32[]{:S(2)}) copy-start(s32[1,2]{1,0:T(1,128)} %snaps.13) | copy-start | bytes 28
  0.6 23.0 %copy-start = (f32[2,3,8,32,512]{4,3,2,1,0:T(8,128)S(1)}, f32[2,3,8,32,512]{4,3,2,1,0:T(8,128)}, u32[]{:S(2)}) copy-start(f32[2,3,8,32,512]{4,3,2,1,0:T(8,128)} %velocity.13) | copy-start | bytes 9437188
  0.7 23.0 %collective-permute-start.1 = (f32[2,8,32,512]{3,2,1,0:T(8,128)}, f32[2,8,32,512]{3,2,1,0:T(8,128)S(1)}, u32[]{:S(2)}, u32[]{:S(2)}) collective-permute-start(f32[2,8,32,512]{3,2,1,0:T(8,128)} %bitcast.2), channel_id=1, source_target_pairs={{0,192},{1,193},{2,194},{3,195},{4,196},{5,197},{6,198},{7,199},{8... | collective-permute-start | bytes 3145736 | tf_op jit(solution)/shard_map/ppermute | solution.py:341
  6.3 6.4 %collective-permute-start.3 = (f32[2,32,512]{2,1,0:T(8,128)}, f32[2,32,512]{2,1,0:T(8,128)S(1)}, u32[]{:S(2)}, u32[]{:S(2)}) collective-permute-start(f32[2,32,512]{2,1,0:T(8,128)} %get-tuple-element.25), channel_id=1, source_target_pairs={{0,129},{1,130},{2,131},{3,132},{4,133},{5,134},{6,135},{7,136},{8... | collective-permute-start | bytes 393224 | tf_op jit(solution)/shard_map/ppermute | solution.py:341
  6.5 17.1 %collective-permute-start.2 = (f32[4,32,512]{2,1,0:T(8,128)}, f32[4,32,512]{2,1,0:T(8,128)S(1)}, u32[]{:S(2)}, u32[]{:S(2)}) collective-permute-start(f32[4,32,512]{2,1,0:T(8,128)} %get-tuple-element.24), channel_id=1, source_target_pairs={{0,193},{1,192},{2,195},{3,194},{4,197},{5,196},{6,199},{7,198},{8... | collective-permute-start | bytes 786440 | tf_op jit(solution)/shard_map/ppermute | solution.py:341
  9.0 18.8 %collective-permute-start.5 = (f32[4,32,512]{2,1,0:T(8,128)}, f32[4,32,512]{2,1,0:T(8,128)S(1)}, u32[]{:S(2)}, u32[]{:S(2)}) collective-permute-start(f32[4,32,512]{2,1,0:T(8,128)} %get-tuple-element.27), channel_id=1, source_target_pairs={{0,64},{1,194},{2,193},{3,196},{4,195},{5,198},{6,197},{7,200},{8,... | collective-permute-start | bytes 786440 | tf_op jit(solution)/shard_map/ppermute | solution.py:341
  12.7 11.0 %collective-permute-start.4 = (f32[2,32,512]{2,1,0:T(8,128)S(1)}, f32[2,32,512]{2,1,0:T(8,128)S(1)}, u32[]{:S(2)}, u32[]{:S(2)}) collective-permute-start(f32[2,32,512]{2,1,0:T(8,128)S(1)} %collective-permute-done.3.own_flow), channel_id=1, source_target_pairs={{0,64},{1,65},{2,66},{3,67},{4,68},{5,69},{6,70},{7,71},{8,72},{9,... | collective-permute-start | bytes 393224 | tf_op jit(solution)/shard_map/ppermute | solution.py:341
  20.6 3.0 %collective-permute-start = (s32[1,2]{1,0:T(1,128)S(1)}, s32[1,2]{1,0:T(1,128)S(1)}, u32[]{:S(2)}, u32[]{:S(2)}) collective-permute-start(s32[1,2]{1,0:T(1,128)S(1)} %copy-done.2), channel_id=1, source_target_pairs={{0,192},{1,193},{2,194},{3,195},{4,196},{5,197},{6,198},{7,199},{8... | collective-permute-start | bytes 32 | tf_op jit(solution)/shard_map/ppermute | solution.py:341
  24.9 13.7 %collective-permute-start.6 = (f32[4,32,512]{2,1,0:T(8,128)S(1)}, f32[4,32,512]{2,1,0:T(8,128)S(1)}, u32[]{:S(2)}, u32[]{:S(2)}) collective-permute-start(f32[4,32,512]{2,1,0:T(8,128)S(1)} %get-tuple-element.32), channel_id=1, source_target_pairs={{0,1},{1,0},{2,3},{3,2},{4,5},{5,4},{6,7},{7,6},{8,9},{9,8},{10,11... | collective-permute-start | bytes 786440 | tf_op jit(solution)/shard_map/ppermute | solution.py:341
  29.1 10.4 %collective-permute-start.7 = (f32[4,32,512]{2,1,0:T(8,128)S(1)}, f32[4,32,512]{2,1,0:T(8,128)S(1)}, u32[]{:S(2)}, u32[]{:S(2)}) collective-permute-start(f32[4,32,512]{2,1,0:T(8,128)S(1)} %get-tuple-element.34), channel_id=1, source_target_pairs={{0,64},{1,2},{2,1},{3,4},{4,3},{5,6},{6,5},{7,8},{8,7},{9,10},{10,... | collective-permute-start | bytes 786440 | tf_op jit(solution)/shard_map/ppermute | solution.py:341
  33.8 1.4 %collective-permute-start.8 = (f32[2,4,8,512]{3,2,1,0:T(8,128)S(1)}, f32[2,4,8,512]{3,2,1,0:T(8,128)S(1)}, u32[]{:S(2)}, u32[]{:S(2)}) collective-permute-start(f32[2,4,8,512]{3,2,1,0:T(8,128)S(1)} %get-tuple-element.39), channel_id=1, source_target_pairs={{0,64},{1,65},{2,66},{3,67},{4,68},{5,69},{6,70},{7,71},{8,72},{9,... | collective-permute-start | bytes 393224 | tf_op jit(solution)/shard_map/ppermute | solution.py:341
  35.2 10.8 %collective-permute-start.9 = (f32[4,8,512]{2,1,0:T(8,128)S(1)}, f32[4,8,512]{2,1,0:T(8,128)S(1)}, u32[]{:S(2)}, u32[]{:S(2)}) collective-permute-start(f32[4,8,512]{2,1,0:T(8,128)S(1)} %get-tuple-element.41), channel_id=1, source_target_pairs={{0,128},{1,129},{2,130},{3,131},{4,132},{5,133},{6,134},{7,135},{8... | collective-permute-start | bytes 196616 | tf_op jit(solution)/shard_map/ppermute | solution.py:341
  40.4 5.6 %collective-permute-start.10 = (f32[4,8,512]{2,1,0:T(8,128)S(1)}, f32[4,8,512]{2,1,0:T(8,128)S(1)}, u32[]{:S(2)}, u32[]{:S(2)}) collective-permute-start(f32[4,8,512]{2,1,0:T(8,128)S(1)} %get-tuple-element.43), channel_id=1, source_target_pairs={{0,64},{1,65},{2,66},{3,67},{4,68},{5,69},{6,70},{7,71},{8,72},{9,... | collective-permute-start | bytes 196616 | tf_op jit(solution)/shard_map/ppermute | solution.py:341
  42.5 3.7 %collective-permute-start.11 = (f32[4,8,512]{2,1,0:T(8,128)S(1)}, f32[4,8,512]{2,1,0:T(8,128)S(1)}, u32[]{:S(2)}, u32[]{:S(2)}) collective-permute-start(f32[4,8,512]{2,1,0:T(8,128)S(1)} %get-tuple-element.44), channel_id=1, source_target_pairs={{0,128},{1,129},{2,130},{3,131},{4,132},{5,133},{6,134},{7,135},{8... | collective-permute-start | bytes 196616 | tf_op jit(solution)/shard_map/ppermute | solution.py:341
  42.5 5.2 %collective-permute-start.12 = (f32[4,8,512]{2,1,0:T(8,128)S(1)}, f32[4,8,512]{2,1,0:T(8,128)S(1)}, u32[]{:S(2)}, u32[]{:S(2)}) collective-permute-start(f32[4,8,512]{2,1,0:T(8,128)S(1)} %get-tuple-element.45), channel_id=1, source_target_pairs={{0,192},{1,193},{2,194},{3,195},{4,196},{5,197},{6,198},{7,199},{8... | collective-permute-start | bytes 196616 | tf_op jit(solution)/shard_map/ppermute | solution.py:341

commit v10 on v9

--- a/solution.py
+++ b/solution.py
@@ -95,7 +95,7 @@
         store(i, j, advanced(here, pairs, (sign * u, v, w), i, j, shape, wanted))
 
 
-def pack(here, inner, flow, sign, message, shape):
+def pack(here, inner, flow, sign, message, shape, rest=None):
     def pairs(f, i, j):
         value = inner(f, i, j)
         return value, value
@@ -105,7 +105,8 @@
         out = advanced(here, pairs, (-sign * u, v, w), i, j, shape)
         for f in (0, 1):
             message[(f,) + spot(i, j)] = here(f, i, j)
-            message[(2 + f,) + spot(i, j)] = out[f]
+            into_message = message.at[2 + f] if f == 0 or rest is None else rest.at[0]
+            into_message[spot(i, j)] = out[f]
 
 
 def take_halo(blocks, partner, halo, own, own_flow, other_flow, snap, now, after, shape):
@@ -117,12 +118,14 @@
         u = jnp.where(high == fetched, own_flow[(snap,) + spot(i, j)], other_flow[(snap,) + spot(i, j)])
         for f in (0, 1):
             current = halo[(f,) + spot(i, j)]
-            later = halo[(2 + f,) + spot(i, j)] + (diffusion[f] - (0.25 * sign) * u) * own(f, i, j)
             if partner == 1:
                 current = jnp.where(inside, current, 0.0)
-                later = jnp.where(inside, later, 0.0)
             now[(f,) + spot(i, j)] = current
-            after[(f, 0) + spot(i, j)] = later
+            if 2 + f < halo.shape[0]:
+                later = halo[(2 + f,) + spot(i, j)] + (diffusion[f] - (0.25 * sign) * u) * own(f, i, j)
+                if partner == 1:
+                    later = jnp.where(inside, later, 0.0)
+                after[(f, 0) + spot(i, j)] = later
 
 
 def plain(ref):
@@ -166,7 +169,7 @@
 
 
 def first_kernel(blocks, slabs, partner, snaps, snaps_next, state, halo, own_flow, other_flow, velocity, start,
-                 widened, edges, message, now):
+                 widened, edges, message, rest, now):
     depth, shape = state.shape[1], state.shape[2:]
     last = lax.axis_index("tm") == slabs - 1
     high, sign = side_of(partner)
@@ -192,7 +195,7 @@
             flow = flow_of(velocity, snaps_next[0, 0], at(k))
             side_layer(outer, here, inner, flow, sign, shape, into(edges, k))
 
-    pack(layer_of(edges, 0), layer_of(edges, 1), flow_of(velocity, snaps[0, 1], at(0)), sign, message, shape)
+    pack(layer_of(edges, 0), layer_of(edges, 1), flow_of(velocity, snaps[0, 1], at(0)), sign, message, shape, rest)
 
 
 def inner_kernel(slabs, snaps, snaps_next, before, widened_one, widened_two, edges_one, edges_two, velocity, start,
@@ -255,7 +258,7 @@
     across[...] = kept[1] + from_core[1]
 
 
-def last_steps(partner, snaps, carried_on, outer, velocity, store, wanted):
+def last_steps(partner, snaps, carried_on, outer, velocity, store, wanted, beyond=None):
     depth, shape = carried_on.shape[1], carried_on.shape[2:]
     high, sign = side_of(partner)
 
@@ -263,6 +266,8 @@
         return high * (depth - 1) + k * (1 - 2 * high)
 
     ring = [layer_of(outer, 0), layer_of(outer, 1), layer_of(carried_on, at(1)), layer_of(carried_on, at(2))]
+    if beyond is not None:
+        ring[0] = beyond
     for k in range(2):
         flow = flow_of(velocity, snaps[0, 0], at(k))
         keep = functools.partial(store, k, ring[k + 1])
@@ -293,15 +298,27 @@
         split_rows(whole, pieces)
 
 
-def finish_kernel(snaps, carried_on, outer_one, outer_two, velocity, inner, out, final, sems):
-    depth = carried_on.shape[1]
-    for partner, outer in enumerate((outer_one, outer_two)):
-        high, unused = side_of(partner)
+def finish_kernel(blocks, snaps, carried_on, outer_one, outer_two, edges_one, edges_two, rest_one, rest_two,
+                  own_flow, other_flow, velocity, inner, out, final, later, sems):
+    depth, shape = carried_on.shape[1], carried_on.shape[2:]
+    place = lax.axis_index("space")
+    inside = jnp.logical_and(place > 0, place < blocks - 1)
+    fetched = lax.rem(lax.axis_index("tm"), 2)
+    for partner, outer, edges, rest in ((0, outer_one, edges_one, rest_one), (1, outer_two, edges_two, rest_two)):
+        high, sign = side_of(partner)
+        for i, j in tiles(shape):
+            at = (snaps[0, 1],) + spot(i, j)
+            u = jnp.where(high == fetched, own_flow[at], other_flow[at])
+            value = rest[(0,) + spot(i, j)] + (diffusion[1] - (0.25 * sign) * u) * edges[(1, 0) + spot(i, j)]
+            later[(partner,) + spot(i, j)] = value if partner == 0 else jnp.where(inside, value, 0.0)
+
+        def beyond(f, i, j, outer=outer, partner=partner):
+            return later[(partner,) + spot(i, j)] if f == 1 else outer[(0, 0) + spot(i, j)]
 
         def store(k, here, i, j, values, high=high):
             into(final, high * (edge_count - 1) + k * (1 - 2 * high))(i, j, values)
 
-        last_steps(partner, snaps, carried_on, outer, velocity, store, (0, 1))
+        last_steps(partner, snaps, carried_on, outer, velocity, store, (0, 1), beyond)
     copies = [
         pltpu.make_async_copy(final.at[:, pl.ds(0, 2)], out.at[:, pl.ds(0, 2)], sems.at[0]),
         pltpu.make_async_copy(final.at[:, pl.ds(2, 2)], out.at[:, pl.ds(depth - 2, 2)], sems.at[1]),
@@ -384,18 +401,19 @@
         halo_two = exchanged(message_two, 1, 1)
         own_flow = moved(flow_out, fetched)
         other_flow = moved(own_flow, lambda t, s: (t ^ 1, s))
-        widened, edges, halo = [None] * 2, [None] * 2, [halo_one, halo_two]
+        widened, edges, halo, halo_rest = [None] * 2, [None] * 2, [halo_one, halo_two], [None] * 2
         for partner in (0, 1):
-            widened[partner], edges[partner], message = pl.pallas_call(
+            widened[partner], edges[partner], message, rest = pl.pallas_call(
                 functools.partial(first_kernel, blocks, slabs, partner),
-                out_shape=(shaped(fields, 4), shaped(fields, 2), layer),
+                out_shape=(shaped(fields, 4), shaped(fields, 2), shaped(3), shaped(1)),
                 in_specs=[smem, smem] + [vmem] * 5 + [hbm],
-                out_specs=(vmem,) * 3,
+                out_specs=(vmem,) * 4,
                 scratch_shapes=[room(fields)],
                 compiler_params=params(32),
                 cost_estimate=cost(1.5),
             )(snap_of_step, snaps_next, state, halo[partner], own_flow, other_flow, velocity, start)
             halo[partner] = exchanged(message, partner, 0)
+            halo_rest[partner] = exchanged(rest, partner, 0)
         pair = jax.ShapeDtypeStruct((2,) + pieces[0].shape, jnp.float32)
         carried_on, inner, kept, to_core = pl.pallas_call(
             functools.partial(inner_kernel, slabs),
@@ -439,15 +457,15 @@
             moved(outer_pieces[by], lambda t, s, by=by: (t ^ by, s)) for by in range(1, slabs)
         ]
         final = pl.pallas_call(
-            finish_kernel,
+            functools.partial(finish_kernel, blocks),
             out_shape=shaped(fields, depth),
-            in_specs=[smem, vmem, vmem, vmem, vmem, hbm],
+            in_specs=[smem] + [vmem] * 10 + [hbm],
             out_specs=hbm,
-            scratch_shapes=[room(fields, edge_count), sem((2,))],
-            input_output_aliases={5: 0},
+            scratch_shapes=[room(fields, edge_count), room(2), sem((2,))],
+            input_output_aliases={11: 0},
             compiler_params=params(32),
             cost_estimate=cost(1),
-        )(snap_of_step, carried_on, outer_one, outer_two, velocity, inner)
+        )(snap_of_step, carried_on, outer_one, outer_two, *edges, *halo_rest, own_flow, other_flow, velocity, inner)
         gradient = pl.pallas_call(
             sum_kernel,
             out_shape=shaped(depth, rows=ny // slabs),

time: 49.2 us -> 49.6 us (level)
  the two profiles are of different devices: /device:TPU:1 before, /device:TPU:103 now
where the time goes in v10:
time: 49.6 us; the launch traced here: 49.5 us
  starting transfers between devices  23.3 us (47%)
  Pallas kernels  13.4 us (27%)
  waiting for transfers between devices  12 us (24%)
  between operations  0.74 us (1%)
    ppermute x15, starting transfers between devices, moved(): return lax.ppermute(array, ('tm', 'space'), pairs)  23.3 us
    ppermute x15, waiting for transfers between devices, moved(): return lax.ppermute(array, ('tm', 'space'), pairs)  12 us
    pallas_call x1, Pallas kernels, body(): pl.pallas_call(functools.partial(inner_kernel, slabs), out_shape=(shaped(...  3.86 us
    pallas_call x1, Pallas kernels, body(): pl.pallas_call(start_kernel, out_shape=(layer, layer, shaped(velocity.sha...  2.7 us
    pallas_call x2, Pallas kernels, body(): pl.pallas_call(functools.partial(first_kernel, blocks, slabs, partner), o...  2.58 us
    pallas_call x1, Pallas kernels, body(): pl.pallas_call(functools.partial(finish_kernel, blocks), out_shape=shaped...  1.85 us
  transfers between devices with their start and end apart: 15, of which 3 were waited for; matrix products, arithmetic and copies ran while one was open for 0% of the time, Pallas kernels for 26%

profile of v10, /device:TPU:103, one launch (start us, length us, event | category | flops | bytes accessed | tf_op | source)
XLA Modules:
  0.0 49.5 jit_solution(17226340446379153271)
XLA Ops:
  0.7 0.8 %collective-permute-start.1 = (f32[2,8,32,512]{3,2,1,0:T(8,128)}, f32[2,8,32,512]{3,2,1,0:T(8,128)S(1)}, u32[]{:S(2)}, u32[]{:S(2)}) collective-permute-start(f32[2,8,32,512]{3,2,1,0:T(8,128)} %bitcast.2), channel_id=1, source_target_pairs={{0,192},{1,193},{2,194},{3,195},{4,196},{5,197},{6,198},{7,199},{8... | collective-permute-start | bytes 3145736 | tf_op jit(solution)/shard_map/ppermute | solution.py:358
  1.4 2.7 %shard_map.50 = (f32[4,32,512]{2,1,0:T(8,128)}, f32[4,32,512]{2,1,0:T(8,128)}, f32[2,32,512]{2,1,0:T(8,128)}) custom-call(s32[1,2]{1,0:T(1,128)} %snaps.13, f32[2,8,32,512]{3,2,1,0:T(8,128)} %bitcast.3, f32[2,3,8,32,512]{4,3,2,1,0:T(8,128)} %velocity.13), custom_call_target="tpu_custom_call" | custom-call | bytes 7200000 | tf_op jit(solution)/shard_map/pallas_call | solution.py:386
  4.1 3.1 %collective-permute-start.3 = (f32[2,32,512]{2,1,0:T(8,128)}, f32[2,32,512]{2,1,0:T(8,128)S(1)}, u32[]{:S(2)}, u32[]{:S(2)}) collective-permute-start(f32[2,32,512]{2,1,0:T(8,128)} %get-tuple-element.27), channel_id=1, source_target_pairs={{0,129},{1,130},{2,131},{3,132},{4,133},{5,134},{6,135},{7,136},{8... | collective-permute-start | bytes 393224 | tf_op jit(solution)/shard_map/ppermute | solution.py:358
  7.2 2.5 %collective-permute-start.2 = (f32[4,32,512]{2,1,0:T(8,128)}, f32[4,32,512]{2,1,0:T(8,128)S(1)}, u32[]{:S(2)}, u32[]{:S(2)}) collective-permute-start(f32[4,32,512]{2,1,0:T(8,128)} %get-tuple-element.26), channel_id=1, source_target_pairs={{0,193},{1,192},{2,195},{3,194},{4,197},{5,196},{6,199},{7,198},{8... | collective-permute-start | bytes 786440 | tf_op jit(solution)/shard_map/ppermute | solution.py:358
  9.7 2.7 %collective-permute-start.4 = (f32[2,32,512]{2,1,0:T(8,128)S(1)}, f32[2,32,512]{2,1,0:T(8,128)S(1)}, u32[]{:S(2)}, u32[]{:S(2)}) collective-permute-start(f32[2,32,512]{2,1,0:T(8,128)S(1)} %collective-permute-done.3.own_flow), channel_id=1, source_target_pairs={{0,64},{1,65},{2,66},{3,67},{4,68},{5,69},{6,70},{7,71},{8,72},{9,... | collective-permute-start | bytes 393224 | tf_op jit(solution)/shard_map/ppermute | solution.py:358
  12.4 8.0 %collective-permute-done.snaps_next = s32[1,2]{1,0:T(1,128)S(1)} collective-permute-done((s32[1,2]{1,0:T(1,128)S(1)}, s32[1,2]{1,0:T(1,128)S(1)}, u32[]{:S(2)}, u32[]{:S(2)}) %collective-permute-start) | collective-permute-done | bytes 40 | tf_op jit(solution)/shard_map/ppermute | solution.py:358
  20.5 2.3 %collective-permute-done.2.halo = f32[4,32,512]{2,1,0:T(8,128)S(1)} collective-permute-done((f32[4,32,512]{2,1,0:T(8,128)}, f32[4,32,512]{2,1,0:T(8,128)S(1)}, u32[]{:S(2)}, u32[]{:S(2)}) %collective-permute-start.2) | collective-permute-done | bytes 262176 | tf_op jit(solution)/shard_map/ppermute | solution.py:358
  22.8 1.3 %shard_map.51 = (f32[2,4,32,512]{3,2,1,0:T(8,128)S(1)}, f32[2,2,32,512]{3,2,1,0:T(8,128)S(1)}, f32[3,32,512]{2,1,0:T(8,128)S(1)}, f32[1,32,512]{2,1,0:T(8,128)S(1)}) custom-call(s32[1,2]{1,0:T(1,128)S(1)} %copy-done.2, s32[1,2]{1,0:T(1,128)S(1)} %collective-permute-done.snaps_next, f32[2,8,32,512]{3,2,1,0:T(8,128)S(1)} %collective-permute-done.1.state.before, ...), custom_call_target="tpu_custom_call" | custom-call | bytes 5400000 | tf_op jit(solution)/shard_map/pallas_call | solution.py:406
  24.1 2.3 %collective-permute-start.6 = (f32[3,32,512]{2,1,0:T(8,128)S(1)}, f32[3,32,512]{2,1,0:T(8,128)S(1)}, u32[]{:S(2)}, u32[]{:S(2)}) collective-permute-start(f32[3,32,512]{2,1,0:T(8,128)S(1)} %get-tuple-element.34), channel_id=1, source_target_pairs={{0,1},{1,0},{2,3},{3,2},{4,5},{5,4},{6,7},{7,6},{8,9},{9,8},{10,11... | collective-permute-start | bytes 589832 | tf_op jit(solution)/shard_map/ppermute | solution.py:358
  26.4 1.3 %shard_map.52 = (f32[2,4,32,512]{3,2,1,0:T(8,128)S(1)}, f32[2,2,32,512]{3,2,1,0:T(8,128)S(1)}, f32[3,32,512]{2,1,0:T(8,128)S(1)}, f32[1,32,512]{2,1,0:T(8,128)S(1)}) custom-call(s32[1,2]{1,0:T(1,128)S(1)} %copy-done.2, s32[1,2]{1,0:T(1,128)S(1)} %collective-permute-done.snaps_next, f32[2,8,32,512]{3,2,1,0:T(8,128)S(1)} %collective-permute-done.1.state.before, ...), custom_call_target="tpu_custom_call" | custom-call | bytes 5400000 | tf_op jit(solution)/shard_map/pallas_call | solution.py:406
  27.7 1.1 %collective-permute-start.7 = (f32[3,32,512]{2,1,0:T(8,128)S(1)}, f32[3,32,512]{2,1,0:T(8,128)S(1)}, u32[]{:S(2)}, u32[]{:S(2)}) collective-permute-start(f32[3,32,512]{2,1,0:T(8,128)S(1)} %get-tuple-element.36), channel_id=1, source_target_pairs={{0,64},{1,2},{2,1},{3,4},{4,3},{5,6},{6,5},{7,8},{8,7},{9,10},{10,... | collective-permute-start | bytes 589832 | tf_op jit(solution)/shard_map/ppermute | solution.py:358
  28.8 3.9 %shard_map.53 = (f32[2,8,32,512]{3,2,1,0:T(8,128)S(1)}, f32[2,8,32,512]{3,2,1,0:T(8,128)}, f32[2,4,8,512]{3,2,1,0:T(8,128)S(1)}, f32[2,4,8,512]{3,2,1,0:T(8,128)S(1)}) custom-call(s32[1,2]{1,0:T(1,128)S(1)} %copy-done.2, s32[1,2]{1,0:T(1,128)S(1)} %collective-permute-done.snaps_next, f32[2,8,32,512]{3,2,1,0:T(8,128)S(1)} %collective-permute-done.1.state.before, ...), custom_call_target="tpu_custom_call" | custom-call | bytes 10800000 | tf_op jit(solution)/shard_map/pallas_call | solution.py:418
  32.7 0.6 %collective-permute-start.10 = (f32[2,4,8,512]{3,2,1,0:T(8,128)S(1)}, f32[2,4,8,512]{3,2,1,0:T(8,128)S(1)}, u32[]{:S(2)}, u32[]{:S(2)}) collective-permute-start(f32[2,4,8,512]{3,2,1,0:T(8,128)S(1)} %get-tuple-element.43), channel_id=1, source_target_pairs={{0,64},{1,65},{2,66},{3,67},{4,68},{5,69},{6,70},{7,71},{8,72},{9,... | collective-permute-start | bytes 393224 | tf_op jit(solution)/shard_map/ppermute | solution.py:358
  33.3 2.7 %collective-permute-start.9 = (f32[1,32,512]{2,1,0:T(8,128)S(1)}, f32[1,32,512]{2,1,0:T(8,128)S(1)}, u32[]{:S(2)}, u32[]{:S(2)}) collective-permute-start(f32[1,32,512]{2,1,0:T(8,128)S(1)} %get-tuple-element.40), channel_id=1, source_target_pairs={{0,64},{1,2},{2,1},{3,4},{4,3},{5,6},{6,5},{7,8},{8,7},{9,10},{10,... | collective-permute-start | bytes 196616 | tf_op jit(solution)/shard_map/ppermute | solution.py:358
  36.0 3.8 %collective-permute-start.8 = (f32[1,32,512]{2,1,0:T(8,128)S(1)}, f32[1,32,512]{2,1,0:T(8,128)S(1)}, u32[]{:S(2)}, u32[]{:S(2)}) collective-permute-start(f32[1,32,512]{2,1,0:T(8,128)S(1)} %get-tuple-element.39), channel_id=1, source_target_pairs={{0,1},{1,0},{2,3},{3,2},{4,5},{5,4},{6,7},{7,6},{8,9},{9,8},{10,11... | collective-permute-start | bytes 196616 | tf_op jit(solution)/shard_map/ppermute | solution.py:358
  39.8 1.0 %collective-permute-start.11 = (f32[4,8,512]{2,1,0:T(8,128)S(1)}, f32[4,8,512]{2,1,0:T(8,128)S(1)}, u32[]{:S(2)}, u32[]{:S(2)}) collective-permute-start(f32[4,8,512]{2,1,0:T(8,128)S(1)} %get-tuple-element.45), channel_id=1, source_target_pairs={{0,128},{1,129},{2,130},{3,131},{4,132},{5,133},{6,134},{7,135},{8... | collective-permute-start | bytes 196616 | tf_op jit(solution)/shard_map/ppermute | solution.py:358
  40.8 0.8 %shard_map.54 = (f32[2,2,32,512]{3,2,1,0:T(8,128)S(1)}, f32[2,32,512]{2,1,0:T(8,128)S(1)}) custom-call(s32[1,2]{1,0:T(1,128)S(1)} %copy-done.2, f32[2,2,32,512]{3,2,1,0:T(8,128)S(1)} %get-tuple-element.31.edges_one.edges, f32[3,32,512]{2,1,0:T(8,128)S(1)} %collective-permute-done.6.halo, f32[2,32,512]{2,1,0:T(8,128)S(1)} %collective-permute-done.3.own_flow, ...), custom_call_target="tpu_custom_call" | custom-call | bytes 1800000 | tf_op jit(solution)/shard_map/pallas_call | solution.py:438
  41.7 0.9 %shard_map.55 = (f32[2,2,32,512]{3,2,1,0:T(8,128)S(1)}, f32[4,8,512]{2,1,0:T(8,128)S(1)}, f32[4,8,512]{2,1,0:T(8,128)S(1)}, f32[4,8,512]{2,1,0:T(8,128)S(1)}, f32[4,8,512]{2,1,0:T(8,128)S(1)}) custom-call(s32[1,2]{1,0:T(1,128)S(1)} %copy-done.2, f32[2,2,32,512]{3,2,1,0:T(8,128)S(1)} %get-tuple-element.32.edges_two.edges, ...), custom_call_target="tpu_custom_call" | custom-call | bytes 1800000 | tf_op jit(solution)/shard_map/pallas_call | solution.py:447
  42.6 1.0 %collective-permute-start.12 = (f32[4,8,512]{2,1,0:T(8,128)S(1)}, f32[4,8,512]{2,1,0:T(8,128)S(1)}, u32[]{:S(2)}, u32[]{:S(2)}) collective-permute-start(f32[4,8,512]{2,1,0:T(8,128)S(1)} %get-tuple-element.47), channel_id=1, source_target_pairs={{0,64},{1,65},{2,66},{3,67},{4,68},{5,69},{6,70},{7,71},{8,72},{9,... | collective-permute-start | bytes 196616 | tf_op jit(solution)/shard_map/ppermute | solution.py:358
  43.6 0.9 %collective-permute-start.13 = (f32[4,8,512]{2,1,0:T(8,128)S(1)}, f32[4,8,512]{2,1,0:T(8,128)S(1)}, u32[]{:S(2)}, u32[]{:S(2)}) collective-permute-start(f32[4,8,512]{2,1,0:T(8,128)S(1)} %get-tuple-element.48), channel_id=1, source_target_pairs={{0,128},{1,129},{2,130},{3,131},{4,132},{5,133},{6,134},{7,135},{8... | collective-permute-start | bytes 196616 | tf_op jit(solution)/shard_map/ppermute | solution.py:358
  44.5 0.8 %collective-permute-start.14 = (f32[4,8,512]{2,1,0:T(8,128)S(1)}, f32[4,8,512]{2,1,0:T(8,128)S(1)}, u32[]{:S(2)}, u32[]{:S(2)}) collective-permute-start(f32[4,8,512]{2,1,0:T(8,128)S(1)} %get-tuple-element.49), channel_id=1, source_target_pairs={{0,192},{1,193},{2,194},{3,195},{4,196},{5,197},{6,198},{7,199},{8... | collective-permute-start | bytes 196616 | tf_op jit(solution)/shard_map/ppermute | solution.py:358
  45.3 1.9 %shard_map.56 = f32[2,8,32,512]{3,2,1,0:T(8,128)} custom-call(s32[1,2]{1,0:T(1,128)S(1)} %copy-done.2, f32[2,8,32,512]{3,2,1,0:T(8,128)S(1)} %get-tuple-element.33.carried_on, f32[2,2,32,512]{3,2,1,0:T(8,128)S(1)} %get-tuple-element.35.outer_one, f32[2,2,32,512]{3,2,1,0:T(8,128)S(1)} %get-tuple-element.38.outer_two, ...), custom_call_target="tpu_custom_call", output_to_operand_aliasing={{}: (11, {})} | custom-call | bytes 3600000 | tf_op jit(solution)/shard_map/pallas_call | solution.py:459
  47.2 1.6 %collective-permute-done.14.refs_3_ = f32[4,8,512]{2,1,0:T(8,128)S(1)} collective-permute-done((f32[4,8,512]{2,1,0:T(8,128)S(1)}, f32[4,8,512]{2,1,0:T(8,128)S(1)}, u32[]{:S(2)}, u32[]{:S(2)}) %collective-permute-start.14) | collective-permute-done | bytes 65568 | tf_op jit(solution)/shard_map/ppermute | solution.py:358
  48.8 0.7 %shard_map.58 = f32[8,8,512]{2,1,0:T(8,128)} custom-call(f32[4,8,512]{2,1,0:T(8,128)S(1)} %get-tuple-element.44.inner, f32[4,8,512]{2,1,0:T(8,128)S(1)} %collective-permute-done.11.inner_across, f32[4,8,512]{2,1,0:T(8,128)S(1)} %get-tuple-element.46.refs_0_, f32[4,8,512]{2,1,0:T(8,128)S(1)} %collective-permute-done.12.refs_1_, ...), custom_call_target="tpu_custom_call" | custom-call | bytes 1800000 | tf_op jit(solution)/shard_map/pallas_call | solution.py:469
  (21 shorter events, 0.1 us)
Async XLA Ops:
  0.6 22.2 %copy-start.1 = (f32[1,2,8,32,512]{4,3,2,1,0:T(8,128)S(1)}, f32[1,2,8,32,512]{4,3,2,1,0:T(8,128)}, u32[]{:S(2)}) copy-start(f32[1,2,8,32,512]{4,3,2,1,0:T(8,128)} %param.3) | copy-start | bytes 3145732
  0.6 11.8 %copy-start.2 = (s32[1,2]{1,0:T(1,128)S(1)}, s32[1,2]{1,0:T(1,128)}, u32[]{:S(2)}) copy-start(s32[1,2]{1,0:T(1,128)} %snaps.13) | copy-start | bytes 28
  0.6 22.2 %copy-start = (f32[2,3,8,32,512]{4,3,2,1,0:T(8,128)S(1)}, f32[2,3,8,32,512]{4,3,2,1,0:T(8,128)}, u32[]{:S(2)}) copy-start(f32[2,3,8,32,512]{4,3,2,1,0:T(8,128)} %velocity.13) | copy-start | bytes 9437188
  0.7 22.1 %collective-permute-start.1 = (f32[2,8,32,512]{3,2,1,0:T(8,128)}, f32[2,8,32,512]{3,2,1,0:T(8,128)S(1)}, u32[]{:S(2)}, u32[]{:S(2)}) collective-permute-start(f32[2,8,32,512]{3,2,1,0:T(8,128)} %bitcast.2), channel_id=1, source_target_pairs={{0,192},{1,193},{2,194},{3,195},{4,196},{5,197},{6,198},{7,199},{8... | collective-permute-start | bytes 3145736 | tf_op jit(solution)/shard_map/ppermute | solution.py:358
  4.1 5.6 %collective-permute-start.3 = (f32[2,32,512]{2,1,0:T(8,128)}, f32[2,32,512]{2,1,0:T(8,128)S(1)}, u32[]{:S(2)}, u32[]{:S(2)}) collective-permute-start(f32[2,32,512]{2,1,0:T(8,128)} %get-tuple-element.27), channel_id=1, source_target_pairs={{0,129},{1,130},{2,131},{3,132},{4,133},{5,134},{6,135},{7,136},{8... | collective-permute-start | bytes 393224 | tf_op jit(solution)/shard_map/ppermute | solution.py:358
  7.2 15.6 %collective-permute-start.2 = (f32[4,32,512]{2,1,0:T(8,128)}, f32[4,32,512]{2,1,0:T(8,128)S(1)}, u32[]{:S(2)}, u32[]{:S(2)}) collective-permute-start(f32[4,32,512]{2,1,0:T(8,128)} %get-tuple-element.26), channel_id=1, source_target_pairs={{0,193},{1,192},{2,195},{3,194},{4,197},{5,196},{6,199},{7,198},{8... | collective-permute-start | bytes 786440 | tf_op jit(solution)/shard_map/ppermute | solution.py:358
  9.7 16.7 %collective-permute-start.5 = (f32[4,32,512]{2,1,0:T(8,128)}, f32[4,32,512]{2,1,0:T(8,128)S(1)}, u32[]{:S(2)}, u32[]{:S(2)}) collective-permute-start(f32[4,32,512]{2,1,0:T(8,128)} %get-tuple-element.29), channel_id=1, source_target_pairs={{0,64},{1,194},{2,193},{3,196},{4,195},{5,198},{6,197},{7,200},{8,... | collective-permute-start | bytes 786440 | tf_op jit(solution)/shard_map/ppermute | solution.py:358
  9.7 10.8 %collective-permute-start.4 = (f32[2,32,512]{2,1,0:T(8,128)S(1)}, f32[2,32,512]{2,1,0:T(8,128)S(1)}, u32[]{:S(2)}, u32[]{:S(2)}) collective-permute-start(f32[2,32,512]{2,1,0:T(8,128)S(1)} %collective-permute-done.3.own_flow), channel_id=1, source_target_pairs={{0,64},{1,65},{2,66},{3,67},{4,68},{5,69},{6,70},{7,71},{8,72},{9,... | collective-permute-start | bytes 393224 | tf_op jit(solution)/shard_map/ppermute | solution.py:358
  12.4 8.0 %collective-permute-start = (s32[1,2]{1,0:T(1,128)S(1)}, s32[1,2]{1,0:T(1,128)S(1)}, u32[]{:S(2)}, u32[]{:S(2)}) collective-permute-start(s32[1,2]{1,0:T(1,128)S(1)} %copy-done.2), channel_id=1, source_target_pairs={{0,192},{1,193},{2,194},{3,195},{4,196},{5,197},{6,198},{7,199},{8... | collective-permute-start | bytes 32 | tf_op jit(solution)/shard_map/ppermute | solution.py:358
  24.1 16.7 %collective-permute-start.6 = (f32[3,32,512]{2,1,0:T(8,128)S(1)}, f32[3,32,512]{2,1,0:T(8,128)S(1)}, u32[]{:S(2)}, u32[]{:S(2)}) collective-permute-start(f32[3,32,512]{2,1,0:T(8,128)S(1)} %get-tuple-element.34), channel_id=1, source_target_pairs={{0,1},{1,0},{2,3},{3,2},{4,5},{5,4},{6,7},{7,6},{8,9},{9,8},{10,11... | collective-permute-start | bytes 589832 | tf_op jit(solution)/shard_map/ppermute | solution.py:358
  27.7 14.0 %collective-permute-start.7 = (f32[3,32,512]{2,1,0:T(8,128)S(1)}, f32[3,32,512]{2,1,0:T(8,128)S(1)}, u32[]{:S(2)}, u32[]{:S(2)}) collective-permute-start(f32[3,32,512]{2,1,0:T(8,128)S(1)} %get-tuple-element.36), channel_id=1, source_target_pairs={{0,64},{1,2},{2,1},{3,4},{4,3},{5,6},{6,5},{7,8},{8,7},{9,10},{10,... | collective-permute-start | bytes 589832 | tf_op jit(solution)/shard_map/ppermute | solution.py:358
  32.7 7.1 %collective-permute-start.10 = (f32[2,4,8,512]{3,2,1,0:T(8,128)S(1)}, f32[2,4,8,512]{3,2,1,0:T(8,128)S(1)}, u32[]{:S(2)}, u32[]{:S(2)}) collective-permute-start(f32[2,4,8,512]{3,2,1,0:T(8,128)S(1)} %get-tuple-element.43), channel_id=1, source_target_pairs={{0,64},{1,65},{2,66},{3,67},{4,68},{5,69},{6,70},{7,71},{8,72},{9,... | collective-permute-start | bytes 393224 | tf_op jit(solution)/shard_map/ppermute | solution.py:358
  33.3 11.2 %collective-permute-start.9 = (f32[1,32,512]{2,1,0:T(8,128)S(1)}, f32[1,32,512]{2,1,0:T(8,128)S(1)}, u32[]{:S(2)}, u32[]{:S(2)}) collective-permute-start(f32[1,32,512]{2,1,0:T(8,128)S(1)} %get-tuple-element.40), channel_id=1, source_target_pairs={{0,64},{1,2},{2,1},{3,4},{4,3},{5,6},{6,5},{7,8},{8,7},{9,10},{10,... | collective-permute-start | bytes 196616 | tf_op jit(solution)/shard_map/ppermute | solution.py:358
  36.0 9.4 %collective-permute-start.8 = (f32[1,32,512]{2,1,0:T(8,128)S(1)}, f32[1,32,512]{2,1,0:T(8,128)S(1)}, u32[]{:S(2)}, u32[]{:S(2)}) collective-permute-start(f32[1,32,512]{2,1,0:T(8,128)S(1)} %get-tuple-element.39), channel_id=1, source_target_pairs={{0,1},{1,0},{2,3},{3,2},{4,5},{5,4},{6,7},{7,6},{8,9},{9,8},{10,11... | collective-permute-start | bytes 196616 | tf_op jit(solution)/shard_map/ppermute | solution.py:358
  39.8 7.4 %collective-permute-start.11 = (f32[4,8,512]{2,1,0:T(8,128)S(1)}, f32[4,8,512]{2,1,0:T(8,128)S(1)}, u32[]{:S(2)}, u32[]{:S(2)}) collective-permute-start(f32[4,8,512]{2,1,0:T(8,128)S(1)} %get-tuple-element.45), channel_id=1, source_target_pairs={{0,128},{1,129},{2,130},{3,131},{4,132},{5,133},{6,134},{7,135},{8... | collective-permute-start | bytes 196616 | tf_op jit(solution)/shard_map/ppermute | solution.py:358
  42.6 4.6 %collective-permute-start.12 = (f32[4,8,512]{2,1,0:T(8,128)S(1)}, f32[4,8,512]{2,1,0:T(8,128)S(1)}, u32[]{:S(2)}, u32[]{:S(2)}) collective-permute-start(f32[4,8,512]{2,1,0:T(8,128)S(1)} %get-tuple-element.47), channel_id=1, source_target_pairs={{0,64},{1,65},{2,66},{3,67},{4,68},{5,69},{6,70},{7,71},{8,72},{9,... | collective-permute-start | bytes 196616 | tf_op jit(solution)/shard_map/ppermute | solution.py:358
  43.6 3.7 %collective-permute-start.13 = (f32[4,8,512]{2,1,0:T(8,128)S(1)}, f32[4,8,512]{2,1,0:T(8,128)S(1)}, u32[]{:S(2)}, u32[]{:S(2)}) collective-permute-start(f32[4,8,512]{2,1,0:T(8,128)S(1)} %get-tuple-element.48), channel_id=1, source_target_pairs={{0,128},{1,129},{2,130},{3,131},{4,132},{5,133},{6,134},{7,135},{8... | collective-permute-start | bytes 196616 | tf_op jit(solution)/shard_map/ppermute | solution.py:358
  44.5 4.4 %collective-permute-start.14 = (f32[4,8,512]{2,1,0:T(8,128)S(1)}, f32[4,8,512]{2,1,0:T(8,128)S(1)}, u32[]{:S(2)}, u32[]{:S(2)}) collective-permute-start(f32[4,8,512]{2,1,0:T(8,128)S(1)} %get-tuple-element.49), channel_id=1, source_target_pairs={{0,192},{1,193},{2,194},{3,195},{4,196},{5,197},{6,198},{7,199},{8... | collective-permute-start | bytes 196616 | tf_op jit(solution)/shard_map/ppermute | solution.py:358

commit v11 on v10

--- a/solution.py
+++ b/solution.py
@@ -169,7 +169,8 @@
 
 
 def first_kernel(blocks, slabs, partner, snaps, snaps_next, state, halo, own_flow, other_flow, velocity, start,
-                 widened, edges, message, rest, now):
+                 widened, edges, message, *scratch):
+    rest, now = scratch if partner == 0 else (None, scratch[0])
     depth, shape = state.shape[1], state.shape[2:]
     last = lax.axis_index("tm") == slabs - 1
     high, sign = side_of(partner)
@@ -298,27 +299,26 @@
         split_rows(whole, pieces)
 
 
-def finish_kernel(blocks, snaps, carried_on, outer_one, outer_two, edges_one, edges_two, rest_one, rest_two,
-                  own_flow, other_flow, velocity, inner, out, final, later, sems):
+def finish_kernel(snaps, carried_on, outer_one, outer_two, edges, rest, own_flow, other_flow, velocity, inner,
+                  out, final, later, sems):
     depth, shape = carried_on.shape[1], carried_on.shape[2:]
-    place = lax.axis_index("space")
-    inside = jnp.logical_and(place > 0, place < blocks - 1)
     fetched = lax.rem(lax.axis_index("tm"), 2)
-    for partner, outer, edges, rest in ((0, outer_one, edges_one, rest_one), (1, outer_two, edges_two, rest_two)):
-        high, sign = side_of(partner)
-        for i, j in tiles(shape):
-            at = (snaps[0, 1],) + spot(i, j)
-            u = jnp.where(high == fetched, own_flow[at], other_flow[at])
-            value = rest[(0,) + spot(i, j)] + (diffusion[1] - (0.25 * sign) * u) * edges[(1, 0) + spot(i, j)]
-            later[(partner,) + spot(i, j)] = value if partner == 0 else jnp.where(inside, value, 0.0)
-
-        def beyond(f, i, j, outer=outer, partner=partner):
-            return later[(partner,) + spot(i, j)] if f == 1 else outer[(0, 0) + spot(i, j)]
+    high, sign = side_of(0)
+    for i, j in tiles(shape):
+        at = (snaps[0, 1],) + spot(i, j)
+        u = jnp.where(high == fetched, own_flow[at], other_flow[at])
+        later[spot(i, j)] = rest[(0,) + spot(i, j)] + (diffusion[1] - (0.25 * sign) * u) * edges[(1, 0) + spot(i, j)]
+
+    def beyond(f, i, j):
+        return later[spot(i, j)] if f == 1 else outer_one[(0, 0) + spot(i, j)]
+
+    for partner, outer in enumerate((outer_one, outer_two)):
+        high, unused = side_of(partner)
 
         def store(k, here, i, j, values, high=high):
             into(final, high * (edge_count - 1) + k * (1 - 2 * high))(i, j, values)
 
-        last_steps(partner, snaps, carried_on, outer, velocity, store, (0, 1), beyond)
+        last_steps(partner, snaps, carried_on, outer, velocity, store, (0, 1), None if partner else beyond)
     copies = [
         pltpu.make_async_copy(final.at[:, pl.ds(0, 2)], out.at[:, pl.ds(0, 2)], sems.at[0]),
         pltpu.make_async_copy(final.at[:, pl.ds(2, 2)], out.at[:, pl.ds(depth - 2, 2)], sems.at[1]),
@@ -401,19 +401,19 @@
         halo_two = exchanged(message_two, 1, 1)
         own_flow = moved(flow_out, fetched)
         other_flow = moved(own_flow, lambda t, s: (t ^ 1, s))
-        widened, edges, halo, halo_rest = [None] * 2, [None] * 2, [halo_one, halo_two], [None] * 2
+        widened, edges, halo, halo_rest = [None] * 2, [None] * 2, [halo_one, halo_two], []
         for partner in (0, 1):
-            widened[partner], edges[partner], message, rest = pl.pallas_call(
+            widened[partner], edges[partner], message, *rest = pl.pallas_call(
                 functools.partial(first_kernel, blocks, slabs, partner),
-                out_shape=(shaped(fields, 4), shaped(fields, 2), shaped(3), shaped(1)),
+                out_shape=(shaped(fields, 4), shaped(fields, 2)) + ((layer,) if partner else (shaped(3), shaped(1))),
                 in_specs=[smem, smem] + [vmem] * 5 + [hbm],
-                out_specs=(vmem,) * 4,
+                out_specs=(vmem,) * (4 - partner),
                 scratch_shapes=[room(fields)],
                 compiler_params=params(32),
                 cost_estimate=cost(1.5),
             )(snap_of_step, snaps_next, state, halo[partner], own_flow, other_flow, velocity, start)
             halo[partner] = exchanged(message, partner, 0)
-            halo_rest[partner] = exchanged(rest, partner, 0)
+            halo_rest += [exchanged(part, partner, 0) for part in rest]
         pair = jax.ShapeDtypeStruct((2,) + pieces[0].shape, jnp.float32)
         carried_on, inner, kept, to_core = pl.pallas_call(
             functools.partial(inner_kernel, slabs),
@@ -457,15 +457,15 @@
             moved(outer_pieces[by], lambda t, s, by=by: (t ^ by, s)) for by in range(1, slabs)
         ]
         final = pl.pallas_call(
-            functools.partial(finish_kernel, blocks),
+            finish_kernel,
             out_shape=shaped(fields, depth),
-            in_specs=[smem] + [vmem] * 10 + [hbm],
+            in_specs=[smem] + [vmem] * 8 + [hbm],
             out_specs=hbm,
-            scratch_shapes=[room(fields, edge_count), room(2), sem((2,))],
-            input_output_aliases={11: 0},
+            scratch_shapes=[room(fields, edge_count), room(), sem((2,))],
+            input_output_aliases={9: 0},
             compiler_params=params(32),
             cost_estimate=cost(1),
-        )(snap_of_step, carried_on, outer_one, outer_two, *edges, *halo_rest, own_flow, other_flow, velocity, inner)
+        )(snap_of_step, carried_on, outer_one, outer_two, edges[0], *halo_rest, own_flow, other_flow, velocity, inner)
         gradient = pl.pallas_call(
             sum_kernel,
             out_shape=shaped(depth, rows=ny // slabs),

time: 49.6 us -> 50.4 us (1.016)
  the two profiles are of different devices: /device:TPU:103 before, /device:TPU:129 now
where the time goes in v11:
time: 50.4 us; the launch traced here: 50.3 us
  starting transfers between devices  23.9 us (47%)
  Pallas kernels  13.4 us (27%)
  waiting for transfers between devices  12.3 us (24%)
  between operations  0.76 us (2%)
    ppermute x14, starting transfers between devices, moved(): return lax.ppermute(array, ('tm', 'space'), pairs)  23.9 us
    ppermute x14, waiting for transfers between devices, moved(): return lax.ppermute(array, ('tm', 'space'), pairs)  12.3 us
    pallas_call x1, Pallas kernels, body(): pl.pallas_call(functools.partial(inner_kernel, slabs), out_shape=(shaped(...  3.87 us
    pallas_call x1, Pallas kernels, body(): pl.pallas_call(start_kernel, out_shape=(layer, layer, shaped(velocity.sha...  2.7 us
    pallas_call x2, Pallas kernels, body(): pl.pallas_call(functools.partial(first_kernel, blocks, slabs, partner), o...  2.57 us
    pallas_call x1, Pallas kernels, body(): pl.pallas_call(finish_kernel, out_shape=shaped(fields, depth), in_specs=[...  1.84 us
  transfers between devices with their start and end apart: 14, of which 6 were waited for; matrix products, arithmetic and copies ran while one was open for 0% of the time, Pallas kernels for 25%

profile of v11, /device:TPU:129, one launch (start us, length us, event | category | flops | bytes accessed | tf_op | source)
XLA Modules:
  0.0 50.3 jit_solution(2040724132663768827)
XLA Ops:
  0.7 0.8 %collective-permute-start.1 = (f32[2,8,32,512]{3,2,1,0:T(8,128)}, f32[2,8,32,512]{3,2,1,0:T(8,128)S(1)}, u32[]{:S(2)}, u32[]{:S(2)}) collective-permute-start(f32[2,8,32,512]{3,2,1,0:T(8,128)} %bitcast.2), channel_id=1, source_target_pairs={{0,192},{1,193},{2,194},{3,195},{4,196},{5,197},{6,198},{7,199},{8... | collective-permute-start | bytes 3145736 | tf_op jit(solution)/shard_map/ppermute | solution.py:358
  1.4 2.7 %shard_map.50 = (f32[4,32,512]{2,1,0:T(8,128)}, f32[4,32,512]{2,1,0:T(8,128)}, f32[2,32,512]{2,1,0:T(8,128)}) custom-call(s32[1,2]{1,0:T(1,128)} %snaps.13, f32[2,8,32,512]{3,2,1,0:T(8,128)} %bitcast.3, f32[2,3,8,32,512]{4,3,2,1,0:T(8,128)} %velocity.13), custom_call_target="tpu_custom_call" | custom-call | bytes 7200000 | tf_op jit(solution)/shard_map/pallas_call | solution.py:386
  4.1 4.5 %collective-permute-start.3 = (f32[2,32,512]{2,1,0:T(8,128)}, f32[2,32,512]{2,1,0:T(8,128)S(1)}, u32[]{:S(2)}, u32[]{:S(2)}) collective-permute-start(f32[2,32,512]{2,1,0:T(8,128)} %get-tuple-element.26), channel_id=1, source_target_pairs={{0,129},{1,130},{2,131},{3,132},{4,133},{5,134},{6,135},{7,136},{8... | collective-permute-start | bytes 393224 | tf_op jit(solution)/shard_map/ppermute | solution.py:358
  8.7 2.8 %collective-permute-start.5 = (f32[4,32,512]{2,1,0:T(8,128)}, f32[4,32,512]{2,1,0:T(8,128)S(1)}, u32[]{:S(2)}, u32[]{:S(2)}) collective-permute-start(f32[4,32,512]{2,1,0:T(8,128)} %get-tuple-element.28), channel_id=1, source_target_pairs={{0,64},{1,194},{2,193},{3,196},{4,195},{5,198},{6,197},{7,200},{8,... | collective-permute-start | bytes 786440 | tf_op jit(solution)/shard_map/ppermute | solution.py:358
  11.4 0.2 collective-permute-done.3.own_flow
  11.7 6.6 %collective-permute-start.4 = (f32[2,32,512]{2,1,0:T(8,128)S(1)}, f32[2,32,512]{2,1,0:T(8,128)S(1)}, u32[]{:S(2)}, u32[]{:S(2)}) collective-permute-start(f32[2,32,512]{2,1,0:T(8,128)S(1)} %collective-permute-done.3.own_flow), channel_id=1, source_target_pairs={{0,64},{1,65},{2,66},{3,67},{4,68},{5,69},{6,70},{7,71},{8,72},{9,... | collective-permute-start | bytes 393224 | tf_op jit(solution)/shard_map/ppermute | solution.py:358
  18.2 3.3 %collective-permute-done.snaps_next = s32[1,2]{1,0:T(1,128)S(1)} collective-permute-done((s32[1,2]{1,0:T(1,128)S(1)}, s32[1,2]{1,0:T(1,128)S(1)}, u32[]{:S(2)}, u32[]{:S(2)}) %collective-permute-start) | collective-permute-done | bytes 40 | tf_op jit(solution)/shard_map/ppermute | solution.py:358
  21.5 1.3 %collective-permute-done.5.halo = f32[4,32,512]{2,1,0:T(8,128)S(1)} collective-permute-done((f32[4,32,512]{2,1,0:T(8,128)}, f32[4,32,512]{2,1,0:T(8,128)S(1)}, u32[]{:S(2)}, u32[]{:S(2)}) %collective-permute-start.5) | collective-permute-done | bytes 262176 | tf_op jit(solution)/shard_map/ppermute | solution.py:358
  22.8 1.3 %shard_map.52 = (f32[2,4,32,512]{3,2,1,0:T(8,128)S(1)}, f32[2,2,32,512]{3,2,1,0:T(8,128)S(1)}, f32[4,32,512]{2,1,0:T(8,128)S(1)}) custom-call(s32[1,2]{1,0:T(1,128)S(1)} %copy-done.2, s32[1,2]{1,0:T(1,128)S(1)} %collective-permute-done.snaps_next, f32[2,8,32,512]{3,2,1,0:T(8,128)S(1)} %collective-permute-done.1.state.before, ...), custom_call_target="tpu_custom_call" | custom-call | bytes 5400000 | tf_op jit(solution)/shard_map/pallas_call | solution.py:406
  24.1 3.2 %collective-permute-start.7 = (f32[4,32,512]{2,1,0:T(8,128)S(1)}, f32[4,32,512]{2,1,0:T(8,128)S(1)}, u32[]{:S(2)}, u32[]{:S(2)}) collective-permute-start(f32[4,32,512]{2,1,0:T(8,128)S(1)} %get-tuple-element.35), channel_id=1, source_target_pairs={{0,64},{1,2},{2,1},{3,4},{4,3},{5,6},{6,5},{7,8},{8,7},{9,10},{10,... | collective-permute-start | bytes 786440 | tf_op jit(solution)/shard_map/ppermute | solution.py:358
  27.3 1.3 %shard_map.51 = (f32[2,4,32,512]{3,2,1,0:T(8,128)S(1)}, f32[2,2,32,512]{3,2,1,0:T(8,128)S(1)}, f32[3,32,512]{2,1,0:T(8,128)S(1)}, f32[1,32,512]{2,1,0:T(8,128)S(1)}) custom-call(s32[1,2]{1,0:T(1,128)S(1)} %copy-done.2, s32[1,2]{1,0:T(1,128)S(1)} %collective-permute-done.snaps_next, f32[2,8,32,512]{3,2,1,0:T(8,128)S(1)} %collective-permute-done.1.state.before, ...), custom_call_target="tpu_custom_call" | custom-call | bytes 5400000 | tf_op jit(solution)/shard_map/pallas_call | solution.py:406
  28.6 0.1 collective-permute-start.6
  28.7 3.9 %shard_map.53 = (f32[2,8,32,512]{3,2,1,0:T(8,128)S(1)}, f32[2,8,32,512]{3,2,1,0:T(8,128)}, f32[2,4,8,512]{3,2,1,0:T(8,128)S(1)}, f32[2,4,8,512]{3,2,1,0:T(8,128)S(1)}) custom-call(s32[1,2]{1,0:T(1,128)S(1)} %copy-done.2, s32[1,2]{1,0:T(1,128)S(1)} %collective-permute-done.snaps_next, f32[2,8,32,512]{3,2,1,0:T(8,128)S(1)} %collective-permute-done.1.state.before, ...), custom_call_target="tpu_custom_call" | custom-call | bytes 10800000 | tf_op jit(solution)/shard_map/pallas_call | solution.py:418
  32.6 0.1 collective-permute-start.9
  32.7 3.2 %collective-permute-start.8 = (f32[1,32,512]{2,1,0:T(8,128)S(1)}, f32[1,32,512]{2,1,0:T(8,128)S(1)}, u32[]{:S(2)}, u32[]{:S(2)}) collective-permute-start(f32[1,32,512]{2,1,0:T(8,128)S(1)} %get-tuple-element.38), channel_id=1, source_target_pairs={{0,1},{1,0},{2,3},{3,2},{4,5},{5,4},{6,7},{7,6},{8,9},{9,8},{10,11... | collective-permute-start | bytes 196616 | tf_op jit(solution)/shard_map/ppermute | solution.py:358
  35.9 0.4 collective-permute-start.10
  36.3 5.8 %collective-permute-done.6.halo = f32[3,32,512]{2,1,0:T(8,128)S(1)} collective-permute-done((f32[3,32,512]{2,1,0:T(8,128)S(1)}, f32[3,32,512]{2,1,0:T(8,128)S(1)}, u32[]{:S(2)}, u32[]{:S(2)}) %collective-permute-start.6) | collective-permute-done | bytes 196640 | tf_op jit(solution)/shard_map/ppermute | solution.py:358
  42.1 0.8 %shard_map.54 = (f32[2,2,32,512]{3,2,1,0:T(8,128)S(1)}, f32[2,32,512]{2,1,0:T(8,128)S(1)}) custom-call(s32[1,2]{1,0:T(1,128)S(1)} %copy-done.2, f32[2,2,32,512]{3,2,1,0:T(8,128)S(1)} %get-tuple-element.30.edges_one.edges, f32[3,32,512]{2,1,0:T(8,128)S(1)} %collective-permute-done.6.halo, f32[2,32,512]{2,1,0:T(8,128)S(1)} %collective-permute-done.3.own_flow, ...), custom_call_target="tpu_custom_call" | custom-call | bytes 1800000 | tf_op jit(solution)/shard_map/pallas_call | solution.py:438
  43.0 0.9 %shard_map.55 = (f32[2,2,32,512]{3,2,1,0:T(8,128)S(1)}, f32[4,8,512]{2,1,0:T(8,128)S(1)}, f32[4,8,512]{2,1,0:T(8,128)S(1)}, f32[4,8,512]{2,1,0:T(8,128)S(1)}, f32[4,8,512]{2,1,0:T(8,128)S(1)}) custom-call(s32[1,2]{1,0:T(1,128)S(1)} %copy-done.2, f32[2,2,32,512]{3,2,1,0:T(8,128)S(1)} %get-tuple-element.31.edges_two.edges, ...), custom_call_target="tpu_custom_call" | custom-call | bytes 1800000 | tf_op jit(solution)/shard_map/pallas_call | solution.py:447
  43.8 0.6 %collective-permute-start.11 = (f32[4,8,512]{2,1,0:T(8,128)S(1)}, f32[4,8,512]{2,1,0:T(8,128)S(1)}, u32[]{:S(2)}, u32[]{:S(2)}) collective-permute-start(f32[4,8,512]{2,1,0:T(8,128)S(1)} %get-tuple-element.45), channel_id=1, source_target_pairs={{0,64},{1,65},{2,66},{3,67},{4,68},{5,69},{6,70},{7,71},{8,72},{9,... | collective-permute-start | bytes 196616 | tf_op jit(solution)/shard_map/ppermute | solution.py:358
  44.4 1.7 %collective-permute-start.13 = (f32[4,8,512]{2,1,0:T(8,128)S(1)}, f32[4,8,512]{2,1,0:T(8,128)S(1)}, u32[]{:S(2)}, u32[]{:S(2)}) collective-permute-start(f32[4,8,512]{2,1,0:T(8,128)S(1)} %get-tuple-element.47), channel_id=1, source_target_pairs={{0,192},{1,193},{2,194},{3,195},{4,196},{5,197},{6,198},{7,199},{8... | collective-permute-start | bytes 196616 | tf_op jit(solution)/shard_map/ppermute | solution.py:358
  46.1 1.8 %shard_map.56 = f32[2,8,32,512]{3,2,1,0:T(8,128)} custom-call(s32[1,2]{1,0:T(1,128)S(1)} %copy-done.2, f32[2,8,32,512]{3,2,1,0:T(8,128)S(1)} %get-tuple-element.32.carried_on, f32[2,2,32,512]{3,2,1,0:T(8,128)S(1)} %get-tuple-element.34.outer_one, f32[2,2,32,512]{3,2,1,0:T(8,128)S(1)} %get-tuple-element.37.outer_two, ...), custom_call_target="tpu_custom_call", output_to_operand_aliasing={{}: (9, {})} | custom-call | bytes 3600000 | tf_op jit(solution)/shard_map/pallas_call | solution.py:459
  48.1 1.6 %collective-permute-done.13.refs_3_ = f32[4,8,512]{2,1,0:T(8,128)S(1)} collective-permute-done((f32[4,8,512]{2,1,0:T(8,128)S(1)}, f32[4,8,512]{2,1,0:T(8,128)S(1)}, u32[]{:S(2)}, u32[]{:S(2)}) %collective-permute-start.13) | collective-permute-done | bytes 65568 | tf_op jit(solution)/shard_map/ppermute | solution.py:358
  49.6 0.7 %shard_map.58 = f32[8,8,512]{2,1,0:T(8,128)} custom-call(f32[4,8,512]{2,1,0:T(8,128)S(1)} %get-tuple-element.42.inner, f32[4,8,512]{2,1,0:T(8,128)S(1)} %collective-permute-done.10.inner_across, f32[4,8,512]{2,1,0:T(8,128)S(1)} %get-tuple-element.44.refs_0_, f32[4,8,512]{2,1,0:T(8,128)S(1)} %collective-permute-done.11.refs_1_, ...), custom_call_target="tpu_custom_call" | custom-call | bytes 1800000 | tf_op jit(solution)/shard_map/pallas_call | solution.py:469
  (19 shorter events, 0.1 us)
Async XLA Ops:
  0.6 22.1 %copy-start.1 = (f32[1,2,8,32,512]{4,3,2,1,0:T(8,128)S(1)}, f32[1,2,8,32,512]{4,3,2,1,0:T(8,128)}, u32[]{:S(2)}) copy-start(f32[1,2,8,32,512]{4,3,2,1,0:T(8,128)} %param.3) | copy-start | bytes 3145732
  0.6 17.6 %copy-start.2 = (s32[1,2]{1,0:T(1,128)S(1)}, s32[1,2]{1,0:T(1,128)}, u32[]{:S(2)}) copy-start(s32[1,2]{1,0:T(1,128)} %snaps.13) | copy-start | bytes 28
  0.6 22.1 %copy-start = (f32[2,3,8,32,512]{4,3,2,1,0:T(8,128)S(1)}, f32[2,3,8,32,512]{4,3,2,1,0:T(8,128)}, u32[]{:S(2)}) copy-start(f32[2,3,8,32,512]{4,3,2,1,0:T(8,128)} %velocity.13) | copy-start | bytes 9437188
  0.7 22.1 %collective-permute-start.1 = (f32[2,8,32,512]{3,2,1,0:T(8,128)}, f32[2,8,32,512]{3,2,1,0:T(8,128)S(1)}, u32[]{:S(2)}, u32[]{:S(2)}) collective-permute-start(f32[2,8,32,512]{3,2,1,0:T(8,128)} %bitcast.2), channel_id=1, source_target_pairs={{0,192},{1,193},{2,194},{3,195},{4,196},{5,197},{6,198},{7,199},{8... | collective-permute-start | bytes 3145736 | tf_op jit(solution)/shard_map/ppermute | solution.py:358
  4.1 7.6 %collective-permute-start.3 = (f32[2,32,512]{2,1,0:T(8,128)}, f32[2,32,512]{2,1,0:T(8,128)S(1)}, u32[]{:S(2)}, u32[]{:S(2)}) collective-permute-start(f32[2,32,512]{2,1,0:T(8,128)} %get-tuple-element.26), channel_id=1, source_target_pairs={{0,129},{1,130},{2,131},{3,132},{4,133},{5,134},{6,135},{7,136},{8... | collective-permute-start | bytes 393224 | tf_op jit(solution)/shard_map/ppermute | solution.py:358
  8.7 14.1 %collective-permute-start.5 = (f32[4,32,512]{2,1,0:T(8,128)}, f32[4,32,512]{2,1,0:T(8,128)S(1)}, u32[]{:S(2)}, u32[]{:S(2)}) collective-permute-start(f32[4,32,512]{2,1,0:T(8,128)} %get-tuple-element.28), channel_id=1, source_target_pairs={{0,64},{1,194},{2,193},{3,196},{4,195},{5,198},{6,197},{7,200},{8,... | collective-permute-start | bytes 786440 | tf_op jit(solution)/shard_map/ppermute | solution.py:358
  11.4 15.9 %collective-permute-start.2 = (f32[4,32,512]{2,1,0:T(8,128)}, f32[4,32,512]{2,1,0:T(8,128)S(1)}, u32[]{:S(2)}, u32[]{:S(2)}) collective-permute-start(f32[4,32,512]{2,1,0:T(8,128)} %get-tuple-element.25), channel_id=1, source_target_pairs={{0,193},{1,192},{2,195},{3,194},{4,197},{5,196},{6,199},{7,198},{8... | collective-permute-start | bytes 786440 | tf_op jit(solution)/shard_map/ppermute | solution.py:358
  11.7 9.8 %collective-permute-start.4 = (f32[2,32,512]{2,1,0:T(8,128)S(1)}, f32[2,32,512]{2,1,0:T(8,128)S(1)}, u32[]{:S(2)}, u32[]{:S(2)}) collective-permute-start(f32[2,32,512]{2,1,0:T(8,128)S(1)} %collective-permute-done.3.own_flow), channel_id=1, source_target_pairs={{0,64},{1,65},{2,66},{3,67},{4,68},{5,69},{6,70},{7,71},{8,72},{9,... | collective-permute-start | bytes 393224 | tf_op jit(solution)/shard_map/ppermute | solution.py:358
  18.2 3.3 %collective-permute-start = (s32[1,2]{1,0:T(1,128)S(1)}, s32[1,2]{1,0:T(1,128)S(1)}, u32[]{:S(2)}, u32[]{:S(2)}) collective-permute-start(s32[1,2]{1,0:T(1,128)S(1)} %copy-done.2), channel_id=1, source_target_pairs={{0,192},{1,193},{2,194},{3,195},{4,196},{5,197},{6,198},{7,199},{8... | collective-permute-start | bytes 32 | tf_op jit(solution)/shard_map/ppermute | solution.py:358
  24.1 18.9 %collective-permute-start.7 = (f32[4,32,512]{2,1,0:T(8,128)S(1)}, f32[4,32,512]{2,1,0:T(8,128)S(1)}, u32[]{:S(2)}, u32[]{:S(2)}) collective-permute-start(f32[4,32,512]{2,1,0:T(8,128)S(1)} %get-tuple-element.35), channel_id=1, source_target_pairs={{0,64},{1,2},{2,1},{3,4},{4,3},{5,6},{6,5},{7,8},{8,7},{9,10},{10,... | collective-permute-start | bytes 786440 | tf_op jit(solution)/shard_map/ppermute | solution.py:358
  28.6 13.5 %collective-permute-start.6 = (f32[3,32,512]{2,1,0:T(8,128)S(1)}, f32[3,32,512]{2,1,0:T(8,128)S(1)}, u32[]{:S(2)}, u32[]{:S(2)}) collective-permute-start(f32[3,32,512]{2,1,0:T(8,128)S(1)} %get-tuple-element.33), channel_id=1, source_target_pairs={{0,1},{1,0},{2,3},{3,2},{4,5},{5,4},{6,7},{7,6},{8,9},{9,8},{10,11... | collective-permute-start | bytes 589832 | tf_op jit(solution)/shard_map/ppermute | solution.py:358
  32.6 3.3 %collective-permute-start.9 = (f32[2,4,8,512]{3,2,1,0:T(8,128)S(1)}, f32[2,4,8,512]{3,2,1,0:T(8,128)S(1)}, u32[]{:S(2)}, u32[]{:S(2)}) collective-permute-start(f32[2,4,8,512]{3,2,1,0:T(8,128)S(1)} %get-tuple-element.41), channel_id=1, source_target_pairs={{0,64},{1,65},{2,66},{3,67},{4,68},{5,69},{6,70},{7,71},{8,72},{9,... | collective-permute-start | bytes 393224 | tf_op jit(solution)/shard_map/ppermute | solution.py:358
  32.7 13.5 %collective-permute-start.8 = (f32[1,32,512]{2,1,0:T(8,128)S(1)}, f32[1,32,512]{2,1,0:T(8,128)S(1)}, u32[]{:S(2)}, u32[]{:S(2)}) collective-permute-start(f32[1,32,512]{2,1,0:T(8,128)S(1)} %get-tuple-element.38), channel_id=1, source_target_pairs={{0,1},{1,0},{2,3},{3,2},{4,5},{5,4},{6,7},{7,6},{8,9},{9,8},{10,11... | collective-permute-start | bytes 196616 | tf_op jit(solution)/shard_map/ppermute | solution.py:358
  35.9 12.1 %collective-permute-start.10 = (f32[4,8,512]{2,1,0:T(8,128)S(1)}, f32[4,8,512]{2,1,0:T(8,128)S(1)}, u32[]{:S(2)}, u32[]{:S(2)}) collective-permute-start(f32[4,8,512]{2,1,0:T(8,128)S(1)} %get-tuple-element.43), channel_id=1, source_target_pairs={{0,128},{1,129},{2,130},{3,131},{4,132},{5,133},{6,134},{7,135},{8... | collective-permute-start | bytes 196616 | tf_op jit(solution)/shard_map/ppermute | solution.py:358
  43.8 4.1 %collective-permute-start.11 = (f32[4,8,512]{2,1,0:T(8,128)S(1)}, f32[4,8,512]{2,1,0:T(8,128)S(1)}, u32[]{:S(2)}, u32[]{:S(2)}) collective-permute-start(f32[4,8,512]{2,1,0:T(8,128)S(1)} %get-tuple-element.45), channel_id=1, source_target_pairs={{0,64},{1,65},{2,66},{3,67},{4,68},{5,69},{6,70},{7,71},{8,72},{9,... | collective-permute-start | bytes 196616 | tf_op jit(solution)/shard_map/ppermute | solution.py:358
  44.4 3.7 %collective-permute-start.12 = (f32[4,8,512]{2,1,0:T(8,128)S(1)}, f32[4,8,512]{2,1,0:T(8,128)S(1)}, u32[]{:S(2)}, u32[]{:S(2)}) collective-permute-start(f32[4,8,512]{2,1,0:T(8,128)S(1)} %get-tuple-element.46), channel_id=1, source_target_pairs={{0,128},{1,129},{2,130},{3,131},{4,132},{5,133},{6,134},{7,135},{8... | collective-permute-start | bytes 196616 | tf_op jit(solution)/shard_map/ppermute | solution.py:358
  44.4 5.2 %collective-permute-start.13 = (f32[4,8,512]{2,1,0:T(8,128)S(1)}, f32[4,8,512]{2,1,0:T(8,128)S(1)}, u32[]{:S(2)}, u32[]{:S(2)}) collective-permute-start(f32[4,8,512]{2,1,0:T(8,128)S(1)} %get-tuple-element.47), channel_id=1, source_target_pairs={{0,192},{1,193},{2,194},{3,195},{4,196},{5,197},{6,198},{7,199},{8... | collective-permute-start | bytes 196616 | tf_op jit(solution)/shard_map/ppermute | solution.py:358

commit v12 on v8

--- a/solution.py
+++ b/solution.py
@@ -375,7 +375,7 @@
                 room(*velocity.shape[:2], 2),
                 sem((5,)),
             ],
-            compiler_params=params(56),
+            compiler_params=params(53),
             cost_estimate=cost(2),
         )(snap_of_step, start, velocity)
         halo_one = exchanged(message_one, 0, 1)

time: 49 us -> 48.8 us (level)
  waiting for transfers between devices: 11.5 us -> 10.1 us
  starting transfers between devices: 23.1 us -> 24.4 us
  local copies, waits for them, and re-layouts: 0.01 us -> 0.66 us
  Pallas kernels: 13 us -> 12.4 us
    ppermute x14, waiting for transfers between devices: 11.5 us -> 10.1 us  [moved(): return lax.ppermute(array, ('tm', 'space'), pairs)]
    ppermute x14, starting transfers between devices: 23.1 us -> 24.4 us  [moved(): return lax.ppermute(array, ('tm', 'space'), pairs)]
    pallas_call x1, Pallas kernels: 2.3 us -> 1.56 us  [body(): pl.pallas_call(start_kernel, out_shape=(layer, layer, shaped(velocity.sha...]
    unnamed x6, local copies, waits for them, and re-layouts: 0.01 us -> 0.66 us
  transfers between devices with their start and end apart: 14 -> 14, of which waited for: 5 -> 5; matrix products, arithmetic and copies ran while one was open for 0% -> 0% of each run, Pallas kernels for 25% -> 24%
where the time goes in v12:
time: 48.8 us; the launch traced here: 48.3 us
  starting transfers between devices  24.4 us (50%)
  Pallas kernels  12.4 us (25%)
  waiting for transfers between devices  10.1 us (21%)
  between operations  0.76 us (2%)
  local copies, waits for them, and re-layouts  0.66 us (1%)
    ppermute x14, starting transfers between devices, moved(): return lax.ppermute(array, ('tm', 'space'), pairs)  24.4 us
    ppermute x14, waiting for transfers between devices, moved(): return lax.ppermute(array, ('tm', 'space'), pairs)  10.1 us
    pallas_call x1, Pallas kernels, body(): pl.pallas_call(functools.partial(inner_kernel, slabs), out_shape=(shaped(...  3.95 us
    pallas_call x2, Pallas kernels, body(): pl.pallas_call(functools.partial(first_kernel, blocks, slabs, partner), o...  2.62 us
    pallas_call x1, Pallas kernels, body(): pl.pallas_call(finish_kernel, out_shape=shaped(fields, depth), in_specs=[...  1.83 us
    pallas_call x1, Pallas kernels, body(): pl.pallas_call(start_kernel, out_shape=(layer, layer, shaped(velocity.sha...  1.56 us
  transfers between devices with their start and end apart: 14, of which 5 were waited for; matrix products, arithmetic and copies ran while one was open for 0% of the time, Pallas kernels for 24%

profile of v12, /device:TPU:1, one launch (start us, length us, event | category | flops | bytes accessed | tf_op | source)
XLA Modules:
  0.0 48.3 jit_solution(15514010491422740400)
XLA Ops:
  0.6 3.3 %collective-permute-start.1 = (f32[2,8,32,512]{3,2,1,0:T(8,128)}, f32[2,8,32,512]{3,2,1,0:T(8,128)S(1)}, u32[]{:S(2)}, u32[]{:S(2)}) collective-permute-start(f32[2,8,32,512]{3,2,1,0:T(8,128)} %bitcast.2), channel_id=1, source_target_pairs={{0,192},{1,193},{2,194},{3,195},{4,196},{5,197},{6,198},{7,199},{8... | collective-permute-start | bytes 3145736 | tf_op jit(solution)/shard_map/ppermute | solution.py:339
  4.0 0.7 %copy-done.2 = s32[1,2]{1,0:T(1,128)S(1)} copy-done((s32[1,2]{1,0:T(1,128)S(1)}, s32[1,2]{1,0:T(1,128)}, u32[]{:S(2)}) %copy-start.2) | copy-done | bytes 32
  4.6 1.6 %shard_map.50 = (f32[4,32,512]{2,1,0:T(8,128)S(1)}, f32[4,32,512]{2,1,0:T(8,128)S(1)}, f32[2,32,512]{2,1,0:T(8,128)S(1)}) custom-call(s32[1,2]{1,0:T(1,128)S(1)} %copy-done.2, f32[2,8,32,512]{3,2,1,0:T(8,128)} %bitcast.3, f32[2,3,8,32,512]{4,3,2,1,0:T(8,128)} %velocity.13), custom_call_target="tpu_custom_call" | custom-call | bytes 7200000 | tf_op jit(solution)/shard_map/pallas_call | solution.py:367
  6.2 0.6 %collective-permute-start.3 = (f32[2,32,512]{2,1,0:T(8,128)S(1)}, f32[2,32,512]{2,1,0:T(8,128)S(1)}, u32[]{:S(2)}, u32[]{:S(2)}) collective-permute-start(f32[2,32,512]{2,1,0:T(8,128)S(1)} %get-tuple-element.25), channel_id=1, source_target_pairs={{0,129},{1,130},{2,131},{3,132},{4,133},{5,134},{6,135},{7,136},{8... | collective-permute-start | bytes 393224 | tf_op jit(solution)/shard_map/ppermute | solution.py:339
  6.8 2.4 %collective-permute-start.2 = (f32[4,32,512]{2,1,0:T(8,128)S(1)}, f32[4,32,512]{2,1,0:T(8,128)S(1)}, u32[]{:S(2)}, u32[]{:S(2)}) collective-permute-start(f32[4,32,512]{2,1,0:T(8,128)S(1)} %get-tuple-element.24), channel_id=1, source_target_pairs={{0,193},{1,192},{2,195},{3,194},{4,197},{5,196},{6,199},{7,198},{8... | collective-permute-start | bytes 786440 | tf_op jit(solution)/shard_map/ppermute | solution.py:339
  9.2 0.1 collective-permute-start.5
  9.3 2.2 %collective-permute-done.3.own_flow = f32[2,32,512]{2,1,0:T(8,128)S(1)} collective-permute-done((f32[2,32,512]{2,1,0:T(8,128)S(1)}, f32[2,32,512]{2,1,0:T(8,128)S(1)}, u32[]{:S(2)}, u32[]{:S(2)}) %collective-permute-start.3) | collective-permute-done | bytes 131104 | tf_op jit(solution)/shard_map/ppermute | solution.py:339
  11.6 8.8 %collective-permute-start.4 = (f32[2,32,512]{2,1,0:T(8,128)S(1)}, f32[2,32,512]{2,1,0:T(8,128)S(1)}, u32[]{:S(2)}, u32[]{:S(2)}) collective-permute-start(f32[2,32,512]{2,1,0:T(8,128)S(1)} %collective-permute-done.3.own_flow), channel_id=1, source_target_pairs={{0,64},{1,65},{2,66},{3,67},{4,68},{5,69},{6,70},{7,71},{8,72},{9,... | collective-permute-start | bytes 393224 | tf_op jit(solution)/shard_map/ppermute | solution.py:339
  20.4 3.0 %collective-permute-done.snaps_next = s32[1,2]{1,0:T(1,128)S(1)} collective-permute-done((s32[1,2]{1,0:T(1,128)S(1)}, s32[1,2]{1,0:T(1,128)S(1)}, u32[]{:S(2)}, u32[]{:S(2)}) %collective-permute-start) | collective-permute-done | bytes 40 | tf_op jit(solution)/shard_map/ppermute | solution.py:339
  23.4 1.3 %shard_map.51 = (f32[2,4,32,512]{3,2,1,0:T(8,128)S(1)}, f32[2,2,32,512]{3,2,1,0:T(8,128)S(1)}, f32[4,32,512]{2,1,0:T(8,128)S(1)}) custom-call(s32[1,2]{1,0:T(1,128)S(1)} %copy-done.2, s32[1,2]{1,0:T(1,128)S(1)} %collective-permute-done.snaps_next, f32[2,8,32,512]{3,2,1,0:T(8,128)S(1)} %collective-permute-done.1.state.before, ...), custom_call_target="tpu_custom_call" | custom-call | bytes 5400000 | tf_op jit(solution)/shard_map/pallas_call | solution.py:387
  24.7 2.8 %collective-permute-start.6 = (f32[4,32,512]{2,1,0:T(8,128)S(1)}, f32[4,32,512]{2,1,0:T(8,128)S(1)}, u32[]{:S(2)}, u32[]{:S(2)}) collective-permute-start(f32[4,32,512]{2,1,0:T(8,128)S(1)} %get-tuple-element.32), channel_id=1, source_target_pairs={{0,1},{1,0},{2,3},{3,2},{4,5},{5,4},{6,7},{7,6},{8,9},{9,8},{10,11... | collective-permute-start | bytes 786440 | tf_op jit(solution)/shard_map/ppermute | solution.py:339
  27.5 1.3 %shard_map.52 = (f32[2,4,32,512]{3,2,1,0:T(8,128)S(1)}, f32[2,2,32,512]{3,2,1,0:T(8,128)S(1)}, f32[4,32,512]{2,1,0:T(8,128)S(1)}) custom-call(s32[1,2]{1,0:T(1,128)S(1)} %copy-done.2, s32[1,2]{1,0:T(1,128)S(1)} %collective-permute-done.snaps_next, f32[2,8,32,512]{3,2,1,0:T(8,128)S(1)} %collective-permute-done.1.state.before, ...), custom_call_target="tpu_custom_call" | custom-call | bytes 5400000 | tf_op jit(solution)/shard_map/pallas_call | solution.py:387
  28.8 0.9 %collective-permute-start.7 = (f32[4,32,512]{2,1,0:T(8,128)S(1)}, f32[4,32,512]{2,1,0:T(8,128)S(1)}, u32[]{:S(2)}, u32[]{:S(2)}) collective-permute-start(f32[4,32,512]{2,1,0:T(8,128)S(1)} %get-tuple-element.34), channel_id=1, source_target_pairs={{0,64},{1,2},{2,1},{3,4},{4,3},{5,6},{6,5},{7,8},{8,7},{9,10},{10,... | collective-permute-start | bytes 786440 | tf_op jit(solution)/shard_map/ppermute | solution.py:339
  29.8 3.9 %shard_map.53 = (f32[2,8,32,512]{3,2,1,0:T(8,128)S(1)}, f32[2,8,32,512]{3,2,1,0:T(8,128)}, f32[4,8,512]{2,1,0:T(8,128)S(1)}, f32[4,8,512]{2,1,0:T(8,128)S(1)}, f...) custom-call(s32[1,2]{1,0:T(1,128)S(1)} %copy-done.2, s32[1,2]{1,0:T(1,128)S(1)} %collective-permute-done.snaps_next, ...), custom_call_target="tpu_custom_call" | custom-call | bytes 10800000 | tf_op jit(solution)/shard_map/pallas_call | solution.py:397
  33.8 1.4 %collective-permute-start.9 = (f32[4,8,512]{2,1,0:T(8,128)S(1)}, f32[4,8,512]{2,1,0:T(8,128)S(1)}, u32[]{:S(2)}, u32[]{:S(2)}) collective-permute-start(f32[4,8,512]{2,1,0:T(8,128)S(1)} %get-tuple-element.40), channel_id=1, source_target_pairs={{0,128},{1,129},{2,130},{3,131},{4,132},{5,133},{6,134},{7,135},{8... | collective-permute-start | bytes 196616 | tf_op jit(solution)/shard_map/ppermute | solution.py:339
  35.2 3.0 %collective-permute-done.6.halo = f32[4,32,512]{2,1,0:T(8,128)S(1)} collective-permute-done((f32[4,32,512]{2,1,0:T(8,128)S(1)}, f32[4,32,512]{2,1,0:T(8,128)S(1)}, u32[]{:S(2)}, u32[]{:S(2)}) %collective-permute-start.6) | collective-permute-done | bytes 262176 | tf_op jit(solution)/shard_map/ppermute | solution.py:339
  38.2 0.9 %shard_map.54 = (f32[2,2,32,512]{3,2,1,0:T(8,128)S(1)}, f32[2,32,512]{2,1,0:T(8,128)S(1)}) custom-call(s32[1,2]{1,0:T(1,128)S(1)} %copy-done.2, f32[2,2,32,512]{3,2,1,0:T(8,128)S(1)} %get-tuple-element.29.edges_one.edges, f32[4,32,512]{2,1,0:T(8,128)S(1)} %collective-permute-done.6.halo, f32[2,32,512]{2,1,0:T(8,128)S(1)} %collective-permute-done.3.own_flow, ...), custom_call_target="tpu_custom_call" | custom-call | bytes 1800000 | tf_op jit(solution)/shard_map/pallas_call | solution.py:411
  39.1 0.9 %shard_map.55 = (f32[2,2,32,512]{3,2,1,0:T(8,128)S(1)}, f32[4,8,512]{2,1,0:T(8,128)S(1)}, f32[4,8,512]{2,1,0:T(8,128)S(1)}, f32[4,8,512]{2,1,0:T(8,128)S(1)}, f32[4,8,512]{2,1,0:T(8,128)S(1)}) custom-call(s32[1,2]{1,0:T(1,128)S(1)} %copy-done.2, f32[2,2,32,512]{3,2,1,0:T(8,128)S(1)} %get-tuple-element.30.edges_two.edges, ...), custom_call_target="tpu_custom_call" | custom-call | bytes 1800000 | tf_op jit(solution)/shard_map/pallas_call | solution.py:420
  40.0 0.8 %collective-permute-start.11 = (f32[4,8,512]{2,1,0:T(8,128)S(1)}, f32[4,8,512]{2,1,0:T(8,128)S(1)}, u32[]{:S(2)}, u32[]{:S(2)}) collective-permute-start(f32[4,8,512]{2,1,0:T(8,128)S(1)} %get-tuple-element.43), channel_id=1, source_target_pairs={{0,64},{1,65},{2,66},{3,67},{4,68},{5,69},{6,70},{7,71},{8,72},{9,... | collective-permute-start | bytes 196616 | tf_op jit(solution)/shard_map/ppermute | solution.py:339
  40.8 3.1 %collective-permute-start.12 = (f32[4,8,512]{2,1,0:T(8,128)S(1)}, f32[4,8,512]{2,1,0:T(8,128)S(1)}, u32[]{:S(2)}, u32[]{:S(2)}) collective-permute-start(f32[4,8,512]{2,1,0:T(8,128)S(1)} %get-tuple-element.44), channel_id=1, source_target_pairs={{0,128},{1,129},{2,130},{3,131},{4,132},{5,133},{6,134},{7,135},{8... | collective-permute-start | bytes 196616 | tf_op jit(solution)/shard_map/ppermute | solution.py:339
  43.9 1.8 %shard_map.56 = f32[2,8,32,512]{3,2,1,0:T(8,128)} custom-call(s32[1,2]{1,0:T(1,128)S(1)} %copy-done.2, f32[2,8,32,512]{3,2,1,0:T(8,128)S(1)} %get-tuple-element.31.carried_on, f32[2,2,32,512]{3,2,1,0:T(8,128)S(1)} %get-tuple-element.33.outer_one, f32[2,2,32,512]{3,2,1,0:T(8,128)S(1)} %get-tuple-element.36.outer_two, ...), custom_call_target="tpu_custom_call", output_to_operand_aliasing={{}: (5, {})} | custom-call | bytes 3600000 | tf_op jit(solution)/shard_map/pallas_call | solution.py:432
  45.8 1.4 %collective-permute-done.12.refs_6_ = f32[4,8,512]{2,1,0:T(8,128)S(1)} collective-permute-done((f32[4,8,512]{2,1,0:T(8,128)S(1)}, f32[4,8,512]{2,1,0:T(8,128)S(1)}, u32[]{:S(2)}, u32[]{:S(2)}) %collective-permute-start.12) | collective-permute-done | bytes 65568 | tf_op jit(solution)/shard_map/ppermute | solution.py:339
  47.2 0.5 %collective-permute-done.13.refs_7_ = f32[4,8,512]{2,1,0:T(8,128)S(1)} collective-permute-done((f32[4,8,512]{2,1,0:T(8,128)S(1)}, f32[4,8,512]{2,1,0:T(8,128)S(1)}, u32[]{:S(2)}, u32[]{:S(2)}) %collective-permute-start.13) | collective-permute-done | bytes 65568 | tf_op jit(solution)/shard_map/ppermute | solution.py:339
  47.7 0.7 %shard_map.57 = f32[8,8,512]{2,1,0:T(8,128)} custom-call(f32[4,8,512]{2,1,0:T(8,128)S(1)} %get-tuple-element.38.refs_0_, f32[4,8,512]{2,1,0:T(8,128)S(1)} %collective-permute-done.8.refs_1_, f32[4,8,512]{2,1,0:T(8,128)S(1)} %collective-permute-done.9.refs_2_, f32[4,8,512]{2,1,0:T(8,128)S(1)} %collective-permute-done.10.refs_3_, ...), custom_call_target="tpu_custom_call" | custom-call | bytes 1800000 | tf_op jit(solution)/shard_map/pallas_call | solution.py:442
  (18 shorter events, 0.1 us)
Async XLA Ops:
  0.6 22.8 %copy-start.1 = (f32[1,2,8,32,512]{4,3,2,1,0:T(8,128)S(1)}, f32[1,2,8,32,512]{4,3,2,1,0:T(8,128)}, u32[]{:S(2)}) copy-start(f32[1,2,8,32,512]{4,3,2,1,0:T(8,128)} %param.3) | copy-start | bytes 3145732
  0.6 22.8 %copy-start = (f32[2,3,8,32,512]{4,3,2,1,0:T(8,128)S(1)}, f32[2,3,8,32,512]{4,3,2,1,0:T(8,128)}, u32[]{:S(2)}) copy-start(f32[2,3,8,32,512]{4,3,2,1,0:T(8,128)} %velocity.13) | copy-start | bytes 9437188
  0.6 22.7 %collective-permute-start.1 = (f32[2,8,32,512]{3,2,1,0:T(8,128)}, f32[2,8,32,512]{3,2,1,0:T(8,128)S(1)}, u32[]{:S(2)}, u32[]{:S(2)}) collective-permute-start(f32[2,8,32,512]{3,2,1,0:T(8,128)} %bitcast.2), channel_id=1, source_target_pairs={{0,192},{1,193},{2,194},{3,195},{4,196},{5,197},{6,198},{7,199},{8... | collective-permute-start | bytes 3145736 | tf_op jit(solution)/shard_map/ppermute | solution.py:339
  4.0 0.7 %copy-start.2 = (s32[1,2]{1,0:T(1,128)S(1)}, s32[1,2]{1,0:T(1,128)}, u32[]{:S(2)}) copy-start(s32[1,2]{1,0:T(1,128)} %snaps.13) | copy-start | bytes 28
  6.2 5.4 %collective-permute-start.3 = (f32[2,32,512]{2,1,0:T(8,128)S(1)}, f32[2,32,512]{2,1,0:T(8,128)S(1)}, u32[]{:S(2)}, u32[]{:S(2)}) collective-permute-start(f32[2,32,512]{2,1,0:T(8,128)S(1)} %get-tuple-element.25), channel_id=1, source_target_pairs={{0,129},{1,130},{2,131},{3,132},{4,133},{5,134},{6,135},{7,136},{8... | collective-permute-start | bytes 393224 | tf_op jit(solution)/shard_map/ppermute | solution.py:339
  6.8 16.6 %collective-permute-start.2 = (f32[4,32,512]{2,1,0:T(8,128)S(1)}, f32[4,32,512]{2,1,0:T(8,128)S(1)}, u32[]{:S(2)}, u32[]{:S(2)}) collective-permute-start(f32[4,32,512]{2,1,0:T(8,128)S(1)} %get-tuple-element.24), channel_id=1, source_target_pairs={{0,193},{1,192},{2,195},{3,194},{4,197},{5,196},{6,199},{7,198},{8... | collective-permute-start | bytes 786440 | tf_op jit(solution)/shard_map/ppermute | solution.py:339
  9.2 18.3 %collective-permute-start.5 = (f32[4,32,512]{2,1,0:T(8,128)S(1)}, f32[4,32,512]{2,1,0:T(8,128)S(1)}, u32[]{:S(2)}, u32[]{:S(2)}) collective-permute-start(f32[4,32,512]{2,1,0:T(8,128)S(1)} %get-tuple-element.27), channel_id=1, source_target_pairs={{0,64},{1,194},{2,193},{3,196},{4,195},{5,198},{6,197},{7,200},{8,... | collective-permute-start | bytes 786440 | tf_op jit(solution)/shard_map/ppermute | solution.py:339
  11.6 11.8 %collective-permute-start.4 = (f32[2,32,512]{2,1,0:T(8,128)S(1)}, f32[2,32,512]{2,1,0:T(8,128)S(1)}, u32[]{:S(2)}, u32[]{:S(2)}) collective-permute-start(f32[2,32,512]{2,1,0:T(8,128)S(1)} %collective-permute-done.3.own_flow), channel_id=1, source_target_pairs={{0,64},{1,65},{2,66},{3,67},{4,68},{5,69},{6,70},{7,71},{8,72},{9,... | collective-permute-start | bytes 393224 | tf_op jit(solution)/shard_map/ppermute | solution.py:339
  20.4 3.0 %collective-permute-start = (s32[1,2]{1,0:T(1,128)S(1)}, s32[1,2]{1,0:T(1,128)S(1)}, u32[]{:S(2)}, u32[]{:S(2)}) collective-permute-start(s32[1,2]{1,0:T(1,128)S(1)} %copy-done.2), channel_id=1, source_target_pairs={{0,192},{1,193},{2,194},{3,195},{4,196},{5,197},{6,198},{7,199},{8... | collective-permute-start | bytes 32 | tf_op jit(solution)/shard_map/ppermute | solution.py:339
  24.7 13.5 %collective-permute-start.6 = (f32[4,32,512]{2,1,0:T(8,128)S(1)}, f32[4,32,512]{2,1,0:T(8,128)S(1)}, u32[]{:S(2)}, u32[]{:S(2)}) collective-permute-start(f32[4,32,512]{2,1,0:T(8,128)S(1)} %get-tuple-element.32), channel_id=1, source_target_pairs={{0,1},{1,0},{2,3},{3,2},{4,5},{5,4},{6,7},{7,6},{8,9},{9,8},{10,11... | collective-permute-start | bytes 786440 | tf_op jit(solution)/shard_map/ppermute | solution.py:339
  28.8 10.2 %collective-permute-start.7 = (f32[4,32,512]{2,1,0:T(8,128)S(1)}, f32[4,32,512]{2,1,0:T(8,128)S(1)}, u32[]{:S(2)}, u32[]{:S(2)}) collective-permute-start(f32[4,32,512]{2,1,0:T(8,128)S(1)} %get-tuple-element.34), channel_id=1, source_target_pairs={{0,64},{1,2},{2,1},{3,4},{4,3},{5,6},{6,5},{7,8},{8,7},{9,10},{10,... | collective-permute-start | bytes 786440 | tf_op jit(solution)/shard_map/ppermute | solution.py:339
  33.7 10.2 %collective-permute-start.8 = (f32[4,8,512]{2,1,0:T(8,128)S(1)}, f32[4,8,512]{2,1,0:T(8,128)S(1)}, u32[]{:S(2)}, u32[]{:S(2)}) collective-permute-start(f32[4,8,512]{2,1,0:T(8,128)S(1)} %get-tuple-element.39), channel_id=1, source_target_pairs={{0,64},{1,65},{2,66},{3,67},{4,68},{5,69},{6,70},{7,71},{8,72},{9,... | collective-permute-start | bytes 196616 | tf_op jit(solution)/shard_map/ppermute | solution.py:339
  33.8 11.9 %collective-permute-start.9 = (f32[4,8,512]{2,1,0:T(8,128)S(1)}, f32[4,8,512]{2,1,0:T(8,128)S(1)}, u32[]{:S(2)}, u32[]{:S(2)}) collective-permute-start(f32[4,8,512]{2,1,0:T(8,128)S(1)} %get-tuple-element.40), channel_id=1, source_target_pairs={{0,128},{1,129},{2,130},{3,131},{4,132},{5,133},{6,134},{7,135},{8... | collective-permute-start | bytes 196616 | tf_op jit(solution)/shard_map/ppermute | solution.py:339
  35.2 10.6 %collective-permute-start.10 = (f32[4,8,512]{2,1,0:T(8,128)S(1)}, f32[4,8,512]{2,1,0:T(8,128)S(1)}, u32[]{:S(2)}, u32[]{:S(2)}) collective-permute-start(f32[4,8,512]{2,1,0:T(8,128)S(1)} %get-tuple-element.41), channel_id=1, source_target_pairs={{0,192},{1,193},{2,194},{3,195},{4,196},{5,197},{6,198},{7,199},{8... | collective-permute-start | bytes 196616 | tf_op jit(solution)/shard_map/ppermute | solution.py:339
  40.0 5.8 %collective-permute-start.11 = (f32[4,8,512]{2,1,0:T(8,128)S(1)}, f32[4,8,512]{2,1,0:T(8,128)S(1)}, u32[]{:S(2)}, u32[]{:S(2)}) collective-permute-start(f32[4,8,512]{2,1,0:T(8,128)S(1)} %get-tuple-element.43), channel_id=1, source_target_pairs={{0,64},{1,65},{2,66},{3,67},{4,68},{5,69},{6,70},{7,71},{8,72},{9,... | collective-permute-start | bytes 196616 | tf_op jit(solution)/shard_map/ppermute | solution.py:339
  40.8 6.4 %collective-permute-start.12 = (f32[4,8,512]{2,1,0:T(8,128)S(1)}, f32[4,8,512]{2,1,0:T(8,128)S(1)}, u32[]{:S(2)}, u32[]{:S(2)}) collective-permute-start(f32[4,8,512]{2,1,0:T(8,128)S(1)} %get-tuple-element.44), channel_id=1, source_target_pairs={{0,128},{1,129},{2,130},{3,131},{4,132},{5,133},{6,134},{7,135},{8... | collective-permute-start | bytes 196616 | tf_op jit(solution)/shard_map/ppermute | solution.py:339
  43.9 3.8 %collective-permute-start.13 = (f32[4,8,512]{2,1,0:T(8,128)S(1)}, f32[4,8,512]{2,1,0:T(8,128)S(1)}, u32[]{:S(2)}, u32[]{:S(2)}) collective-permute-start(f32[4,8,512]{2,1,0:T(8,128)S(1)} %get-tuple-element.45), channel_id=1, source_target_pairs={{0,192},{1,193},{2,194},{3,195},{4,196},{5,197},{6,198},{7,199},{8... | collective-permute-start | bytes 196616 | tf_op jit(solution)/shard_map/ppermute | solution.py:339

commit v13 on v11

--- a/solution.py
+++ b/solution.py
@@ -170,7 +170,7 @@
 
 def first_kernel(blocks, slabs, partner, snaps, snaps_next, state, halo, own_flow, other_flow, velocity, start,
                  widened, edges, message, *scratch):
-    rest, now = scratch if partner == 0 else (None, scratch[0])
+    rest, now = scratch if partner == 1 else (None, scratch[0])
     depth, shape = state.shape[1], state.shape[2:]
     last = lax.axis_index("tm") == slabs - 1
     high, sign = side_of(partner)
@@ -299,18 +299,21 @@
         split_rows(whole, pieces)
 
 
-def finish_kernel(snaps, carried_on, outer_one, outer_two, edges, rest, own_flow, other_flow, velocity, inner,
+def finish_kernel(blocks, snaps, carried_on, outer_one, outer_two, edges, rest, own_flow, other_flow, velocity, inner,
                   out, final, later, sems):
     depth, shape = carried_on.shape[1], carried_on.shape[2:]
     fetched = lax.rem(lax.axis_index("tm"), 2)
-    high, sign = side_of(0)
+    place = lax.axis_index("space")
+    inside = jnp.logical_and(place > 0, place < blocks - 1)
+    high, sign = side_of(1)
     for i, j in tiles(shape):
         at = (snaps[0, 1],) + spot(i, j)
         u = jnp.where(high == fetched, own_flow[at], other_flow[at])
-        later[spot(i, j)] = rest[(0,) + spot(i, j)] + (diffusion[1] - (0.25 * sign) * u) * edges[(1, 0) + spot(i, j)]
+        value = rest[(0,) + spot(i, j)] + (diffusion[1] - (0.25 * sign) * u) * edges[(1, 0) + spot(i, j)]
+        later[spot(i, j)] = jnp.where(inside, value, 0.0)
 
     def beyond(f, i, j):
-        return later[spot(i, j)] if f == 1 else outer_one[(0, 0) + spot(i, j)]
+        return later[spot(i, j)] if f == 1 else outer_two[(0, 0) + spot(i, j)]
 
     for partner, outer in enumerate((outer_one, outer_two)):
         high, unused = side_of(partner)
@@ -318,7 +321,7 @@
         def store(k, here, i, j, values, high=high):
             into(final, high * (edge_count - 1) + k * (1 - 2 * high))(i, j, values)
 
-        last_steps(partner, snaps, carried_on, outer, velocity, store, (0, 1), None if partner else beyond)
+        last_steps(partner, snaps, carried_on, outer, velocity, store, (0, 1), beyond if partner else None)
     copies = [
         pltpu.make_async_copy(final.at[:, pl.ds(0, 2)], out.at[:, pl.ds(0, 2)], sems.at[0]),
         pltpu.make_async_copy(final.at[:, pl.ds(2, 2)], out.at[:, pl.ds(depth - 2, 2)], sems.at[1]),
@@ -405,9 +408,9 @@
         for partner in (0, 1):
             widened[partner], edges[partner], message, *rest = pl.pallas_call(
                 functools.partial(first_kernel, blocks, slabs, partner),
-                out_shape=(shaped(fields, 4), shaped(fields, 2)) + ((layer,) if partner else (shaped(3), shaped(1))),
+                out_shape=(shaped(fields, 4), shaped(fields, 2)) + ((shaped(3), shaped(1)) if partner else (layer,)),
                 in_specs=[smem, smem] + [vmem] * 5 + [hbm],
-                out_specs=(vmem,) * (4 - partner),
+                out_specs=(vmem,) * (3 + partner),
                 scratch_shapes=[room(fields)],
                 compiler_params=params(32),
                 cost_estimate=cost(1.5),
@@ -457,7 +460,7 @@
             moved(outer_pieces[by], lambda t, s, by=by: (t ^ by, s)) for by in range(1, slabs)
         ]
         final = pl.pallas_call(
-            finish_kernel,
+            functools.partial(finish_kernel, blocks),
             out_shape=shaped(fields, depth),
             in_specs=[smem] + [vmem] * 8 + [hbm],
             out_specs=hbm,
@@ -465,7 +468,7 @@
             input_output_aliases={9: 0},
             compiler_params=params(32),
             cost_estimate=cost(1),
-        )(snap_of_step, carried_on, outer_one, outer_two, edges[0], *halo_rest, own_flow, other_flow, velocity, inner)
+        )(snap_of_step, carried_on, outer_one, outer_two, edges[1], *halo_rest, own_flow, other_flow, velocity, inner)
         gradient = pl.pallas_call(
             sum_kernel,
             out_shape=shaped(depth, rows=ny // slabs),

time: 50.4 us -> 48.5 us (0.962)
  the two profiles are of different devices: /device:TPU:129 before, /device:TPU:1 now
where the time goes in v13:
time: 48.5 us; the launch traced here: 47.7 us
  starting transfers between devices  23.3 us (48%)
  Pallas kernels  13 us (27%)
  waiting for transfers between devices  10.6 us (22%)
  between operations  0.76 us (2%)
    ppermute x14, starting transfers between devices, moved(): return lax.ppermute(array, ('tm', 'space'), pairs)  23.3 us
    ppermute x14, waiting for transfers between devices, moved(): return lax.ppermute(array, ('tm', 'space'), pairs)  10.6 us
    pallas_call x1, Pallas kernels, body(): pl.pallas_call(functools.partial(inner_kernel, slabs), out_shape=(shaped(...  3.86 us
    pallas_call x2, Pallas kernels, body(): pl.pallas_call(functools.partial(first_kernel, blocks, slabs, partner), o...  2.57 us
    pallas_call x1, Pallas kernels, body(): pl.pallas_call(start_kernel, out_shape=(layer, layer, shaped(velocity.sha...  2.3 us
    pallas_call x1, Pallas kernels, body(): pl.pallas_call(functools.partial(finish_kernel, blocks), out_shape=shaped...  1.85 us
  transfers between devices with their start and end apart: 14, of which 5 were waited for; matrix products, arithmetic and copies ran while one was open for 0% of the time, Pallas kernels for 26%

profile of v13, /device:TPU:1, one launch (start us, length us, event | category | flops | bytes accessed | tf_op | source)
XLA Modules:
  0.0 47.7 jit_solution(4001333877969369334)
XLA Ops:
  0.7 3.3 %collective-permute-start.1 = (f32[2,8,32,512]{3,2,1,0:T(8,128)}, f32[2,8,32,512]{3,2,1,0:T(8,128)S(1)}, u32[]{:S(2)}, u32[]{:S(2)}) collective-permute-start(f32[2,8,32,512]{3,2,1,0:T(8,128)} %bitcast.2), channel_id=1, source_target_pairs={{0,192},{1,193},{2,194},{3,195},{4,196},{5,197},{6,198},{7,199},{8... | collective-permute-start | bytes 3145736 | tf_op jit(solution)/shard_map/ppermute | solution.py:361
  4.0 2.3 %shard_map.50 = (f32[4,32,512]{2,1,0:T(8,128)}, f32[4,32,512]{2,1,0:T(8,128)}, f32[2,32,512]{2,1,0:T(8,128)}) custom-call(s32[1,2]{1,0:T(1,128)} %snaps.13, f32[2,8,32,512]{3,2,1,0:T(8,128)} %bitcast.3, f32[2,3,8,32,512]{4,3,2,1,0:T(8,128)} %velocity.13), custom_call_target="tpu_custom_call" | custom-call | bytes 7200000 | tf_op jit(solution)/shard_map/pallas_call | solution.py:389
  6.3 0.2 collective-permute-start.3
  6.5 2.4 %collective-permute-start.2 = (f32[4,32,512]{2,1,0:T(8,128)}, f32[4,32,512]{2,1,0:T(8,128)S(1)}, u32[]{:S(2)}, u32[]{:S(2)}) collective-permute-start(f32[4,32,512]{2,1,0:T(8,128)} %get-tuple-element.25), channel_id=1, source_target_pairs={{0,193},{1,192},{2,195},{3,194},{4,197},{5,196},{6,199},{7,198},{8... | collective-permute-start | bytes 786440 | tf_op jit(solution)/shard_map/ppermute | solution.py:361
  9.0 0.5 collective-permute-start.5
  9.4 3.2 %collective-permute-done.3.own_flow = f32[2,32,512]{2,1,0:T(8,128)S(1)} collective-permute-done((f32[2,32,512]{2,1,0:T(8,128)}, f32[2,32,512]{2,1,0:T(8,128)S(1)}, u32[]{:S(2)}, u32[]{:S(2)}) %collective-permute-start.3) | collective-permute-done | bytes 131104 | tf_op jit(solution)/shard_map/ppermute | solution.py:361
  12.7 8.0 %collective-permute-start.4 = (f32[2,32,512]{2,1,0:T(8,128)S(1)}, f32[2,32,512]{2,1,0:T(8,128)S(1)}, u32[]{:S(2)}, u32[]{:S(2)}) collective-permute-start(f32[2,32,512]{2,1,0:T(8,128)S(1)} %collective-permute-done.3.own_flow), channel_id=1, source_target_pairs={{0,64},{1,65},{2,66},{3,67},{4,68},{5,69},{6,70},{7,71},{8,72},{9,... | collective-permute-start | bytes 393224 | tf_op jit(solution)/shard_map/ppermute | solution.py:361
  20.7 3.0 %collective-permute-done.snaps_next = s32[1,2]{1,0:T(1,128)S(1)} collective-permute-done((s32[1,2]{1,0:T(1,128)S(1)}, s32[1,2]{1,0:T(1,128)S(1)}, u32[]{:S(2)}, u32[]{:S(2)}) %collective-permute-start) | collective-permute-done | bytes 40 | tf_op jit(solution)/shard_map/ppermute | solution.py:361
  23.6 1.3 %shard_map.51 = (f32[2,4,32,512]{3,2,1,0:T(8,128)S(1)}, f32[2,2,32,512]{3,2,1,0:T(8,128)S(1)}, f32[4,32,512]{2,1,0:T(8,128)S(1)}) custom-call(s32[1,2]{1,0:T(1,128)S(1)} %copy-done.2, s32[1,2]{1,0:T(1,128)S(1)} %collective-permute-done.snaps_next, f32[2,8,32,512]{3,2,1,0:T(8,128)S(1)} %collective-permute-done.1.state.before, ...), custom_call_target="tpu_custom_call" | custom-call | bytes 5400000 | tf_op jit(solution)/shard_map/pallas_call | solution.py:409
  24.9 2.8 %collective-permute-start.6 = (f32[4,32,512]{2,1,0:T(8,128)S(1)}, f32[4,32,512]{2,1,0:T(8,128)S(1)}, u32[]{:S(2)}, u32[]{:S(2)}) collective-permute-start(f32[4,32,512]{2,1,0:T(8,128)S(1)} %get-tuple-element.33), channel_id=1, source_target_pairs={{0,1},{1,0},{2,3},{3,2},{4,5},{5,4},{6,7},{7,6},{8,9},{9,8},{10,11... | collective-permute-start | bytes 786440 | tf_op jit(solution)/shard_map/ppermute | solution.py:361
  27.8 1.3 %shard_map.52 = (f32[2,4,32,512]{3,2,1,0:T(8,128)S(1)}, f32[2,2,32,512]{3,2,1,0:T(8,128)S(1)}, f32[3,32,512]{2,1,0:T(8,128)S(1)}, f32[1,32,512]{2,1,0:T(8,128)S(1)}) custom-call(s32[1,2]{1,0:T(1,128)S(1)} %copy-done.2, s32[1,2]{1,0:T(1,128)S(1)} %collective-permute-done.snaps_next, f32[2,8,32,512]{3,2,1,0:T(8,128)S(1)} %collective-permute-done.1.state.before, ...), custom_call_target="tpu_custom_call" | custom-call | bytes 5400000 | tf_op jit(solution)/shard_map/pallas_call | solution.py:409
  29.1 0.8 %collective-permute-start.7 = (f32[3,32,512]{2,1,0:T(8,128)S(1)}, f32[3,32,512]{2,1,0:T(8,128)S(1)}, u32[]{:S(2)}, u32[]{:S(2)}) collective-permute-start(f32[3,32,512]{2,1,0:T(8,128)S(1)} %get-tuple-element.35), channel_id=1, source_target_pairs={{0,64},{1,2},{2,1},{3,4},{4,3},{5,6},{6,5},{7,8},{8,7},{9,10},{10,... | collective-permute-start | bytes 589832 | tf_op jit(solution)/shard_map/ppermute | solution.py:361
  29.9 3.9 %shard_map.53 = (f32[2,8,32,512]{3,2,1,0:T(8,128)S(1)}, f32[2,8,32,512]{3,2,1,0:T(8,128)}, f32[2,4,8,512]{3,2,1,0:T(8,128)S(1)}, f32[2,4,8,512]{3,2,1,0:T(8,128)S(1)}) custom-call(s32[1,2]{1,0:T(1,128)S(1)} %copy-done.2, s32[1,2]{1,0:T(1,128)S(1)} %collective-permute-done.snaps_next, f32[2,8,32,512]{3,2,1,0:T(8,128)S(1)} %collective-permute-done.1.state.before, ...), custom_call_target="tpu_custom_call" | custom-call | bytes 10800000 | tf_op jit(solution)/shard_map/pallas_call | solution.py:421
  33.7 0.1 collective-permute-start.9
  33.8 0.5 %collective-permute-start.8 = (f32[1,32,512]{2,1,0:T(8,128)S(1)}, f32[1,32,512]{2,1,0:T(8,128)S(1)}, u32[]{:S(2)}, u32[]{:S(2)}) collective-permute-start(f32[1,32,512]{2,1,0:T(8,128)S(1)} %get-tuple-element.38), channel_id=1, source_target_pairs={{0,64},{1,2},{2,1},{3,4},{4,3},{5,6},{6,5},{7,8},{8,7},{9,10},{10,... | collective-permute-start | bytes 196616 | tf_op jit(solution)/shard_map/ppermute | solution.py:361
  34.3 0.8 %collective-permute-done.9.from_core = f32[2,4,8,512]{3,2,1,0:T(8,128)S(1)} collective-permute-done((f32[2,4,8,512]{3,2,1,0:T(8,128)S(1)}, f32[2,4,8,512]{3,2,1,0:T(8,128)S(1)}, u32[]{:S(2)}, u32[]{:S(2)}) %collective-permute-start.9) | collective-permute-done | bytes 131104 | tf_op jit(solution)/shard_map/ppermute | solution.py:361
  35.3 1.9 %collective-permute-done.6.halo = f32[4,32,512]{2,1,0:T(8,128)S(1)} collective-permute-done((f32[4,32,512]{2,1,0:T(8,128)S(1)}, f32[4,32,512]{2,1,0:T(8,128)S(1)}, u32[]{:S(2)}, u32[]{:S(2)}) %collective-permute-start.6) | collective-permute-done | bytes 262176 | tf_op jit(solution)/shard_map/ppermute | solution.py:361
  37.2 0.9 %shard_map.54 = (f32[2,2,32,512]{3,2,1,0:T(8,128)S(1)}, f32[2,32,512]{2,1,0:T(8,128)S(1)}) custom-call(s32[1,2]{1,0:T(1,128)S(1)} %copy-done.2, f32[2,2,32,512]{3,2,1,0:T(8,128)S(1)} %get-tuple-element.30.edges_one.edges, f32[4,32,512]{2,1,0:T(8,128)S(1)} %collective-permute-done.6.halo, f32[2,32,512]{2,1,0:T(8,128)S(1)} %collective-permute-done.3.own_flow, ...), custom_call_target="tpu_custom_call" | custom-call | bytes 1800000 | tf_op jit(solution)/shard_map/pallas_call | solution.py:441
  38.1 0.9 %shard_map.55 = (f32[2,2,32,512]{3,2,1,0:T(8,128)S(1)}, f32[4,8,512]{2,1,0:T(8,128)S(1)}, f32[4,8,512]{2,1,0:T(8,128)S(1)}, f32[4,8,512]{2,1,0:T(8,128)S(1)}, f32[4,8,512]{2,1,0:T(8,128)S(1)}) custom-call(s32[1,2]{1,0:T(1,128)S(1)} %copy-done.2, f32[2,2,32,512]{3,2,1,0:T(8,128)S(1)} %get-tuple-element.31.edges_two.edges, ...), custom_call_target="tpu_custom_call" | custom-call | bytes 1800000 | tf_op jit(solution)/shard_map/pallas_call | solution.py:450
  39.0 2.8 %collective-permute-start.11 = (f32[4,8,512]{2,1,0:T(8,128)S(1)}, f32[4,8,512]{2,1,0:T(8,128)S(1)}, u32[]{:S(2)}, u32[]{:S(2)}) collective-permute-start(f32[4,8,512]{2,1,0:T(8,128)S(1)} %get-tuple-element.45), channel_id=1, source_target_pairs={{0,64},{1,65},{2,66},{3,67},{4,68},{5,69},{6,70},{7,71},{8,72},{9,... | collective-permute-start | bytes 196616 | tf_op jit(solution)/shard_map/ppermute | solution.py:361
  41.8 1.7 %collective-permute-start.13 = (f32[4,8,512]{2,1,0:T(8,128)S(1)}, f32[4,8,512]{2,1,0:T(8,128)S(1)}, u32[]{:S(2)}, u32[]{:S(2)}) collective-permute-start(f32[4,8,512]{2,1,0:T(8,128)S(1)} %get-tuple-element.47), channel_id=1, source_target_pairs={{0,192},{1,193},{2,194},{3,195},{4,196},{5,197},{6,198},{7,199},{8... | collective-permute-start | bytes 196616 | tf_op jit(solution)/shard_map/ppermute | solution.py:361
  43.5 1.8 %shard_map.56 = f32[2,8,32,512]{3,2,1,0:T(8,128)} custom-call(s32[1,2]{1,0:T(1,128)S(1)} %copy-done.2, f32[2,8,32,512]{3,2,1,0:T(8,128)S(1)} %get-tuple-element.32.carried_on, f32[2,2,32,512]{3,2,1,0:T(8,128)S(1)} %get-tuple-element.34.outer_one, f32[2,2,32,512]{3,2,1,0:T(8,128)S(1)} %get-tuple-element.37.outer_two, ...), custom_call_target="tpu_custom_call", output_to_operand_aliasing={{}: (9, {})} | custom-call | bytes 3600000 | tf_op jit(solution)/shard_map/pallas_call | solution.py:462
  45.4 1.6 %collective-permute-done.13.refs_3_ = f32[4,8,512]{2,1,0:T(8,128)S(1)} collective-permute-done((f32[4,8,512]{2,1,0:T(8,128)S(1)}, f32[4,8,512]{2,1,0:T(8,128)S(1)}, u32[]{:S(2)}, u32[]{:S(2)}) %collective-permute-start.13) | collective-permute-done | bytes 65568 | tf_op jit(solution)/shard_map/ppermute | solution.py:361
  47.0 0.7 %shard_map.58 = f32[8,8,512]{2,1,0:T(8,128)} custom-call(f32[4,8,512]{2,1,0:T(8,128)S(1)} %get-tuple-element.42.inner, f32[4,8,512]{2,1,0:T(8,128)S(1)} %collective-permute-done.10.inner_across, f32[4,8,512]{2,1,0:T(8,128)S(1)} %get-tuple-element.44.refs_0_, f32[4,8,512]{2,1,0:T(8,128)S(1)} %collective-permute-done.11.refs_1_, ...), custom_call_target="tpu_custom_call" | custom-call | bytes 1800000 | tf_op jit(solution)/shard_map/pallas_call | solution.py:472
  (19 shorter events, 0.2 us)
Async XLA Ops:
  0.6 23.0 %copy-start.1 = (f32[1,2,8,32,512]{4,3,2,1,0:T(8,128)S(1)}, f32[1,2,8,32,512]{4,3,2,1,0:T(8,128)}, u32[]{:S(2)}) copy-start(f32[1,2,8,32,512]{4,3,2,1,0:T(8,128)} %param.3) | copy-start | bytes 3145732
  0.6 20.0 %copy-start.2 = (s32[1,2]{1,0:T(1,128)S(1)}, s32[1,2]{1,0:T(1,128)}, u32[]{:S(2)}) copy-start(s32[1,2]{1,0:T(1,128)} %snaps.13) | copy-start | bytes 28
  0.6 23.0 %copy-start = (f32[2,3,8,32,512]{4,3,2,1,0:T(8,128)S(1)}, f32[2,3,8,32,512]{4,3,2,1,0:T(8,128)}, u32[]{:S(2)}) copy-start(f32[2,3,8,32,512]{4,3,2,1,0:T(8,128)} %velocity.13) | copy-start | bytes 9437188
  0.7 23.0 %collective-permute-start.1 = (f32[2,8,32,512]{3,2,1,0:T(8,128)}, f32[2,8,32,512]{3,2,1,0:T(8,128)S(1)}, u32[]{:S(2)}, u32[]{:S(2)}) collective-permute-start(f32[2,8,32,512]{3,2,1,0:T(8,128)} %bitcast.2), channel_id=1, source_target_pairs={{0,192},{1,193},{2,194},{3,195},{4,196},{5,197},{6,198},{7,199},{8... | collective-permute-start | bytes 3145736 | tf_op jit(solution)/shard_map/ppermute | solution.py:361
  6.3 6.4 %collective-permute-start.3 = (f32[2,32,512]{2,1,0:T(8,128)}, f32[2,32,512]{2,1,0:T(8,128)S(1)}, u32[]{:S(2)}, u32[]{:S(2)}) collective-permute-start(f32[2,32,512]{2,1,0:T(8,128)} %get-tuple-element.26), channel_id=1, source_target_pairs={{0,129},{1,130},{2,131},{3,132},{4,133},{5,134},{6,135},{7,136},{8... | collective-permute-start | bytes 393224 | tf_op jit(solution)/shard_map/ppermute | solution.py:361
  6.5 17.1 %collective-permute-start.2 = (f32[4,32,512]{2,1,0:T(8,128)}, f32[4,32,512]{2,1,0:T(8,128)S(1)}, u32[]{:S(2)}, u32[]{:S(2)}) collective-permute-start(f32[4,32,512]{2,1,0:T(8,128)} %get-tuple-element.25), channel_id=1, source_target_pairs={{0,193},{1,192},{2,195},{3,194},{4,197},{5,196},{6,199},{7,198},{8... | collective-permute-start | bytes 786440 | tf_op jit(solution)/shard_map/ppermute | solution.py:361
  9.0 18.8 %collective-permute-start.5 = (f32[4,32,512]{2,1,0:T(8,128)}, f32[4,32,512]{2,1,0:T(8,128)S(1)}, u32[]{:S(2)}, u32[]{:S(2)}) collective-permute-start(f32[4,32,512]{2,1,0:T(8,128)} %get-tuple-element.28), channel_id=1, source_target_pairs={{0,64},{1,194},{2,193},{3,196},{4,195},{5,198},{6,197},{7,200},{8,... | collective-permute-start | bytes 786440 | tf_op jit(solution)/shard_map/ppermute | solution.py:361
  12.7 11.0 %collective-permute-start.4 = (f32[2,32,512]{2,1,0:T(8,128)S(1)}, f32[2,32,512]{2,1,0:T(8,128)S(1)}, u32[]{:S(2)}, u32[]{:S(2)}) collective-permute-start(f32[2,32,512]{2,1,0:T(8,128)S(1)} %collective-permute-done.3.own_flow), channel_id=1, source_target_pairs={{0,64},{1,65},{2,66},{3,67},{4,68},{5,69},{6,70},{7,71},{8,72},{9,... | collective-permute-start | bytes 393224 | tf_op jit(solution)/shard_map/ppermute | solution.py:361
  20.6 3.0 %collective-permute-start = (s32[1,2]{1,0:T(1,128)S(1)}, s32[1,2]{1,0:T(1,128)S(1)}, u32[]{:S(2)}, u32[]{:S(2)}) collective-permute-start(s32[1,2]{1,0:T(1,128)S(1)} %copy-done.2), channel_id=1, source_target_pairs={{0,192},{1,193},{2,194},{3,195},{4,196},{5,197},{6,198},{7,199},{8... | collective-permute-start | bytes 32 | tf_op jit(solution)/shard_map/ppermute | solution.py:361
  24.9 12.3 %collective-permute-start.6 = (f32[4,32,512]{2,1,0:T(8,128)S(1)}, f32[4,32,512]{2,1,0:T(8,128)S(1)}, u32[]{:S(2)}, u32[]{:S(2)}) collective-permute-start(f32[4,32,512]{2,1,0:T(8,128)S(1)} %get-tuple-element.33), channel_id=1, source_target_pairs={{0,1},{1,0},{2,3},{3,2},{4,5},{5,4},{6,7},{7,6},{8,9},{9,8},{10,11... | collective-permute-start | bytes 786440 | tf_op jit(solution)/shard_map/ppermute | solution.py:361
  29.1 9.0 %collective-permute-start.7 = (f32[3,32,512]{2,1,0:T(8,128)S(1)}, f32[3,32,512]{2,1,0:T(8,128)S(1)}, u32[]{:S(2)}, u32[]{:S(2)}) collective-permute-start(f32[3,32,512]{2,1,0:T(8,128)S(1)} %get-tuple-element.35), channel_id=1, source_target_pairs={{0,64},{1,2},{2,1},{3,4},{4,3},{5,6},{6,5},{7,8},{8,7},{9,10},{10,... | collective-permute-start | bytes 589832 | tf_op jit(solution)/shard_map/ppermute | solution.py:361
  33.7 1.4 %collective-permute-start.9 = (f32[2,4,8,512]{3,2,1,0:T(8,128)S(1)}, f32[2,4,8,512]{3,2,1,0:T(8,128)S(1)}, u32[]{:S(2)}, u32[]{:S(2)}) collective-permute-start(f32[2,4,8,512]{3,2,1,0:T(8,128)S(1)} %get-tuple-element.41), channel_id=1, source_target_pairs={{0,64},{1,65},{2,66},{3,67},{4,68},{5,69},{6,70},{7,71},{8,72},{9,... | collective-permute-start | bytes 393224 | tf_op jit(solution)/shard_map/ppermute | solution.py:361
  33.8 9.6 %collective-permute-start.8 = (f32[1,32,512]{2,1,0:T(8,128)S(1)}, f32[1,32,512]{2,1,0:T(8,128)S(1)}, u32[]{:S(2)}, u32[]{:S(2)}) collective-permute-start(f32[1,32,512]{2,1,0:T(8,128)S(1)} %get-tuple-element.38), channel_id=1, source_target_pairs={{0,64},{1,2},{2,1},{3,4},{4,3},{5,6},{6,5},{7,8},{8,7},{9,10},{10,... | collective-permute-start | bytes 196616 | tf_op jit(solution)/shard_map/ppermute | solution.py:361
  35.2 10.1 %collective-permute-start.10 = (f32[4,8,512]{2,1,0:T(8,128)S(1)}, f32[4,8,512]{2,1,0:T(8,128)S(1)}, u32[]{:S(2)}, u32[]{:S(2)}) collective-permute-start(f32[4,8,512]{2,1,0:T(8,128)S(1)} %get-tuple-element.43), channel_id=1, source_target_pairs={{0,128},{1,129},{2,130},{3,131},{4,132},{5,133},{6,134},{7,135},{8... | collective-permute-start | bytes 196616 | tf_op jit(solution)/shard_map/ppermute | solution.py:361
  39.0 6.4 %collective-permute-start.11 = (f32[4,8,512]{2,1,0:T(8,128)S(1)}, f32[4,8,512]{2,1,0:T(8,128)S(1)}, u32[]{:S(2)}, u32[]{:S(2)}) collective-permute-start(f32[4,8,512]{2,1,0:T(8,128)S(1)} %get-tuple-element.45), channel_id=1, source_target_pairs={{0,64},{1,65},{2,66},{3,67},{4,68},{5,69},{6,70},{7,71},{8,72},{9,... | collective-permute-start | bytes 196616 | tf_op jit(solution)/shard_map/ppermute | solution.py:361
  41.8 3.7 %collective-permute-start.12 = (f32[4,8,512]{2,1,0:T(8,128)S(1)}, f32[4,8,512]{2,1,0:T(8,128)S(1)}, u32[]{:S(2)}, u32[]{:S(2)}) collective-permute-start(f32[4,8,512]{2,1,0:T(8,128)S(1)} %get-tuple-element.46), channel_id=1, source_target_pairs={{0,128},{1,129},{2,130},{3,131},{4,132},{5,133},{6,134},{7,135},{8... | collective-permute-start | bytes 196616 | tf_op jit(solution)/shard_map/ppermute | solution.py:361
  41.8 5.2 %collective-permute-start.13 = (f32[4,8,512]{2,1,0:T(8,128)S(1)}, f32[4,8,512]{2,1,0:T(8,128)S(1)}, u32[]{:S(2)}, u32[]{:S(2)}) collective-permute-start(f32[4,8,512]{2,1,0:T(8,128)S(1)} %get-tuple-element.47), channel_id=1, source_target_pairs={{0,192},{1,193},{2,194},{3,195},{4,196},{5,197},{6,198},{7,199},{8... | collective-permute-start | bytes 196616 | tf_op jit(solution)/shard_map/ppermute | solution.py:361
